TPU v7x, 32 devices: a whole 2x2x4 slice. The times are simulated.
32 devices in a mesh: cell: 4 (over z), gene: 8 (over y, x, core).
Axes of the slice: x: 2, y: 2, z: 4, core: 2. Of those that a mesh axis runs over, the one named last changes fastest.
Arguments:
- genes: bfloat16 [4, 1024, 1120], P('cell', 'gene'), may hold values from -30 to 30
- prefix: bfloat16 [4, 64, 1120], P('cell'), may hold values from -30 to 30
- cot_genes: float32 [4, 1024, 1120], P('cell', 'gene'), may hold values from -6 to 6
- cot_prefix: float32 [4, 64, 1120], P('cell', 'gene'), may hold values from -6 to 6
- w_qkv: bfloat16 [2, 1120, 3360], P(None, 'gene'), may hold values from -0.25 to 0.25
- w_out: bfloat16 [2, 1120, 1120], P(None, 'gene'), may hold values from -0.75 to 0.75
- w_up: bfloat16 [2, 1120, 4480], P(None, 'gene'), may hold values from -0.1875 to 0.1875
- w_down: bfloat16 [2, 4480, 1120], P(None, 'gene'), may hold values from -0.09375 to 0.09375
- norm1_gain: float32 [2, 1120], replicated, may hold values from 0.5 to 1.5
- norm1_bias: float32 [2, 1120], replicated, may hold values from -3 to 3
- norm2_gain: float32 [2, 1120], replicated, may hold values from 0.5 to 1.5
- norm2_bias: float32 [2, 1120], replicated, may hold values from -3 to 3
- bias_q: float32 [2, 1120], replicated, may hold values from -3 to 3
- bias_v: float32 [2, 1120], replicated, may hold values from -3 to 3
- bias_out: float32 [2, 1120], replicated, may hold values from -3 to 3
- bias_up: float32 [2, 4480], replicated, may hold values from -3 to 3
- bias_down: float32 [2, 1120], replicated, may hold values from -3 to 3
Outputs:
- out_genes: float32 [4, 1024, 1120], P('cell', 'gene')
- out_prefix: float32 [4, 64, 1120], P('cell', 'gene')
- grad_genes: float32 [4, 1024, 1120], P('cell', 'gene')
- grad_prefix: float32 [4, 64, 1120], P('cell', 'gene')
- grad_w_qkv: float32 [2, 1120, 3360], P(None, 'gene')
- grad_w_out: float32 [2, 1120, 1120], P(None, 'gene')
- grad_w_up: float32 [2, 1120, 4480], P(None, 'gene')
- grad_w_down: float32 [2, 4480, 1120], P(None, 'gene')
- grad_norm1_gain: float32 [2, 1120], P(None, 'gene')
- grad_norm1_bias: float32 [2, 1120], P(None, 'gene')
- grad_norm2_gain: float32 [2, 1120], P(None, 'gene')
- grad_norm2_bias: float32 [2, 1120], P(None, 'gene')
- grad_bias_q: float32 [2, 1120], P(None, 'gene')
- grad_bias_v: float32 [2, 1120], P(None, 'gene')
- grad_bias_out: float32 [2, 1120], P(None, 'gene')
- grad_bias_up: float32 [2, 4480], P(None, 'gene')
- grad_bias_down: float32 [2, 1120], P(None, 'gene')
All inputs are finite; a program needn't handle non-finite values.
Results may differ from a plain program's by a relative error of at most 0.03.
Values may be sent and summed in bfloat16 or wider, within the bound.
No kernel may reach another device: no remote copies, remote signals or barrier semaphores. Data moves between devices by JAX's collectives and lax.ppermute only.
A program may use at most 512 MiB of HBM per device.

v0:
```python
import jax
import jax.numpy as jnp
from jax import lax
from jax.sharding import PartitionSpec as P

D = 1120
HEADS = 20
HEAD_DIM = 56
PREFIX = 64
LAYERS = 2


def normalize_rows(values, scale_vec, shift_vec):
    average = jnp.mean(values, axis=-1, keepdims=True)
    centred = values - average
    variance = jnp.mean(centred * centred, axis=-1, keepdims=True)
    inverse = lax.rsqrt(variance + 1e-05)
    unit_rows = centred * inverse
    return (unit_rows * scale_vec + shift_vec, unit_rows, inverse)


def normalize_back(grad_norm, scale_vec, unit_rows, inverse):
    scaled = grad_norm * scale_vec
    return inverse * (
        scaled
        - jnp.mean(scaled, axis=-1, keepdims=True)
        - unit_rows * jnp.mean(scaled * unit_rows, axis=-1, keepdims=True)
    )


def smooth_gate(values):
    return jax.nn.gelu(values, approximate=True)


def matmul(left, right):
    return jnp.dot(left, right, preferred_element_type=jnp.float32)


def matmul_right_t(left, right):
    return lax.dot_general(
        left, right, (((1,), (1,)), ((), ())), preferred_element_type=jnp.float32
    )


def matmul_left_t(left, right):
    return lax.dot_general(
        left, right, (((0,), (0,)), ((), ())), preferred_element_type=jnp.float32
    )


def keep_same(running):
    return running


def masked_scores(heads_q, key_block, key_pos, query_pos):
    scores = jnp.einsum(
        "qhd,khd->hqk", heads_q, key_block, preferred_element_type=jnp.float32
    ) * HEAD_DIM ** (-0.5)
    allowed = key_pos[None, None, :] <= query_pos[None, :, None]
    return jnp.where(allowed, scores, -jnp.inf)


def split_blocks(gene_keys, gene_vals):
    total_rows = gene_keys.shape[0]
    block_rows = min(total_rows, 512)
    block_count = total_rows // block_rows
    key_blocks = gene_keys.reshape(block_count, block_rows, HEADS, HEAD_DIM)
    val_blocks = gene_vals.reshape(block_count, block_rows, HEADS, HEAD_DIM)
    block_starts = PREFIX + block_rows * jnp.arange(block_count, dtype=jnp.int32)
    return (key_blocks, val_blocks, block_starts, block_rows)


def attention_forward(heads_q, query_pos, parts, exact):
    pre_keys, pre_vals, gene_keys, gene_vals = parts
    key_blocks, val_blocks, block_starts, block_rows = split_blocks(gene_keys, gene_vals)
    pre_k = pre_keys.reshape(PREFIX, HEADS, HEAD_DIM)
    pre_v = pre_vals.reshape(PREFIX, HEADS, HEAD_DIM)
    pre_pos = jnp.arange(PREFIX, dtype=jnp.int32)
    offsets = jnp.arange(block_rows, dtype=jnp.int32)
    last_query = jnp.max(query_pos)
    prefix_scores = masked_scores(heads_q, pre_k, pre_pos, query_pos)
    row_max = jnp.max(prefix_scores, axis=-1)
    row_sum = jnp.sum(jnp.exp(prefix_scores - row_max[..., None]), axis=-1)

    def stats_step(carry, element):
        key_block, block_start = element

        def stats_visit_block(running):
            old_max, old_sum = running
            scores = masked_scores(heads_q, key_block, block_start + offsets, query_pos)
            new_max = jnp.maximum(old_max, jnp.max(scores, axis=-1))
            new_sum = old_sum * jnp.exp(old_max - new_max) + jnp.sum(
                jnp.exp(scores - new_max[..., None]), axis=-1
            )
            return (new_max, new_sum)

        return (lax.cond(block_start <= last_query, stats_visit_block, keep_same, carry), None)

    (row_max, row_sum), _ = lax.scan(stats_step, (row_max, row_sum), (key_blocks, block_starts))

    def add_block(totals, scores, val_block):
        probs = jnp.exp(scores - row_max[..., None]) / row_sum[..., None]
        low_probs = probs.astype(jnp.bfloat16)
        rounded_sum = totals[0] + jnp.einsum(
            "hqk,khd->qhd", low_probs, val_block, preferred_element_type=jnp.float32
        )
        if exact:
            remainder = (probs - low_probs.astype(jnp.float32)).astype(jnp.bfloat16)
            extra = jnp.einsum(
                "hqk,khd->qhd", remainder, val_block, preferred_element_type=jnp.float32
            )
            return (rounded_sum, totals[1] + extra)
        return (rounded_sum, totals[1])

    zero_heads = jnp.zeros(heads_q.shape, jnp.float32)
    totals = add_block((zero_heads, zero_heads), prefix_scores, pre_v)

    def value_step(carry, element):
        key_block, val_block, block_start = element

        def value_visit_block(running):
            scores = masked_scores(heads_q, key_block, block_start + offsets, query_pos)
            return add_block(running, scores, val_block)

        return (lax.cond(block_start <= last_query, value_visit_block, keep_same, carry), None)

    totals, _ = lax.scan(value_step, totals, (key_blocks, val_blocks, block_starts))
    return (totals[0], totals[0] + totals[1], row_max, row_sum)


def attention_backward(heads_q, query_pos, parts, row_max, row_sum, delta, heads_g):
    pre_keys, pre_vals, gene_keys, gene_vals = parts
    key_blocks, val_blocks, block_starts, block_rows = split_blocks(gene_keys, gene_vals)
    pre_k = pre_keys.reshape(PREFIX, HEADS, HEAD_DIM)
    pre_v = pre_vals.reshape(PREFIX, HEADS, HEAD_DIM)
    pre_pos = jnp.arange(PREFIX, dtype=jnp.int32)
    offsets = jnp.arange(block_rows, dtype=jnp.int32)
    last_query = jnp.max(query_pos)

    def block_grads(query_total, scores, key_block, val_block):
        probs = jnp.exp(scores - row_max[..., None]) / row_sum[..., None]
        prob_grad = jnp.einsum(
            "qhd,khd->hqk", heads_g, val_block, preferred_element_type=jnp.float32
        )
        score_grad = (probs * (prob_grad - delta[..., None])).astype(jnp.bfloat16)
        query_total = query_total + jnp.einsum(
            "hqk,khd->qhd", score_grad, key_block, preferred_element_type=jnp.float32
        )
        key_grad = jnp.einsum(
            "hqk,qhd->khd", score_grad, heads_q, preferred_element_type=jnp.float32
        )
        val_grad = jnp.einsum(
            "hqk,qhd->khd", probs.astype(jnp.bfloat16), heads_g, preferred_element_type=jnp.float32
        )
        return (query_total, key_grad, val_grad)

    zero_heads = jnp.zeros(heads_q.shape, jnp.float32)
    prefix_scores = masked_scores(heads_q, pre_k, pre_pos, query_pos)
    query_total, pre_key_grad, pre_val_grad = block_grads(zero_heads, prefix_scores, pre_k, pre_v)

    def grad_step(carry, element):
        key_block, val_block, block_start = element

        def grad_visit_block(running):
            scores = masked_scores(heads_q, key_block, block_start + offsets, query_pos)
            return block_grads(running, scores, key_block, val_block)

        def skip_block(running):
            empty = jnp.zeros((block_rows, HEADS, HEAD_DIM), jnp.float32)
            return (running, empty, empty)

        query_next, key_grad, val_grad = lax.cond(
            block_start <= last_query, grad_visit_block, skip_block, carry
        )
        return (query_next, (key_grad, val_grad))

    query_total, (gene_key_grad, gene_val_grad) = lax.scan(
        grad_step, query_total, (key_blocks, val_blocks, block_starts)
    )
    score_scale = HEAD_DIM ** (-0.5)
    return (
        query_total * score_scale,
        pre_key_grad * score_scale,
        pre_val_grad,
        gene_key_grad * score_scale,
        gene_val_grad,
    )


def body(
    genes,
    prefix,
    cot_genes,
    cot_prefix,
    w_qkv,
    w_out,
    w_up,
    w_down,
    norm1_gain,
    norm1_bias,
    norm2_gain,
    norm2_bias,
    bias_q,
    bias_v,
    bias_out,
    bias_up,
    bias_down,
):
    groups = lax.axis_size("gene")
    position = lax.axis_index("gene")
    gene_rows = genes.shape[1]
    prefix_rows = PREFIX // groups
    prefix_start = position * prefix_rows
    own_prefix = lax.dynamic_slice_in_dim(prefix[0], prefix_start, prefix_rows, 0)
    inputs = jnp.concatenate([own_prefix, genes[0]], 0).astype(jnp.float32)
    query_pos = jnp.concatenate(
        [
            prefix_start + jnp.arange(prefix_rows, dtype=jnp.int32),
            PREFIX + position * gene_rows + jnp.arange(gene_rows, dtype=jnp.int32),
        ]
    )

    def project(rows, weight_qkv, level):
        normed, unit_one, inverse_one = normalize_rows(rows, norm1_gain[level], norm1_bias[level])
        low_one = normed.astype(jnp.bfloat16)
        mixed = matmul(low_one, weight_qkv)
        queries = (mixed[:, :D] + bias_q[level]).astype(jnp.bfloat16)
        key_rows = mixed[:, D : 2 * D].astype(jnp.bfloat16)
        val_rows = (mixed[:, 2 * D :] + bias_v[level]).astype(jnp.bfloat16)
        return (low_one, unit_one, inverse_one, queries, key_rows, val_rows)

    def finish(rows, attn_low, weights, level):
        middle = rows + matmul(attn_low, weights[1]) + bias_out[level]
        normed, unit_two, inverse_two = normalize_rows(middle, norm2_gain[level], norm2_bias[level])
        low_two = normed.astype(jnp.bfloat16)
        pre_act = matmul(low_two, weights[2]) + bias_up[level]
        active = smooth_gate(pre_act).astype(jnp.bfloat16)
        result = middle + matmul(active, weights[3]) + bias_down[level]
        return {
            "middle": middle,
            "unit_two": unit_two,
            "inverse_two": inverse_two,
            "low_two": low_two,
            "pre_act": pre_act,
            "active": active,
            "result": result,
        }

    saved = []
    current = inputs
    for level in range(LAYERS):
        weights = (
            lax.all_gather(w_qkv[level], "gene", axis=0, tiled=True),
            lax.all_gather(w_out[level], "gene", axis=0, tiled=True),
            lax.all_gather(w_up[level], "gene", axis=0, tiled=True),
            lax.all_gather(w_down[level], "gene", axis=0, tiled=True),
        )
        low_one, unit_one, inverse_one, queries, key_rows, val_rows = project(
            current, weights[0], level
        )
        parts = (
            lax.all_gather(key_rows[:prefix_rows], "gene", axis=0, tiled=True),
            lax.all_gather(val_rows[:prefix_rows], "gene", axis=0, tiled=True),
            lax.all_gather(key_rows[prefix_rows:], "gene", axis=0, tiled=True),
            lax.all_gather(val_rows[prefix_rows:], "gene", axis=0, tiled=True),
        )
        heads_q = queries.reshape(queries.shape[0], HEADS, HEAD_DIM)
        attn_sum, unused_exact, unused_max, unused_sum = attention_forward(
            heads_q, query_pos, parts, False
        )
        attn_low = attn_sum.reshape(attn_sum.shape[0], D).astype(jnp.bfloat16)
        section_out = finish(current, attn_low, weights, level)
        saved.append((current, weights, parts))
        current = section_out["result"]
    grad = jnp.concatenate([cot_prefix[0], cot_genes[0]], 0)
    layer_grads = [None] * LAYERS
    for level in reversed(range(LAYERS)):
        rows, weights, parts = saved[level]
        weights = (
            lax.all_gather(w_qkv[level], "gene", axis=0, tiled=True),
            lax.all_gather(w_out[level], "gene", axis=0, tiled=True),
            lax.all_gather(w_up[level], "gene", axis=0, tiled=True),
            lax.all_gather(w_down[level], "gene", axis=0, tiled=True),
        )
        low_one, unit_one, inverse_one, queries, key_rows, val_rows = project(
            rows, weights[0], level
        )
        parts = (
            lax.all_gather(key_rows[:prefix_rows], "gene", axis=0, tiled=True),
            lax.all_gather(val_rows[:prefix_rows], "gene", axis=0, tiled=True),
            lax.all_gather(key_rows[prefix_rows:], "gene", axis=0, tiled=True),
            lax.all_gather(val_rows[prefix_rows:], "gene", axis=0, tiled=True),
        )
        heads_q = queries.reshape(queries.shape[0], HEADS, HEAD_DIM)
        attn_sum, attn_exact, row_max, row_sum = attention_forward(heads_q, query_pos, parts, True)
        attn_low = attn_sum.reshape(attn_sum.shape[0], D).astype(jnp.bfloat16)
        section_out = finish(rows, attn_low, weights, level)
        down_grad = grad.astype(jnp.bfloat16)
        g_wdown = matmul_left_t(section_out["active"], down_grad)
        g_bdown = jnp.sum(down_grad.astype(jnp.float32), 0)
        act_grad = matmul_right_t(down_grad, weights[3])
        unused_value, gate_back = jax.vjp(smooth_gate, section_out["pre_act"])
        pre_grad = gate_back(act_grad)[0].astype(jnp.bfloat16)
        g_wup = matmul_left_t(section_out["low_two"], pre_grad)
        g_bup = jnp.sum(pre_grad.astype(jnp.float32), 0)
        norm_grad = matmul_right_t(pre_grad, weights[2])
        g_gain_two = jnp.sum(norm_grad * section_out["unit_two"], 0)
        g_shift_two = jnp.sum(norm_grad, 0)
        middle_grad = grad + normalize_back(
            norm_grad, norm2_gain[level], section_out["unit_two"], section_out["inverse_two"]
        )
        branch_grad = middle_grad.astype(jnp.bfloat16)
        g_wout = matmul_left_t(attn_low, branch_grad)
        g_bout = jnp.sum(branch_grad.astype(jnp.float32), 0)
        attended_grad = matmul_right_t(branch_grad, weights[1]).astype(jnp.bfloat16)
        heads_g = attended_grad.reshape(attended_grad.shape[0], HEADS, HEAD_DIM)
        delta = jnp.einsum("qhd,qhd->hq", heads_g.astype(jnp.float32), attn_exact)
        query_grad, pre_key_grad, pre_val_grad, gene_key_grad, gene_val_grad = attention_backward(
            heads_q, query_pos, parts, row_max, row_sum, delta, heads_g
        )
        shares = (
            lax.psum_scatter(
                pre_key_grad.reshape(PREFIX, D).astype(jnp.bfloat16),
                "gene",
                scatter_dimension=0,
                tiled=True,
            ).astype(jnp.float32),
            lax.psum_scatter(
                pre_val_grad.reshape(PREFIX, D).astype(jnp.bfloat16),
                "gene",
                scatter_dimension=0,
                tiled=True,
            ).astype(jnp.float32),
            lax.psum_scatter(
                gene_key_grad.reshape(-1, D).astype(jnp.bfloat16),
                "gene",
                scatter_dimension=0,
                tiled=True,
            ).astype(jnp.float32),
            lax.psum_scatter(
                gene_val_grad.reshape(-1, D).astype(jnp.bfloat16),
                "gene",
                scatter_dimension=0,
                tiled=True,
            ).astype(jnp.float32),
        )
        key_grad = jnp.concatenate([shares[0], shares[2]], 0)
        val_grad = jnp.concatenate([shares[1], shares[3]], 0)
        qkv_grad = jnp.concatenate(
            [query_grad.reshape(query_grad.shape[0], D), key_grad, val_grad], 1
        ).astype(jnp.bfloat16)
        g_wqkv = matmul_left_t(low_one, qkv_grad)
        qkv_float = qkv_grad.astype(jnp.float32)
        g_bq = jnp.sum(qkv_float[:, :D], 0)
        g_bv = jnp.sum(qkv_float[:, 2 * D :], 0)
        first_grad = matmul_right_t(qkv_grad, weights[0])
        g_gain_one = jnp.sum(first_grad * unit_one, 0)
        g_shift_one = jnp.sum(first_grad, 0)
        grad = middle_grad + normalize_back(first_grad, norm1_gain[level], unit_one, inverse_one)
        layer_grads[level] = (
            g_wqkv,
            g_wout,
            g_wup,
            g_wdown,
            g_gain_one,
            g_shift_one,
            g_gain_two,
            g_shift_two,
            g_bq,
            g_bv,
            g_bout,
            g_bup,
            g_bdown,
        )
    first_set = layer_grads[0]
    second_set = layer_grads[1]
    gene_shares = (
        lax.psum_scatter(
            first_set[0].astype(jnp.bfloat16), "gene", scatter_dimension=0, tiled=True
        ).astype(jnp.float32),
        lax.psum_scatter(
            first_set[1].astype(jnp.bfloat16), "gene", scatter_dimension=0, tiled=True
        ).astype(jnp.float32),
        lax.psum_scatter(
            first_set[2].astype(jnp.bfloat16), "gene", scatter_dimension=0, tiled=True
        ).astype(jnp.float32),
        lax.psum_scatter(
            first_set[3].astype(jnp.bfloat16), "gene", scatter_dimension=0, tiled=True
        ).astype(jnp.float32),
        lax.psum_scatter(
            first_set[4].astype(jnp.bfloat16), "gene", scatter_dimension=0, tiled=True
        ).astype(jnp.float32),
        lax.psum_scatter(
            first_set[5].astype(jnp.bfloat16), "gene", scatter_dimension=0, tiled=True
        ).astype(jnp.float32),
        lax.psum_scatter(
            first_set[6].astype(jnp.bfloat16), "gene", scatter_dimension=0, tiled=True
        ).astype(jnp.float32),
        lax.psum_scatter(
            first_set[7].astype(jnp.bfloat16), "gene", scatter_dimension=0, tiled=True
        ).astype(jnp.float32),
        lax.psum_scatter(
            first_set[8].astype(jnp.bfloat16), "gene", scatter_dimension=0, tiled=True
        ).astype(jnp.float32),
        lax.psum_scatter(
            first_set[9].astype(jnp.bfloat16), "gene", scatter_dimension=0, tiled=True
        ).astype(jnp.float32),
        lax.psum_scatter(
            first_set[10].astype(jnp.bfloat16), "gene", scatter_dimension=0, tiled=True
        ).astype(jnp.float32),
        lax.psum_scatter(
            first_set[11].astype(jnp.bfloat16), "gene", scatter_dimension=0, tiled=True
        ).astype(jnp.float32),
        lax.psum_scatter(
            first_set[12].astype(jnp.bfloat16), "gene", scatter_dimension=0, tiled=True
        ).astype(jnp.float32),
        lax.psum_scatter(
            second_set[0].astype(jnp.bfloat16), "gene", scatter_dimension=0, tiled=True
        ).astype(jnp.float32),
        lax.psum_scatter(
            second_set[1].astype(jnp.bfloat16), "gene", scatter_dimension=0, tiled=True
        ).astype(jnp.float32),
        lax.psum_scatter(
            second_set[2].astype(jnp.bfloat16), "gene", scatter_dimension=0, tiled=True
        ).astype(jnp.float32),
        lax.psum_scatter(
            second_set[3].astype(jnp.bfloat16), "gene", scatter_dimension=0, tiled=True
        ).astype(jnp.float32),
        lax.psum_scatter(
            second_set[4].astype(jnp.bfloat16), "gene", scatter_dimension=0, tiled=True
        ).astype(jnp.float32),
        lax.psum_scatter(
            second_set[5].astype(jnp.bfloat16), "gene", scatter_dimension=0, tiled=True
        ).astype(jnp.float32),
        lax.psum_scatter(
            second_set[6].astype(jnp.bfloat16), "gene", scatter_dimension=0, tiled=True
        ).astype(jnp.float32),
        lax.psum_scatter(
            second_set[7].astype(jnp.bfloat16), "gene", scatter_dimension=0, tiled=True
        ).astype(jnp.float32),
        lax.psum_scatter(
            second_set[8].astype(jnp.bfloat16), "gene", scatter_dimension=0, tiled=True
        ).astype(jnp.float32),
        lax.psum_scatter(
            second_set[9].astype(jnp.bfloat16), "gene", scatter_dimension=0, tiled=True
        ).astype(jnp.float32),
        lax.psum_scatter(
            second_set[10].astype(jnp.bfloat16), "gene", scatter_dimension=0, tiled=True
        ).astype(jnp.float32),
        lax.psum_scatter(
            second_set[11].astype(jnp.bfloat16), "gene", scatter_dimension=0, tiled=True
        ).astype(jnp.float32),
        lax.psum_scatter(
            second_set[12].astype(jnp.bfloat16), "gene", scatter_dimension=0, tiled=True
        ).astype(jnp.float32),
    )
    summed = (
        lax.psum(gene_shares[0].astype(jnp.bfloat16), "cell").astype(jnp.float32),
        lax.psum(gene_shares[1].astype(jnp.bfloat16), "cell").astype(jnp.float32),
        lax.psum(gene_shares[2].astype(jnp.bfloat16), "cell").astype(jnp.float32),
        lax.psum(gene_shares[3].astype(jnp.bfloat16), "cell").astype(jnp.float32),
        lax.psum(gene_shares[4].astype(jnp.bfloat16), "cell").astype(jnp.float32),
        lax.psum(gene_shares[5].astype(jnp.bfloat16), "cell").astype(jnp.float32),
        lax.psum(gene_shares[6].astype(jnp.bfloat16), "cell").astype(jnp.float32),
        lax.psum(gene_shares[7].astype(jnp.bfloat16), "cell").astype(jnp.float32),
        lax.psum(gene_shares[8].astype(jnp.bfloat16), "cell").astype(jnp.float32),
        lax.psum(gene_shares[9].astype(jnp.bfloat16), "cell").astype(jnp.float32),
        lax.psum(gene_shares[10].astype(jnp.bfloat16), "cell").astype(jnp.float32),
        lax.psum(gene_shares[11].astype(jnp.bfloat16), "cell").astype(jnp.float32),
        lax.psum(gene_shares[12].astype(jnp.bfloat16), "cell").astype(jnp.float32),
        lax.psum(gene_shares[13].astype(jnp.bfloat16), "cell").astype(jnp.float32),
        lax.psum(gene_shares[14].astype(jnp.bfloat16), "cell").astype(jnp.float32),
        lax.psum(gene_shares[15].astype(jnp.bfloat16), "cell").astype(jnp.float32),
        lax.psum(gene_shares[16].astype(jnp.bfloat16), "cell").astype(jnp.float32),
        lax.psum(gene_shares[17].astype(jnp.bfloat16), "cell").astype(jnp.float32),
        lax.psum(gene_shares[18].astype(jnp.bfloat16), "cell").astype(jnp.float32),
        lax.psum(gene_shares[19].astype(jnp.bfloat16), "cell").astype(jnp.float32),
        lax.psum(gene_shares[20].astype(jnp.bfloat16), "cell").astype(jnp.float32),
        lax.psum(gene_shares[21].astype(jnp.bfloat16), "cell").astype(jnp.float32),
        lax.psum(gene_shares[22].astype(jnp.bfloat16), "cell").astype(jnp.float32),
        lax.psum(gene_shares[23].astype(jnp.bfloat16), "cell").astype(jnp.float32),
        lax.psum(gene_shares[24].astype(jnp.bfloat16), "cell").astype(jnp.float32),
        lax.psum(gene_shares[25].astype(jnp.bfloat16), "cell").astype(jnp.float32),
    )
    totals = tuple((jnp.stack([summed[member], summed[member + 13]]) for member in range(13)))
    return (
        current[prefix_rows:][None],
        current[:prefix_rows][None],
        grad[prefix_rows:][None],
        grad[:prefix_rows][None],
        totals[0],
        totals[1],
        totals[2],
        totals[3],
        totals[4],
        totals[5],
        totals[6],
        totals[7],
        totals[8],
        totals[9],
        totals[10],
        totals[11],
        totals[12],
    )


def solution(mesh):
    placed = (
        P("cell", "gene", None),
        P("cell", None, None),
        P("cell", "gene", None),
        P("cell", "gene", None),
        P(None, "gene", None),
        P(None, "gene", None),
        P(None, "gene", None),
        P(None, "gene", None),
        P(),
        P(),
        P(),
        P(),
        P(),
        P(),
        P(),
        P(),
        P(),
    )
    return jax.shard_map(
        body,
        mesh=mesh,
        in_specs=placed,
        out_specs=(
            P("cell", "gene", None),
            P("cell", "gene", None),
            P("cell", "gene", None),
            P("cell", "gene", None),
            P(None, "gene", None),
            P(None, "gene", None),
            P(None, "gene", None),
            P(None, "gene", None),
            P(None, "gene"),
            P(None, "gene"),
            P(None, "gene"),
            P(None, "gene"),
            P(None, "gene"),
            P(None, "gene"),
            P(None, "gene"),
            P(None, "gene"),
            P(None, "gene"),
        ),
        check_vma=False,
    )
```

profile of v0, /device:TPU:0, one launch (start us, length us, event | category | flops | bytes accessed | tf_op | source)
XLA Modules:
  0.0 1969.8 jit_solution(2752872127268773059)
XLA Ops:
  7.3 6.5 fusion.418
  15.4 85.7 %all-gather.29.cloned.1.call-done = bf16[1,1120,3360]{2,0,1:T(2,128)(2,1)} async-done(((bf16[1,140,3360]{2,0,1:T(2,128)(2,1)}), bf16[1,1120,3360]{2,0,1:T(2,128)(2,1)}) %all-gather.29.cloned.1.call-update) | async-done | bytes 7526416 | tf_op jit(solution)/shard_map/all_gather | solution.py:253
  101.0 8.2 fusion.421
  119.1 5.0 fusion.417
  132.2 9.2 all_gather.65
  142.6 8.6 all_gather.66
  162.6 9.4 while.126
  164.6 5.5 conditional.24
  173.4 4.6 copy.136
  178.1 6.5 reshape.531
  188.1 9.6 while.127
  190.0 5.4 conditional.25
  197.8 15.2 all-gather.31.cloned.1.call-done
  216.6 60.8 %all-gather.35.cloned.1.call-done = bf16[1,4480,1120]{2,1,0:T(8,128)(2,1)} async-done(((bf16[1,560,1120]{2,1,0:T(8,128)(2,1)}), bf16[1,4480,1120]{2,1,0:T(8,128)(2,1)}) %all-gather.35.cloned.1.call-update) | async-done | bytes 10035216 | tf_op jit(solution)/shard_map/all_gather | solution.py:256
  277.4 106.1 %all-gather.33.cloned.1.call-done = bf16[1,1120,4480]{2,0,1:T(2,128)(2,1)} async-done(((bf16[1,140,4480]{2,0,1:T(2,128)(2,1)}), bf16[1,1120,4480]{2,0,1:T(2,128)(2,1)}) %all-gather.33.cloned.1.call-update) | async-done | bytes 10035216 | tf_op jit(solution)/shard_map/all_gather | solution.py:255
  383.5 14.4 fusion.424
  398.2 71.6 %all-gather.37.cloned.1.call-done = bf16[1,1120,3360]{2,0,1:T(2,128)(2,1)} async-done(((bf16[1,140,3360]{2,0,1:T(2,128)(2,1)}), bf16[1,1120,3360]{2,0,1:T(2,128)(2,1)}) %all-gather.37.cloned.1.call-update) | async-done | bytes 7526416 | tf_op jit(solution)/shard_map/all_gather | solution.py:253
  469.8 7.0 fusion.427
  485.7 9.3 all_gather.73
  496.1 8.7 all_gather.74
  517.4 21.5 %all-gather.27.cloned.1.call-done = bf16[1024,1120]{1,0:T(8,128)(2,1)} async-done(((bf16[128,1120]{1,0:T(8,128)(2,1)}), bf16[1024,1120]{1,0:T(8,128)(2,1)}) %all-gather.27.cloned.1.call-update) | async-done | bytes 2293776 | tf_op jit(solution)/shard_map/all_gather | solution.py:265
  548.2 9.4 while.128
  550.2 5.5 conditional.26
  559.4 12.8 while.130
  561.3 8.7 conditional.28
  573.1 8.3 all-gather.39.cloned.1.call-done
  586.4 101.3 %all-gather.41.cloned.1.call-done = bf16[1,1120,4480]{2,0,1:T(2,128)(2,1)} async-done(((bf16[1,140,4480]{2,0,1:T(2,128)(2,1)}), bf16[1,1120,4480]{2,0,1:T(2,128)(2,1)}) %all-gather.41.cloned.1.call-update) | async-done | bytes 10035216 | tf_op jit(solution)/shard_map/all_gather | solution.py:255
  687.7 10.1 fusion.203
  697.8 54.8 %all-gather.43.cloned.1.call-done = bf16[1,4480,1120]{2,1,0:T(8,128)(2,1)} async-done(((bf16[1,560,1120]{2,1,0:T(8,128)(2,1)}), bf16[1,4480,1120]{2,1,0:T(8,128)(2,1)}) %all-gather.43.cloned.1.call-update) | async-done | bytes 10035216 | tf_op jit(solution)/shard_map/all_gather | solution.py:256
  752.6 8.8 fusion.432
  761.4 11.5 multiply_reduce_fusion
  787.5 19.6 while.131
  789.8 10.5 conditional.29
  826.5 12.7 while.132
  828.4 8.8 conditional.30
  843.5 10.5 fusion.197
  858.7 26.6 %reduce-scatter.37.cloned.1.call-done = bf16[128,1120]{1,0:T(8,128)(2,1)} async-done(((bf16[1024,1120]{1,0:T(8,128)(2,1)}), bf16[128,1120]{1,0:T(8,128)(2,1)}) %reduce-scatter.37.cloned.1.call-update) | async-done | bytes 286736
  886.5 45.1 %reduce-scatter.35.cloned.1.call-done = bf16[128,1120]{1,0:T(8,128)(2,1)} async-done(((bf16[1024,1120]{1,0:T(8,128)(2,1)}), bf16[128,1120]{1,0:T(8,128)(2,1)}) %reduce-scatter.35.cloned.1.call-update) | async-done | bytes 286736
  933.5 9.9 multiply_reduce_fusion.2
  945.1 8.0 fusion.433
  953.1 11.7 multiply_reduce_fusion.1
  977.0 19.5 while.133
  979.0 10.5 conditional.31
  1012.9 9.2 convolution_convert_fusion
  1024.5 9.2 while.129
  1026.4 5.3 conditional.27
  1040.5 6.8 convolution_convert_fusion.2
  1047.3 7.6 convolution_convert_fusion.1
  1056.4 6.8 convolution_convert_fusion.3
  1063.3 155.7 %fusion.20 = bf16[144,4480]{1,0:T(8,128)(2,1)S(1)} fusion(bf16[1120,4480]{1,0:T(8,128)(2,1)} %convolution_convert_fusion.3), kind=kCustom, calls=%all-reduce-scatter.4 | all-reduce-scatter fusion | flops 5160961 | bytes 11325952
  1225.2 6.0 convolution_convert_fusion.4
  1234.9 10.2 concatenate.46
  1248.8 8.9 convolution_convert_fusion.5
  1257.7 348.8 %fusion.414 = (bf16[144,3360]{1,0:T(8,128)(2,1)}, bf16[144,3360]{1,0:T(8,128)(2,1)}, bf16[144,1120]{1,0:T(8,128)(2,1)}, bf16[144,1120]{1,0:T(8,128)(2,1)}, bf16[144,4480]{1,0:T(8,128)(2,1)}) fusion(bf16[1120,3360]{1,0:T(8,128)(2,1)} %convolution_convert_fusion.4, bf16[1120,3360]{1,0:T(8,128)(2,1)} %convolution_convert_fusion.5, ...), kind=kCustom, calls=%all-reduce-scatter.6 | all-reduce-scatter fusion | flops 15482881 | bytes 33976832
  1625.9 4.7 concatenate.45
  1638.0 9.0 concatenate.43
  1647.0 7.2 concatenate.42
  1657.9 10.2 concatenate.47
  1671.9 15.0 fusion.255
  1690.8 8.8 fusion.340
  1703.2 26.8 %all-reduce.34 = (bf16[1120]{0:T(1024)(128)(2,1)S(1)}, bf16[1120]{0:T(1024)(128)(2,1)S(1)}, bf16[1120]{0:T(1024)(128)(2,1)S(1)}, bf16[1120]{0:T(1024)(128)(2,1)S...) all-reduce(bf16[1120]{0:T(1024)(128)(2,1)S(1)} %copy-done.173, ...), channel_id=27, replica_groups=mesh['cell'=4,'gene'=8] {'gene'}, use_global_device_ids=true, to_apply=%region_90.91.clone | all-reduce | flops 26880 | bytes 107520
  1731.5 24.8 %all-reduce.37 = (bf16[1,140]{1,0:T(2,128)(2,1)S(1)}, bf16[1,140]{1,0:T(2,128)(2,1)S(1)}, bf16[1,140]{1,0:T(2,128)(2,1)S(1)}, bf16[1,140]{1,0:T(2,128)(2,1)S(1)}...) all-reduce(bf16[1,140]{1,0:T(2,128)(2,1)S(1)} %stack.199, ...), channel_id=1, replica_groups=mesh['cell'=4,'gene'=8] {'cell'}, use_global_device_ids=true, to_apply=%region_91.92 | all-reduce | flops 3360 | bytes 13440 | tf_op jit(solution)/shard_map/psum | solution.py:475
  1762.2 185.0 %all-reduce.48.cloned.1.call-done = (bf16[1,140,3360]{2,1,0:T(8,128)(2,1)}, bf16[1,140,3360]{2,1,0:T(8,128)(2,1)}, bf16[1,140,1120]{2,1,0:T(8,128)(2,1)}, bf16[1...) async-done(((bf16[1,140,3360]{2,1,0:T(8,128)(2,1)}, ...) | async-done | bytes 7526416 | tf_op jit(solution)/shard_map/psum | solution.py:471
  1955.2 4.9 copy.172
  (736 shorter events, 325.3 us)
Async XLA Ops:
  7.2 93.8 %all-gather.29.cloned.1.call-start = ((), (), s32[]{:S(2)}) async-start(), calls=%async_computation.12 | async-start | bytes 17418240 | tf_op jit(solution)/shard_map/all_gather | solution.py:253
  13.8 139.4 %all-gather.21.cloned.1.call-start = ((), (), s32[]{:S(2)}) async-start(), calls=%async_computation.6 | async-start | bytes 2654208 | tf_op jit(solution)/shard_map/all_gather | solution.py:264
  14.1 199.0 %copy-start.38 = (bf16[1,128,1120]{2,1,0:T(8,128)(2,1)}, bf16[1,128,1120]{2,1,0:T(8,128)(2,1)S(1)}, u32[]{:S(2)}) copy-start(bf16[1,128,1120]{2,1,0:T(8,128)(2,1)S(1)} %copy.130) | copy-start | bytes 860164
  14.1 199.0 %copy-start.97 = (bf16[8,1120]{1,0:T(8,128)(2,1)}, bf16[8,1120]{1,0:T(8,128)(2,1)S(1)}, u32[]{:S(2)}) copy-start(bf16[8,1120]{1,0:T(8,128)(2,1)S(1)} %dynamic-slice_bitcast_fusion.6) | copy-start | bytes 53764
  15.1 94.2 %copy-start.118 = (f32[1120]{0:T(1024)}, f32[1120]{0:T(1024)S(1)}, u32[]{:S(2)}) copy-start(f32[1120]{0:T(1024)S(1)} %get-tuple-element.2077) | copy-start | bytes 13444
  15.1 94.2 %copy-start.157 = (f32[1120]{0:T(1024)}, f32[1120]{0:T(1024)S(1)}, u32[]{:S(2)}) copy-start(f32[1120]{0:T(1024)S(1)} %get-tuple-element.1787) | copy-start | bytes 13444
  15.1 454.7 %copy-start.120 = (f32[1120]{0:T(1024)}, f32[1120]{0:T(1024)S(1)}, u32[]{:S(2)}) copy-start(f32[1120]{0:T(1024)S(1)} %get-tuple-element.2078) | copy-start | bytes 13444
  15.1 94.2 %copy-start.144 = (f32[136]{0:T(256)}, f32[136]{0:T(256)S(1)}, u32[]{:S(2)}) copy-start(f32[136]{0:T(256)S(1)} %broadcast_multiply_fusion.13) | copy-start | bytes 1636
  15.3 93.9 %copy-start.164 = (f32[136]{0:T(256)}, f32[136]{0:T(256)S(1)}, u32[]{:S(2)}) copy-start(f32[136]{0:T(256)S(1)} %add_rsqrt_fusion.5) | copy-start | bytes 1636
  110.2 63.2 %all-gather.23.cloned.1.call-start = ((), (), s32[]{:S(2)}) async-start(), calls=%async_computation.7 | async-start | bytes 2654208 | tf_op jit(solution)/shard_map/all_gather | solution.py:265
  113.2 99.8 %all-gather.31.cloned.1.call-start = ((), (), s32[]{:S(2)}) async-start(), calls=%async_computation.13 | async-start | bytes 5806080 | tf_op jit(solution)/shard_map/all_gather | solution.py:254
  115.3 162.1 %all-gather.35.cloned.1.call-start = ((), (), s32[]{:S(2)}) async-start(), calls=%async_computation.15 | async-start | bytes 11612160 | tf_op jit(solution)/shard_map/all_gather | solution.py:256
  119.0 264.5 %all-gather.33.cloned.1.call-start = ((), (), s32[]{:S(2)}) async-start(), calls=%async_computation.14 | async-start | bytes 22579200 | tf_op jit(solution)/shard_map/all_gather | solution.py:255
  124.1 345.7 %all-gather.37.cloned.1.call-start = ((), (), s32[]{:S(2)}) async-start(), calls=%async_computation.16 | async-start | bytes 17418240 | tf_op jit(solution)/shard_map/all_gather | solution.py:253
  124.9 383.1 %all-gather.25.cloned.1.call-start = ((), (), s32[]{:S(2)}) async-start(), calls=%async_computation.8 | async-start | bytes 2654208 | tf_op jit(solution)/shard_map/all_gather | solution.py:264
  129.3 254.2 %copy-start.106 = (f32[1120]{0:T(1024)}, f32[1120]{0:T(1024)S(1)}, u32[]{:S(2)}) copy-start(f32[1120]{0:T(1024)S(1)} %get-tuple-element.1773) | copy-start | bytes 13444
  130.0 253.5 %copy-start.112 = (f32[1120]{0:T(1024)}, f32[1120]{0:T(1024)S(1)}, u32[]{:S(2)}) copy-start(f32[1120]{0:T(1024)S(1)} %get-tuple-element.2083) | copy-start | bytes 13444
  188.1 24.9 %copy-start.162 = (f32[1120]{0:T(1024)S(1)}, f32[1120]{0:T(1024)}, u32[]{:S(2)}) copy-start(f32[1120]{0:T(1024)} %get-tuple-element.1779) | copy-start | bytes 13444
  197.7 18.6 copy-start.2
  197.7 18.6 copy-start.45
  197.7 18.6 copy-start.90
  213.1 170.4 %copy-start.131 = (f32[4480]{0:T(1024)S(1)}, f32[4480]{0:T(1024)}, u32[]{:S(2)}) copy-start(f32[4480]{0:T(1024)} %get-tuple-element.1771) | copy-start | bytes 53764
  213.1 170.4 %copy-start.163 = (f32[1120]{0:T(1024)S(1)}, f32[1120]{0:T(1024)}, u32[]{:S(2)}) copy-start(f32[1120]{0:T(1024)} %get-tuple-element.1777) | copy-start | bytes 13444
  383.5 86.3 %copy-start.159 = (f32[1120]{0:T(1024)S(1)}, f32[1120]{0:T(1024)}, u32[]{:S(2)}) copy-start(f32[1120]{0:T(1024)} %get-tuple-element.1786) | copy-start | bytes 13444
  398.0 78.8 %copy-start.54 = (f32[136,1120]{1,0:T(8,128)}, f32[136,1120]{1,0:T(8,128)S(1)}, u32[]{:S(2)}) copy-start(f32[136,1120]{1,0:T(8,128)S(1)} %get-tuple-element.2056) | copy-start | bytes 1827844
  398.0 78.8 %copy-start.146 = (f32[136]{0:T(256)}, f32[136]{0:T(256)S(1)}, u32[]{:S(2)}) copy-start(f32[136]{0:T(256)S(1)} %broadcast_multiply_fusion.11) | copy-start | bytes 1636
  398.2 78.6 %copy-start.166 = (f32[136]{0:T(256)}, f32[136]{0:T(256)S(1)}, u32[]{:S(2)}) copy-start(f32[136]{0:T(256)S(1)} %add_rsqrt_fusion.3) | copy-start | bytes 1636
  477.9 60.9 %all-gather.27.cloned.1.call-start = ((), (), s32[]{:S(2)}) async-start(), calls=%async_computation.9 | async-start | bytes 2654208 | tf_op jit(solution)/shard_map/all_gather | solution.py:265
  479.0 102.4 %all-gather.39.cloned.1.call-start = ((), (), s32[]{:S(2)}) async-start(), calls=%async_computation.17 | async-start | bytes 5806080 | tf_op jit(solution)/shard_map/all_gather | solution.py:254
  479.6 208.1 %all-gather.41.cloned.1.call-start = ((), (), s32[]{:S(2)}) async-start(), calls=%async_computation.18 | async-start | bytes 22579200 | tf_op jit(solution)/shard_map/all_gather | solution.py:255
  480.3 272.3 %all-gather.43.cloned.1.call-start = ((), (), s32[]{:S(2)}) async-start(), calls=%async_computation.19 | async-start | bytes 11612160 | tf_op jit(solution)/shard_map/all_gather | solution.py:256
  480.9 374.1 %all-reduce.46.cloned.1.call-start = ((), (), s32[]{:S(2)}) async-start(), calls=%async_computation.25 | async-start | bytes 1146880
  581.4 106.3 %copy-start.104 = (f32[1120]{0:T(1024)S(1)}, f32[1120]{0:T(1024)}, u32[]{:S(2)}) copy-start(f32[1120]{0:T(1024)} %get-tuple-element.1772) | copy-start | bytes 13444
  585.0 187.9 %copy-start.20 = (f32[136,1120]{1,0:T(8,128)}, f32[136,1120]{1,0:T(8,128)S(1)}, u32[]{:S(2)}) copy-start(f32[136,1120]{1,0:T(8,128)S(1)} %get-tuple-element.2064) | copy-start | bytes 1827844
  761.4 13.3 slice-start.2
  761.4 13.2 slice-start.3
  784.7 100.6 %reduce-scatter.37.cloned.1.call-start = ((), (), s32[]{:S(2)}) async-start(), calls=%async_computation.21 | async-start | bytes 2654208
  814.6 117.0 %reduce-scatter.35.cloned.1.call-start = ((), (), s32[]{:S(2)}) async-start(), calls=%async_computation.20 | async-start | bytes 2654208
  823.1 408.1 %all-reduce.44.cloned.1.call-start = ((), (), s32[]{:S(2)}) async-start(), calls=%async_computation.24 | async-start | bytes 1146880
  843.2 121.6 %copy-start.22 = (f32[136,1120]{1,0:T(8,128)}, f32[136,1120]{1,0:T(8,128)S(1)}, u32[]{:S(2)}) copy-start(f32[136,1120]{1,0:T(8,128)S(1)} %get-tuple-element.2068) | copy-start | bytes 1827844
  886.5 56.9 %copy-start.75 = (bf16[128,1120]{0,1:T(8,128)(2,1)}, bf16[128,1120]{0,1:T(8,128)(2,1)S(1)}, u32[]{:S(2)}) copy-start(bf16[128,1120]{0,1:T(8,128)(2,1)S(1)} %copy.196) | copy-start | bytes 860164
  944.4 20.5 %copy-start.52 = (f32[136,1120]{1,0:T(8,128)}, f32[136,1120]{1,0:T(8,128)S(1)}, u32[]{:S(2)}) copy-start(f32[136,1120]{1,0:T(8,128)S(1)} %get-tuple-element.2019) | copy-start | bytes 1827844
  953.1 11.7 copy-start.73
  953.1 12.6 slice-start
  953.1 12.6 slice-start.1
  974.2 270.9 %reduce-scatter.41.cloned.1.call-start = ((), (), s32[]{:S(2)}) async-start(), calls=%async_computation.23 | async-start | bytes 2654208
  1003.8 243.2 %reduce-scatter.39.cloned.1.call-start = ((), (), s32[]{:S(2)}) async-start(), calls=%async_computation.22 | async-start | bytes 2654208
  1012.9 657.9 %reduce-scatter.33.cloned.1.call-start = ((), (), s32[]{:S(2)}) async-start(), calls=%async_computation.11 | async-start | bytes 11612160 | tf_op jit(solution)/shard_map/reduce_scatter | solution.py:426
  1022.2 648.6 %reduce-scatter.31.cloned.1.call-start = ((), (), s32[]{:S(2)}) async-start(), calls=%async_computation.10 | async-start | bytes 11612160 | tf_op jit(solution)/shard_map/reduce_scatter | solution.py:387
  1055.0 892.3 %all-reduce.48.cloned.1.call-start = ((), (), s32[]{:S(2)}) async-start(), calls=%async_computation.26 | async-start | bytes 15630336 | tf_op jit(solution)/shard_map/psum | solution.py:471
  1063.3 158.5 %copy-start.11 = (f32[136,20,56]{0,2,1:T(8,128)S(1)}, f32[136,20,56]{0,2,1:T(8,128)}, u32[]{:S(2)}) copy-start(f32[136,20,56]{0,2,1:T(8,128)} %get-tuple-element.1236) | copy-start | bytes 1827844
  1219.7 15.2 collective-permute-start.4
  1233.0 15.8 copy-start.39
  1233.0 15.8 copy-start.98
  1233.0 15.8 copy-start.119
  1233.0 15.8 copy-start.145
  1233.0 15.8 copy-start.165
  1606.6 12.9 copy-start.37
  1606.6 14.9 copy-start.24
  1607.7 18.2 collective-permute-start.3
  1611.1 19.5 collective-permute-start.2
  1616.9 21.1 %collective-permute-start.1 = (bf16[28,3360]{1,0:T(8,128)(2,1)}, bf16[28,3360]{1,0:T(8,128)(2,1)}, u32[]{:S(2)}, u32[]{:S(2)}) collective-permute-start(bf16[28,3360]{1,0:T(8,128)(2,1)} %slice.255), channel_id=1, source_target_pairs={{0,1},{1,2},{2,3},{3,4},{4,5},{5,6},{6,7},{8,9},{9,10},{10,11},{11... | collective-permute-start | bytes 564488
  1620.2 26.8 %collective-permute-start = (bf16[28,3360]{1,0:T(8,128)(2,1)}, bf16[28,3360]{1,0:T(8,128)(2,1)S(1)}, u32[]{:S(2)}, u32[]{:S(2)}) collective-permute-start(bf16[28,3360]{1,0:T(8,128)(2,1)} %slice.254), channel_id=1, source_target_pairs={{0,1},{1,2},{2,3},{3,4},{4,5},{5,6},{6,7},{8,9},{9,10},{10,11},{11... | collective-permute-start | bytes 564488
  1622.3 35.6 %collective-permute-start.5 = (bf16[28,4480]{1,0:T(8,128)(2,1)}, bf16[28,4480]{1,0:T(8,128)(2,1)}, u32[]{:S(2)}, u32[]{:S(2)}) collective-permute-start(bf16[28,4480]{1,0:T(8,128)(2,1)} %slice.259), channel_id=1, source_target_pairs={{0,1},{1,2},{2,3},{3,4},{4,5},{5,6},{6,7},{8,9},{9,10},{10,11},{11... | collective-permute-start | bytes 752648
  (148 other events, 569.5 us)
Sparse Core Ops, SparseCore 0:
  13.9 87.0 all-gather.28
  110.3 29.2 all-gather.20
  141.5 29.0 all-gather.22
  172.3 40.7 all-gather.30
  214.8 62.5 all-gather.34
  279.7 103.7 all-gather.32
  385.4 84.3 all-gather.36
  478.0 29.8 all-gather.24
  509.8 29.0 all-gather.26
  540.6 40.7 all-gather.38
  583.9 103.7 all-gather.40
  690.0 62.5 all-gather.42
  784.8 54.9 all-reduce.45
  843.4 41.8 reduce-scatter.36
  889.1 42.4 reduce-scatter.34
  974.3 54.9 all-reduce.43
  1032.5 43.0 reduce-scatter.40
  1079.2 51.6 reduce-scatter.38
  1134.4 102.8 reduce-scatter.32
  1241.1 126.6 reduce-scatter.30
  1671.0 276.2 all-reduce.47
where the time goes:
time: 1980 us; the launch traced here: 1970 us
  waiting for transfers between devices  786 us (40%)
  blocking collectives  592 us (30%)
  matrix products  255 us (13%)
  local copies, waits for them, and re-layouts  245 us (12%)
  other arithmetic  43.8 us (2%)
  between operations  20.7 us (1%)
    unnamed x3, blocking collectives  531 us
    all_gather x2, waiting for transfers between devices, body(): lax.all_gather(w_up[level], 'gene', axis=0, tiled=True)  207 us
    psum x1, waiting for transfers between devices, body(): lax.psum(gene_shares[13].astype(jnp.bfloat16), 'cell').astype(jnp.float32)  185 us
    all_gather x2, waiting for transfers between devices, body(): lax.all_gather(w_qkv[level], 'gene', axis=0, tiled=True)  157 us
    unnamed x422, local copies, waits for them, and re-layouts  122 us
    all_gather x2, waiting for transfers between devices, body(): lax.all_gather(w_down[level], 'gene', axis=0, tiled=True)  116 us
    dot_general x10, matrix products, matmul(): return jnp.dot(left, right, preferred_element_type=jnp.float32)  79.2 us
    unnamed x33, waiting for transfers between devices  74.5 us
  transfers between devices with their start and end apart: 27, of which 13 were waited for; matrix products, arithmetic and copies ran while one was open for 47% of the time, Pallas kernels for 0%

commit v1 on v0

v1 whole, which is shorter than its diff:
```python
import functools
import math

import jax
import jax.numpy as jnp
from jax import lax
from jax.experimental import pallas as pl
from jax.experimental.pallas import tpu as pltpu
from jax.sharding import PartitionSpec as P

D = 1120
HEADS = 20
HEAD_DIM = 56
FF = 4480
PREFIX = 64
LAYERS = 2
LANES = 128
HALF = 64
TILE = 2 * LANES
EXTRA = 8
SCALE = HEAD_DIM ** (-0.5)
SCALE2 = SCALE * math.log2(math.e)
BF = jnp.bfloat16
F32 = jnp.float32


def dot(left, right, left_dim=1, right_dim=0):
    return lax.dot_general(
        left, right, (((left_dim,), (right_dim,)), ((), ())), preferred_element_type=F32
    )


class Plan:
    def __init__(self, groups, gene_rows):
        self.groups = groups
        self.gene_rows = gene_rows
        self.pre_rows = PREFIX // groups
        self.pre_block = -(-self.pre_rows // 8) * 8
        self.own_rows = gene_rows + self.pre_block
        self.piece_rows = self.own_rows + EXTRA
        self.genes = groups * gene_rows
        self.prefix = groups * self.pre_block
        self.total = self.genes + self.prefix
        self.all_rows = groups * self.piece_rows
        self.cols = D // groups
        self.hidden = FF // groups
        self.chunk = 256
        spans = [
            (self.cols * at // HEAD_DIM, -(-self.cols * (at + 1) // HEAD_DIM))
            for at in range(groups)
        ]
        self.window = max(last - first for first, last in spans)
        self.first_heads = [min(first, HEADS - self.window) for first, _ in spans]
        self.offsets = sorted(
            {self.cols * at - HEAD_DIM * first for at, first in enumerate(self.first_heads)}
        )
        self.wide = self.window * HEAD_DIM
        self.by_pairs = groups == 8


SCALAR = pl.BlockSpec(memory_space=pltpu.SMEM)
WHOLE = pl.BlockSpec(memory_space=pltpu.VMEM)


def call(kernel, name, args, outs, scratch=(), specs=None, flops=0):
    specs = specs or {}
    in_specs = [specs.get(at, WHOLE) for at in range(len(args))]
    moved = sum(math.prod(a.shape) * a.dtype.itemsize for a in args)
    moved += sum(math.prod(o.shape) * o.dtype.itemsize for o in outs)
    return pl.pallas_call(
        kernel,
        in_specs=in_specs,
        out_specs=[WHOLE] * len(outs),
        out_shape=outs,
        scratch_shapes=list(scratch),
        compiler_params=pltpu.CompilerParams(vmem_limit_bytes=58 << 20),
        cost_estimate=pl.CostEstimate(flops=flops, bytes_accessed=moved, transcendentals=0),
        name=name,
    )(*args)


def shape_of(*dims, dtype=BF):
    return jax.ShapeDtypeStruct(dims, dtype)


def aligned(at, size):
    return pl.ds(pl.multiple_of(at * size, size), size)


def normed_of(values):
    centred = values - jnp.mean(values, axis=-1, keepdims=True)
    variance = jnp.mean(centred * centred, axis=-1, keepdims=True)
    inverse = lax.rsqrt(variance + 1e-05)
    return centred * inverse, inverse


def write_piece(plan, piece_ref, rows, tail):
    if plan.pre_rows < plan.pre_block:
        at = lax.broadcasted_iota(jnp.int32, rows.shape, 0)
        rows = jnp.where(at < plan.gene_rows + plan.pre_rows, rows, 0.0)
    whole = jnp.concatenate([rows, tail], 0)
    piece_ref[...] = whole.astype(BF)


def begin_kernel(plan, gene_ref, pre_ref, gain_ref, shift_ref, rows_ref, piece_ref):
    rows = jnp.concatenate([gene_ref[...].astype(F32), pre_ref[...].astype(F32)], 0)
    rows_ref[...] = rows
    unit, _ = normed_of(rows)
    normed = unit * gain_ref[0:1, :] + shift_ref[0:1, :]
    write_piece(plan, piece_ref, normed, jnp.zeros((EXTRA, D), F32))


def add_parts(refs):
    total = refs[0][...].astype(F32)
    for ref in refs[1:]:
        total = total + ref[...].astype(F32)
    return total


def middle_kernel(plan, parts, level, gain_level, *refs):
    part_refs, (base_ref, bias_ref, gain_ref, shift_ref, rows_ref, piece_ref) = (
        refs[:parts],
        refs[parts:],
    )
    rows = base_ref[...] + add_parts(part_refs) + bias_ref[level : level + 1, :]
    rows_ref[...] = rows
    unit, _ = normed_of(rows)
    at = slice(gain_level, gain_level + 1)
    write_piece(
        plan, piece_ref, unit * gain_ref[at, :] + shift_ref[at, :], jnp.zeros((EXTRA, D), F32)
    )


def finish_kernel(plan, parts, level, *refs):
    part_refs, (base_ref, bias_ref, gene_ref, pre_ref) = refs[:parts], refs[parts:]
    rows = base_ref[...] + add_parts(part_refs) + bias_ref[level : level + 1, :]
    gene_ref[...] = rows[: plan.gene_rows]
    pre_ref[...] = rows[plan.gene_rows :]


def norm_back(parts, level, refs):
    part_refs, (x_ref, gain_ref, base_ref) = refs[:parts], refs[parts : parts + 3]
    grad_norm = add_parts(part_refs)
    unit, inverse = normed_of(x_ref[...])
    scaled = grad_norm * gain_ref[level : level + 1, :]
    grad = base_ref[...] + inverse * (
        scaled
        - jnp.mean(scaled, axis=-1, keepdims=True)
        - unit * jnp.mean(scaled * unit, axis=-1, keepdims=True)
    )
    sums = (
        jnp.sum(grad_norm * unit, axis=0, keepdims=True),
        jnp.sum(grad_norm, axis=0, keepdims=True),
    )
    return grad, sums


def tail_of(sums):
    return jnp.concatenate([sums[0], sums[1], jnp.zeros((EXTRA - 2, D), F32)], 0)


def back_kernel(plan, parts, level, *refs):
    grad, sums = norm_back(parts, level, refs)
    grad_ref, piece_ref = refs[parts + 3 :]
    grad_ref[...] = grad
    write_piece(plan, piece_ref, grad, tail_of(sums))


def back_end_kernel(plan, parts, level, *refs):
    grad, sums = norm_back(parts, level, refs)
    gene_ref, pre_ref, sums_ref = refs[parts + 3 :]
    gene_ref[...] = grad[: plan.gene_rows]
    pre_ref[...] = grad[plan.gene_rows :]
    sums_ref[...] = tail_of(sums)


def cot_kernel(plan, gene_ref, pre_ref, rows_ref, piece_ref):
    rows = jnp.concatenate([gene_ref[...], pre_ref[...]], 0)
    rows_ref[...] = rows
    write_piece(plan, piece_ref, rows, jnp.zeros((EXTRA, D), F32))


def chunks_of(plan):
    genes, rows, prefix = plan.genes, plan.chunk, plan.prefix
    chunks = []
    for first in range(0, genes, rows):
        blocks = [(genes, prefix, False)]
        blocks += [(start, rows, start == first) for start in range(0, first + rows, rows)]
        chunks.append((first, rows, blocks))
    chunks.append((genes, prefix, [(genes, prefix, True)]))
    return chunks


def masked(plan, scores, start, diagonal):
    holes = start == plan.genes and plan.pre_rows < plan.pre_block
    if not (diagonal or holes):
        return scores
    key_at = lax.broadcasted_iota(jnp.int32, scores.shape, 0)
    query_at = lax.broadcasted_iota(jnp.int32, scores.shape, 1)
    keep = key_at <= query_at if diagonal else None
    if holes:
        real = lax.rem(key_at, plan.pre_block) < plan.pre_rows
        keep = real if keep is None else keep & real
    return jnp.where(keep, scores, -jnp.inf)


def collect(plan, me, piece_refs, whole_ref, pre_ref):
    sums = 0.0
    for at, ref in enumerate(piece_refs):
        owner = me ^ at
        whole_ref[aligned(owner, plan.gene_rows), :] = ref[: plan.gene_rows, :]
        pre_ref[aligned(owner, plan.pre_block), :] = ref[plan.gene_rows : plan.own_rows, :].astype(F32)
        sums = sums + ref[plan.own_rows :, :].astype(F32)
    whole_ref[plan.genes :, :] = pre_ref[...].astype(BF)
    return sums


def give_blocks(plan, me, block_refs, rows_ref, weight, weight_dim, pre_ref):
    pre_ref[...] = dot(rows_ref[plan.genes :, :], weight, 1, weight_dim)
    for at, ref in enumerate(block_refs):
        owner = me ^ at
        ref[: plan.gene_rows, :] = dot(
            rows_ref[aligned(owner, plan.gene_rows), :], weight, 1, weight_dim
        ).astype(BF)
        ref[plan.gene_rows :, :] = pre_ref[aligned(owner, plan.pre_block), :].astype(BF)


def attend_kernel(plan, level, me_ref, *refs):
    pieces, refs = refs[: plan.groups], refs[plan.groups :]
    weight_ref, bias_ref, select_ref, out_weight_ref = refs[:4]
    low_ref, qkv_ref, mixed_ref, lse_ref = refs[4:8]
    blocks, (pre_ref, turned_ref, score_ref, padded_ref) = (
        refs[8 : 8 + plan.groups],
        refs[8 + plan.groups :],
    )
    me = me_ref[0]
    collect(plan, me, pieces, low_ref, pre_ref)
    for first in range(0, plan.total, plan.chunk):
        rows = slice(first, min(first + plan.chunk, plan.total))
        qkv_ref[rows, :] = (dot(low_ref[rows, :], weight_ref[...]) + bias_ref[...]).astype(BF)
    for head in range(plan.window):
        query_at = slice(TILE * head, TILE * head + LANES)
        value_at = slice(TILE * head + LANES, TILE * (head + 1))
        turned_ref[...] = qkv_ref[:, value_at].astype(F32).T.astype(BF)
        for first, count, parts in chunks_of(plan):
            query = qkv_ref[first : first + count, query_at]
            top = None
            for start, size, diagonal in parts:
                scores = dot(qkv_ref[start : start + size, value_at], query, 1, 1)
                scores = masked(plan, scores, start, diagonal)
                score_ref[start : start + size, :count] = scores
                high = jnp.max(scores, axis=0, keepdims=True)
                top = high if top is None else jnp.maximum(top, high)
            top = top * SCALE2
            total, mixed = 0.0, 0.0
            for start, size, _ in parts:
                weights = jnp.exp2(score_ref[start : start + size, :count] * SCALE2 - top)
                total = total + jnp.sum(weights, axis=0, keepdims=True)
                mixed = mixed + dot(turned_ref[:, start : start + size], weights.astype(BF))
            padded_ref[first : first + count, LANES * head : LANES * (head + 1)] = (
                (mixed * (1.0 / total)).T.astype(BF)
            )
            lse_ref[head, :, first : first + count] = top + jnp.log2(total)
    mixed_ref[...] = dot(padded_ref[...], select_ref[...]).astype(BF)
    give_blocks(plan, me, blocks, mixed_ref, out_weight_ref[level], 0, pre_ref)


def attend_back_kernel(plan, me_ref, *refs):
    pieces, refs = refs[: plan.groups], refs[plan.groups :]
    out_weight_ref, qkv_ref, lse_ref, select_ref, weight_ref = refs[:5]
    low_ref, qkv_grad_ref, sums_ref, out_bias_ref, qkv_bias_ref = refs[5:10]
    blocks = refs[10 : 10 + plan.groups]
    pre_ref, grad_ref, turned_ref, prob_ref, pgrad_ref, pair_ref, padded_ref = refs[10 + plan.groups :]
    me = me_ref[0]
    sums_ref[...] = collect(plan, me, pieces, low_ref, pre_ref)
    out_bias_ref[...] = jnp.sum(low_ref[...].astype(F32), axis=0, keepdims=True)
    for first in range(0, plan.total, plan.chunk):
        rows = slice(first, min(first + plan.chunk, plan.total))
        grad_ref[rows, :] = dot(low_ref[rows, :], out_weight_ref[...], 1, 1).astype(BF)
    lane = lax.broadcasted_iota(jnp.int32, (1, LANES), 1)
    pair_scale = jnp.where(lane < HALF, SCALE, 1.0)
    for head in range(plan.window):
        query_at = slice(TILE * head, TILE * head + LANES)
        value_at = slice(TILE * head + LANES, TILE * (head + 1))
        grad_at = slice(LANES * head, LANES * (head + 1))
        turned_ref[...] = qkv_ref[:, value_at].astype(F32).T.astype(BF)
        pair_ref[...] = jnp.zeros_like(pair_ref)
        for first, count, parts in chunks_of(plan):
            query = qkv_ref[first : first + count, query_at]
            grad = grad_ref[first : first + count, grad_at]
            lse = lse_ref[head, :, first : first + count]
            delta = 0.0
            for start, size, diagonal in parts:
                pair = qkv_ref[start : start + size, value_at]
                scores = masked(plan, dot(pair, query, 1, 1), start, diagonal)
                probs = jnp.exp2(scores * SCALE2 - lse)
                prob_grad = dot(pair, grad, 1, 1)
                delta = delta + jnp.sum(probs * prob_grad, axis=0, keepdims=True)
                prob_ref[start : start + size, :count] = probs
                pgrad_ref[start : start + size, :count] = prob_grad
            query_grad = 0.0
            for start, size, _ in parts:
                probs = prob_ref[start : start + size, :count]
                score_grad = (probs * (pgrad_ref[start : start + size, :count] - delta)).astype(BF)
                pair_ref[start : start + size, :] += dot(probs.astype(BF), grad) + dot(score_grad, query)
                query_grad = query_grad + dot(turned_ref[:, start : start + size], score_grad)
            padded_ref[first : first + count, query_at] = (query_grad.T * SCALE).astype(BF)
        padded_ref[:, value_at] = (pair_ref[...] * pair_scale).astype(BF)
    qkv_grad_ref[...] = dot(padded_ref[...], select_ref[...]).astype(BF)
    qkv_bias_ref[...] = jnp.sum(qkv_grad_ref[...].astype(F32), axis=0, keepdims=True)
    give_blocks(plan, me, blocks, qkv_grad_ref, weight_ref[...], 1, pre_ref)


ROOT = math.sqrt(2.0 / math.pi)
CUBE = 0.044715


def lift_kernel(plan, level, *refs):
    pieces, refs = refs[: plan.groups], refs[plan.groups :]
    up_ref, bias_ref, down_ref, low_ref, pre_ref, active_ref = refs[:6]
    blocks = refs[6:]
    size = plan.piece_rows
    for at, ref in enumerate(pieces):
        low_ref[at * size : (at + 1) * size, :] = ref[...]
    step = 2 * size
    for first in range(0, plan.all_rows, step):
        rows = slice(first, first + step)
        pre = dot(low_ref[rows, :], up_ref[...]) + bias_ref[...]
        pre_ref[rows, :] = pre
        active = (0.5 * pre * (1.0 + jnp.tanh(ROOT * (pre + CUBE * pre * pre * pre)))).astype(BF)
        active_ref[rows, :] = active
        lifted = dot(active, down_ref[level])
        for at in range(2):
            blocks[first // size + at][...] = lifted[at * size : at * size + plan.own_rows].astype(BF)


def lift_back_kernel(plan, level, *refs):
    pieces, refs = refs[: plan.groups], refs[plan.groups :]
    up_ref, pre_ref, down_ref = refs[:3]
    low_ref, pre_grad_ref, sums_ref, down_bias_ref, up_bias_ref = refs[3:8]
    blocks = refs[8:]
    size = plan.piece_rows
    at_row = lax.broadcasted_iota(jnp.int32, (size, D), 0)
    sums, down_bias, up_bias = 0.0, 0.0, 0.0
    for at, ref in enumerate(pieces):
        rows = ref[...].astype(F32)
        sums = sums + rows[plan.own_rows :]
        rows = jnp.where(at_row < plan.own_rows, rows, 0.0)
        down_bias = down_bias + jnp.sum(rows, axis=0, keepdims=True)
        low_ref[at * size : (at + 1) * size, :] = rows.astype(BF)
    sums_ref[...] = sums
    down_bias_ref[...] = down_bias
    step = 2 * size
    for first in range(0, plan.all_rows, step):
        rows = slice(first, first + step)
        act_grad = dot(low_ref[rows, :], down_ref[level], 1, 1)
        pre = pre_ref[rows, :]
        square = pre * pre
        turn = jnp.tanh(ROOT * pre * (1.0 + CUBE * square))
        slope = 0.5 * (1.0 + turn) + (0.5 * ROOT) * pre * (1.0 - turn * turn) * (1.0 + 3.0 * CUBE * square)
        pre_grad = (act_grad * slope).astype(BF)
        pre_grad_ref[rows, :] = pre_grad
        up_bias = up_bias + jnp.sum(pre_grad.astype(F32), axis=0, keepdims=True)
        norm_grad = dot(pre_grad, up_ref[...], 1, 1)
        for at in range(2):
            blocks[first // size + at][...] = norm_grad[at * size : at * size + plan.own_rows].astype(BF)
    up_bias_ref[...] = up_bias


def send_qkv_kernel(plan, level, me_ref, weight_ref, *refs):
    outs, (stack_ref,) = refs[: plan.groups], refs[plan.groups :]
    wide = plan.wide
    for to, head in enumerate(plan.first_heads):
        for block in range(3):
            begin = block * D + head * HEAD_DIM
            stack_ref[to, :, block * wide : (block + 1) * wide] = weight_ref[
                level, :, begin : begin + wide
            ].astype(F32)
    for at, ref in enumerate(outs):
        ref[...] = stack_ref[me_ref[0] ^ at].astype(BF)


def take_qkv_kernel(plan, me_ref, *refs):
    pieces, (padded_ref, own_ref, stack_ref, wide_ref, cut_ref) = (
        refs[: plan.groups],
        refs[plan.groups :],
    )
    me = me_ref[0]
    offset = me_ref[1]
    cols, wide = plan.cols, plan.wide
    for at, ref in enumerate(pieces):
        stack_ref[at] = ref[...].astype(F32)
    wide_ref[...] = jnp.zeros_like(wide_ref)
    for source in range(plan.groups):
        rows = slice(cols * source, cols * (source + 1))
        value = stack_ref[me ^ source]
        for block, to in enumerate((0, LANES, LANES + HALF)):
            part = value[:, block * wide : (block + 1) * wide]
            for head in range(plan.window):
                wide_ref[rows, TILE * head + to : TILE * head + to + HEAD_DIM] = part[
                    :, head * HEAD_DIM : (head + 1) * HEAD_DIM
                ]
            own = part[:, plan.offsets[0] : plan.offsets[0] + cols]
            for choice in plan.offsets[1:]:
                own = jnp.where(offset == choice, part[:, choice : choice + cols], own)
            cut_ref[rows, block * cols : (block + 1) * cols] = own
    padded_ref[...] = wide_ref[...].astype(BF)
    own_ref[...] = cut_ref[...].astype(BF)


def send_up_kernel(plan, level, me_ref, weight_ref, *refs):
    outs, (stack_ref,) = refs[: plan.groups], refs[plan.groups :]
    for to in range(plan.groups):
        stack_ref[to] = weight_ref[level, :, to * plan.hidden : (to + 1) * plan.hidden].astype(F32)
    for at, ref in enumerate(outs):
        ref[...] = stack_ref[me_ref[0] ^ at].astype(BF)


def take_up_kernel(plan, me_ref, *refs):
    pieces, (up_ref, stack_ref, whole_ref) = refs[: plan.groups], refs[plan.groups :]
    for at, ref in enumerate(pieces):
        stack_ref[at] = ref[...].astype(F32)
    for source in range(plan.groups):
        whole_ref[plan.cols * source : plan.cols * (source + 1), :] = stack_ref[me_ref[0] ^ source]
    up_ref[...] = whole_ref[...].astype(BF)


def weight_grad_kernel(plan, me_ref, left_ref, right_ref, *refs):
    outs, (whole_ref, stack_ref) = refs[: plan.groups], refs[plan.groups :]
    for first in range(0, D, TILE):
        rows = slice(first, min(first + TILE, D))
        whole_ref[rows, :] = dot(left_ref[:, rows], right_ref[...], 0, 0)
    for to in range(plan.groups):
        stack_ref[to] = whole_ref[plan.cols * to : plan.cols * (to + 1), :]
    for at, ref in enumerate(outs):
        ref[...] = stack_ref[me_ref[0] ^ at].astype(BF)


def join_kernel(plan, blocks, me_ref, *refs):
    parts, out_ref = refs[:LAYERS], refs[LAYERS]
    each = parts[0].shape[2] // blocks
    for level, ref in enumerate(parts):
        for source in range(plan.groups):
            value = ref[me_ref[0] ^ source].astype(F32)
            for block in range(blocks):
                begin = (block * plan.groups + source) * each
                out_ref[level, :, begin : begin + each] = value[:, block * each : (block + 1) * each]


def body(
    genes,
    prefix,
    cot_genes,
    cot_prefix,
    w_qkv,
    w_out,
    w_up,
    w_down,
    norm1_gain,
    norm1_bias,
    norm2_gain,
    norm2_bias,
    bias_q,
    bias_v,
    bias_out,
    bias_up,
    bias_down,
):
    groups = lax.axis_size("gene")
    cells = lax.axis_size("cell")
    me = lax.axis_index("gene")
    cell = lax.axis_index("cell")
    plan = Plan(groups, genes.shape[1])
    cols, wide, window, hidden = plan.cols, plan.wide, plan.window, plan.hidden
    own_rows, piece_rows = plan.own_rows, plan.piece_rows
    first_head = jnp.asarray(plan.first_heads, jnp.int32)[me]
    offset = me * cols - first_head * HEAD_DIM
    turn = me if plan.by_pairs else jnp.zeros_like(me)
    where = jnp.stack([turn, offset]).astype(jnp.int32)
    here = functools.partial

    def swap(value, bits):
        return lax.ppermute(value, "gene", [(at, at ^ bits) for at in range(groups)])

    def gather(piece):
        if not plan.by_pairs:
            stack = lax.all_gather(piece, "gene", axis=0)
            return [stack[at] for at in range(groups)]
        near = [piece] + [swap(piece, bits) for bits in (2, 4, 6)]
        far = [swap(value, 1) for value in near]
        return [value for pair in zip(near, far) for value in pair]

    def scatter_sum(blocks):
        if not plan.by_pairs:
            return [lax.psum_scatter(jnp.stack(blocks), "gene", scatter_dimension=0)]
        parts = []
        for bits in (2, 4, 6):
            other = swap(blocks[bits ^ 1], 1)
            total = (blocks[bits].astype(F32) + other.astype(F32)).astype(BF)
            parts.append(swap(total, bits))
        return [blocks[0], swap(blocks[1], 1)] + parts

    def exchange(pieces):
        if not plan.by_pairs:
            stack = lax.all_to_all(jnp.stack(pieces), "gene", 0, 0)
            return [stack[at] for at in range(groups)]
        return [pieces[0]] + [swap(pieces[bits], bits) for bits in range(1, groups)]

    def sum_cells(value):
        if cells != 4:
            return lax.psum(value, "cell").astype(F32)
        outer = lax.ppermute(value, "cell", [(0, 1), (3, 2)])
        half = (value.astype(F32) + outer.astype(F32)).astype(BF)
        other = lax.ppermute(half, "cell", [(1, 2), (2, 1)])
        total = (half.astype(F32) + other.astype(F32)).astype(BF)
        back = lax.ppermute(total, "cell", [(1, 0), (2, 3)])
        return jnp.where((cell == 1) | (cell == 2), total, back).astype(F32)

    def reshard_qkv(level):
        pieces = call(
            here(send_qkv_kernel, plan, level),
            "send_qkv",
            [where, w_qkv],
            [shape_of(cols, 3 * wide)] * groups,
            [pltpu.VMEM((groups, cols, 3 * wide), F32)],
            {0: SCALAR},
        )
        return call(
            here(take_qkv_kernel, plan),
            "take_qkv",
            [where] + exchange(pieces),
            [shape_of(D, window * TILE), shape_of(D, 3 * cols)],
            [
                pltpu.VMEM((groups, cols, 3 * wide), F32),
                pltpu.VMEM((D, window * TILE), F32),
                pltpu.VMEM((D, 3 * cols), F32),
            ],
            {0: SCALAR},
        )

    def reshard_up(level):
        pieces = call(
            here(send_up_kernel, plan, level),
            "send_up",
            [where, w_up],
            [shape_of(cols, hidden)] * groups,
            [pltpu.VMEM((groups, cols, hidden), F32)],
            {0: SCALAR},
        )
        return call(
            here(take_up_kernel, plan),
            "take_up",
            [where] + exchange(pieces),
            [shape_of(D, hidden)],
            [pltpu.VMEM((groups, cols, hidden), F32), pltpu.VMEM((D, hidden), F32)],
            {0: SCALAR},
        )[0]

    at_row = jnp.arange(window * TILE)
    lane = at_row % TILE
    block = jnp.where(lane < LANES, 0, jnp.where(lane < LANES + HALF, 1, 2))
    inner = lane % HALF
    inner_ok = (inner < HEAD_DIM) & ((lane < HALF) | (lane >= LANES))
    source = jnp.where(inner_ok, block * cols + (at_row // TILE) * HEAD_DIM + inner - offset, -1)
    in_block = source - block * cols
    source = jnp.where((in_block >= 0) & (in_block < cols), source, -1)
    select = (source[:, None] == jnp.arange(3 * cols)[None, :]).astype(BF)
    at_out = jnp.arange(window * LANES)
    inner = at_out % LANES - HALF
    out_col = (at_out // LANES) * HEAD_DIM + inner
    out_ok = (inner >= 0) & (inner < HEAD_DIM)
    out_select = (
        jnp.where(out_ok, out_col - offset, -1)[:, None] == jnp.arange(cols)[None, :]
    ).astype(BF)

    def out_window(level):
        pairs = plan.by_pairs
        if pairs:
            other = swap(w_out[level], 1)
            rows = jnp.concatenate([w_out[level], other], 0)
            owner = jnp.concatenate([me * cols + jnp.arange(cols), (me ^ 1) * cols + jnp.arange(cols)])
        else:
            rows = lax.all_gather(w_out[level], "gene", axis=0, tiled=True)
            owner = jnp.arange(D)
        wanted = jnp.where(out_ok, first_head * HEAD_DIM + out_col, -1)
        pick = (wanted[:, None] == owner[None, :]).astype(BF)
        return dot(pick, rows).astype(BF)

    def padded_bias(level):
        def cut(vec):
            part = lax.dynamic_slice_in_dim(vec[level], first_head * HEAD_DIM, wide, 0)
            return jnp.pad(part.reshape(window, HEAD_DIM), ((0, 0), (0, HALF - HEAD_DIM)))

        nothing = jnp.zeros((window, HALF), F32)
        return jnp.stack([cut(bias_q), nothing, nothing, cut(bias_v)], 1).reshape(1, window * TILE)

    qkv_biases = [padded_bias(level) for level in range(LAYERS)]
    up_biases = [
        lax.dynamic_slice_in_dim(bias_up[level], me * hidden, hidden, 0)[None]
        for level in range(LAYERS)
    ]
    rows_f32 = shape_of(own_rows, D, dtype=F32)
    piece_like = shape_of(piece_rows, D)
    blocks_like = [shape_of(own_rows, D)] * groups
    vector = shape_of(1, D, dtype=F32)
    sums_like = shape_of(EXTRA, D, dtype=F32)

    own_prefix = lax.dynamic_slice_in_dim(prefix[0], me * plan.pre_rows, plan.pre_rows, 0)
    filler = ((0, plan.pre_block - plan.pre_rows), (0, 0))
    rows, piece = call(
        here(begin_kernel, plan),
        "begin",
        [genes[0], jnp.pad(own_prefix, filler), norm1_gain, norm1_bias],
        [rows_f32, piece_like],
    )
    saved = []
    qkv_weights, up_weights, out_windows = [None] * LAYERS, [None] * LAYERS, [None] * LAYERS
    result = None
    for level in range(LAYERS):
        qkv_weights[level] = reshard_qkv(level)
        up_weights[level] = reshard_up(level)
        out_windows[level] = out_window(level)
    for level in range(LAYERS):
        pieces = gather(piece)
        outs = call(
            here(attend_kernel, plan, level),
            "attend",
            [where] + pieces + [qkv_weights[level][0], qkv_biases[level], out_select, w_out],
            [
                shape_of(plan.total, D),
                shape_of(plan.total, window * TILE),
                shape_of(plan.total, cols),
                shape_of(window, 1, plan.total, dtype=F32),
            ]
            + blocks_like,
            [
                pltpu.VMEM((plan.prefix, D), F32),
                pltpu.VMEM((LANES, plan.total), BF),
                pltpu.VMEM((plan.total, plan.chunk), F32),
                pltpu.VMEM((plan.total, window * LANES), BF),
            ],
            {0: SCALAR},
            flops=4 * 10**9,
        )
        low_one, qkv, mixed, lse = outs[:4]
        parts = scatter_sum(outs[4:])
        middle, piece = call(
            here(middle_kernel, plan, len(parts), level, level),
            "middle",
            parts + [rows, bias_out, norm2_gain, norm2_bias],
            [rows_f32, piece_like],
        )
        outs = call(
            here(lift_kernel, plan, level),
            "lift",
            gather(piece) + [up_weights[level], up_biases[level], w_down],
            [
                shape_of(plan.all_rows, D),
                shape_of(plan.all_rows, hidden, dtype=F32),
                shape_of(plan.all_rows, hidden),
            ]
            + blocks_like,
            flops=3 * 10**9,
        )
        low_two, pre_act, active = outs[:3]
        saved.append((rows, low_one, qkv, mixed, lse, middle, low_two, pre_act, active))
        parts = scatter_sum(outs[3:])
        if level + 1 < LAYERS:
            rows, piece = call(
                here(middle_kernel, plan, len(parts), level, level + 1),
                "next_rows",
                parts + [middle, bias_down, norm1_gain, norm1_bias],
                [rows_f32, piece_like],
            )
        else:
            result = call(
                here(finish_kernel, plan, len(parts), level),
                "finish",
                parts + [middle, bias_down],
                [
                    shape_of(plan.gene_rows, D, dtype=F32),
                    shape_of(plan.pre_block, D, dtype=F32),
                ],
            )

    grad, piece = call(
        here(cot_kernel, plan),
        "cotangent",
        [cot_genes[0], jnp.pad(cot_prefix[0], filler)],
        [rows_f32, piece_like],
    )
    weight_sums = [[None] * LAYERS for _ in range(4)]
    small = [[None] * LAYERS for _ in range(9)]

    def own_slice(rows_in):
        return lax.dynamic_slice_in_dim(rows_in, me * cols, cols, 1)

    for level in reversed(range(LAYERS)):
        rows, low_one, qkv, mixed, lse, middle, low_two, pre_act, active = saved[level]
        outs = call(
            here(lift_back_kernel, plan, level),
            "lift_back",
            gather(piece) + [up_weights[level], pre_act, w_down],
            [
                shape_of(plan.all_rows, D),
                shape_of(plan.all_rows, hidden),
                sums_like,
                vector,
                shape_of(1, hidden, dtype=F32),
            ]
            + blocks_like,
            flops=3 * 10**9,
        )
        low_grad, pre_grad, sums, down_bias, up_bias = outs[:5]
        if level + 1 < LAYERS:
            small[0][level + 1], small[1][level + 1] = sums[0:1], sums[1:2]
        small[8][level], small[7][level] = down_bias, up_bias
        parts = scatter_sum(outs[5:])
        weight_sums[3][level] = sum_cells(dot(active, low_grad, 0, 0).astype(BF))
        up_parts = call(
            here(weight_grad_kernel, plan),
            "up_grad",
            [where, low_two, pre_grad],
            [shape_of(cols, hidden)] * groups,
            [pltpu.VMEM((D, hidden), F32), pltpu.VMEM((groups, cols, hidden), F32)],
            {0: SCALAR},
            flops=14 * 10**8,
        )
        weight_sums[2][level] = sum_cells(jnp.stack(exchange(up_parts)))
        middle_grad, piece = call(
            here(back_kernel, plan, len(parts), level),
            "middle_back",
            parts + [middle, norm2_gain, grad],
            [rows_f32, piece_like],
        )
        outs = call(
            here(attend_back_kernel, plan),
            "attend_back",
            [where]
            + gather(piece)
            + [out_windows[level], qkv, lse, select, qkv_weights[level][1]],
            [
                shape_of(plan.total, D),
                shape_of(plan.total, 3 * cols),
                sums_like,
                vector,
                shape_of(1, 3 * cols, dtype=F32),
            ]
            + blocks_like,
            [
                pltpu.VMEM((plan.prefix, D), F32),
                pltpu.VMEM((plan.total, window * LANES), BF),
                pltpu.VMEM((LANES, plan.total), BF),
                pltpu.VMEM((plan.total, plan.chunk), F32),
                pltpu.VMEM((plan.total, plan.chunk), F32),
                pltpu.VMEM((plan.total, LANES), F32),
                pltpu.VMEM((plan.total, window * TILE), BF),
            ],
            {0: SCALAR},
            flops=8 * 10**9,
        )
        low_grad, qkv_grad, sums, out_bias, qkv_bias = outs[:5]
        small[2][level], small[3][level] = sums[0:1], sums[1:2]
        small[6][level] = out_bias
        small[4][level], small[5][level] = qkv_bias[:, :cols], qkv_bias[:, 2 * cols :]
        parts = scatter_sum(outs[5:])
        weight_sums[1][level] = sum_cells(dot(mixed, low_grad, 0, 0).astype(BF))
        qkv_parts = call(
            here(weight_grad_kernel, plan),
            "qkv_grad",
            [where, low_one, qkv_grad],
            [shape_of(cols, 3 * cols)] * groups,
            [pltpu.VMEM((D, 3 * cols), F32), pltpu.VMEM((groups, cols, 3 * cols), F32)],
            {0: SCALAR},
            flops=10**9,
        )
        weight_sums[0][level] = sum_cells(jnp.stack(exchange(qkv_parts)))
        if level:
            grad, piece = call(
                here(back_kernel, plan, len(parts), level),
                "rows_back",
                parts + [rows, norm1_gain, middle_grad],
                [rows_f32, piece_like],
            )
        else:
            gene_grad, pre_grad, sums = call(
                here(back_end_kernel, plan, len(parts), level),
                "rows_back_end",
                parts + [rows, norm1_gain, middle_grad],
                [
                    shape_of(plan.gene_rows, D, dtype=F32),
                    shape_of(plan.pre_block, D, dtype=F32),
                    sums_like,
                ],
            )

    long_rows = [small[which][level] for which in (2, 3, 6, 8) for level in range(LAYERS)]
    long_rows += [small[which][level] for which in (0, 1) for level in range(1, LAYERS)]
    packed = own_slice(jnp.concatenate(long_rows, 0))
    short_rows = [small[which][level] for which in (4, 5) for level in range(LAYERS)]
    short_rows += [small[7][level].reshape(hidden // cols, cols) for level in range(LAYERS)]
    packed = sum_cells(jnp.concatenate([packed] + short_rows, 0).astype(BF))
    last = lax.psum(sums[:2].astype(BF), ("gene", "cell"))
    last = own_slice(last.astype(F32))
    base = 4 * LAYERS
    ends = base + 2 * (LAYERS - 1)
    per = LAYERS - 1
    vectors = [
        jnp.concatenate([last[0:1], packed[base : base + per]], 0),
        jnp.concatenate([last[1:2], packed[base + per : ends]], 0),
        packed[0:LAYERS],
        packed[LAYERS : 2 * LAYERS],
        packed[ends : ends + LAYERS],
        packed[ends + LAYERS : ends + 2 * LAYERS],
        packed[2 * LAYERS : 3 * LAYERS],
        packed[ends + 2 * LAYERS :].reshape(LAYERS, hidden),
        packed[3 * LAYERS : 4 * LAYERS],
    ]

    def join(parts, blocks, width):
        return call(
            here(join_kernel, plan, blocks),
            "join",
            [where] + [part.astype(BF) for part in parts],
            [shape_of(LAYERS, cols, width, dtype=F32)],
            specs={0: SCALAR},
        )[0]

    return (
        result[0][None],
        result[1][: plan.pre_rows][None],
        gene_grad[None],
        pre_grad[: plan.pre_rows][None],
        join(weight_sums[0], 3, 3 * D),
        jnp.stack(weight_sums[1]),
        join(weight_sums[2], 1, FF),
        jnp.stack(weight_sums[3]),
        *vectors,
    )


def solution(mesh):
    rows = P("cell", "gene", None)
    weight = P(None, "gene", None)
    vector = P(None, "gene")
    return jax.shard_map(
        body,
        mesh=mesh,
        in_specs=(rows, P("cell", None, None), rows, rows) + (weight,) * 4 + (P(),) * 9,
        out_specs=(rows,) * 4 + (weight,) * 4 + (vector,) * 9,
        check_vma=False,
    )
```

time: 1980 us -> 1010 us (0.51)
  blocking collectives: 592 us -> 48.7 us
  waiting for transfers between devices: 786 us -> 414 us
  matrix products: 255 us -> 16.1 us
  Pallas kernels: 0 us -> 199 us
  starting transfers between devices: 14.4 us -> 192 us
  local copies, waits for them, and re-layouts: 245 us -> 74 us
    unnamed x3 -> x0, blocking collectives: 531 us -> none
    all_gather x12 -> x0, waiting for transfers between devices: 526 us -> none  [the longest x2 207 us: body(): lax.all_gather(w_up[level], 'gene', axis=0, tiled=True)]
    ppermute x0 -> x197, waiting for transfers between devices: none -> 414 us  [the longest x170 310 us: swap(): lax.ppermute(value, 'gene', [(at, at ^ bits) for at in range(groups)])]
    dot_general x60 -> x6, matrix products: 255 us -> 16.1 us  [dot(): lax.dot_general(left, right, (((left_dim,), (right_dim,)), ((), ())), pre...]
    pallas_call x0 -> x32, Pallas kernels: none -> 199 us  [call(): pl.pallas_call(kernel, in_specs=in_specs, out_specs=[WHOLE] * len(outs),...]
    ppermute x0 -> x197, starting transfers between devices: none -> 192 us  [the longest x170 127 us: swap(): lax.ppermute(value, 'gene', [(at, at ^ bits) for at in range(groups)])]
    psum x1 -> x0, waiting for transfers between devices: 185 us -> none  [body(): lax.psum(gene_shares[13].astype(jnp.bfloat16), 'cell').astype(jnp.float32)]
    unnamed x422 -> x416, local copies, waits for them, and re-layouts: 122 us -> 45.9 us
  transfers between devices with their start and end apart: 27 -> 197, of which waited for: 13 -> 70; matrix products, arithmetic and copies ran while one was open for 47% -> 12% of each run, Pallas kernels for 0% -> 16%
where the time goes in v1:
time: 1010 us; the launch traced here: 1000 us
  waiting for transfers between devices  414 us (41%)
  Pallas kernels  199 us (20%)
  starting transfers between devices  192 us (19%)
  local copies, waits for them, and re-layouts  74 us (7%)
  other arithmetic  52.9 us (5%)
  blocking collectives  48.7 us (5%)
  matrix products  16.1 us (2%)
    ppermute x170, waiting for transfers between devices, swap(): lax.ppermute(value, 'gene', [(at, at ^ bits) for at in range(groups)])  310 us
    pallas_call x32, Pallas kernels, call(): pl.pallas_call(kernel, in_specs=in_specs, out_specs=[WHOLE] * len(outs),...  199 us
    ppermute x170, starting transfers between devices, swap(): lax.ppermute(value, 'gene', [(at, at ^ bits) for at in range(groups)])  127 us
    ppermute x9, waiting for transfers between devices, sum_cells(): back = lax.ppermute(total, 'cell', [(1, 0), (2, 3)])  90.4 us
    psum x1, blocking collectives, body(): last = lax.psum(sums[:2].astype(BF), ('gene', 'cell'))  48.7 us
    unnamed x416, local copies, waits for them, and re-layouts  45.9 us
    ppermute x9, starting transfers between devices, sum_cells(): outer = lax.ppermute(value, 'cell', [(0, 1), (3, 2)])  39.4 us
  transfers between devices with their start and end apart: 197, of which 70 were waited for; matrix products, arithmetic and copies ran while one was open for 12% of the time, Pallas kernels for 16%

profile of v1, /device:TPU:0, one launch (start us, length us, event | category | flops | bytes accessed | tf_op | source)
XLA Modules:
  0.0 1000.5 jit_solution(14170022492960489547)
XLA Ops:
  21.1 6.2 collective-permute-done.8.refs_2_
  41.7 4.9 collective-permute-done.13.refs_7_
  47.2 8.0 take_qkv.2
  56.3 13.7 %attend.2 = (bf16[1088,1120]{1,0:T(8,128)(2,1)}, bf16[1088,768]{1,0:T(8,128)(2,1)}, bf16[1088,140]{1,0:T(8,128)(2,1)}, f32[3,1,1088]{2,1,0:T(1,128)}, bf16[136,1...) custom-call(s32[2]{0:T(128)} %pad_add_fusion.1.me_ref, ...), custom_call_target="tpu_custom_call" | custom-call | flops 4000000000 | bytes 11901704 | tf_op jit(solution)/shard_map/attend/pallas_call | solution.py:70
  85.4 6.0 collective-permute-done.18.refs_3_
  99.9 12.7 %collective-permute-done.30.refs_3_ = bf16[140,560]{1,0:T(8,128)(2,1)S(1)} collective-permute-done((bf16[140,560]{1,0:T(8,128)(2,1)S(1)}, bf16[140,560]{1,0:T(8,128)(2,1)S(1)}, u32[]{:S(2)}, u32[]{:S(2)}) %collective-permute-start.30) | collective-permute-done | bytes 156832 | tf_op jit(solution)/shard_map/ppermute | solution.py:483
  117.4 7.0 collective-permute-done.32.refs_5_
  136.3 10.0 lift.2
  159.6 7.3 collective-permute-done.39.refs_3_
  175.8 15.9 %collective-permute-done.50.refs_2_ = bf16[140,504]{1,0:T(8,128)(2,1)S(1)} collective-permute-done((bf16[140,504]{1,0:T(8,128)(2,1)S(1)}, bf16[140,504]{1,0:T(8,128)(2,1)S(1)}, u32[]{:S(2)}, u32[]{:S(2)}) %collective-permute-start.50) | collective-permute-done | bytes 141152 | tf_op jit(solution)/shard_map/ppermute | solution.py:483
  193.1 5.2 collective-permute-done.52.refs_4_
  200.9 5.5 collective-permute-done.54.refs_6_
  207.5 5.7 collective-permute-done.55.refs_7_
  213.9 8.0 take_qkv.3
  222.8 13.5 %attend.3 = (bf16[1088,1120]{1,0:T(8,128)(2,1)}, bf16[1088,768]{1,0:T(8,128)(2,1)}, bf16[1088,140]{1,0:T(8,128)(2,1)}, f32[3,1,1088]{2,1,0:T(1,128)}, bf16[136,1...) custom-call(s32[2]{0:T(128)} %pad_add_fusion.1.me_ref, ...), custom_call_target="tpu_custom_call" | custom-call | flops 4000000000 | bytes 11901704 | tf_op jit(solution)/shard_map/attend/pallas_call | solution.py:70
  259.9 5.6 collective-permute-done.62.refs_4_
  288.0 5.4 collective-permute-done.64.refs_2_
  293.4 13.0 %collective-permute-done.66.refs_4_ = bf16[144,1120]{1,0:T(8,128)(2,1)S(1)} collective-permute-done((bf16[144,1120]{1,0:T(8,128)(2,1)}, bf16[144,1120]{1,0:T(8,128)(2,1)S(1)}, u32[]{:S(2)}, u32[]{:S(2)}) %collective-permute-start.66) | collective-permute-done | bytes 322592 | tf_op jit(solution)/shard_map/ppermute | solution.py:483
  319.9 10.0 lift.3
  330.9 10.5 %lift_back.2 = (bf16[1152,1120]{1,0:T(8,128)(2,1)}, bf16[1152,560]{1,0:T(8,128)(2,1)}, f32[8,1120]{1,0:T(8,128)}, f32[1,1120]{1,0:T(1,128)}, f32[1,560]{1,0:T(1,...) custom-call(bf16[144,1120]{1,0:T(8,128)(2,1)} %get-tuple-element.279, ...), custom_call_target="tpu_custom_call" | custom-call | flops 3000000000 | bytes 15274560 | tf_op jit(solution)/shard_map/lift_back/pallas_call | solution.py:70
  341.5 5.9 up_grad.3
  348.2 4.9 convolution_convert_fusion
  354.6 5.3 collective-permute-done.179
  360.1 6.6 collective-permute-done.180
  369.1 4.8 collective-permute-done.181
  374.5 6.1 collective-permute-done.182
  386.6 6.3 collective-permute-done.93.refs_2_
  392.9 8.4 collective-permute-done.95.refs_3_
  403.1 6.8 collective-permute-done.97.refs_4_
  422.3 16.3 %collective-permute-done.81.refs_3_ = bf16[136,1120]{1,0:T(8,128)(2,1)S(1)} collective-permute-done((bf16[136,1120]{1,0:T(8,128)(2,1)S(1)}, bf16[136,1120]{1,0:T(8,128)(2,1)S(1)}, u32[]{:S(2)}, u32[]{:S(2)}) %collective-permute-start.81) | collective-permute-done | bytes 304672 | tf_op jit(solution)/shard_map/ppermute | solution.py:483
  454.9 18.0 %attend_back.2 = (bf16[1088,1120]{1,0:T(8,128)(2,1)}, bf16[1088,420]{1,0:T(8,128)(2,1)}, f32[8,1120]{1,0:T(8,128)}, f32[1,1120]{1,0:T(1,128)}, f32[1,420]{1,0:T(...) custom-call(s32[2]{0:T(128)} %pad_add_fusion.1.me_ref, ...), custom_call_target="tpu_custom_call" | custom-call | flops 8000000000 | bytes 12540952 | tf_op jit(solution)/shard_map/attend_back/pallas_call | solution.py:70
  474.0 4.9 qkv_grad.3
  488.1 5.0 collective-permute-done.153
  493.2 5.7 collective-permute-done.154
  504.8 5.5 collective-permute-done.156
  515.9 7.8 collective-permute-done.165
  534.0 5.4 collective-permute-start.159
  572.8 10.5 %lift_back.3 = (bf16[1152,1120]{1,0:T(8,128)(2,1)}, bf16[1152,560]{1,0:T(8,128)(2,1)}, f32[8,1120]{1,0:T(8,128)}, f32[1,1120]{1,0:T(1,128)}, f32[1,560]{1,0:T(1,...) custom-call(bf16[144,1120]{1,0:T(8,128)(2,1)} %get-tuple-element.303, ...), custom_call_target="tpu_custom_call" | custom-call | flops 3000000000 | bytes 15274560 | tf_op jit(solution)/shard_map/lift_back/pallas_call | solution.py:70
  585.5 5.8 up_grad.2
  601.3 5.7 collective-permute-done.169
  607.0 6.5 collective-permute-done.170
  614.7 5.2 collective-permute-done.171
  619.9 6.6 collective-permute-done.172
  638.1 9.0 collective-permute-start.188
  649.2 7.2 collective-permute-done.122.refs_2_
  695.9 18.1 %attend_back.3 = (bf16[1088,1120]{1,0:T(8,128)(2,1)}, bf16[1088,420]{1,0:T(8,128)(2,1)}, f32[8,1120]{1,0:T(8,128)}, f32[1,1120]{1,0:T(1,128)}, f32[1,420]{1,0:T(...) custom-call(s32[2]{0:T(128)} %pad_add_fusion.1.me_ref, ...), custom_call_target="tpu_custom_call" | custom-call | flops 8000000000 | bytes 12540952 | tf_op jit(solution)/shard_map/attend_back/pallas_call | solution.py:70
  716.6 7.5 collective-permute-start.194
  726.8 4.9 qkv_grad.2
  734.0 27.5 %collective-permute-done.196 = bf16[22,140]{1,0:T(8,128)(2,1)S(1)} collective-permute-done((bf16[22,140]{1,0:T(8,128)(2,1)S(1)}, bf16[22,140]{1,0:T(8,128)(2,1)S(1)}, u32[]{:S(2)}, u32[]{:S(2)}) %collective-permute-start.196) | collective-permute-done | bytes 6192 | tf_op jit(solution)/shard_map/ppermute | solution.py:516
  764.1 5.2 collective-permute-done.143
  769.3 5.9 collective-permute-done.144
  776.2 4.8 collective-permute-done.145
  781.0 5.8 collective-permute-done.146
  788.4 4.9 collective-permute-done.147
  793.5 6.2 collective-permute-done.148
  811.6 6.1 collective-permute-done.162
  824.1 5.5 collective-permute-start.149
  839.4 48.7 %psum.7 = bf16[2,1120]{1,0:T(2,128)(2,1)S(1)} all-reduce(bf16[2,1120]{1,0:T(2,128)(2,1)S(1)} %slice.146), channel_id=1, replica_groups=mesh['cell'=4,'gene'=8] {'gene','cell'}, use_global_device_ids=true, to_apply=%region_0.1 | all-reduce | flops 2240 | bytes 8960 | tf_op jit(solution)/shard_map/psum | solution.py:803
  911.0 24.0 %collective-permute-done.190 = bf16[560,1120]{1,0:T(8,128)(2,1)S(1)} collective-permute-done((bf16[560,1120]{1,0:T(8,128)(2,1)S(1)}, bf16[560,1120]{1,0:T(8,128)(2,1)S(1)}, u32[]{:S(2)}, u32[]{:S(2)}) %collective-permute-start.190) | collective-permute-done | bytes 1254432 | tf_op jit(solution)/shard_map/ppermute | solution.py:516
  937.8 27.9 %collective-permute-done.177 = bf16[8,140,560]{2,0,1:T(8,128)(2,1)S(1)} collective-permute-done((bf16[8,140,560]{2,0,1:T(8,128)(2,1)S(1)}, bf16[8,140,560]{2,0,1:T(8,128)(2,1)S(1)}, u32[]{:S(2)}, u32[]{:S(2)}) %collective-permute-start.177) | collective-permute-done | bytes 1254432 | tf_op jit(solution)/shard_map/ppermute | solution.py:516
  967.2 4.9 join.3
  972.2 7.3 copy.148
  979.5 8.5 collective-permute-done.151
  994.2 6.1 copy.146
  (914 shorter events, 412.4 us)
Async XLA Ops:
  5.1 33.1 %collective-permute-start.1 = (bf16[144,1120]{1,0:T(8,128)(2,1)}, bf16[144,1120]{1,0:T(8,128)(2,1)S(1)}, u32[]{:S(2)}, u32[]{:S(2)}) collective-permute-start(bf16[144,1120]{1,0:T(8,128)(2,1)} %get-tuple-element.203.refs_0_), channel_id=1, source_target_pairs={{0,2},{1,3},{2,0},{3,1},{4,6},{5,7},{6,4},{7,5},{8,10},{9,11},{10,... | collective-permute-start | bytes 967688 | tf_op jit(solution)/shard_map/ppermute | solution.py:483
  8.1 30.6 %collective-permute-start.3 = (bf16[144,1120]{1,0:T(8,128)(2,1)}, bf16[144,1120]{1,0:T(8,128)(2,1)S(1)}, u32[]{:S(2)}, u32[]{:S(2)}) collective-permute-start(bf16[144,1120]{1,0:T(8,128)(2,1)} %get-tuple-element.203.refs_0_), channel_id=1, source_target_pairs={{0,4},{1,5},{2,6},{3,7},{4,0},{5,1},{6,2},{7,3},{8,12},{9,13},{10,... | collective-permute-start | bytes 967688 | tf_op jit(solution)/shard_map/ppermute | solution.py:483
  9.6 29.2 %collective-permute-start.5 = (bf16[144,1120]{1,0:T(8,128)(2,1)}, bf16[144,1120]{1,0:T(8,128)(2,1)S(1)}, u32[]{:S(2)}, u32[]{:S(2)}) collective-permute-start(bf16[144,1120]{1,0:T(8,128)(2,1)} %get-tuple-element.203.refs_0_), channel_id=1, source_target_pairs={{0,6},{1,7},{2,4},{3,5},{4,2},{5,3},{6,0},{7,1},{8,14},{9,15},{10,... | collective-permute-start | bytes 967688 | tf_op jit(solution)/shard_map/ppermute | solution.py:483
  95.0 30.6 %collective-permute-start.22 = (bf16[144,1120]{1,0:T(8,128)(2,1)}, bf16[144,1120]{1,0:T(8,128)(2,1)S(1)}, u32[]{:S(2)}, u32[]{:S(2)}) collective-permute-start(bf16[144,1120]{1,0:T(8,128)(2,1)} %get-tuple-element.222.refs_0_), channel_id=1, source_target_pairs={{0,2},{1,3},{2,0},{3,1},{4,6},{5,7},{6,4},{7,5},{8,10},{9,11},{10,... | collective-permute-start | bytes 967688 | tf_op jit(solution)/shard_map/ppermute | solution.py:483
  95.8 30.3 %collective-permute-start.24 = (bf16[144,1120]{1,0:T(8,128)(2,1)}, bf16[144,1120]{1,0:T(8,128)(2,1)S(1)}, u32[]{:S(2)}, u32[]{:S(2)}) collective-permute-start(bf16[144,1120]{1,0:T(8,128)(2,1)} %get-tuple-element.222.refs_0_), channel_id=1, source_target_pairs={{0,4},{1,5},{2,6},{3,7},{4,0},{5,1},{6,2},{7,3},{8,12},{9,13},{10,... | collective-permute-start | bytes 967688 | tf_op jit(solution)/shard_map/ppermute | solution.py:483
  96.8 29.3 %collective-permute-start.26 = (bf16[144,1120]{1,0:T(8,128)(2,1)}, bf16[144,1120]{1,0:T(8,128)(2,1)S(1)}, u32[]{:S(2)}, u32[]{:S(2)}) collective-permute-start(bf16[144,1120]{1,0:T(8,128)(2,1)} %get-tuple-element.222.refs_0_), channel_id=1, source_target_pairs={{0,6},{1,7},{2,4},{3,5},{4,2},{5,3},{6,0},{7,1},{8,14},{9,15},{10,... | collective-permute-start | bytes 967688 | tf_op jit(solution)/shard_map/ppermute | solution.py:483
  157.5 18.2 %collective-permute-start.49 = (bf16[140,504]{1,0:T(8,128)(2,1)}, bf16[140,504]{1,0:T(8,128)(2,1)S(1)}, u32[]{:S(2)}, u32[]{:S(2)}) collective-permute-start(bf16[140,504]{1,0:T(8,128)(2,1)} %get-tuple-element.242), channel_id=1, source_target_pairs={{0,1},{1,0},{2,3},{3,2},{4,5},{5,4},{6,7},{7,6},{8,9},{9,8},{10,11... | collective-permute-start | bytes 423368 | tf_op jit(solution)/shard_map/ppermute | solution.py:483
  170.5 27.9 %collective-permute-start.43 = (bf16[144,1120]{1,0:T(8,128)(2,1)}, bf16[144,1120]{1,0:T(8,128)(2,1)S(1)}, u32[]{:S(2)}, u32[]{:S(2)}) collective-permute-start(bf16[144,1120]{1,0:T(8,128)(2,1)} %get-tuple-element.240.refs_0_), channel_id=1, source_target_pairs={{0,2},{1,3},{2,0},{3,1},{4,6},{5,7},{6,4},{7,5},{8,10},{9,11},{10,... | collective-permute-start | bytes 967688 | tf_op jit(solution)/shard_map/ppermute | solution.py:483
  172.2 26.6 %collective-permute-start.45 = (bf16[144,1120]{1,0:T(8,128)(2,1)}, bf16[144,1120]{1,0:T(8,128)(2,1)S(1)}, u32[]{:S(2)}, u32[]{:S(2)}) collective-permute-start(bf16[144,1120]{1,0:T(8,128)(2,1)} %get-tuple-element.240.refs_0_), channel_id=1, source_target_pairs={{0,4},{1,5},{2,6},{3,7},{4,0},{5,1},{6,2},{7,3},{8,12},{9,13},{10,... | collective-permute-start | bytes 967688 | tf_op jit(solution)/shard_map/ppermute | solution.py:483
  172.5 26.5 %collective-permute-start.47 = (bf16[144,1120]{1,0:T(8,128)(2,1)}, bf16[144,1120]{1,0:T(8,128)(2,1)S(1)}, u32[]{:S(2)}, u32[]{:S(2)}) collective-permute-start(bf16[144,1120]{1,0:T(8,128)(2,1)} %get-tuple-element.240.refs_0_), channel_id=1, source_target_pairs={{0,6},{1,7},{2,4},{3,5},{4,2},{5,3},{6,0},{7,1},{8,14},{9,15},{10,... | collective-permute-start | bytes 967688 | tf_op jit(solution)/shard_map/ppermute | solution.py:483
  198.3 23.6 %collective-permute-start.42 = (bf16[144,1120]{1,0:T(8,128)(2,1)}, bf16[144,1120]{1,0:T(8,128)(2,1)S(1)}, u32[]{:S(2)}, u32[]{:S(2)}) collective-permute-start(bf16[144,1120]{1,0:T(8,128)(2,1)} %get-tuple-element.240.refs_0_), channel_id=1, source_target_pairs={{0,1},{1,0},{2,3},{3,2},{4,5},{5,4},{6,7},{7,6},{8,9},{9,8},{10,11... | collective-permute-start | bytes 967688 | tf_op jit(solution)/shard_map/ppermute | solution.py:483
  198.3 23.5 %collective-permute-start.44 = (bf16[144,1120]{1,0:T(8,128)(2,1)S(1)}, bf16[144,1120]{1,0:T(8,128)(2,1)S(1)}, u32[]{:S(2)}, u32[]{:S(2)}) collective-permute-start(bf16[144,1120]{1,0:T(8,128)(2,1)S(1)} %collective-permute-done.43.refs_2_), channel_id=1, source_target_pairs={{0,1},{1,0},{2,3},{3,2},{4,5},{5,4},{6,7},{7,6},{8,9},{9,8},{10,11... | collective-permute-start | bytes 967688 | tf_op jit(solution)/shard_map/ppermute | solution.py:483
  198.8 23.1 %collective-permute-start.46 = (bf16[144,1120]{1,0:T(8,128)(2,1)S(1)}, bf16[144,1120]{1,0:T(8,128)(2,1)S(1)}, u32[]{:S(2)}, u32[]{:S(2)}) collective-permute-start(bf16[144,1120]{1,0:T(8,128)(2,1)S(1)} %collective-permute-done.45.refs_4_), channel_id=1, source_target_pairs={{0,1},{1,0},{2,3},{3,2},{4,5},{5,4},{6,7},{7,6},{8,9},{9,8},{10,11... | collective-permute-start | bytes 967688 | tf_op jit(solution)/shard_map/ppermute | solution.py:483
  198.9 23.0 %collective-permute-start.48 = (bf16[144,1120]{1,0:T(8,128)(2,1)S(1)}, bf16[144,1120]{1,0:T(8,128)(2,1)}, u32[]{:S(2)}, u32[]{:S(2)}) collective-permute-start(bf16[144,1120]{1,0:T(8,128)(2,1)S(1)} %collective-permute-done.47.refs_6_), channel_id=1, source_target_pairs={{0,1},{1,0},{2,3},{3,2},{4,5},{5,4},{6,7},{7,6},{8,9},{9,8},{10,11... | collective-permute-start | bytes 967688 | tf_op jit(solution)/shard_map/ppermute | solution.py:483
  251.7 27.3 %collective-permute-start.105 = (bf16[140,1120]{1,0:T(8,128)(2,1)S(1)}, bf16[140,1120]{1,0:T(8,128)(2,1)}, u32[]{:S(2)}, u32[]{:S(2)}) collective-permute-start(bf16[140,1120]{1,0:T(8,128)(2,1)S(1)} %get-tuple-element.458), channel_id=1, source_target_pairs={{0,1},{1,0},{2,3},{3,2},{4,5},{5,4},{6,7},{7,6},{8,9},{9,8},{10,11... | collective-permute-start | bytes 940808 | tf_op jit(solution)/shard_map/ppermute | solution.py:483
  253.9 21.6 %collective-permute-start.74 = (bf16[140,560]{1,0:T(8,128)(2,1)}, bf16[140,560]{1,0:T(8,128)(2,1)S(1)}, u32[]{:S(2)}, u32[]{:S(2)}) collective-permute-start(bf16[140,560]{1,0:T(8,128)(2,1)} %get-tuple-element.265), channel_id=1, source_target_pairs={{0,5},{1,4},{2,7},{3,6},{4,1},{5,0},{6,3},{7,2},{8,13},{9,12},{10,... | collective-permute-start | bytes 470408 | tf_op jit(solution)/shard_map/ppermute | solution.py:483
  279.0 27.4 %collective-permute-start.66 = (bf16[144,1120]{1,0:T(8,128)(2,1)}, bf16[144,1120]{1,0:T(8,128)(2,1)S(1)}, u32[]{:S(2)}, u32[]{:S(2)}) collective-permute-start(bf16[144,1120]{1,0:T(8,128)(2,1)} %get-tuple-element.259.refs_0_), channel_id=1, source_target_pairs={{0,4},{1,5},{2,6},{3,7},{4,0},{5,1},{6,2},{7,3},{8,12},{9,13},{10,... | collective-permute-start | bytes 967688 | tf_op jit(solution)/shard_map/ppermute | solution.py:483
  279.5 30.1 %collective-permute-start.68 = (bf16[144,1120]{1,0:T(8,128)(2,1)}, bf16[144,1120]{1,0:T(8,128)(2,1)}, u32[]{:S(2)}, u32[]{:S(2)}) collective-permute-start(bf16[144,1120]{1,0:T(8,128)(2,1)} %get-tuple-element.259.refs_0_), channel_id=1, source_target_pairs={{0,6},{1,7},{2,4},{3,5},{4,2},{5,3},{6,0},{7,1},{8,14},{9,15},{10,... | collective-permute-start | bytes 967688 | tf_op jit(solution)/shard_map/ppermute | solution.py:483
  286.3 25.6 %collective-permute-start.89 = (bf16[144,1120]{1,0:T(8,128)(2,1)}, bf16[144,1120]{1,0:T(8,128)(2,1)}, u32[]{:S(2)}, u32[]{:S(2)}) collective-permute-start(bf16[144,1120]{1,0:T(8,128)(2,1)} %get-tuple-element.279.refs_0_), channel_id=1, source_target_pairs={{0,6},{1,7},{2,4},{3,5},{4,2},{5,3},{6,0},{7,1},{8,14},{9,15},{10,... | collective-permute-start | bytes 967688 | tf_op jit(solution)/shard_map/ppermute | solution.py:483
  288.0 24.0 %collective-permute-start.63 = (bf16[144,1120]{1,0:T(8,128)(2,1)}, bf16[144,1120]{1,0:T(8,128)(2,1)S(1)}, u32[]{:S(2)}, u32[]{:S(2)}) collective-permute-start(bf16[144,1120]{1,0:T(8,128)(2,1)} %get-tuple-element.259.refs_0_), channel_id=1, source_target_pairs={{0,1},{1,0},{2,3},{3,2},{4,5},{5,4},{6,7},{7,6},{8,9},{9,8},{10,11... | collective-permute-start | bytes 967688 | tf_op jit(solution)/shard_map/ppermute | solution.py:483
  293.4 19.1 %collective-permute-start.65 = (bf16[144,1120]{1,0:T(8,128)(2,1)S(1)}, bf16[144,1120]{1,0:T(8,128)(2,1)S(1)}, u32[]{:S(2)}, u32[]{:S(2)}) collective-permute-start(bf16[144,1120]{1,0:T(8,128)(2,1)S(1)} %collective-permute-done.64.refs_2_), channel_id=1, source_target_pairs={{0,1},{1,0},{2,3},{3,2},{4,5},{5,4},{6,7},{7,6},{8,9},{9,8},{10,11... | collective-permute-start | bytes 967688 | tf_op jit(solution)/shard_map/ppermute | solution.py:483
  311.9 18.5 %collective-permute-start.84 = (bf16[144,1120]{1,0:T(8,128)(2,1)}, bf16[144,1120]{1,0:T(8,128)(2,1)}, u32[]{:S(2)}, u32[]{:S(2)}) collective-permute-start(bf16[144,1120]{1,0:T(8,128)(2,1)} %get-tuple-element.279.refs_0_), channel_id=1, source_target_pairs={{0,1},{1,0},{2,3},{3,2},{4,5},{5,4},{6,7},{7,6},{8,9},{9,8},{10,11... | collective-permute-start | bytes 967688 | tf_op jit(solution)/shard_map/ppermute | solution.py:483
  312.0 18.4 %collective-permute-start.86 = (bf16[144,1120]{1,0:T(8,128)(2,1)S(1)}, bf16[144,1120]{1,0:T(8,128)(2,1)}, u32[]{:S(2)}, u32[]{:S(2)}) collective-permute-start(bf16[144,1120]{1,0:T(8,128)(2,1)S(1)} %collective-permute-done.85.refs_2_), channel_id=1, source_target_pairs={{0,1},{1,0},{2,3},{3,2},{4,5},{5,4},{6,7},{7,6},{8,9},{9,8},{10,11... | collective-permute-start | bytes 967688 | tf_op jit(solution)/shard_map/ppermute | solution.py:483
  312.5 18.3 %collective-permute-start.88 = (bf16[144,1120]{1,0:T(8,128)(2,1)S(1)}, bf16[144,1120]{1,0:T(8,128)(2,1)}, u32[]{:S(2)}, u32[]{:S(2)}) collective-permute-start(bf16[144,1120]{1,0:T(8,128)(2,1)S(1)} %collective-permute-done.87.refs_4_), channel_id=1, source_target_pairs={{0,1},{1,0},{2,3},{3,2},{4,5},{5,4},{6,7},{7,6},{8,9},{9,8},{10,11... | collective-permute-start | bytes 967688 | tf_op jit(solution)/shard_map/ppermute | solution.py:483
  329.9 88.4 %collective-permute-start.77 = (bf16[136,1120]{1,0:T(8,128)(2,1)}, bf16[136,1120]{1,0:T(8,128)(2,1)S(1)}, u32[]{:S(2)}, u32[]{:S(2)}) collective-permute-start(bf16[136,1120]{1,0:T(8,128)(2,1)} %get-tuple-element.269), channel_id=1, source_target_pairs={{0,1},{1,0},{2,3},{3,2},{4,5},{5,4},{6,7},{7,6},{8,9},{9,8},{10,11... | collective-permute-start | bytes 913928 | tf_op jit(solution)/shard_map/ppermute | solution.py:483
  330.3 50.4 %collective-permute-start.78 = (bf16[136,1120]{1,0:T(8,128)(2,1)}, bf16[136,1120]{1,0:T(8,128)(2,1)}, u32[]{:S(2)}, u32[]{:S(2)}) collective-permute-start(bf16[136,1120]{1,0:T(8,128)(2,1)} %get-tuple-element.271), channel_id=1, source_target_pairs={{0,1},{1,0},{2,3},{3,2},{4,5},{5,4},{6,7},{7,6},{8,9},{9,8},{10,11... | collective-permute-start | bytes 913928 | tf_op jit(solution)/shard_map/ppermute | solution.py:483
  330.4 55.0 %collective-permute-start.80 = (bf16[136,1120]{1,0:T(8,128)(2,1)}, bf16[136,1120]{1,0:T(8,128)(2,1)S(1)}, u32[]{:S(2)}, u32[]{:S(2)}) collective-permute-start(bf16[136,1120]{1,0:T(8,128)(2,1)} %get-tuple-element.273), channel_id=1, source_target_pairs={{0,1},{1,0},{2,3},{3,2},{4,5},{5,4},{6,7},{7,6},{8,9},{9,8},{10,11... | collective-permute-start | bytes 913928 | tf_op jit(solution)/shard_map/ppermute | solution.py:483
  341.4 44.2 %collective-permute-start.91 = (bf16[136,1120]{1,0:T(8,128)(2,1)}, bf16[136,1120]{1,0:T(8,128)(2,1)S(1)}, u32[]{:S(2)}, u32[]{:S(2)}) collective-permute-start(bf16[136,1120]{1,0:T(8,128)(2,1)} %get-tuple-element.282), channel_id=1, source_target_pairs={{0,1},{1,0},{2,3},{3,2},{4,5},{5,4},{6,7},{7,6},{8,9},{9,8},{10,11... | collective-permute-start | bytes 913928 | tf_op jit(solution)/shard_map/ppermute | solution.py:483
  385.5 32.9 %collective-permute-start.82 = (bf16[136,1120]{1,0:T(8,128)(2,1)}, bf16[136,1120]{1,0:T(8,128)(2,1)S(1)}, u32[]{:S(2)}, u32[]{:S(2)}) collective-permute-start(bf16[136,1120]{1,0:T(8,128)(2,1)} %get-tuple-element.275), channel_id=1, source_target_pairs={{0,1},{1,0},{2,3},{3,2},{4,5},{5,4},{6,7},{7,6},{8,9},{9,8},{10,11... | collective-permute-start | bytes 913928 | tf_op jit(solution)/shard_map/ppermute | solution.py:483
  385.6 28.9 %collective-permute-start.183 = (bf16[140,560]{1,0:T(8,128)(2,1)}, bf16[140,560]{1,0:T(8,128)(2,1)S(1)}, u32[]{:S(2)}, u32[]{:S(2)}) collective-permute-start(bf16[140,560]{1,0:T(8,128)(2,1)} %get-tuple-element.371), channel_id=1, source_target_pairs={{0,6},{1,7},{2,4},{3,5},{4,2},{5,3},{6,0},{7,1},{8,14},{9,15},{10,... | collective-permute-start | bytes 470408 | tf_op jit(solution)/shard_map/ppermute | solution.py:483
  392.9 24.0 %collective-permute-start.184 = (bf16[140,560]{1,0:T(8,128)(2,1)}, bf16[140,560]{1,0:T(8,128)(2,1)S(1)}, u32[]{:S(2)}, u32[]{:S(2)}) collective-permute-start(bf16[140,560]{1,0:T(8,128)(2,1)} %get-tuple-element.372), channel_id=1, source_target_pairs={{0,7},{1,6},{2,5},{3,4},{4,3},{5,2},{6,1},{7,0},{8,15},{9,14},{10,... | collective-permute-start | bytes 470408 | tf_op jit(solution)/shard_map/ppermute | solution.py:483
  414.5 24.1 %collective-permute-start.81 = (bf16[136,1120]{1,0:T(8,128)(2,1)S(1)}, bf16[136,1120]{1,0:T(8,128)(2,1)S(1)}, u32[]{:S(2)}, u32[]{:S(2)}) collective-permute-start(bf16[136,1120]{1,0:T(8,128)(2,1)S(1)} %add_convert_fusion.29), channel_id=1, source_target_pairs={{0,4},{1,5},{2,6},{3,7},{4,0},{5,1},{6,2},{7,3},{8,12},{9,13},{10,... | collective-permute-start | bytes 913928 | tf_op jit(solution)/shard_map/ppermute | solution.py:483
  416.9 21.7 %collective-permute-start.99 = (bf16[144,1120]{1,0:T(8,128)(2,1)}, bf16[144,1120]{1,0:T(8,128)(2,1)}, u32[]{:S(2)}, u32[]{:S(2)}) collective-permute-start(bf16[144,1120]{1,0:T(8,128)(2,1)} %get-tuple-element.290.refs_0_), channel_id=1, source_target_pairs={{0,2},{1,3},{2,0},{3,1},{4,6},{5,7},{6,4},{7,5},{8,10},{9,11},{10,... | collective-permute-start | bytes 967688 | tf_op jit(solution)/shard_map/ppermute | solution.py:483
  418.3 25.1 %collective-permute-start.101 = (bf16[144,1120]{1,0:T(8,128)(2,1)}, bf16[144,1120]{1,0:T(8,128)(2,1)}, u32[]{:S(2)}, u32[]{:S(2)}) collective-permute-start(bf16[144,1120]{1,0:T(8,128)(2,1)} %get-tuple-element.290.refs_0_), channel_id=1, source_target_pairs={{0,4},{1,5},{2,6},{3,7},{4,0},{5,1},{6,2},{7,3},{8,12},{9,13},{10,... | collective-permute-start | bytes 967688 | tf_op jit(solution)/shard_map/ppermute | solution.py:483
  418.3 25.0 %collective-permute-start.103 = (bf16[144,1120]{1,0:T(8,128)(2,1)}, bf16[144,1120]{1,0:T(8,128)(2,1)}, u32[]{:S(2)}, u32[]{:S(2)}) collective-permute-start(bf16[144,1120]{1,0:T(8,128)(2,1)} %get-tuple-element.290.refs_0_), channel_id=1, source_target_pairs={{0,6},{1,7},{2,4},{3,5},{4,2},{5,3},{6,0},{7,1},{8,14},{9,15},{10,... | collective-permute-start | bytes 967688 | tf_op jit(solution)/shard_map/ppermute | solution.py:483
  420.5 23.7 %collective-permute-start.83 = (bf16[136,1120]{1,0:T(8,128)(2,1)S(1)}, bf16[136,1120]{1,0:T(8,128)(2,1)S(1)}, u32[]{:S(2)}, u32[]{:S(2)}) collective-permute-start(bf16[136,1120]{1,0:T(8,128)(2,1)S(1)} %add_convert_fusion.28), channel_id=1, source_target_pairs={{0,6},{1,7},{2,4},{3,5},{4,2},{5,3},{6,0},{7,1},{8,14},{9,15},{10,... | collective-permute-start | bytes 913928 | tf_op jit(solution)/shard_map/ppermute | solution.py:483
  444.3 39.1 %collective-permute-start.191 = (bf16[560,1120]{1,0:T(8,128)(2,1)}, bf16[560,1120]{1,0:T(8,128)(2,1)}, u32[]{:S(2)}, u32[]{:S(2)}) collective-permute-start(bf16[560,1120]{1,0:T(8,128)(2,1)} %convolution_convert_fusion), channel_id=1, source_target_pairs={{0,8},{24,16},{1,9},{25,17},{2,10},{26,18},{3,11},{27,19},{4,12},{... | collective-permute-start | bytes 3763208 | tf_op jit(solution)/shard_map/ppermute | solution.py:512
  453.4 96.4 %collective-permute-start.185 = (bf16[8,140,560]{2,0,1:T(8,128)(2,1)S(1)}, bf16[8,140,560]{2,0,1:T(8,128)(2,1)S(1)}, u32[]{:S(2)}, u32[]{:S(2)}) collective-permute-start(bf16[8,140,560]{2,0,1:T(8,128)(2,1)S(1)} %copy.138), channel_id=1, source_target_pairs={{0,8},{24,16},{1,9},{25,17},{2,10},{26,18},{3,11},{27,19},{4,12},{... | collective-permute-start | bytes 3763208 | tf_op jit(solution)/shard_map/ppermute | solution.py:512
  472.9 54.4 %collective-permute-start.106 = (bf16[136,1120]{1,0:T(8,128)(2,1)}, bf16[136,1120]{1,0:T(8,128)(2,1)}, u32[]{:S(2)}, u32[]{:S(2)}) collective-permute-start(bf16[136,1120]{1,0:T(8,128)(2,1)} %get-tuple-element.295), channel_id=1, source_target_pairs={{0,1},{1,0},{2,3},{3,2},{4,5},{5,4},{6,7},{7,6},{8,9},{9,8},{10,11... | collective-permute-start | bytes 913928 | tf_op jit(solution)/shard_map/ppermute | solution.py:483
  473.4 37.1 %collective-permute-start.107 = (bf16[136,1120]{1,0:T(8,128)(2,1)}, bf16[136,1120]{1,0:T(8,128)(2,1)}, u32[]{:S(2)}, u32[]{:S(2)}) collective-permute-start(bf16[136,1120]{1,0:T(8,128)(2,1)} %get-tuple-element.297), channel_id=1, source_target_pairs={{0,1},{1,0},{2,3},{3,2},{4,5},{5,4},{6,7},{7,6},{8,9},{9,8},{10,11... | collective-permute-start | bytes 913928 | tf_op jit(solution)/shard_map/ppermute | solution.py:483
  473.9 39.3 %collective-permute-start.109 = (bf16[136,1120]{1,0:T(8,128)(2,1)}, bf16[136,1120]{1,0:T(8,128)(2,1)S(1)}, u32[]{:S(2)}, u32[]{:S(2)}) collective-permute-start(bf16[136,1120]{1,0:T(8,128)(2,1)} %get-tuple-element.299), channel_id=1, source_target_pairs={{0,1},{1,0},{2,3},{3,2},{4,5},{5,4},{6,7},{7,6},{8,9},{9,8},{10,11... | collective-permute-start | bytes 913928 | tf_op jit(solution)/shard_map/ppermute | solution.py:483
  527.3 19.9 %collective-permute-start.166 = (bf16[140,1120]{1,0:T(8,128)(2,1)S(1)}, bf16[140,1120]{1,0:T(8,128)(2,1)}, u32[]{:S(2)}, u32[]{:S(2)}) collective-permute-start(bf16[140,1120]{1,0:T(8,128)(2,1)S(1)} %add_convert_fusion.13), channel_id=1, source_target_pairs={{8,16},{16,8},{9,17},{17,9},{10,18},{18,10},{11,19},{19,11},{12,20... | collective-permute-start | bytes 940808 | tf_op jit(solution)/shard_map/ppermute | solution.py:514
  534.0 28.2 %collective-permute-start.159 = (bf16[8,140,420]{2,0,1:T(8,128)(2,1)}, bf16[8,140,420]{2,0,1:T(8,128)(2,1)}, u32[]{:S(2)}, u32[]{:S(2)}) collective-permute-start(bf16[8,140,420]{2,0,1:T(8,128)(2,1)} %copy.126), channel_id=1, source_target_pairs={{0,8},{24,16},{1,9},{25,17},{2,10},{26,18},{3,11},{27,19},{4,12},{... | collective-permute-start | bytes 2822408 | tf_op jit(solution)/shard_map/ppermute | solution.py:512
  562.2 34.3 %collective-permute-start.192 = (bf16[560,1120]{1,0:T(8,128)(2,1)}, bf16[560,1120]{1,0:T(8,128)(2,1)}, u32[]{:S(2)}, u32[]{:S(2)}) collective-permute-start(bf16[560,1120]{1,0:T(8,128)(2,1)} %add_convert_fusion.5), channel_id=1, source_target_pairs={{8,16},{16,8},{9,17},{17,9},{10,18},{18,10},{11,19},{19,11},{12,20... | collective-permute-start | bytes 3763208 | tf_op jit(solution)/shard_map/ppermute | solution.py:514
  568.4 103.3 %collective-permute-start.186 = (bf16[8,140,560]{2,0,1:T(8,128)(2,1)S(1)}, bf16[8,140,560]{2,0,1:T(8,128)(2,1)}, u32[]{:S(2)}, u32[]{:S(2)}) collective-permute-start(bf16[8,140,560]{2,0,1:T(8,128)(2,1)S(1)} %copy.140), channel_id=1, source_target_pairs={{8,16},{16,8},{9,17},{17,9},{10,18},{18,10},{11,19},{19,11},{12,20... | collective-permute-start | bytes 3763208 | tf_op jit(solution)/shard_map/ppermute | solution.py:514
  570.1 106.2 %collective-permute-start.160 = (bf16[8,140,420]{2,0,1:T(8,128)(2,1)}, bf16[8,140,420]{2,0,1:T(8,128)(2,1)}, u32[]{:S(2)}, u32[]{:S(2)}) collective-permute-start(bf16[8,140,420]{2,0,1:T(8,128)(2,1)} %copy.128), channel_id=1, source_target_pairs={{8,16},{16,8},{9,17},{17,9},{10,18},{18,10},{11,19},{19,11},{12,20... | collective-permute-start | bytes 2822408 | tf_op jit(solution)/shard_map/ppermute | solution.py:514
  583.3 43.2 %collective-permute-start.121 = (bf16[136,1120]{1,0:T(8,128)(2,1)}, bf16[136,1120]{1,0:T(8,128)(2,1)}, u32[]{:S(2)}, u32[]{:S(2)}) collective-permute-start(bf16[136,1120]{1,0:T(8,128)(2,1)} %get-tuple-element.308), channel_id=1, source_target_pairs={{0,1},{1,0},{2,3},{3,2},{4,5},{5,4},{6,7},{7,6},{8,9},{9,8},{10,11... | collective-permute-start | bytes 913928 | tf_op jit(solution)/shard_map/ppermute | solution.py:483
  583.8 45.1 %collective-permute-start.123 = (bf16[136,1120]{1,0:T(8,128)(2,1)}, bf16[136,1120]{1,0:T(8,128)(2,1)S(1)}, u32[]{:S(2)}, u32[]{:S(2)}) collective-permute-start(bf16[136,1120]{1,0:T(8,128)(2,1)} %get-tuple-element.310), channel_id=1, source_target_pairs={{0,1},{1,0},{2,3},{3,2},{4,5},{5,4},{6,7},{7,6},{8,9},{9,8},{10,11... | collective-permute-start | bytes 913928 | tf_op jit(solution)/shard_map/ppermute | solution.py:483
  626.5 20.6 %collective-permute-start.125 = (bf16[136,1120]{1,0:T(8,128)(2,1)S(1)}, bf16[136,1120]{1,0:T(8,128)(2,1)S(1)}, u32[]{:S(2)}, u32[]{:S(2)}) collective-permute-start(bf16[136,1120]{1,0:T(8,128)(2,1)S(1)} %copy-done.149), channel_id=1, source_target_pairs={{0,1},{1,0},{2,3},{3,2},{4,5},{5,4},{6,7},{7,6},{8,9},{9,8},{10,11... | collective-permute-start | bytes 913928 | tf_op jit(solution)/shard_map/ppermute | solution.py:483
  638.1 48.1 %collective-permute-start.188 = (bf16[560,1120]{1,0:T(8,128)(2,1)S(1)}, bf16[560,1120]{1,0:T(8,128)(2,1)S(1)}, u32[]{:S(2)}, u32[]{:S(2)}) collective-permute-start(bf16[560,1120]{1,0:T(8,128)(2,1)S(1)} %convolution_convert_fusion.1), channel_id=1, source_target_pairs={{0,8},{24,16},{1,9},{25,17},{2,10},{26,18},{3,11},{27,19},{4,12},{... | collective-permute-start | bytes 3763208 | tf_op jit(solution)/shard_map/ppermute | solution.py:512
  676.3 40.3 %collective-permute-start.193 = (bf16[560,1120]{1,0:T(8,128)(2,1)}, bf16[560,1120]{1,0:T(8,128)(2,1)S(1)}, u32[]{:S(2)}, u32[]{:S(2)}) collective-permute-start(bf16[560,1120]{1,0:T(8,128)(2,1)} %add_convert_fusion.4), channel_id=1, source_target_pairs={{8,0},{16,24},{9,1},{17,25},{10,2},{18,26},{11,3},{19,27},{12,4},{... | collective-permute-start | bytes 3763208 | tf_op jit(solution)/shard_map/ppermute | solution.py:516
  687.7 113.7 %collective-permute-start.175 = (bf16[8,140,560]{2,0,1:T(8,128)(2,1)}, bf16[8,140,560]{2,0,1:T(8,128)(2,1)}, u32[]{:S(2)}, u32[]{:S(2)}) collective-permute-start(bf16[8,140,560]{2,0,1:T(8,128)(2,1)} %copy.132), channel_id=1, source_target_pairs={{0,8},{24,16},{1,9},{25,17},{2,10},{26,18},{3,11},{27,19},{4,12},{... | collective-permute-start | bytes 3763208 | tf_op jit(solution)/shard_map/ppermute | solution.py:512
  691.0 114.0 %collective-permute-start.187 = (bf16[8,140,560]{2,0,1:T(8,128)(2,1)}, bf16[8,140,560]{2,0,1:T(8,128)(2,1)}, u32[]{:S(2)}, u32[]{:S(2)}) collective-permute-start(bf16[8,140,560]{2,0,1:T(8,128)(2,1)} %copy.142), channel_id=1, source_target_pairs={{8,0},{16,24},{9,1},{17,25},{10,2},{18,26},{11,3},{19,27},{12,4},{... | collective-permute-start | bytes 3763208 | tf_op jit(solution)/shard_map/ppermute | solution.py:516
  692.3 127.2 %collective-permute-start.161 = (bf16[8,140,420]{2,0,1:T(8,128)(2,1)}, bf16[8,140,420]{2,0,1:T(8,128)(2,1)}, u32[]{:S(2)}, u32[]{:S(2)}) collective-permute-start(bf16[8,140,420]{2,0,1:T(8,128)(2,1)} %copy.130), channel_id=1, source_target_pairs={{8,0},{16,24},{9,1},{17,25},{10,2},{18,26},{11,3},{19,27},{12,4},{... | collective-permute-start | bytes 2822408 | tf_op jit(solution)/shard_map/ppermute | solution.py:516
  693.7 203.5 %collective-permute-start.189 = (bf16[560,1120]{1,0:T(8,128)(2,1)}, bf16[560,1120]{1,0:T(8,128)(2,1)}, u32[]{:S(2)}, u32[]{:S(2)}) collective-permute-start(bf16[560,1120]{1,0:T(8,128)(2,1)} %add_convert_fusion.7), channel_id=1, source_target_pairs={{8,16},{16,8},{9,17},{17,9},{10,18},{18,10},{11,19},{19,11},{12,20... | collective-permute-start | bytes 3763208 | tf_op jit(solution)/shard_map/ppermute | solution.py:514
  731.7 29.9 %collective-permute-start.196 = (bf16[22,140]{1,0:T(8,128)(2,1)S(1)}, bf16[22,140]{1,0:T(8,128)(2,1)S(1)}, u32[]{:S(2)}, u32[]{:S(2)}) collective-permute-start(bf16[22,140]{1,0:T(8,128)(2,1)S(1)} %add_convert_fusion.40), channel_id=1, source_target_pairs={{8,0},{16,24},{9,1},{17,25},{10,2},{18,26},{11,3},{19,27},{12,4},{... | collective-permute-start | bytes 18488 | tf_op jit(solution)/shard_map/ppermute | solution.py:516
  799.7 24.4 %collective-permute-start.135 = (bf16[136,1120]{1,0:T(8,128)(2,1)}, bf16[136,1120]{1,0:T(8,128)(2,1)S(1)}, u32[]{:S(2)}, u32[]{:S(2)}) collective-permute-start(bf16[136,1120]{1,0:T(8,128)(2,1)} %get-tuple-element.319), channel_id=1, source_target_pairs={{0,1},{1,0},{2,3},{3,2},{4,5},{5,4},{6,7},{7,6},{8,9},{9,8},{10,11... | collective-permute-start | bytes 913928 | tf_op jit(solution)/shard_map/ppermute | solution.py:483
  810.4 19.2 %collective-permute-start.137 = (bf16[136,1120]{1,0:T(8,128)(2,1)S(1)}, bf16[136,1120]{1,0:T(8,128)(2,1)S(1)}, u32[]{:S(2)}, u32[]{:S(2)}) collective-permute-start(bf16[136,1120]{1,0:T(8,128)(2,1)S(1)} %add_convert_fusion.18), channel_id=1, source_target_pairs={{0,2},{1,3},{2,0},{3,1},{4,6},{5,7},{6,4},{7,5},{8,10},{9,11},{10,... | collective-permute-start | bytes 913928 | tf_op jit(solution)/shard_map/ppermute | solution.py:483
  824.1 69.8 %collective-permute-start.149 = (bf16[8,140,420]{2,0,1:T(8,128)(2,1)}, bf16[8,140,420]{2,0,1:T(8,128)(2,1)}, u32[]{:S(2)}, u32[]{:S(2)}) collective-permute-start(bf16[8,140,420]{2,0,1:T(8,128)(2,1)} %copy.120), channel_id=1, source_target_pairs={{0,8},{24,16},{1,9},{25,17},{2,10},{26,18},{3,11},{27,19},{4,12},{... | collective-permute-start | bytes 2822408 | tf_op jit(solution)/shard_map/ppermute | solution.py:512
  829.6 75.5 %collective-permute-start.176 = (bf16[8,140,560]{2,0,1:T(8,128)(2,1)}, bf16[8,140,560]{2,0,1:T(8,128)(2,1)}, u32[]{:S(2)}, u32[]{:S(2)}) collective-permute-start(bf16[8,140,560]{2,0,1:T(8,128)(2,1)} %copy.134), channel_id=1, source_target_pairs={{8,16},{16,8},{9,17},{17,9},{10,18},{18,10},{11,19},{19,11},{12,20... | collective-permute-start | bytes 3763208 | tf_op jit(solution)/shard_map/ppermute | solution.py:514
  833.1 58.3 %collective-permute-start.163 = (bf16[140,1120]{1,0:T(8,128)(2,1)}, bf16[140,1120]{1,0:T(8,128)(2,1)}, u32[]{:S(2)}, u32[]{:S(2)}) collective-permute-start(bf16[140,1120]{1,0:T(8,128)(2,1)} %add_convert_fusion.15), channel_id=1, source_target_pairs={{8,16},{16,8},{9,17},{17,9},{10,18},{18,10},{11,19},{19,11},{12,20... | collective-permute-start | bytes 940808 | tf_op jit(solution)/shard_map/ppermute | solution.py:514
  899.2 35.8 %collective-permute-start.190 = (bf16[560,1120]{1,0:T(8,128)(2,1)S(1)}, bf16[560,1120]{1,0:T(8,128)(2,1)S(1)}, u32[]{:S(2)}, u32[]{:S(2)}) collective-permute-start(bf16[560,1120]{1,0:T(8,128)(2,1)S(1)} %add_convert_fusion.6), channel_id=1, source_target_pairs={{8,0},{16,24},{9,1},{17,25},{10,2},{18,26},{11,3},{19,27},{12,4},{... | collective-permute-start | bytes 3763208 | tf_op jit(solution)/shard_map/ppermute | solution.py:516
  907.0 58.7 %collective-permute-start.177 = (bf16[8,140,560]{2,0,1:T(8,128)(2,1)S(1)}, bf16[8,140,560]{2,0,1:T(8,128)(2,1)S(1)}, u32[]{:S(2)}, u32[]{:S(2)}) collective-permute-start(bf16[8,140,560]{2,0,1:T(8,128)(2,1)S(1)} %copy.136), channel_id=1, source_target_pairs={{8,0},{16,24},{9,1},{17,25},{10,2},{18,26},{11,3},{19,27},{12,4},{... | collective-permute-start | bytes 3763208 | tf_op jit(solution)/shard_map/ppermute | solution.py:516
  909.5 78.5 %collective-permute-start.151 = (bf16[8,140,420]{2,0,1:T(8,128)(2,1)S(1)}, bf16[8,140,420]{2,0,1:T(8,128)(2,1)S(1)}, u32[]{:S(2)}, u32[]{:S(2)}) collective-permute-start(bf16[8,140,420]{2,0,1:T(8,128)(2,1)S(1)} %copy.124), channel_id=1, source_target_pairs={{8,0},{16,24},{9,1},{17,25},{10,2},{18,26},{11,3},{19,27},{12,4},{... | collective-permute-start | bytes 2822408 | tf_op jit(solution)/shard_map/ppermute | solution.py:516
  (322 other events, 3791.5 us)

commit v2 on v1

v2 whole, which is shorter than its diff:
```python
import functools
import math

import jax
import jax.numpy as jnp
from jax import lax
from jax.experimental import pallas as pl
from jax.experimental.pallas import tpu as pltpu
from jax.sharding import PartitionSpec as P

D = 1120
HEADS = 20
HEAD_DIM = 56
FF = 4480
PREFIX = 64
LAYERS = 2
LANES = 128
HALF = 64
SCALE = HEAD_DIM ** (-0.5)
SCALE2 = SCALE * math.log2(math.e)
BF = jnp.bfloat16
F32 = jnp.float32
COST = 1000


def dot(left, right, left_dim=1, right_dim=0):
    return lax.dot_general(
        left, right, (((left_dim,), (right_dim,)), ((), ())), preferred_element_type=F32
    )


class Plan:
    def __init__(self, groups, gene_rows):
        self.groups = groups
        self.chips = groups // 2
        self.gene_rows = gene_rows
        self.pre_rows = PREFIX // groups
        self.pre_block = -(-self.pre_rows // 8) * 8
        self.own_rows = gene_rows + self.pre_block
        self.step_rows = -(-self.own_rows // 16) * 16
        self.genes = self.chips * gene_rows
        self.prefix = self.chips * self.pre_block
        self.rows = self.genes + self.prefix
        self.all_rows = self.chips * self.step_rows
        self.cols = D // groups
        self.chip_cols = D // self.chips
        self.hidden = FF // groups
        self.chip_hidden = FF // self.chips
        self.part = -(-self.cols // 16) * 16
        self.features = groups * self.part
        spans = [
            (self.chip_cols * at // HEAD_DIM, -(-self.chip_cols * (at + 1) // HEAD_DIM))
            for at in range(self.chips)
        ]
        self.window = max(last - first for first, last in spans)
        self.first_heads = [min(first, HEADS - self.window) for first, _ in spans]
        self.wide = self.window * HEAD_DIM
        self.lanes = self.window * LANES
        self.by_links = groups == 8

    def halves(self, total):
        step = -(-total // 32) * 16
        return [slice(first, min(first + step, total)) for first in range(0, total, step)]


SCALAR = pl.BlockSpec(memory_space=pltpu.SMEM)
WHOLE = pl.BlockSpec(memory_space=pltpu.VMEM)


def call(kernel, name, args, outs, scratch=(), scalar=False):
    got = pl.pallas_call(
        kernel,
        in_specs=[SCALAR if scalar and at == 0 else WHOLE for at in range(len(args))],
        out_specs=[WHOLE] * len(outs),
        out_shape=outs,
        scratch_shapes=list(scratch),
        compiler_params=pltpu.CompilerParams(vmem_limit_bytes=58 << 20),
        cost_estimate=pl.CostEstimate(flops=COST, bytes_accessed=COST, transcendentals=0),
        name=name,
    )(*args)
    return list(got)


def shape_of(*dims, dtype=BF):
    return jax.ShapeDtypeStruct(dims, dtype)


def aligned(at, size):
    return pl.ds(pl.multiple_of(at * size, size), size)


def normed_of(values):
    centred = values - jnp.mean(values, axis=-1, keepdims=True)
    variance = jnp.mean(centred * centred, axis=-1, keepdims=True)
    inverse = lax.rsqrt(variance + 1e-05)
    return centred * inverse, inverse


def spread(plan, rows):
    filler = jnp.zeros((rows.shape[0], plan.part - plan.cols), rows.dtype)
    parts = []
    for at in range(plan.groups):
        parts += [rows[:, at * plan.cols : (at + 1) * plan.cols], filler]
    return jnp.concatenate(parts, 1)


def unspread(plan, rows):
    return jnp.concatenate(
        [rows[:, at * plan.part : at * plan.part + plan.cols] for at in range(plan.groups)], 1
    )


def real_rows(plan, rows):
    if plan.pre_rows == plan.pre_block:
        return rows
    at = lax.broadcasted_iota(jnp.int32, rows.shape, 0)
    return jnp.where(at < plan.gene_rows + plan.pre_rows, rows, 0.0)


def normed_piece(plan, rows, gain_ref, shift_ref, level):
    unit, _ = normed_of(rows)
    normed = unit * gain_ref[level : level + 1, :] + shift_ref[level : level + 1, :]
    return spread(plan, real_rows(plan, normed)).astype(BF)


def begin_kernel(plan, gene_ref, pre_ref, gain_ref, shift_ref, rows_ref, piece_ref):
    rows = jnp.concatenate([gene_ref[...].astype(F32).T, pre_ref[...].astype(F32)], 0)
    rows_ref[...] = rows
    piece_ref[...] = normed_piece(plan, rows, gain_ref, shift_ref, 0)


def add_parts(refs):
    total = refs[0][...].astype(F32)
    for ref in refs[1:]:
        total = total + ref[...].astype(F32)
    return total


def middle_kernel(plan, parts, level, gain_level, *refs):
    part_refs, (base_ref, bias_ref, gain_ref, shift_ref, rows_ref, piece_ref) = (
        refs[:parts],
        refs[parts:],
    )
    rows = base_ref[...] + add_parts(part_refs) + bias_ref[level : level + 1, :]
    rows_ref[...] = rows
    piece_ref[...] = normed_piece(plan, rows, gain_ref, shift_ref, gain_level)


def finish_kernel(plan, parts, level, *refs):
    part_refs, (base_ref, bias_ref, gene_ref, pre_ref) = refs[:parts], refs[parts:]
    rows = base_ref[...] + add_parts(part_refs) + bias_ref[level : level + 1, :]
    gene_ref[...] = rows[: plan.gene_rows].T
    pre_ref[...] = rows[plan.gene_rows :]


def norm_back(plan, parts, level, refs):
    part_refs, (x_ref, gain_ref, base_ref) = refs[:parts], refs[parts : parts + 3]
    grad_norm = unspread(plan, add_parts(part_refs))
    unit, inverse = normed_of(x_ref[...])
    scaled = grad_norm * gain_ref[level : level + 1, :]
    return base_ref[...] + inverse * (
        scaled
        - jnp.mean(scaled, axis=-1, keepdims=True)
        - unit * jnp.mean(scaled * unit, axis=-1, keepdims=True)
    )


def back_kernel(plan, parts, level, *refs):
    grad = norm_back(plan, parts, level, refs)
    grad_ref, piece_ref = refs[parts + 3 :]
    grad_ref[...] = grad
    piece_ref[...] = real_rows(plan, grad).astype(BF)


def back_end_kernel(plan, parts, level, *refs):
    grad = norm_back(plan, parts, level, refs)
    gene_ref, pre_ref = refs[parts + 3 :]
    gene_ref[...] = grad[: plan.gene_rows].T
    pre_ref[...] = grad[plan.gene_rows :]


def cot_kernel(plan, gene_ref, pre_ref, rows_ref, piece_ref):
    rows = jnp.concatenate([gene_ref[...].T, pre_ref[...]], 0)
    rows_ref[...] = rows
    piece_ref[...] = real_rows(plan, rows).astype(BF)


def query_chunks(plan):
    both, genes = 2 * plan.gene_rows, 2 * plan.genes
    chunks = []
    for chip in range(plan.chips):
        blocks = [(genes, 2 * plan.prefix, False)]
        blocks += [(start, both, start == chip * both) for start in range(0, (chip + 1) * both, both)]
        chunks.append((chip * plan.gene_rows, plan.gene_rows, blocks))
    chunks.append((plan.genes, plan.prefix, [(genes, 2 * plan.prefix, True)]))
    return chunks


def masked(plan, scores, start, diagonal, core):
    in_prefix = start == 2 * plan.genes
    holes = in_prefix and plan.pre_rows < plan.pre_block
    if not (diagonal or holes):
        return scores
    key_at = lax.broadcasted_iota(jnp.int32, scores.shape, 0)
    query_at = lax.broadcasted_iota(jnp.int32, scores.shape, 1)
    keep = None
    if diagonal:
        block = plan.pre_block if in_prefix else plan.gene_rows
        inner = lax.rem(query_at, block)
        keep = key_at <= 2 * query_at - inner + core * block
    if holes:
        real = lax.rem(key_at, plan.pre_block) < plan.pre_rows
        keep = real if keep is None else keep & real
    return jnp.where(keep, scores, -jnp.inf)


def collect(plan, chip, piece_refs, whole_ref, pre_ref):
    for at, ref in enumerate(piece_refs):
        owner = chip ^ at
        whole_ref[aligned(owner, plan.gene_rows), :] = ref[: plan.gene_rows, :]
        pre_ref[aligned(owner, plan.pre_block), :] = ref[plan.gene_rows :, :].astype(F32)
    whole_ref[plan.genes :, :] = pre_ref[...].astype(BF)


def collect_weight(plan, me, part_refs, weight_ref):
    for at, ref in enumerate(part_refs):
        weight_ref[aligned(me ^ at, plan.part), :] = ref[...]


def give_blocks(plan, chip, block_refs, rows_ref, weight, weight_dim, pre_ref):
    pre_ref[...] = dot(rows_ref[plan.genes :, :], weight, 1, weight_dim)
    for at, ref in enumerate(block_refs):
        owner = chip ^ at
        ref[: plan.gene_rows, :] = dot(
            rows_ref[aligned(owner, plan.gene_rows), :], weight, 1, weight_dim
        ).astype(BF)
        ref[plan.gene_rows :, :] = pre_ref[aligned(owner, plan.pre_block), :].astype(BF)


def project_kernel(plan, me_ref, *refs):
    chips, groups = plan.chips, plan.groups
    pieces, parts, refs = refs[:chips], refs[chips : chips + groups], refs[chips + groups :]
    bias_ref, widen_ref, low_ref, query_ref, pair_ref, weight_ref, pre_ref = refs
    me = me_ref[0]
    collect(plan, me_ref[1], pieces, low_ref, pre_ref)
    collect_weight(plan, me, parts, weight_ref)
    for rows in plan.halves(plan.rows):
        narrow = (dot(low_ref[rows, :], weight_ref[...]) + bias_ref[...]).astype(BF)
        wide = dot(narrow, widen_ref[...]).astype(BF)
        query_ref[rows, :] = wide[:, : plan.lanes]
        pair_ref[rows, :] = wide[:, plan.lanes :]


def order_pairs(plan, core, mine_ref, other_ref, keys_ref, pre_ref):
    for chip in range(plan.chips):
        for ref, place in ((mine_ref, 2 * chip + core), (other_ref, 2 * chip + 1 - core)):
            genes = slice(chip * plan.gene_rows, (chip + 1) * plan.gene_rows)
            keys_ref[aligned(place, plan.gene_rows), :] = ref[genes, :]
            prefix = slice(
                plan.genes + chip * plan.pre_block, plan.genes + (chip + 1) * plan.pre_block
            )
            pre_ref[aligned(place, plan.pre_block), :] = ref[prefix, :].astype(F32)
    keys_ref[2 * plan.genes :, :] = pre_ref[...].astype(BF)


def attend_kernel(plan, me_ref, *refs):
    query_ref, mine_ref, other_ref, select_ref, out_weight_ref = refs[:5]
    keys_ref, mixed_ref, lse_ref = refs[5:8]
    blocks = refs[8 : 8 + plan.chips]
    key_pre_ref, out_pre_ref, turned_ref, score_ref, padded_ref = refs[8 + plan.chips :]
    core = me_ref[2]
    order_pairs(plan, core, mine_ref, other_ref, keys_ref, key_pre_ref)
    for head in range(plan.window):
        at = slice(LANES * head, LANES * (head + 1))
        turned_ref[...] = keys_ref[:, at].astype(F32).T.astype(BF)
        for first, count, key_parts in query_chunks(plan):
            query = query_ref[first : first + count, at]
            top = None
            for start, size, diagonal in key_parts:
                scores = dot(keys_ref[start : start + size, at], query, 1, 1)
                scores = masked(plan, scores, start, diagonal, core)
                score_ref[start : start + size, :count] = scores
                high = jnp.max(scores, axis=0, keepdims=True)
                top = high if top is None else jnp.maximum(top, high)
            top = top * SCALE2
            total, mixed = 0.0, 0.0
            for start, size, _ in key_parts:
                weights = jnp.exp2(score_ref[start : start + size, :count] * SCALE2 - top)
                total = total + jnp.sum(weights, axis=0, keepdims=True)
                mixed = mixed + dot(turned_ref[:, start : start + size], weights.astype(BF))
            padded_ref[first : first + count, at] = (mixed * (1.0 / total)).T.astype(BF)
            lse_ref[head, :, first : first + count] = top + jnp.log2(total)
    mixed_ref[...] = dot(padded_ref[...], select_ref[...]).astype(BF)
    give_blocks(plan, me_ref[1], blocks, mixed_ref, out_weight_ref[...], 0, out_pre_ref)


def attend_back_kernel(plan, me_ref, *refs):
    pieces, refs = refs[: plan.chips], refs[plan.chips :]
    out_weight_ref, query_ref, keys_ref, lse_ref = refs[:4]
    low_ref, query_grad_ref, mine_ref, other_ref, out_bias_ref = refs[4:9]
    pre_ref, grad_ref, turned_ref, prob_ref, pgrad_ref, pair_ref = refs[9:]
    core = me_ref[2]
    collect(plan, me_ref[1], pieces, low_ref, pre_ref)
    out_bias_ref[...] = jnp.sum(low_ref[...].astype(F32), axis=0, keepdims=True)
    for rows in plan.halves(plan.rows):
        grad_ref[rows, :] = dot(low_ref[rows, :], out_weight_ref[...], 1, 1).astype(BF)
    lane = lax.broadcasted_iota(jnp.int32, (1, LANES), 1)
    pair_scale = jnp.where(lane < HALF, SCALE, 1.0)
    for head in range(plan.window):
        at = slice(LANES * head, LANES * (head + 1))
        turned_ref[...] = keys_ref[:, at].astype(F32).T.astype(BF)
        pair_ref[...] = jnp.zeros_like(pair_ref)
        for first, count, key_parts in query_chunks(plan):
            query = query_ref[first : first + count, at]
            grad = grad_ref[first : first + count, at]
            lse = lse_ref[head, :, first : first + count]
            delta = 0.0
            for start, size, diagonal in key_parts:
                pair = keys_ref[start : start + size, at]
                scores = masked(plan, dot(pair, query, 1, 1), start, diagonal, core)
                probs = jnp.exp2(scores * SCALE2 - lse)
                prob_grad = dot(pair, grad, 1, 1)
                delta = delta + jnp.sum(probs * prob_grad, axis=0, keepdims=True)
                prob_ref[start : start + size, :count] = probs
                pgrad_ref[start : start + size, :count] = prob_grad
            query_grad = 0.0
            for start, size, _ in key_parts:
                probs = prob_ref[start : start + size, :count]
                score_grad = (probs * (pgrad_ref[start : start + size, :count] - delta)).astype(BF)
                pair_ref[start : start + size, :] += dot(probs.astype(BF), grad) + dot(score_grad, query)
                query_grad = query_grad + dot(turned_ref[:, start : start + size], score_grad)
            query_grad_ref[first : first + count, at] = (query_grad.T * SCALE).astype(BF)
        for chip in range(plan.chips):
            for ref, place in ((mine_ref, 2 * chip + core), (other_ref, 2 * chip + 1 - core)):
                genes = slice(chip * plan.gene_rows, (chip + 1) * plan.gene_rows)
                ref[genes, at] = (pair_ref[aligned(place, plan.gene_rows), :] * pair_scale).astype(ref.dtype)
                prefix = slice(
                    plan.genes + chip * plan.pre_block, plan.genes + (chip + 1) * plan.pre_block
                )
                place = pl.ds(
                    pl.multiple_of(2 * plan.genes + place * plan.pre_block, plan.pre_block), plan.pre_block
                )
                ref[prefix, at] = (pair_ref[place, :] * pair_scale).astype(ref.dtype)


def project_back_kernel(plan, me_ref, *refs):
    query_grad_ref, mine_ref, other_ref, select_ref, weight_ref, qkv_grad_ref, bias_ref = refs[:7]
    blocks, (pre_ref,) = refs[7 : 7 + plan.chips], refs[7 + plan.chips :]
    for rows in plan.halves(plan.rows):
        pairs = (mine_ref[rows, :] + other_ref[rows, :].astype(F32)).astype(BF)
        qkv_grad_ref[rows, :] = (
            dot(query_grad_ref[rows, :], select_ref[: plan.lanes, :])
            + dot(pairs, select_ref[plan.lanes :, :])
        ).astype(BF)
    bias_ref[...] = jnp.sum(qkv_grad_ref[...].astype(F32), axis=0, keepdims=True)
    give_blocks(plan, me_ref[1], blocks, qkv_grad_ref, weight_ref[...], 1, pre_ref)


ROOT = math.sqrt(2.0 / math.pi)
CUBE = 0.044715


def stack_pieces(plan, pieces, low_ref):
    size = plan.step_rows
    for at, ref in enumerate(pieces):
        low_ref[at * size : at * size + plan.own_rows, :] = ref[...]
        if plan.own_rows < size:
            low_ref[at * size + plan.own_rows : (at + 1) * size, :] = jnp.zeros(
                (size - plan.own_rows, low_ref.shape[1]), BF
            )


def collect_down(plan, level, core, mine_ref, other_ref, down_ref):
    if plan.hidden % 16 == 0:
        down_ref[aligned(core, plan.hidden), :] = mine_ref[level]
        down_ref[aligned(1 - core, plan.hidden), :] = other_ref[level]
        return
    mine, other = mine_ref[level].astype(F32), other_ref[level].astype(F32)
    halves = [jnp.where(core == 0, mine, other), jnp.where(core == 0, other, mine)]
    down_ref[...] = jnp.concatenate(halves, 0).astype(BF)


def lift_kernel(plan, level, me_ref, *refs):
    chips, groups = plan.chips, plan.groups
    pieces, parts, refs = refs[:chips], refs[chips : chips + groups], refs[chips + groups :]
    bias_ref, mine_ref, other_ref, low_ref, pre_ref, active_ref, up_ref = refs[:7]
    blocks, (down_ref,) = refs[7:-1], refs[-1:]
    collect_weight(plan, me_ref[0], parts, up_ref)
    collect_down(plan, level, me_ref[2], mine_ref, other_ref, down_ref)
    stack_pieces(plan, pieces, low_ref)
    size = plan.step_rows
    for first in range(0, plan.all_rows, 2 * size):
        rows = slice(first, first + 2 * size)
        pre = dot(low_ref[rows, :], up_ref[...]) + bias_ref[...]
        pre_ref[rows, :] = pre
        active = (0.5 * pre * (1.0 + jnp.tanh(ROOT * (pre + CUBE * pre * pre * pre)))).astype(BF)
        active_ref[rows, :] = active
        lifted = dot(active, down_ref[...])
        for at in range(2):
            blocks[first // size + at][...] = lifted[at * size : at * size + plan.own_rows].astype(BF)


def lift_back_kernel(plan, level, me_ref, *refs):
    pieces, refs = refs[: plan.chips], refs[plan.chips :]
    up_ref, pre_ref, mine_ref, other_ref, low_ref, pre_grad_ref, down_bias_ref, up_bias_ref = refs[:8]
    blocks, (down_ref,) = refs[8:-1], refs[-1:]
    collect_down(plan, level, me_ref[2], mine_ref, other_ref, down_ref)
    stack_pieces(plan, pieces, low_ref)
    size = plan.step_rows
    down_bias_ref[...] = jnp.sum(low_ref[...].astype(F32), axis=0, keepdims=True)
    up_bias = 0.0
    for first in range(0, plan.all_rows, 2 * size):
        rows = slice(first, first + 2 * size)
        act_grad = dot(low_ref[rows, :], down_ref[...], 1, 1)
        pre = pre_ref[rows, :]
        square = pre * pre
        turn = jnp.tanh(ROOT * pre * (1.0 + CUBE * square))
        slope = 0.5 * (1.0 + turn) + (0.5 * ROOT) * pre * (1.0 - turn * turn) * (1.0 + 3.0 * CUBE * square)
        pre_grad = (act_grad * slope).astype(BF)
        pre_grad_ref[rows, :] = pre_grad
        up_bias = up_bias + jnp.sum(pre_grad.astype(F32), axis=0, keepdims=True)
        norm_grad = dot(pre_grad, up_ref[...], 1, 1)
        for at in range(2):
            blocks[first // size + at][...] = norm_grad[at * size : at * size + plan.own_rows].astype(BF)
    up_bias_ref[...] = up_bias


def send_kernel(plan, level, starts, width, me_ref, weight_ref, *refs):
    outs, (stack_ref,) = refs[: plan.chips], refs[plan.chips :]
    for to, begins in enumerate(starts):
        for at, begin in enumerate(begins):
            stack_ref[to, : plan.cols, at * width : (at + 1) * width] = weight_ref[
                level, :, begin : begin + width
            ]
        if plan.cols < plan.part:
            stack_ref[to, plan.cols :, :] = jnp.zeros(
                (plan.part - plan.cols, stack_ref.shape[2]), BF
            )
    for at, ref in enumerate(outs):
        ref[...] = stack_ref[me_ref[1] ^ at]


def weight_grad_kernel(plan, me_ref, left_ref, right_ref, weight_ref, sums_ref, vector_ref, *refs):
    passengers, (mine_ref, other_ref, whole_ref) = refs[:-3], refs[-3:]
    width = right_ref.shape[1]
    step = 2 * plan.part
    for first in range(0, plan.features, step):
        rows = slice(first, first + step)
        product = dot(left_ref[:, rows], right_ref[...], 0, 0)
        weight = weight_ref[rows, :].astype(F32)
        shift_grad = jnp.sum(weight * sums_ref[...], axis=1, keepdims=True)
        both = jnp.sum(weight * product, axis=1, keepdims=True)
        turned = vector_ref[:, rows].T
        gain_grad = (both - turned[:, 0:1] * shift_grad) / turned[:, 1:2]
        whole_ref[rows, :width] = product
        whole_ref[rows, width : width + 2] = jnp.concatenate([shift_grad, gain_grad], 1)
    for at in range(plan.chips):
        owner = me_ref[0] ^ (2 * at)
        mine_ref[at, :, : width + 2] = whole_ref[aligned(owner, plan.part), :].astype(BF)
        other_ref[at, :, : width + 2] = whole_ref[aligned(owner ^ 1, plan.part), :].astype(BF)
        for ref, rider in zip((mine_ref, other_ref), passengers):
            rows = rider.shape[0]
            lanes = slice(at * plan.chip_cols, (at + 1) * plan.chip_cols)
            filler = jnp.zeros((plan.part - rows, plan.chip_cols), F32)
            ref[at, :, width + 2 :] = jnp.concatenate([rider[:, lanes], filler], 0).astype(BF)


def join_kernel(plan, blocks, width, me_ref, *refs):
    parts, (out_ref, vector_ref) = refs[:LAYERS], refs[LAYERS:]
    each = width // blocks
    for level, ref in enumerate(parts):
        vectors = 0.0
        for source in range(plan.chips):
            value = ref[me_ref[1] ^ source].astype(F32)
            for block in range(blocks):
                begin = (block * plan.chips + source) * each
                out_ref[:, level, begin : begin + each] = value[
                    : plan.cols, block * each : (block + 1) * each
                ]
            vectors = vectors + value[:, width : width + 2]
        padded = jnp.concatenate([vectors, jnp.zeros((plan.part, LANES - 2), F32)], 1)
        vector_ref[level] = padded.T[:8]


def body(
    genes,
    prefix,
    cot_genes,
    cot_prefix,
    w_qkv,
    w_out,
    w_up,
    w_down,
    norm1_gain,
    norm1_bias,
    norm2_gain,
    norm2_bias,
    bias_q,
    bias_v,
    bias_out,
    bias_up,
    bias_down,
):
    groups = lax.axis_size("gene")
    cells = lax.axis_size("cell")
    me = lax.axis_index("gene")
    cell = lax.axis_index("cell")
    chip, core = me // 2, me % 2
    plan = Plan(groups, genes.shape[1])
    chips, cols, chip_cols, wide = plan.chips, plan.cols, plan.chip_cols, plan.wide
    hidden, chip_hidden = plan.hidden, plan.chip_hidden
    first_head = jnp.asarray(plan.first_heads, jnp.int32)[chip]
    offset = chip * chip_cols - first_head * HEAD_DIM
    turn = chip if plan.by_links else jnp.zeros_like(chip)
    where = jnp.stack([2 * turn + core, turn, core]).astype(jnp.int32)
    same_core = [[2 * at + one for at in range(chips)] for one in range(2)]
    here = functools.partial

    def after(value, *others):
        return lax.optimization_barrier((value,) + others)[0]

    def after_all(values, *others):
        return list(lax.optimization_barrier((tuple(values), others))[0])

    def together(*lists):
        return [list(got) for got in lax.optimization_barrier(tuple(tuple(x) for x in lists))]

    def swap(value, bits):
        return lax.ppermute(value, "gene", [(at, at ^ bits) for at in range(groups)])

    def to_chips(parts):
        if not plan.by_links:
            got = lax.all_to_all(jnp.stack(parts), "gene", 0, 0, axis_index_groups=same_core)
            return [got[at] for at in range(chips)]
        return [parts[0]] + [swap(parts[at], 2 * at) for at in range(1, chips)]

    def gather(piece):
        if not plan.by_links:
            got = lax.all_gather(piece, "gene", axis=0, axis_index_groups=same_core)
            return [got[at] for at in range(chips)]
        return to_chips([piece] * chips)

    def scatter(blocks):
        if not plan.by_links:
            return [
                lax.psum_scatter(
                    jnp.stack(blocks), "gene", scatter_dimension=0, axis_index_groups=same_core
                )
            ]
        return to_chips(blocks)

    def across(near):
        far = [swap(value, 1) for value in near]
        return [value for pair in zip(near, far) for value in pair]

    class CellSum:
        def __init__(self, mine, other, *steps):
            self.value = (mine.astype(F32) + other.astype(F32)).astype(BF)
            self.steps = list(steps) if cells == 4 else [steps[-1]]
            waiting.append(self)

        def move(self):
            if cells != 4:
                return lax.psum(self.value, "cell")
            inwards, between, outwards = [(0, 1), (3, 2)], [(1, 2), (2, 1)], [(1, 0), (2, 3)]
            pairs = {3: inwards, 2: between, 1: outwards}[len(self.steps)]
            return lax.ppermute(self.value, "cell", pairs)

        def land(self, got):
            if cells != 4:
                self.value = got
            elif len(self.steps) > 1:
                self.value = (self.value.astype(F32) + got.astype(F32)).astype(BF)
            else:
                self.value = jnp.where((cell == 1) | (cell == 2), self.value, got)
            self.steps.pop(0)

    waiting = []

    def beside(step, *lists):
        moving = [item for item in waiting if item.steps and item.steps[0] == step]
        *lists, landed = together(*lists, [item.move() for item in moving])
        for item, got in zip(moving, landed):
            item.land(got)
        return lists

    def send(weight, level, starts, width, *others):
        total = len(starts[0]) * width
        return call(
            here(send_kernel, plan, level, starts, width),
            "send",
            [after(where, *others), weight],
            [shape_of(plan.part, total)] * chips,
            [pltpu.VMEM((chips, plan.part, total), BF)],
            True,
        )

    qkv_starts = [
        [block * D + head * HEAD_DIM for block in range(3)] for head in plan.first_heads
    ]
    up_starts = [[to * chip_hidden] for to in range(chips)]

    def chooser(wanted, there):
        return (wanted[:, None] == there[None, :]).astype(BF)

    def own_of(block, column, real):
        ok = real & (column >= offset) & (column < offset + chip_cols)
        return jnp.where(ok, block * chip_cols + column - offset, -1)

    window_at = jnp.arange(3 * wide)
    block, column = window_at // wide, window_at % wide
    lane = (column // HEAD_DIM) * LANES + column % HEAD_DIM
    lane = lane + jnp.where(block == 0, 0, plan.lanes + HALF * (block - 1))
    widen = chooser(lane, jnp.arange(2 * plan.lanes))
    own_columns = jnp.arange(3 * chip_cols)
    cut = chooser(own_of(block, column, True), own_columns)
    lanes = jnp.arange(2 * plan.lanes)
    inner = lanes % LANES
    is_pair = lanes >= plan.lanes
    block = jnp.where(is_pair, 1 + inner // HALF, 0)
    inner = jnp.where(is_pair, inner % HALF, inner)
    column = (lanes % plan.lanes) // LANES * HEAD_DIM + inner
    select = chooser(own_of(block, column, inner < HEAD_DIM), own_columns)
    at_out = jnp.arange(plan.lanes)
    inner = at_out % LANES - HALF
    out_col = (at_out // LANES) * HEAD_DIM + inner
    out_ok = (inner >= 0) & (inner < HEAD_DIM)
    out_select = chooser(own_of(0, out_col, out_ok), jnp.arange(chip_cols))

    def by_core(mine, other):
        first, second = jnp.where(core == 0, mine, other), jnp.where(core == 0, other, mine)
        return jnp.concatenate([first, second], 1)

    def out_windows(chip_out):
        if plan.by_links:
            rows, owner = chip_out, chip * chip_cols + jnp.arange(chip_cols)
        else:
            rows = lax.all_gather(w_out, "gene", axis=1, tiled=True)
            owner = jnp.arange(D)
        pick = chooser(jnp.where(out_ok, first_head * HEAD_DIM + out_col, -1), owner)
        return [dot(pick, rows[level]).astype(BF) for level in range(LAYERS)]

    def window_of(vec):
        return lax.dynamic_slice_in_dim(vec, first_head * HEAD_DIM, wide, 1)

    def norm_vectors(token):
        every = jnp.stack([norm1_bias, norm1_gain, norm2_bias, norm2_gain])
        every = after(every, token).reshape(2, 2, LAYERS, groups, cols)
        every = jnp.pad(every, ((0, 0),) * 4 + ((0, plan.part - cols),), constant_values=1.0)
        every = every.transpose(0, 2, 1, 3, 4).reshape(2 * LAYERS, 2, plan.features)
        every = jnp.pad(every, ((0, 0), (0, 6), (0, 0)))
        return [every[at] for at in range(2 * LAYERS)]

    def up_biases_of(token):
        return lax.dynamic_slice_in_dim(after(bias_up, token), chip * chip_hidden, chip_hidden, 1)

    rows_f32 = shape_of(plan.own_rows, D, dtype=F32)
    normed_like = shape_of(plan.own_rows, plan.features)
    grad_like = shape_of(plan.own_rows, D)
    row_blocks = [grad_like] * chips
    feature_blocks = [normed_like] * chips
    vector = shape_of(1, D, dtype=F32)
    ends_like = [
        shape_of(D, plan.gene_rows, dtype=F32),
        shape_of(plan.pre_block, D, dtype=F32),
    ]

    own_prefix = lax.dynamic_slice_in_dim(prefix[0], me * plan.pre_rows, plan.pre_rows, 0)
    filler = ((0, plan.pre_block - plan.pre_rows), (0, 0))
    rows, piece = call(
        here(begin_kernel, plan),
        "begin",
        [genes[0].T, jnp.pad(own_prefix, filler), norm1_gain, norm1_bias],
        [rows_f32, normed_like],
    )
    qkv_parts, up_parts = [None] * LAYERS, [None] * LAYERS
    qkv_sent = send(w_qkv, 0, qkv_starts, wide, piece)
    pieces, near = gather(piece), to_chips(qkv_sent)
    token = qkv_sent[-1]
    up_sent = send(w_up, 0, up_starts, chip_hidden, token)
    qkv_biases = jnp.concatenate(
        [window_of(bias_q), jnp.zeros((LAYERS, wide), F32), window_of(bias_v)], 1
    )
    held_out = after(w_out, token)
    chip_out = by_core(held_out, swap(held_out, 1))
    out_weights = [chip_out[level] for level in range(LAYERS)]
    pieces, near, up_sent, _ = together(
        pieces, near, up_sent, [widen, out_select, qkv_biases] + out_weights
    )
    (qkv_parts[0],) = together(across(near))

    saved = []
    for level in range(LAYERS):
        last = level + 1 == LAYERS
        if level:
            (pieces, far) = together(gather(piece), across(near[chips // 2 :]))
            qkv_parts[level] = qkv_far + far
        up_near = to_chips(after_all(up_sent, *pieces, *qkv_parts[level]))
        low_one, query, pair, qkv_weight = call(
            here(project_kernel, plan),
            "project",
            [where] + pieces + qkv_parts[level] + [qkv_biases[level : level + 1], widen],
            [
                shape_of(plan.rows, plan.features),
                shape_of(plan.rows, plan.lanes),
                shape_of(plan.rows, plan.lanes),
                shape_of(plan.features, 3 * wide),
            ],
            [pltpu.VMEM((plan.prefix, plan.features), F32)],
            True,
        )
        outs = call(
            here(attend_kernel, plan),
            "attend",
            [where, query, pair, swap(pair, 1), out_select, out_weights[level]],
            [
                shape_of(2 * plan.rows, plan.lanes),
                shape_of(plan.rows, chip_cols),
                shape_of(plan.window, 1, plan.rows, dtype=F32),
            ]
            + row_blocks,
            [
                pltpu.VMEM((2 * plan.prefix, plan.lanes), F32),
                pltpu.VMEM((plan.prefix, D), F32),
                pltpu.VMEM((LANES, 2 * plan.rows), BF),
                pltpu.VMEM((2 * plan.rows, plan.gene_rows), F32),
                pltpu.VMEM((plan.rows, plan.lanes), BF),
            ],
            True,
        )
        outs, up_near = together(outs, up_near)
        keys, mixed, lse = outs[:3]
        spare = []
        if level == 0:
            spare = [swap(after(w_down, mixed), 1), up_biases_of(mixed)]
        if not last:
            spare = spare + send(w_qkv, level + 1, qkv_starts, wide, mixed)
        parts, up_far, spare = together(scatter(outs[3:]), across(up_near[: chips // 2]), spare)
        if level == 0:
            other_down, up_biases = spare[:2]
        qkv_sent = spare[-chips:]
        middle, piece = call(
            here(middle_kernel, plan, len(parts), level, level),
            "middle",
            parts + [rows, bias_out, norm2_gain, norm2_bias],
            [rows_f32, normed_like],
        )
        if last:
            cot_grad, cot_piece = call(
                here(cot_kernel, plan),
                "cotangent",
                [after(cot_genes[0].T, piece), jnp.pad(cot_prefix[0], filler)],
                [rows_f32, grad_like],
            )
            spare = [cot_grad, cot_piece]
        else:
            spare = send(w_up, level + 1, up_starts, chip_hidden, piece)
        pieces, far, spare = together(gather(piece), across(up_near[chips // 2 :]), spare)
        up_parts[level] = up_far + far
        if last:
            cot_grad, cot_piece = spare
            near = gather(after(cot_piece, *pieces))
        else:
            up_sent = spare
            near = to_chips(after_all(qkv_sent, *pieces))
        outs = call(
            here(lift_kernel, plan, level),
            "lift",
            [where]
            + pieces
            + up_parts[level]
            + [up_biases[level : level + 1], w_down, other_down],
            [
                shape_of(plan.all_rows, plan.features),
                shape_of(plan.all_rows, chip_hidden, dtype=F32),
                shape_of(plan.all_rows, chip_hidden),
                shape_of(plan.features, chip_hidden),
            ]
            + row_blocks,
            [pltpu.VMEM((chip_hidden, D), BF)],
            True,
        )
        outs, near = together(outs, near)
        low_two, pre_act, active, up_weight = outs[:4]
        saved.append(
            (rows, low_one, query, keys, mixed, lse, qkv_weight, middle, low_two, pre_act, active, up_weight)
        )
        if last:
            cot_pieces = near
            last_blocks, last_middle = outs[4:], middle
        else:
            spare = []
            if level == 0:
                spare = out_windows(after(chip_out, low_two)) + [select] + norm_vectors(low_two)
            parts, qkv_far, spare = together(scatter(outs[4:]), across(near[: chips // 2]), spare)
            if level == 0:
                windows, select, vectors = spare[:LAYERS], spare[LAYERS], spare[LAYERS + 1 :]
            rows, piece = call(
                here(middle_kernel, plan, len(parts), level, level + 1),
                "next_rows",
                parts + [middle, bias_down, norm1_gain, norm1_bias],
                [rows_f32, normed_like],
            )

    def of_cores(value, size, dim):
        return [
            lax.dynamic_slice_in_dim(value, at * size, size, dim) for at in (core, 1 - core)
        ]

    grad, pieces = cot_grad, cot_pieces
    down_sums, up_sums, qkv_sums = ([None] * LAYERS for _ in range(3))
    long_rows, short_rows, up_rows = [None] * (2 * LAYERS), [None] * (2 * LAYERS), [None] * LAYERS
    for level in reversed(range(LAYERS)):
        rows, low_one, query, keys, mixed, lse, qkv_weight, middle, low_two, pre_act, active, up_weight = saved[level]
        if level + 1 < LAYERS:
            (pieces,) = beside(f"rows {level}", gather(piece))
        outs = call(
            here(lift_back_kernel, plan, level),
            "lift_back",
            [where] + pieces + [up_weight, pre_act, w_down, other_down],
            [
                shape_of(plan.all_rows, D),
                shape_of(plan.all_rows, chip_hidden),
                vector,
                shape_of(1, chip_hidden, dtype=F32),
            ]
            + feature_blocks,
            [pltpu.VMEM((chip_hidden, D), BF)],
            True,
        )
        (outs,) = beside(f"lifted {level}", outs)
        low_grad, pre_grad, long_rows[level], up_rows[level] = outs[:4]
        up_mine, up_other = call(
            here(weight_grad_kernel, plan),
            "up_grad",
            [where, low_two, pre_grad, up_weight, up_rows[level], vectors[LAYERS + level]],
            [shape_of(chips, plan.part, chip_hidden + 2)] * 2,
            [pltpu.VMEM((plan.features, chip_hidden + 2), F32)],
            True,
        )
        down_mine, down_other = of_cores(dot(active, low_grad, 0, 0).astype(BF), hidden, 0)
        parts, (up_mine, up_other, down_mine, down_other) = beside(
            f"lift {level}", scatter(outs[4:]), [up_mine, up_other, down_mine, down_other]
        )
        middle_grad, piece = call(
            here(back_kernel, plan, len(parts), level),
            "middle_back",
            parts + [middle, norm2_gain, grad],
            [rows_f32, grad_like],
        )
        (middle_grad, piece, up_got, down_got), = beside(
            f"turn {level}", [middle_grad, piece, swap(up_other, 1), swap(down_other, 1)]
        )
        if level:
            down_sums[level] = CellSum(down_mine, down_got, "attend 1", "project 1", "lifted 0")
            up_sums[level] = CellSum(up_mine, up_got, "project 1", "lifted 0", "turn 0")
        else:
            down_sums[level] = CellSum(down_mine, down_got, "attend 0", "qkv 0", "end 1")
            up_sums[level] = CellSum(up_mine, up_got, "qkv 0", "end 1", "end 2")
        (pieces,) = beside(f"middle {level}", gather(piece))
        outs = call(
            here(attend_back_kernel, plan),
            "attend_back",
            [where] + pieces + [windows[level], query, keys, lse],
            [
                shape_of(plan.rows, D),
                shape_of(plan.rows, plan.lanes),
                shape_of(plan.rows, plan.lanes, dtype=F32),
                shape_of(plan.rows, plan.lanes),
                vector,
            ],
            [
                pltpu.VMEM((plan.prefix, D), F32),
                pltpu.VMEM((plan.rows, plan.lanes), BF),
                pltpu.VMEM((LANES, 2 * plan.rows), BF),
                pltpu.VMEM((2 * plan.rows, plan.gene_rows), F32),
                pltpu.VMEM((2 * plan.rows, plan.gene_rows), F32),
                pltpu.VMEM((2 * plan.rows, LANES), F32),
            ],
            True,
        )
        (outs,) = beside(f"attend {level}", outs)
        low_grad, query_grad, pair_mine, pair_other, long_rows[LAYERS + level] = outs
        own_weight = qkv_weight
        if wide != chip_cols:
            own_weight = dot(qkv_weight, cut).astype(BF)
        outs = call(
            here(project_back_kernel, plan),
            "project_back",
            [where, query_grad, pair_mine, swap(pair_other, 1), select, own_weight],
            [shape_of(plan.rows, 3 * chip_cols), shape_of(1, 3 * chip_cols, dtype=F32)]
            + feature_blocks,
            [pltpu.VMEM((plan.prefix, plan.features), F32)],
            True,
        )
        qkv_grad, qkv_bias = outs[:2]
        short_rows[level] = qkv_bias[:, :chip_cols]
        short_rows[LAYERS + level] = qkv_bias[:, 2 * chip_cols :]
        riders = of_cores(dot(mixed, low_grad, 0, 0), cols, 0)
        if not level:
            long_own = lax.dynamic_slice_in_dim(
                jnp.concatenate(long_rows, 0), chip * chip_cols, chip_cols, 1
            )
            small = [
                jnp.concatenate([vec.reshape(-1) for vec in vecs])
                for vecs in zip(
                    of_cores(long_own, cols, 1),
                    of_cores(jnp.concatenate(short_rows, 0), cols, 1),
                    of_cores(jnp.concatenate(up_rows, 0), hidden, 1),
                )
            ]
            extra = -(-small[0].size // D)
            small = [jnp.pad(vec, (0, extra * D - vec.size)).reshape(extra, D) for vec in small]
            riders = [jnp.concatenate(pair, 0) for pair in zip(riders, small)]
        width = 3 * chip_cols + 2 + chip_cols
        qkv_mine, qkv_other = call(
            here(weight_grad_kernel, plan),
            "qkv_grad",
            [where, low_one, qkv_grad, own_weight, qkv_bias, vectors[level]] + riders,
            [shape_of(chips, plan.part, width)] * 2,
            [pltpu.VMEM((plan.features, 3 * chip_cols + 2), F32)],
            True,
        )
        parts = scatter(outs[2:])
        if level:
            parts, (qkv_mine, qkv_other) = beside(
                "project 1", parts, [qkv_mine, qkv_other]
            )
            grad, piece = call(
                here(back_kernel, plan, len(parts), level),
                "rows_back",
                parts + [rows, norm1_gain, middle_grad],
                [rows_f32, grad_like],
            )
            grad, piece, qkv_got = together([grad, piece, swap(qkv_other, 1)])[0]
            qkv_sums[level] = [CellSum(qkv_mine, qkv_got, "turn 0", "attend 0", "qkv 0")]

    def messages_of(item, width):
        return [item.value[at, :, :width] for at in range(chips)]

    ((qkv_mine, qkv_other),) = beside("qkv 0", [qkv_mine, qkv_other])
    (qkv_got,) = together([swap(qkv_other, 1)])[0]
    qkv_sums[0] = [CellSum(qkv_mine, qkv_got, "end 1", "end 2", "end 3")]
    (parts,) = beside("end 1", parts)
    ends = call(
        here(back_end_kernel, plan, len(parts), 0),
        "rows_back_end",
        parts + [rows, norm1_gain, middle_grad],
        ends_like,
    )
    up_width, qkv_width = chip_hidden + 2, 3 * chip_cols + 2
    parts, ends = beside(
        "end 2",
        scatter(after_all(last_blocks, parts[0])),
        ends,
    )
    result = call(
        here(finish_kernel, plan, len(parts), LAYERS - 1),
        "finish",
        parts + [last_middle, bias_down],
        ends_like,
    )
    near, far, result = beside(
        "end 3",
        to_chips(after_all(messages_of(up_sums[1], up_width), result[0])),
        to_chips(after_all(messages_of(qkv_sums[1][0], qkv_width), result[0])),
        result,
    )
    last_near = to_chips(messages_of(qkv_sums[0][0], qkv_width))
    last_up = to_chips(messages_of(up_sums[0], up_width))
    up_parts = [jnp.stack(last_up), jnp.stack(near)]
    qkv_parts = [jnp.stack(last_near), jnp.stack(far)]
    out_sums = []
    for items in qkv_sums:
        riders = [items[0].value[at, :, qkv_width:] for at in range(chips)]
        out_sums.append(jnp.concatenate(riders, 1))
    small = out_sums[0][cols : cols + extra].reshape(-1).astype(F32)
    out_sums = [value[:cols] for value in out_sums]
    down_sums = [item.value for item in down_sums]
    size = LAYERS * cols
    b_down, b_out, b_q, b_v = (small[at * size : (at + 1) * size].reshape(LAYERS, cols) for at in range(4))
    b_up = small[4 * size : 4 * size + LAYERS * hidden].reshape(LAYERS, hidden)

    def join(parts, blocks, width):
        whole, vectors = call(
            here(join_kernel, plan, blocks, width),
            "join",
            [where] + parts,
            [
                shape_of(cols, LAYERS, blocks * D if blocks > 1 else FF, dtype=F32),
                shape_of(LAYERS, 8, plan.part, dtype=F32),
            ],
            scalar=True,
        )
        return whole.transpose(1, 0, 2), vectors[:, 0, :cols], vectors[:, 1, :cols]

    g_up, shift_two, gain_two = join(up_parts, 1, chip_hidden)
    g_qkv, shift_one, gain_one = join(qkv_parts, 3, 3 * chip_cols)
    return (
        result[0].T[None],
        result[1][: plan.pre_rows][None],
        ends[0].T[None],
        ends[1][: plan.pre_rows][None],
        g_qkv,
        jnp.stack(out_sums).astype(F32),
        g_up,
        jnp.stack(down_sums).astype(F32),
        gain_one,
        shift_one,
        gain_two,
        shift_two,
        b_q,
        b_v,
        b_out,
        b_up,
        b_down,
    )


def solution(mesh):
    rows = P("cell", "gene", None)
    weight = P(None, "gene", None)
    vector = P(None, "gene")
    return jax.shard_map(
        body,
        mesh=mesh,
        in_specs=(rows, P("cell", None, None), rows, rows) + (weight,) * 4 + (P(),) * 9,
        out_specs=(rows,) * 4 + (weight,) * 4 + (vector,) * 9,
        check_vma=False,
    )
```

time: 1010 us -> 664 us (0.66)
  waiting for transfers between devices: 414 us -> 197 us
  starting transfers between devices: 192 us -> 134 us
  blocking collectives: 48.7 us -> 0 us
  local copies, waits for them, and re-layouts: 74 us -> 41.8 us
  Pallas kernels: 199 us -> 211 us
    ppermute x170 -> x100, waiting for transfers between devices: 310 us -> 160 us  [swap(): lax.ppermute(value, 'gene', [(at, at ^ bits) for at in range(groups)])]
    ppermute x27 -> x18, waiting for transfers between devices: 104 us -> 37.1 us  [move(): return lax.ppermute(self.value, 'cell', pairs)]
    psum x1 -> x0, blocking collectives: 48.7 us -> none  [body(): last = lax.psum(sums[:2].astype(BF), ('gene', 'cell'))]
    ppermute x170 -> x100, starting transfers between devices: 127 us -> 90.1 us  [swap(): lax.ppermute(value, 'gene', [(at, at ^ bits) for at in range(groups)])]
    unnamed x416 -> x289, local copies, waits for them, and re-layouts: 45.9 us -> 23.1 us
    ppermute x27 -> x18, starting transfers between devices: 65 us -> 44 us  [move(): return lax.ppermute(self.value, 'cell', pairs)]
    pallas_call x32, Pallas kernels: 199 us -> 211 us  [call(): pl.pallas_call(kernel, in_specs=[SCALAR if scalar and at == 0 else WHOLE...]
    convert_element_type x10 -> x1, local copies, waits for them, and re-layouts: 12.5 us -> 0.08 us  [body(): small = out_sums[0][cols:cols + extra].reshape(-1).astype(F32)]
  transfers between devices with their start and end apart: 197 -> 118, of which waited for: 70 -> 48; matrix products, arithmetic and copies ran while one was open for 12% -> 11% of each run, Pallas kernels for 16% -> 24%
where the time goes in v2:
time: 664 us; the launch traced here: 654 us
  Pallas kernels  211 us (32%)
  waiting for transfers between devices  197 us (30%)
  starting transfers between devices  134 us (20%)
  other arithmetic  54.1 us (8%)
  local copies, waits for them, and re-layouts  41.8 us (6%)
  matrix products  13.4 us (2%)
    pallas_call x32, Pallas kernels, call(): pl.pallas_call(kernel, in_specs=[SCALAR if scalar and at == 0 else WHOLE...  211 us
    ppermute x100, waiting for transfers between devices, swap(): lax.ppermute(value, 'gene', [(at, at ^ bits) for at in range(groups)])  160 us
    ppermute x100, starting transfers between devices, swap(): lax.ppermute(value, 'gene', [(at, at ^ bits) for at in range(groups)])  90.1 us
    ppermute x18, starting transfers between devices, move(): return lax.ppermute(self.value, 'cell', pairs)  44 us
    ppermute x18, waiting for transfers between devices, move(): return lax.ppermute(self.value, 'cell', pairs)  37.1 us
    unnamed x289, local copies, waits for them, and re-layouts  23.1 us
    convert_element_type x12, other arithmetic, land(): self.value = (self.value.astype(F32) + got.astype(F32)).astype(BF)  22 us
    dot_general x6, matrix products, dot(): lax.dot_general(left, right, (((left_dim,), (right_dim,)), ((), ())), pre...  13.4 us
  transfers between devices with their start and end apart: 118, of which 48 were waited for; matrix products, arithmetic and copies ran while one was open for 11% of the time, Pallas kernels for 24%

profile of v2, /device:TPU:0, one launch (start us, length us, event | category | flops | bytes accessed | tf_op | source)
XLA Modules:
  0.0 654.1 jit_solution(1788153468388149670)
XLA Ops:
  9.5 3.2 copy.46.weight_ref
  12.7 3.1 send.4
  21.4 3.2 send.5
  31.4 4.6 collective-permute-done.3.refs_6_
  41.2 7.6 %project.2 = (bf16[544,1152]{1,0:T(8,128)(2,1)}, bf16[544,640]{1,0:T(8,128)(2,1)}, bf16[544,640]{1,0:T(8,128)(2,1)}, bf16[1152,840]{1,0:T(8,128)(2,1)}) custom-call(s32[3]{0:T(128)} %pad_add_fusion.me_ref, bf16[136,1152]{1,0:T(8,128)(2,1)} %get-tuple-element.424.refs_0_, bf16[136,1152]{1,0:T(8,128)(2,1)} %collective-permute-done.refs_1_, ...), custom_call_target="tpu_custom_call" | custom-call | flops 1000 | bytes 1000 | tf_op jit(solution)/shard_map/project/pallas_call | solution.py:71
  53.4 11.3 %attend.2 = (bf16[1088,640]{1,0:T(8,128)(2,1)}, bf16[544,280]{1,0:T(8,128)(2,1)}, f32[5,1,544]{2,1,0:T(1,128)}, bf16[136,1120]{1,0:T(8,128)(2,1)}, bf16[136,1120...) custom-call(s32[3]{0:T(128)} %pad_add_fusion.me_ref, ...), custom_call_target="tpu_custom_call" | custom-call | flops 1000 | bytes 1000 | tf_op jit(solution)/shard_map/attend/pallas_call | solution.py:71
  71.9 5.8 collective-permute-done.15.refs_1_
  82.9 4.5 collective-permute-done.16.refs_2_
  94.7 3.3 send.7
  98.0 3.4 collective-permute-done.21.refs_1_
  101.4 7.1 %collective-permute-done.22.refs_2_ = bf16[136,1152]{1,0:T(8,128)(2,1)S(1)} collective-permute-done((bf16[136,1152]{1,0:T(8,128)(2,1)}, bf16[136,1152]{1,0:T(8,128)(2,1)S(1)}, u32[]{:S(2)}, u32[]{:S(2)}) %collective-permute-start.22) | collective-permute-done | bytes 313376 | tf_op jit(solution)/shard_map/ppermute | solution.py:529
  112.7 9.2 %lift.2 = (bf16[576,1152]{1,0:T(8,128)(2,1)}, f32[576,1120]{1,0:T(8,128)}, bf16[576,1120]{1,0:T(8,128)(2,1)}, bf16[1152,1120]{1,0:T(8,128)(2,1)}, bf16[136,1120]...) custom-call(s32[3]{0:T(128)} %pad_add_fusion.me_ref, ...), custom_call_target="tpu_custom_call" | custom-call | flops 1000 | bytes 1000 | tf_op jit(solution)/shard_map/lift/pallas_call | solution.py:71
  132.0 5.2 collective-permute-done.29.refs_1_
  137.2 4.4 collective-permute-done.30.refs_2_
  150.6 4.8 collective-permute-done.34.refs_1_
  155.5 4.8 collective-permute-done.35.refs_2_
  161.1 7.7 %project.3 = (bf16[544,1152]{1,0:T(8,128)(2,1)}, bf16[544,640]{1,0:T(8,128)(2,1)}, bf16[544,640]{1,0:T(8,128)(2,1)}, bf16[1152,840]{1,0:T(8,128)(2,1)}) custom-call(s32[3]{0:T(128)} %pad_add_fusion.me_ref, bf16[136,1152]{1,0:T(8,128)(2,1)} %get-tuple-element.531.refs_0_, bf16[136,1152]{1,0:T(8,128)(2,1)} %copy-done.82, bf16[136,1152]{1,0:T(8,128)(2,1)} %copy-done.83, ...), custom_call_target="tpu_custom_call" | custom-call | flops 1000 | bytes 1000 | tf_op jit(solution)/shard_map/project/pallas_call | solution.py:71
  173.2 11.1 %attend.3 = (bf16[1088,640]{1,0:T(8,128)(2,1)}, bf16[544,280]{1,0:T(8,128)(2,1)}, f32[5,1,544]{2,1,0:T(1,128)}, bf16[136,1120]{1,0:T(8,128)(2,1)}, bf16[136,1120...) custom-call(s32[3]{0:T(128)} %pad_add_fusion.me_ref, ...), custom_call_target="tpu_custom_call" | custom-call | flops 1000 | bytes 1000 | tf_op jit(solution)/shard_map/attend/pallas_call | solution.py:71
  190.3 7.0 %collective-permute-done.43.refs_1_ = bf16[136,1120]{1,0:T(8,128)(2,1)S(1)} collective-permute-done((bf16[136,1120]{1,0:T(8,128)(2,1)}, bf16[136,1120]{1,0:T(8,128)(2,1)S(1)}, u32[]{:S(2)}, u32[]{:S(2)}) %collective-permute-start.43) | collective-permute-done | bytes 304672 | tf_op jit(solution)/shard_map/ppermute | solution.py:529
  197.3 7.2 %collective-permute-done.44.refs_2_ = bf16[136,1120]{1,0:T(8,128)(2,1)S(1)} collective-permute-done((bf16[136,1120]{1,0:T(8,128)(2,1)}, bf16[136,1120]{1,0:T(8,128)(2,1)S(1)}, u32[]{:S(2)}, u32[]{:S(2)}) %collective-permute-start.44) | collective-permute-done | bytes 304672 | tf_op jit(solution)/shard_map/ppermute | solution.py:529
  205.4 3.2 middle.3
  214.5 4.7 collective-permute-done.48.refs_1_
  219.1 6.3 collective-permute-done.49.refs_2_
  229.0 9.2 %lift.3 = (bf16[576,1152]{1,0:T(8,128)(2,1)}, f32[576,1120]{1,0:T(8,128)}, bf16[576,1120]{1,0:T(8,128)(2,1)}, bf16[1152,1120]{1,0:T(8,128)(2,1)}, bf16[136,1120]...) custom-call(s32[3]{0:T(128)} %pad_add_fusion.me_ref, ...), custom_call_target="tpu_custom_call" | custom-call | flops 1000 | bytes 1000 | tf_op jit(solution)/shard_map/lift/pallas_call | solution.py:71
  238.3 4.2 collective-permute-done.54.refs_2_
  242.5 10.2 %lift_back.2 = (bf16[576,1120]{1,0:T(8,128)(2,1)}, bf16[576,1120]{1,0:T(8,128)(2,1)}, f32[1,1120]{1,0:T(1,128)}, f32[1,1120]{1,0:T(1,128)}, bf16[136,1152]{1,0:T...) custom-call(s32[3]{0:T(128)} %pad_add_fusion.me_ref, ...), custom_call_target="tpu_custom_call" | custom-call | flops 1000 | bytes 1000 | tf_op jit(solution)/shard_map/lift_back/pallas_call | solution.py:71
  256.2 3.7 convolution_convert_fusion.1
  259.9 7.9 %up_grad.2 = (bf16[4,144,1122]{2,1,0:T(8,128)(2,1)}, bf16[4,144,1122]{2,1,0:T(8,128)(2,1)}) custom-call(s32[3]{0:T(128)} %pad_add_fusion.me_ref, bf16[576,1152]{1,0:T(8,128)(2,1)} %get-tuple-element.609.left_ref, bf16[576,1120]{1,0:T(8,128)(2,1)} %get-tuple-element.610.right_ref, bf16[1152,1120]{1,0:T(8,128)(2,1)} %get-tuple-element.603.refs_4_.weight_ref, ...), custom_call_target="tpu_custom_call" | custom-call | flops 1000 | bytes 1000 | tf_op jit(solution)/shard_map/up_grad/pallas_call | solution.py:71
  268.9 3.3 middle_back.2
  273.4 3.7 collective-permute-start.64
  283.5 4.1 collective-permute-done.61.refs_1_
  287.5 6.1 collective-permute-done.62.refs_2_
  294.3 15.4 %attend_back.2 = (bf16[544,1120]{1,0:T(8,128)(2,1)}, bf16[544,640]{1,0:T(8,128)(2,1)}, f32[544,640]{1,0:T(8,128)}, bf16[544,640]{1,0:T(8,128)(2,1)}, f32[1,1120]{1,0:T(1,128)}) custom-call(s32[3]{0:T(128)} %pad_add_fusion.me_ref, bf16[136,1120]{1,0:T(8,128)(2,1)} %get-tuple-element.630.refs_0_, bf16[136,1120]{1,0:T(8,128)(2,1)} %copy-done.85, ...), custom_call_target="tpu_custom_call" | custom-call | flops 1000 | bytes 1000 | tf_op jit(solution)/shard_map/attend_back/pallas_call | solution.py:71
  313.3 9.0 %project_back.2 = (bf16[544,840]{1,0:T(8,128)(2,1)}, f32[1,840]{1,0:T(1,128)}, bf16[136,1152]{1,0:T(8,128)(2,1)}, bf16[136,1152]{1,0:T(8,128)(2,1)}, bf16[136,11...) custom-call(s32[3]{0:T(128)} %pad_add_fusion.me_ref, bf16[544,640]{1,0:T(8,128)(2,1)} %get-tuple-element.644.refs_0_, ...), custom_call_target="tpu_custom_call" | custom-call | flops 1000 | bytes 1000 | tf_op jit(solution)/shard_map/project_back/pallas_call | solution.py:71
  327.8 7.9 %qkv_grad.2 = (bf16[4,144,1122]{2,1,0:T(8,128)(2,1)}, bf16[4,144,1122]{2,1,0:T(8,128)(2,1)}) custom-call(s32[3]{0:T(128)} %pad_add_fusion.me_ref, bf16[544,1152]{1,0:T(8,128)(2,1)} %get-tuple-element.653.left_ref, bf16[544,840]{1,0:T(8,128)(2,1)} %get-tuple-element.654.right_ref, bf16[1152,840]{1,0:T(8,128)(2,1)} %get-tuple-element.648.refs_4_.weight_ref, ...), custom_call_target="tpu_custom_call" | custom-call | flops 1000 | bytes 1000 | tf_op jit(solution)/shard_map/qkv_grad/pallas_call | solution.py:71
  335.7 4.4 collective-permute-done.67.refs_2_
  347.4 3.3 rows_back.1
  355.9 5.2 collective-permute-done.72.refs_1_
  361.2 7.8 %collective-permute-start.83 = (bf16[4,144,1122]{2,1,0:T(8,128)(2,1)S(1)}, bf16[4,144,1122]{2,1,0:T(8,128)(2,1)}, u32[]{:S(2)}, u32[]{:S(2)}) collective-permute-start(bf16[4,144,1122]{2,1,0:T(8,128)(2,1)S(1)} %add_convert_fusion.8), channel_id=1, source_target_pairs={{0,8},{24,16},{1,9},{25,17},{2,10},{26,18},{3,11},{27,19},{4,12},{... | collective-permute-start | bytes 3877640 | tf_op jit(solution)/shard_map/ppermute | solution.py:567
  369.7 10.2 %lift_back.3 = (bf16[576,1120]{1,0:T(8,128)(2,1)}, bf16[576,1120]{1,0:T(8,128)(2,1)}, f32[1,1120]{1,0:T(1,128)}, f32[1,1120]{1,0:T(1,128)}, bf16[136,1152]{1,0:T...) custom-call(s32[3]{0:T(128)} %pad_add_fusion.me_ref, ...), custom_call_target="tpu_custom_call" | custom-call | flops 1000 | bytes 1000 | tf_op jit(solution)/shard_map/lift_back/pallas_call | solution.py:71
  386.4 3.9 convolution_convert_fusion
  390.3 7.7 %up_grad.3 = (bf16[4,144,1122]{2,1,0:T(8,128)(2,1)}, bf16[4,144,1122]{2,1,0:T(8,128)(2,1)}) custom-call(s32[3]{0:T(128)} %pad_add_fusion.me_ref, bf16[576,1152]{1,0:T(8,128)(2,1)} %get-tuple-element.520.left_ref, bf16[576,1120]{1,0:T(8,128)(2,1)} %get-tuple-element.692.right_ref, bf16[1152,1120]{1,0:T(8,128)(2,1)} %get-tuple-element.676.refs_4_.weight_ref, ...), custom_call_target="tpu_custom_call" | custom-call | flops 1000 | bytes 1000 | tf_op jit(solution)/shard_map/up_grad/pallas_call | solution.py:71
  401.7 3.3 middle_back.3
  405.0 12.1 %collective-permute-done.82 = bf16[4,144,1122]{2,1,0:T(8,128)(2,1)S(1)} collective-permute-done((bf16[4,144,1122]{2,1,0:T(8,128)(2,1)S(1)}, bf16[4,144,1122]{2,1,0:T(8,128)(2,1)S(1)}, u32[]{:S(2)}, u32[]{:S(2)}) %collective-permute-start.82) | collective-permute-done | bytes 1292576 | tf_op jit(solution)/shard_map/ppermute | solution.py:567
  417.2 3.2 add_convert_fusion.7
  423.8 3.2 collective-permute-start.88
  430.9 3.1 add_convert_fusion.5
  442.3 15.4 %attend_back.3 = (bf16[544,1120]{1,0:T(8,128)(2,1)}, bf16[544,640]{1,0:T(8,128)(2,1)}, f32[544,640]{1,0:T(8,128)}, bf16[544,640]{1,0:T(8,128)(2,1)}, f32[1,1120]{1,0:T(1,128)}) custom-call(s32[3]{0:T(128)} %pad_add_fusion.me_ref, bf16[136,1120]{1,0:T(8,128)(2,1)} %get-tuple-element.716.refs_0_, bf16[136,1120]{1,0:T(8,128)(2,1)} %copy-done.86, ...), custom_call_target="tpu_custom_call" | custom-call | flops 1000 | bytes 1000 | tf_op jit(solution)/shard_map/attend_back/pallas_call | solution.py:71
  469.8 8.9 %project_back.3 = (bf16[544,840]{1,0:T(8,128)(2,1)}, f32[1,840]{1,0:T(1,128)}, bf16[136,1152]{1,0:T(8,128)(2,1)}, bf16[136,1152]{1,0:T(8,128)(2,1)}, bf16[136,11...) custom-call(s32[3]{0:T(128)} %pad_add_fusion.me_ref, bf16[544,640]{1,0:T(8,128)(2,1)} %get-tuple-element.731.refs_0_, ...), custom_call_target="tpu_custom_call" | custom-call | flops 1000 | bytes 1000 | tf_op jit(solution)/shard_map/project_back/pallas_call | solution.py:71
  481.9 7.9 %qkv_grad.3 = (bf16[4,144,1122]{2,1,0:T(8,128)(2,1)}, bf16[4,144,1122]{2,1,0:T(8,128)(2,1)}) custom-call(s32[3]{0:T(128)} %pad_add_fusion.me_ref, bf16[544,1152]{1,0:T(8,128)(2,1)} %get-tuple-element.740.left_ref, bf16[544,840]{1,0:T(8,128)(2,1)} %get-tuple-element.741.right_ref, bf16[1152,840]{1,0:T(8,128)(2,1)} %get-tuple-element.734.refs_4_.weight_ref, ...), custom_call_target="tpu_custom_call" | custom-call | flops 1000 | bytes 1000 | tf_op jit(solution)/shard_map/qkv_grad/pallas_call | solution.py:71
  489.8 3.5 collective-permute-done.93
  500.2 5.1 collective-permute-start.99
  510.2 6.8 %collective-permute-done.90.refs_1_ = bf16[136,1152]{1,0:T(8,128)(2,1)S(1)} collective-permute-done((bf16[136,1152]{1,0:T(8,128)(2,1)S(1)}, bf16[136,1152]{1,0:T(8,128)(2,1)S(1)}, u32[]{:S(2)}, u32[]{:S(2)}) %collective-permute-start.90) | collective-permute-done | bytes 313376 | tf_op jit(solution)/shard_map/ppermute | solution.py:529
  519.5 6.5 collective-permute-done.92.refs_3_
  526.1 5.2 collective-permute-done.96
  545.4 3.3 rows_back_end.1
  551.4 5.8 collective-permute-done.101.refs_2_
  557.2 13.8 %collective-permute-done.103 = bf16[4,144,1122]{2,1,0:T(8,128)(2,1)} collective-permute-done((bf16[4,144,1122]{2,1,0:T(8,128)(2,1)S(1)}, bf16[4,144,1122]{2,1,0:T(8,128)(2,1)}, u32[]{:S(2)}, u32[]{:S(2)}) %collective-permute-start.103) | collective-permute-done | bytes 1292576 | tf_op jit(solution)/shard_map/ppermute | solution.py:567
  582.8 3.4 collective-permute-done.108
  588.0 5.3 collective-permute-done.115
  599.0 13.5 %collective-permute-done.117 = bf16[144,1122]{1,0:T(8,128)(2,1)S(1)} collective-permute-done((bf16[144,1122]{1,0:T(8,128)(2,1)S(1)}, bf16[144,1122]{1,0:T(8,128)(2,1)S(1)}, u32[]{:S(2)}, u32[]{:S(2)}) %collective-permute-start.117) | collective-permute-done | bytes 323168 | tf_op jit(solution)/shard_map/ppermute | solution.py:529
  615.5 4.2 collective-permute-done.110
  625.3 6.2 join.3
  645.2 6.8 %join.2 = (f32[140,2,3360]{2,1,0:T(2,128)}, f32[2,8,144]{2,1,0:T(8,128)}) custom-call(s32[3]{0:T(128)} %pad_add_fusion.me_ref, bf16[4,144,842]{2,1,0:T(8,128)(2,1)} %pad_maximum_fusion.3.refs_0_, bf16[4,144,842]{2,1,0:T(8,128)(2,1)} %pad_maximum_fusion.4.refs_1_), custom_call_target="tpu_custom_call" | custom-call | flops 1000 | bytes 1000 | tf_op jit(solution)/shard_map/join/pallas_call | solution.py:71
  (594 shorter events, 245.4 us)
Async XLA Ops:
  4.5 33.3 %collective-permute-start = (bf16[136,1152]{1,0:T(8,128)(2,1)}, bf16[136,1152]{1,0:T(8,128)(2,1)}, u32[]{:S(2)}, u32[]{:S(2)}) collective-permute-start(bf16[136,1152]{1,0:T(8,128)(2,1)} %get-tuple-element.424.refs_0_), channel_id=1, source_target_pairs={{0,2},{1,3},{2,0},{3,1},{4,6},{5,7},{6,4},{7,5},{8,10},{9,11},{10,... | collective-permute-start | bytes 940040 | tf_op jit(solution)/shard_map/ppermute | solution.py:529
  7.4 30.4 %collective-permute-start.1 = (bf16[136,1152]{1,0:T(8,128)(2,1)}, bf16[136,1152]{1,0:T(8,128)(2,1)}, u32[]{:S(2)}, u32[]{:S(2)}) collective-permute-start(bf16[136,1152]{1,0:T(8,128)(2,1)} %get-tuple-element.424.refs_0_), channel_id=1, source_target_pairs={{0,4},{1,5},{2,6},{3,7},{4,0},{5,1},{6,2},{7,3},{8,12},{9,13},{10,... | collective-permute-start | bytes 940040 | tf_op jit(solution)/shard_map/ppermute | solution.py:529
  8.9 28.8 %collective-permute-start.2 = (bf16[136,1152]{1,0:T(8,128)(2,1)}, bf16[136,1152]{1,0:T(8,128)(2,1)}, u32[]{:S(2)}, u32[]{:S(2)}) collective-permute-start(bf16[136,1152]{1,0:T(8,128)(2,1)} %get-tuple-element.424.refs_0_), channel_id=1, source_target_pairs={{0,6},{1,7},{2,4},{3,5},{4,2},{5,3},{6,0},{7,1},{8,14},{9,15},{10,... | collective-permute-start | bytes 940040 | tf_op jit(solution)/shard_map/ppermute | solution.py:529
  15.8 13.5 %collective-permute-start.5 = (bf16[144,840]{1,0:T(8,128)(2,1)}, bf16[144,840]{1,0:T(8,128)(2,1)}, u32[]{:S(2)}, u32[]{:S(2)}) collective-permute-start(bf16[144,840]{1,0:T(8,128)(2,1)} %get-tuple-element.417), channel_id=1, source_target_pairs={{0,6},{1,7},{2,4},{3,5},{4,2},{5,3},{6,0},{7,1},{8,14},{9,15},{10,... | collective-permute-start | bytes 725768 | tf_op jit(solution)/shard_map/ppermute | solution.py:529
  49.0 15.7 %collective-permute-start.12 = (bf16[144,1120]{1,0:T(8,128)(2,1)}, bf16[144,1120]{1,0:T(8,128)(2,1)S(1)}, u32[]{:S(2)}, u32[]{:S(2)}) collective-permute-start(bf16[144,1120]{1,0:T(8,128)(2,1)} %get-tuple-element.454), channel_id=1, source_target_pairs={{0,2},{1,3},{2,0},{3,1},{4,6},{5,7},{6,4},{7,5},{8,10},{9,11},{10,... | collective-permute-start | bytes 967688 | tf_op jit(solution)/shard_map/ppermute | solution.py:529
  50.5 16.9 %collective-permute-start.13 = (bf16[144,1120]{1,0:T(8,128)(2,1)S(1)}, bf16[144,1120]{1,0:T(8,128)(2,1)S(1)}, u32[]{:S(2)}, u32[]{:S(2)}) collective-permute-start(bf16[144,1120]{1,0:T(8,128)(2,1)S(1)} %copy-done.130), channel_id=1, source_target_pairs={{0,4},{1,5},{2,6},{3,7},{4,0},{5,1},{6,2},{7,3},{8,12},{9,13},{10,... | collective-permute-start | bytes 967688 | tf_op jit(solution)/shard_map/ppermute | solution.py:529
  51.0 16.4 %collective-permute-start.14 = (bf16[144,1120]{1,0:T(8,128)(2,1)S(1)}, bf16[144,1120]{1,0:T(8,128)(2,1)S(1)}, u32[]{:S(2)}, u32[]{:S(2)}) collective-permute-start(bf16[144,1120]{1,0:T(8,128)(2,1)S(1)} %copy-done.129), channel_id=1, source_target_pairs={{0,6},{1,7},{2,4},{3,5},{4,2},{5,3},{6,0},{7,1},{8,14},{9,15},{10,... | collective-permute-start | bytes 967688 | tf_op jit(solution)/shard_map/ppermute | solution.py:529
  67.4 20.6 %collective-permute-start.20 = (bf16[2,560,1120]{2,1,0:T(8,128)(2,1)S(1)}, bf16[2,560,1120]{2,1,0:T(8,128)(2,1)}, u32[]{:S(2)}, u32[]{:S(2)}) collective-permute-start(bf16[2,560,1120]{2,1,0:T(8,128)(2,1)S(1)} %copy-done.2), channel_id=1, source_target_pairs={{0,1},{1,0},{2,3},{3,2},{4,5},{5,4},{6,7},{7,6},{8,9},{9,8},{10,11... | collective-permute-start | bytes 7526408 | tf_op jit(solution)/shard_map/ppermute | solution.py:529
  70.5 17.4 %collective-permute-start.18 = (bf16[144,1120]{1,0:T(8,128)(2,1)}, bf16[144,1120]{1,0:T(8,128)(2,1)S(1)}, u32[]{:S(2)}, u32[]{:S(2)}) collective-permute-start(bf16[144,1120]{1,0:T(8,128)(2,1)} %get-tuple-element.488.refs_4_), channel_id=1, source_target_pairs={{0,1},{1,0},{2,3},{3,2},{4,5},{5,4},{6,7},{7,6},{8,9},{9,8},{10,11... | collective-permute-start | bytes 967688 | tf_op jit(solution)/shard_map/ppermute | solution.py:529
  70.6 17.3 %collective-permute-start.19 = (bf16[144,1120]{1,0:T(8,128)(2,1)}, bf16[144,1120]{1,0:T(8,128)(2,1)S(1)}, u32[]{:S(2)}, u32[]{:S(2)}) collective-permute-start(bf16[144,1120]{1,0:T(8,128)(2,1)} %copy-done.30), channel_id=1, source_target_pairs={{0,1},{1,0},{2,3},{3,2},{4,5},{5,4},{6,7},{7,6},{8,9},{9,8},{10,11... | collective-permute-start | bytes 967688 | tf_op jit(solution)/shard_map/ppermute | solution.py:529
  71.1 16.3 %collective-permute-start.16 = (bf16[136,1120]{1,0:T(8,128)(2,1)}, bf16[136,1120]{1,0:T(8,128)(2,1)S(1)}, u32[]{:S(2)}, u32[]{:S(2)}) collective-permute-start(bf16[136,1120]{1,0:T(8,128)(2,1)} %get-tuple-element.459), channel_id=1, source_target_pairs={{0,4},{1,5},{2,6},{3,7},{4,0},{5,1},{6,2},{7,3},{8,12},{9,13},{10,... | collective-permute-start | bytes 913928 | tf_op jit(solution)/shard_map/ppermute | solution.py:529
  92.4 16.1 %collective-permute-start.22 = (bf16[136,1152]{1,0:T(8,128)(2,1)}, bf16[136,1152]{1,0:T(8,128)(2,1)S(1)}, u32[]{:S(2)}, u32[]{:S(2)}) collective-permute-start(bf16[136,1152]{1,0:T(8,128)(2,1)} %get-tuple-element.484.refs_0_), channel_id=1, source_target_pairs={{0,4},{1,5},{2,6},{3,7},{4,0},{5,1},{6,2},{7,3},{8,12},{9,13},{10,... | collective-permute-start | bytes 940040 | tf_op jit(solution)/shard_map/ppermute | solution.py:529
  92.8 15.7 %collective-permute-start.23 = (bf16[136,1152]{1,0:T(8,128)(2,1)}, bf16[136,1152]{1,0:T(8,128)(2,1)S(1)}, u32[]{:S(2)}, u32[]{:S(2)}) collective-permute-start(bf16[136,1152]{1,0:T(8,128)(2,1)} %get-tuple-element.484.refs_0_), channel_id=1, source_target_pairs={{0,6},{1,7},{2,4},{3,5},{4,2},{5,3},{6,0},{7,1},{8,14},{9,15},{10,... | collective-permute-start | bytes 940040 | tf_op jit(solution)/shard_map/ppermute | solution.py:529
  127.4 14.2 %collective-permute-start.30 = (bf16[136,1120]{1,0:T(8,128)(2,1)S(1)}, bf16[136,1120]{1,0:T(8,128)(2,1)S(1)}, u32[]{:S(2)}, u32[]{:S(2)}) collective-permute-start(bf16[136,1120]{1,0:T(8,128)(2,1)S(1)} %copy-done.135), channel_id=1, source_target_pairs={{0,4},{1,5},{2,6},{3,7},{4,0},{5,1},{6,2},{7,3},{8,12},{9,13},{10,... | collective-permute-start | bytes 913928 | tf_op jit(solution)/shard_map/ppermute | solution.py:529
  146.4 13.9 %collective-permute-start.35 = (bf16[136,1152]{1,0:T(8,128)(2,1)}, bf16[136,1152]{1,0:T(8,128)(2,1)S(1)}, u32[]{:S(2)}, u32[]{:S(2)}) collective-permute-start(bf16[136,1152]{1,0:T(8,128)(2,1)} %get-tuple-element.531.refs_0_), channel_id=1, source_target_pairs={{0,4},{1,5},{2,6},{3,7},{4,0},{5,1},{6,2},{7,3},{8,12},{9,13},{10,... | collective-permute-start | bytes 940040 | tf_op jit(solution)/shard_map/ppermute | solution.py:529
  168.8 15.5 %collective-permute-start.40 = (bf16[144,1120]{1,0:T(8,128)(2,1)S(1)}, bf16[144,1120]{1,0:T(8,128)(2,1)S(1)}, u32[]{:S(2)}, u32[]{:S(2)}) collective-permute-start(bf16[144,1120]{1,0:T(8,128)(2,1)S(1)} %copy-done.128), channel_id=1, source_target_pairs={{0,2},{1,3},{2,0},{3,1},{4,6},{5,7},{6,4},{7,5},{8,10},{9,11},{10,... | collective-permute-start | bytes 967688 | tf_op jit(solution)/shard_map/ppermute | solution.py:529
  169.2 17.0 %collective-permute-start.41 = (bf16[144,1120]{1,0:T(8,128)(2,1)S(1)}, bf16[144,1120]{1,0:T(8,128)(2,1)S(1)}, u32[]{:S(2)}, u32[]{:S(2)}) collective-permute-start(bf16[144,1120]{1,0:T(8,128)(2,1)S(1)} %copy-done.127), channel_id=1, source_target_pairs={{0,4},{1,5},{2,6},{3,7},{4,0},{5,1},{6,2},{7,3},{8,12},{9,13},{10,... | collective-permute-start | bytes 967688 | tf_op jit(solution)/shard_map/ppermute | solution.py:529
  171.0 15.2 %collective-permute-start.42 = (bf16[144,1120]{1,0:T(8,128)(2,1)S(1)}, bf16[144,1120]{1,0:T(8,128)(2,1)S(1)}, u32[]{:S(2)}, u32[]{:S(2)}) collective-permute-start(bf16[144,1120]{1,0:T(8,128)(2,1)S(1)} %copy-done.126), channel_id=1, source_target_pairs={{0,6},{1,7},{2,4},{3,5},{4,2},{5,3},{6,0},{7,1},{8,14},{9,15},{10,... | collective-permute-start | bytes 967688 | tf_op jit(solution)/shard_map/ppermute | solution.py:529
  186.2 18.3 %collective-permute-start.46 = (bf16[144,1120]{1,0:T(8,128)(2,1)S(1)}, bf16[144,1120]{1,0:T(8,128)(2,1)S(1)}, u32[]{:S(2)}, u32[]{:S(2)}) collective-permute-start(bf16[144,1120]{1,0:T(8,128)(2,1)S(1)} %copy-done.29), channel_id=1, source_target_pairs={{0,1},{1,0},{2,3},{3,2},{4,5},{5,4},{6,7},{7,6},{8,9},{9,8},{10,11... | collective-permute-start | bytes 967688 | tf_op jit(solution)/shard_map/ppermute | solution.py:529
  186.3 18.3 %collective-permute-start.47 = (bf16[144,1120]{1,0:T(8,128)(2,1)S(1)}, bf16[144,1120]{1,0:T(8,128)(2,1)S(1)}, u32[]{:S(2)}, u32[]{:S(2)}) collective-permute-start(bf16[144,1120]{1,0:T(8,128)(2,1)S(1)} %collective-permute-done.40.refs_6_), channel_id=1, source_target_pairs={{0,1},{1,0},{2,3},{3,2},{4,5},{5,4},{6,7},{7,6},{8,9},{9,8},{10,11... | collective-permute-start | bytes 967688 | tf_op jit(solution)/shard_map/ppermute | solution.py:529
  188.5 16.0 %collective-permute-start.44 = (bf16[136,1120]{1,0:T(8,128)(2,1)}, bf16[136,1120]{1,0:T(8,128)(2,1)S(1)}, u32[]{:S(2)}, u32[]{:S(2)}) collective-permute-start(bf16[136,1120]{1,0:T(8,128)(2,1)} %get-tuple-element.562), channel_id=1, source_target_pairs={{0,4},{1,5},{2,6},{3,7},{4,0},{5,1},{6,2},{7,3},{8,12},{9,13},{10,... | collective-permute-start | bytes 913928 | tf_op jit(solution)/shard_map/ppermute | solution.py:529
  188.9 15.6 %collective-permute-start.45 = (bf16[136,1120]{1,0:T(8,128)(2,1)}, bf16[136,1120]{1,0:T(8,128)(2,1)S(1)}, u32[]{:S(2)}, u32[]{:S(2)}) collective-permute-start(bf16[136,1120]{1,0:T(8,128)(2,1)} %get-tuple-element.563), channel_id=1, source_target_pairs={{0,6},{1,7},{2,4},{3,5},{4,2},{5,3},{6,0},{7,1},{8,14},{9,15},{10,... | collective-permute-start | bytes 913928 | tf_op jit(solution)/shard_map/ppermute | solution.py:529
  197.3 17.2 %collective-permute-start.51 = (bf16[144,1120]{1,0:T(8,128)(2,1)S(1)}, bf16[144,1120]{1,0:T(8,128)(2,1)S(1)}, u32[]{:S(2)}, u32[]{:S(2)}) collective-permute-start(bf16[144,1120]{1,0:T(8,128)(2,1)S(1)} %collective-permute-done.41.refs_8_), channel_id=1, source_target_pairs={{0,1},{1,0},{2,3},{3,2},{4,5},{5,4},{6,7},{7,6},{8,9},{9,8},{10,11... | collective-permute-start | bytes 967688 | tf_op jit(solution)/shard_map/ppermute | solution.py:529
  209.1 16.3 %collective-permute-start.49 = (bf16[136,1152]{1,0:T(8,128)(2,1)}, bf16[136,1152]{1,0:T(8,128)(2,1)S(1)}, u32[]{:S(2)}, u32[]{:S(2)}) collective-permute-start(bf16[136,1152]{1,0:T(8,128)(2,1)} %get-tuple-element.577.refs_0_), channel_id=1, source_target_pairs={{0,4},{1,5},{2,6},{3,7},{4,0},{5,1},{6,2},{7,3},{8,12},{9,13},{10,... | collective-permute-start | bytes 940040 | tf_op jit(solution)/shard_map/ppermute | solution.py:529
  210.8 14.6 %collective-permute-start.50 = (bf16[136,1152]{1,0:T(8,128)(2,1)}, bf16[136,1152]{1,0:T(8,128)(2,1)S(1)}, u32[]{:S(2)}, u32[]{:S(2)}) collective-permute-start(bf16[136,1152]{1,0:T(8,128)(2,1)} %get-tuple-element.577.refs_0_), channel_id=1, source_target_pairs={{0,6},{1,7},{2,4},{3,5},{4,2},{5,3},{6,0},{7,1},{8,14},{9,15},{10,... | collective-permute-start | bytes 940040 | tf_op jit(solution)/shard_map/ppermute | solution.py:529
  227.1 15.4 %collective-permute-start.54 = (bf16[136,1120]{1,0:T(8,128)(2,1)}, bf16[136,1120]{1,0:T(8,128)(2,1)}, u32[]{:S(2)}, u32[]{:S(2)}) collective-permute-start(bf16[136,1120]{1,0:T(8,128)(2,1)} %get-tuple-element.599.refs_0_), channel_id=1, source_target_pairs={{0,4},{1,5},{2,6},{3,7},{4,0},{5,1},{6,2},{7,3},{8,12},{9,13},{10,... | collective-permute-start | bytes 913928 | tf_op jit(solution)/shard_map/ppermute | solution.py:529
  227.5 15.0 %collective-permute-start.55 = (bf16[136,1120]{1,0:T(8,128)(2,1)}, bf16[136,1120]{1,0:T(8,128)(2,1)}, u32[]{:S(2)}, u32[]{:S(2)}) collective-permute-start(bf16[136,1120]{1,0:T(8,128)(2,1)} %get-tuple-element.599.refs_0_), channel_id=1, source_target_pairs={{0,6},{1,7},{2,4},{3,5},{4,2},{5,3},{6,0},{7,1},{8,14},{9,15},{10,... | collective-permute-start | bytes 913928 | tf_op jit(solution)/shard_map/ppermute | solution.py:529
  252.7 15.4 %collective-permute-start.56 = (bf16[136,1152]{1,0:T(8,128)(2,1)}, bf16[136,1152]{1,0:T(8,128)(2,1)S(1)}, u32[]{:S(2)}, u32[]{:S(2)}) collective-permute-start(bf16[136,1152]{1,0:T(8,128)(2,1)} %get-tuple-element.606), channel_id=1, source_target_pairs={{0,2},{1,3},{2,0},{3,1},{4,6},{5,7},{6,4},{7,5},{8,10},{9,11},{10,... | collective-permute-start | bytes 940040 | tf_op jit(solution)/shard_map/ppermute | solution.py:529
  253.1 15.0 %collective-permute-start.57 = (bf16[136,1152]{1,0:T(8,128)(2,1)}, bf16[136,1152]{1,0:T(8,128)(2,1)S(1)}, u32[]{:S(2)}, u32[]{:S(2)}) collective-permute-start(bf16[136,1152]{1,0:T(8,128)(2,1)} %get-tuple-element.607), channel_id=1, source_target_pairs={{0,4},{1,5},{2,6},{3,7},{4,0},{5,1},{6,2},{7,3},{8,12},{9,13},{10,... | collective-permute-start | bytes 940040 | tf_op jit(solution)/shard_map/ppermute | solution.py:529
  273.4 36.4 %collective-permute-start.64 = (bf16[560,1120]{1,0:T(8,128)(2,1)S(1)}, bf16[560,1120]{1,0:T(8,128)(2,1)S(1)}, u32[]{:S(2)}, u32[]{:S(2)}) collective-permute-start(bf16[560,1120]{1,0:T(8,128)(2,1)S(1)} %add_convert_fusion.17), channel_id=1, source_target_pairs={{0,8},{24,16},{1,9},{25,17},{2,10},{26,18},{3,11},{27,19},{4,12},{... | collective-permute-start | bytes 3763208 | tf_op jit(solution)/shard_map/ppermute | solution.py:567
  278.0 15.6 %collective-permute-start.62 = (bf16[136,1120]{1,0:T(8,128)(2,1)S(1)}, bf16[136,1120]{1,0:T(8,128)(2,1)S(1)}, u32[]{:S(2)}, u32[]{:S(2)}) collective-permute-start(bf16[136,1120]{1,0:T(8,128)(2,1)S(1)} %copy-done.81), channel_id=1, source_target_pairs={{0,4},{1,5},{2,6},{3,7},{4,0},{5,1},{6,2},{7,3},{8,12},{9,13},{10,... | collective-permute-start | bytes 913928 | tf_op jit(solution)/shard_map/ppermute | solution.py:529
  279.2 15.2 %collective-permute-start.63 = (bf16[136,1120]{1,0:T(8,128)(2,1)S(1)}, bf16[136,1120]{1,0:T(8,128)(2,1)}, u32[]{:S(2)}, u32[]{:S(2)}) collective-permute-start(bf16[136,1120]{1,0:T(8,128)(2,1)S(1)} %copy-done.81), channel_id=1, source_target_pairs={{0,6},{1,7},{2,4},{3,5},{4,2},{5,3},{6,0},{7,1},{8,14},{9,15},{10,... | collective-permute-start | bytes 913928 | tf_op jit(solution)/shard_map/ppermute | solution.py:529
  281.1 54.6 %collective-permute-start.70 = (bf16[4,144,1122]{2,1,0:T(8,128)(2,1)S(1)}, bf16[4,144,1122]{2,1,0:T(8,128)(2,1)}, u32[]{:S(2)}, u32[]{:S(2)}) collective-permute-start(bf16[4,144,1122]{2,1,0:T(8,128)(2,1)S(1)} %add_convert_fusion.11), channel_id=1, source_target_pairs={{0,8},{24,16},{1,9},{25,17},{2,10},{26,18},{3,11},{27,19},{4,12},{... | collective-permute-start | bytes 3877640 | tf_op jit(solution)/shard_map/ppermute | solution.py:567
  310.2 29.9 %collective-permute-start.69 = (bf16[560,1120]{1,0:T(8,128)(2,1)S(1)}, bf16[560,1120]{1,0:T(8,128)(2,1)}, u32[]{:S(2)}, u32[]{:S(2)}) collective-permute-start(bf16[560,1120]{1,0:T(8,128)(2,1)S(1)} %add_convert_fusion.16), channel_id=1, source_target_pairs={{8,16},{16,8},{9,17},{17,9},{10,18},{18,10},{11,19},{19,11},{12,20... | collective-permute-start | bytes 3763208 | tf_op jit(solution)/shard_map/ppermute | solution.py:567
  323.6 16.4 %collective-permute-start.67 = (bf16[136,1152]{1,0:T(8,128)(2,1)}, bf16[136,1152]{1,0:T(8,128)(2,1)S(1)}, u32[]{:S(2)}, u32[]{:S(2)}) collective-permute-start(bf16[136,1152]{1,0:T(8,128)(2,1)} %get-tuple-element.651), channel_id=1, source_target_pairs={{0,4},{1,5},{2,6},{3,7},{4,0},{5,1},{6,2},{7,3},{8,12},{9,13},{10,... | collective-permute-start | bytes 940040 | tf_op jit(solution)/shard_map/ppermute | solution.py:529
  324.2 15.8 %collective-permute-start.68 = (bf16[136,1152]{1,0:T(8,128)(2,1)}, bf16[136,1152]{1,0:T(8,128)(2,1)S(1)}, u32[]{:S(2)}, u32[]{:S(2)}) collective-permute-start(bf16[136,1152]{1,0:T(8,128)(2,1)} %get-tuple-element.652), channel_id=1, source_target_pairs={{0,6},{1,7},{2,4},{3,5},{4,2},{5,3},{6,0},{7,1},{8,14},{9,15},{10,... | collective-permute-start | bytes 940040 | tf_op jit(solution)/shard_map/ppermute | solution.py:529
  342.5 37.4 %collective-permute-start.76 = (bf16[4,144,1122]{2,1,0:T(8,128)(2,1)S(1)}, bf16[4,144,1122]{2,1,0:T(8,128)(2,1)}, u32[]{:S(2)}, u32[]{:S(2)}) collective-permute-start(bf16[4,144,1122]{2,1,0:T(8,128)(2,1)S(1)} %add_convert_fusion.10), channel_id=1, source_target_pairs={{8,16},{16,8},{9,17},{17,9},{10,18},{18,10},{11,19},{19,11},{12,20... | collective-permute-start | bytes 3877640 | tf_op jit(solution)/shard_map/ppermute | solution.py:567
  345.9 34.0 %collective-permute-start.75 = (bf16[560,1120]{1,0:T(8,128)(2,1)S(1)}, bf16[560,1120]{1,0:T(8,128)(2,1)}, u32[]{:S(2)}, u32[]{:S(2)}) collective-permute-start(bf16[560,1120]{1,0:T(8,128)(2,1)S(1)} %add_convert_fusion.15), channel_id=1, source_target_pairs={{8,0},{16,24},{9,1},{17,25},{10,2},{18,26},{11,3},{19,27},{12,4},{... | collective-permute-start | bytes 3763208 | tf_op jit(solution)/shard_map/ppermute | solution.py:567
  351.5 17.5 %collective-permute-start.73 = (bf16[136,1120]{1,0:T(8,128)(2,1)}, bf16[136,1120]{1,0:T(8,128)(2,1)S(1)}, u32[]{:S(2)}, u32[]{:S(2)}) collective-permute-start(bf16[136,1120]{1,0:T(8,128)(2,1)} %get-tuple-element.672.refs_0_), channel_id=1, source_target_pairs={{0,4},{1,5},{2,6},{3,7},{4,0},{5,1},{6,2},{7,3},{8,12},{9,13},{10,... | collective-permute-start | bytes 913928 | tf_op jit(solution)/shard_map/ppermute | solution.py:529
  352.7 16.3 %collective-permute-start.74 = (bf16[136,1120]{1,0:T(8,128)(2,1)}, bf16[136,1120]{1,0:T(8,128)(2,1)}, u32[]{:S(2)}, u32[]{:S(2)}) collective-permute-start(bf16[136,1120]{1,0:T(8,128)(2,1)} %get-tuple-element.672.refs_0_), channel_id=1, source_target_pairs={{0,6},{1,7},{2,4},{3,5},{4,2},{5,3},{6,0},{7,1},{8,14},{9,15},{10,... | collective-permute-start | bytes 913928 | tf_op jit(solution)/shard_map/ppermute | solution.py:529
  361.2 43.9 %collective-permute-start.83 = (bf16[4,144,1122]{2,1,0:T(8,128)(2,1)S(1)}, bf16[4,144,1122]{2,1,0:T(8,128)(2,1)}, u32[]{:S(2)}, u32[]{:S(2)}) collective-permute-start(bf16[4,144,1122]{2,1,0:T(8,128)(2,1)S(1)} %add_convert_fusion.8), channel_id=1, source_target_pairs={{0,8},{24,16},{1,9},{25,17},{2,10},{26,18},{3,11},{27,19},{4,12},{... | collective-permute-start | bytes 3877640 | tf_op jit(solution)/shard_map/ppermute | solution.py:567
  379.9 21.0 %collective-permute-start.77 = (bf16[136,1152]{1,0:T(8,128)(2,1)}, bf16[136,1152]{1,0:T(8,128)(2,1)S(1)}, u32[]{:S(2)}, u32[]{:S(2)}) collective-permute-start(bf16[136,1152]{1,0:T(8,128)(2,1)} %get-tuple-element.689), channel_id=1, source_target_pairs={{0,2},{1,3},{2,0},{3,1},{4,6},{5,7},{6,4},{7,5},{8,10},{9,11},{10,... | collective-permute-start | bytes 940040 | tf_op jit(solution)/shard_map/ppermute | solution.py:529
  381.2 19.7 %collective-permute-start.78 = (bf16[136,1152]{1,0:T(8,128)(2,1)}, bf16[136,1152]{1,0:T(8,128)(2,1)S(1)}, u32[]{:S(2)}, u32[]{:S(2)}) collective-permute-start(bf16[136,1152]{1,0:T(8,128)(2,1)} %get-tuple-element.690), channel_id=1, source_target_pairs={{0,4},{1,5},{2,6},{3,7},{4,0},{5,1},{6,2},{7,3},{8,12},{9,13},{10,... | collective-permute-start | bytes 940040 | tf_op jit(solution)/shard_map/ppermute | solution.py:529
  381.9 19.0 %collective-permute-start.79 = (bf16[136,1152]{1,0:T(8,128)(2,1)}, bf16[136,1152]{1,0:T(8,128)(2,1)}, u32[]{:S(2)}, u32[]{:S(2)}) collective-permute-start(bf16[136,1152]{1,0:T(8,128)(2,1)} %get-tuple-element.691), channel_id=1, source_target_pairs={{0,6},{1,7},{2,4},{3,5},{4,2},{5,3},{6,0},{7,1},{8,14},{9,15},{10,... | collective-permute-start | bytes 940040 | tf_op jit(solution)/shard_map/ppermute | solution.py:529
  385.1 32.1 %collective-permute-start.82 = (bf16[4,144,1122]{2,1,0:T(8,128)(2,1)S(1)}, bf16[4,144,1122]{2,1,0:T(8,128)(2,1)S(1)}, u32[]{:S(2)}, u32[]{:S(2)}) collective-permute-start(bf16[4,144,1122]{2,1,0:T(8,128)(2,1)S(1)} %add_convert_fusion.9), channel_id=1, source_target_pairs={{8,0},{16,24},{9,1},{17,25},{10,2},{18,26},{11,3},{19,27},{12,4},{... | collective-permute-start | bytes 3877640 | tf_op jit(solution)/shard_map/ppermute | solution.py:567
  400.9 16.2 %collective-permute-start.80 = (bf16[4,144,1122]{2,1,0:T(8,128)(2,1)}, bf16[4,144,1122]{2,1,0:T(8,128)(2,1)}, u32[]{:S(2)}, u32[]{:S(2)}) collective-permute-start(bf16[4,144,1122]{2,1,0:T(8,128)(2,1)} %get-tuple-element.706), channel_id=1, source_target_pairs={{0,1},{1,0},{2,3},{3,2},{4,5},{5,4},{6,7},{7,6},{8,9},{9,8},{10,11... | collective-permute-start | bytes 3877640 | tf_op jit(solution)/shard_map/ppermute | solution.py:529
  401.0 16.1 %collective-permute-start.81 = (bf16[560,1120]{1,0:T(8,128)(2,1)}, bf16[560,1120]{1,0:T(8,128)(2,1)}, u32[]{:S(2)}, u32[]{:S(2)}) collective-permute-start(bf16[560,1120]{1,0:T(8,128)(2,1)} %get-tuple-element.707), channel_id=1, source_target_pairs={{0,1},{1,0},{2,3},{3,2},{4,5},{5,4},{6,7},{7,6},{8,9},{9,8},{10,11... | collective-permute-start | bytes 3763208 | tf_op jit(solution)/shard_map/ppermute | solution.py:529
  420.4 37.4 %collective-permute-start.87 = (bf16[4,144,1122]{2,1,0:T(8,128)(2,1)}, bf16[4,144,1122]{2,1,0:T(8,128)(2,1)}, u32[]{:S(2)}, u32[]{:S(2)}) collective-permute-start(bf16[4,144,1122]{2,1,0:T(8,128)(2,1)} %add_convert_fusion.7), channel_id=1, source_target_pairs={{8,16},{16,8},{9,17},{17,9},{10,18},{18,10},{11,19},{19,11},{12,20... | collective-permute-start | bytes 3877640 | tf_op jit(solution)/shard_map/ppermute | solution.py:567
  423.8 33.9 %collective-permute-start.88 = (bf16[560,1120]{1,0:T(8,128)(2,1)S(1)}, bf16[560,1120]{1,0:T(8,128)(2,1)}, u32[]{:S(2)}, u32[]{:S(2)}) collective-permute-start(bf16[560,1120]{1,0:T(8,128)(2,1)S(1)} %add_convert_fusion.14), channel_id=1, source_target_pairs={{0,8},{24,16},{1,9},{25,17},{2,10},{26,18},{3,11},{27,19},{4,12},{... | collective-permute-start | bytes 3763208 | tf_op jit(solution)/shard_map/ppermute | solution.py:567
  436.6 53.2 %collective-permute-start.95 = (bf16[4,144,1122]{2,1,0:T(8,128)(2,1)}, bf16[4,144,1122]{2,1,0:T(8,128)(2,1)}, u32[]{:S(2)}, u32[]{:S(2)}) collective-permute-start(bf16[4,144,1122]{2,1,0:T(8,128)(2,1)} %add_convert_fusion.5), channel_id=1, source_target_pairs={{0,8},{24,16},{1,9},{25,17},{2,10},{26,18},{3,11},{27,19},{4,12},{... | collective-permute-start | bytes 3877640 | tf_op jit(solution)/shard_map/ppermute | solution.py:567
  460.5 29.3 %collective-permute-start.94 = (bf16[560,1120]{1,0:T(8,128)(2,1)}, bf16[560,1120]{1,0:T(8,128)(2,1)}, u32[]{:S(2)}, u32[]{:S(2)}) collective-permute-start(bf16[560,1120]{1,0:T(8,128)(2,1)} %add_convert_fusion.13), channel_id=1, source_target_pairs={{8,16},{16,8},{9,17},{17,9},{10,18},{18,10},{11,19},{19,11},{12,20... | collective-permute-start | bytes 3763208 | tf_op jit(solution)/shard_map/ppermute | solution.py:567
  465.5 27.7 %collective-permute-start.93 = (bf16[4,144,1122]{2,1,0:T(8,128)(2,1)}, bf16[4,144,1122]{2,1,0:T(8,128)(2,1)}, u32[]{:S(2)}, u32[]{:S(2)}) collective-permute-start(bf16[4,144,1122]{2,1,0:T(8,128)(2,1)} %add_convert_fusion.6), channel_id=1, source_target_pairs={{8,0},{16,24},{9,1},{17,25},{10,2},{18,26},{11,3},{19,27},{12,4},{... | collective-permute-start | bytes 3877640 | tf_op jit(solution)/shard_map/ppermute | solution.py:567
  495.3 36.0 %collective-permute-start.97 = (bf16[4,144,1122]{2,1,0:T(8,128)(2,1)S(1)}, bf16[4,144,1122]{2,1,0:T(8,128)(2,1)S(1)}, u32[]{:S(2)}, u32[]{:S(2)}) collective-permute-start(bf16[4,144,1122]{2,1,0:T(8,128)(2,1)S(1)} %add_convert_fusion.4), channel_id=1, source_target_pairs={{8,16},{16,8},{9,17},{17,9},{10,18},{18,10},{11,19},{19,11},{12,20... | collective-permute-start | bytes 3877640 | tf_op jit(solution)/shard_map/ppermute | solution.py:567
  498.2 33.0 %collective-permute-start.96 = (bf16[560,1120]{1,0:T(8,128)(2,1)S(1)}, bf16[560,1120]{1,0:T(8,128)(2,1)S(1)}, u32[]{:S(2)}, u32[]{:S(2)}) collective-permute-start(bf16[560,1120]{1,0:T(8,128)(2,1)S(1)} %add_convert_fusion.12), channel_id=1, source_target_pairs={{8,0},{16,24},{9,1},{17,25},{10,2},{18,26},{11,3},{19,27},{12,4},{... | collective-permute-start | bytes 3763208 | tf_op jit(solution)/shard_map/ppermute | solution.py:567
  500.2 33.7 %collective-permute-start.99 = (bf16[4,144,1122]{2,1,0:T(8,128)(2,1)S(1)}, bf16[4,144,1122]{2,1,0:T(8,128)(2,1)S(1)}, u32[]{:S(2)}, u32[]{:S(2)}) collective-permute-start(bf16[4,144,1122]{2,1,0:T(8,128)(2,1)S(1)} %add_convert_fusion.3), channel_id=1, source_target_pairs={{0,8},{24,16},{1,9},{25,17},{2,10},{26,18},{3,11},{27,19},{4,12},{... | collective-permute-start | bytes 3877640 | tf_op jit(solution)/shard_map/ppermute | solution.py:567
  535.2 21.9 %collective-permute-start.104 = (bf16[4,144,1122]{2,1,0:T(8,128)(2,1)}, bf16[4,144,1122]{2,1,0:T(8,128)(2,1)}, u32[]{:S(2)}, u32[]{:S(2)}) collective-permute-start(bf16[4,144,1122]{2,1,0:T(8,128)(2,1)} %add_convert_fusion.1), channel_id=1, source_target_pairs={{8,16},{16,8},{9,17},{17,9},{10,18},{18,10},{11,19},{19,11},{12,20... | collective-permute-start | bytes 3877640 | tf_op jit(solution)/shard_map/ppermute | solution.py:567
  537.3 33.6 %collective-permute-start.103 = (bf16[4,144,1122]{2,1,0:T(8,128)(2,1)S(1)}, bf16[4,144,1122]{2,1,0:T(8,128)(2,1)}, u32[]{:S(2)}, u32[]{:S(2)}) collective-permute-start(bf16[4,144,1122]{2,1,0:T(8,128)(2,1)S(1)} %add_convert_fusion.2), channel_id=1, source_target_pairs={{8,0},{16,24},{9,1},{17,25},{10,2},{18,26},{11,3},{19,27},{12,4},{... | collective-permute-start | bytes 3877640 | tf_op jit(solution)/shard_map/ppermute | solution.py:567
  542.0 15.2 %collective-permute-start.101 = (bf16[136,1120]{1,0:T(8,128)(2,1)}, bf16[136,1120]{1,0:T(8,128)(2,1)S(1)}, u32[]{:S(2)}, u32[]{:S(2)}) collective-permute-start(bf16[136,1120]{1,0:T(8,128)(2,1)} %get-tuple-element.761), channel_id=1, source_target_pairs={{0,4},{1,5},{2,6},{3,7},{4,0},{5,1},{6,2},{7,3},{8,12},{9,13},{10,... | collective-permute-start | bytes 913928 | tf_op jit(solution)/shard_map/ppermute | solution.py:529
  542.8 14.4 %collective-permute-start.102 = (bf16[136,1120]{1,0:T(8,128)(2,1)}, bf16[136,1120]{1,0:T(8,128)(2,1)S(1)}, u32[]{:S(2)}, u32[]{:S(2)}) collective-permute-start(bf16[136,1120]{1,0:T(8,128)(2,1)} %get-tuple-element.762), channel_id=1, source_target_pairs={{0,6},{1,7},{2,4},{3,5},{4,2},{5,3},{6,0},{7,1},{8,14},{9,15},{10,... | collective-permute-start | bytes 913928 | tf_op jit(solution)/shard_map/ppermute | solution.py:529
  573.0 46.7 %collective-permute-start.111 = (bf16[4,144,1122]{2,1,0:T(8,128)(2,1)S(1)}, bf16[4,144,1122]{2,1,0:T(8,128)(2,1)S(1)}, u32[]{:S(2)}, u32[]{:S(2)}) collective-permute-start(bf16[4,144,1122]{2,1,0:T(8,128)(2,1)S(1)} %add_convert_fusion), channel_id=1, source_target_pairs={{8,0},{16,24},{9,1},{17,25},{10,2},{18,26},{11,3},{19,27},{12,4},{... | collective-permute-start | bytes 3877640 | tf_op jit(solution)/shard_map/ppermute | solution.py:567
  586.2 33.5 %collective-permute-start.105 = (bf16[144,1122]{1,0:T(8,128)(2,1)S(1)}, bf16[144,1122]{1,0:T(8,128)(2,1)S(1)}, u32[]{:S(2)}, u32[]{:S(2)}) collective-permute-start(bf16[144,1122]{1,0:T(8,128)(2,1)S(1)} %copy-done.46), channel_id=1, source_target_pairs={{0,2},{1,3},{2,0},{3,1},{4,6},{5,7},{6,4},{7,5},{8,10},{9,11},{10,... | collective-permute-start | bytes 969416 | tf_op jit(solution)/shard_map/ppermute | solution.py:529
  587.4 32.3 %collective-permute-start.106 = (bf16[144,1122]{1,0:T(8,128)(2,1)S(1)}, bf16[144,1122]{1,0:T(8,128)(2,1)S(1)}, u32[]{:S(2)}, u32[]{:S(2)}) collective-permute-start(bf16[144,1122]{1,0:T(8,128)(2,1)S(1)} %copy-done.45), channel_id=1, source_target_pairs={{0,4},{1,5},{2,6},{3,7},{4,0},{5,1},{6,2},{7,3},{8,12},{9,13},{10,... | collective-permute-start | bytes 969416 | tf_op jit(solution)/shard_map/ppermute | solution.py:529
  593.3 26.4 %collective-permute-start.107 = (bf16[144,1122]{1,0:T(8,128)(2,1)S(1)}, bf16[144,1122]{1,0:T(8,128)(2,1)S(1)}, u32[]{:S(2)}, u32[]{:S(2)}) collective-permute-start(bf16[144,1122]{1,0:T(8,128)(2,1)S(1)} %copy-done.44), channel_id=1, source_target_pairs={{0,6},{1,7},{2,4},{3,5},{4,2},{5,3},{6,0},{7,1},{8,14},{9,15},{10,... | collective-permute-start | bytes 969416 | tf_op jit(solution)/shard_map/ppermute | solution.py:529
  594.5 18.0 %collective-permute-start.117 = (bf16[144,1122]{1,0:T(8,128)(2,1)S(1)}, bf16[144,1122]{1,0:T(8,128)(2,1)S(1)}, u32[]{:S(2)}, u32[]{:S(2)}) collective-permute-start(bf16[144,1122]{1,0:T(8,128)(2,1)S(1)} %get-tuple-element.846), channel_id=1, source_target_pairs={{0,6},{1,7},{2,4},{3,5},{4,2},{5,3},{6,0},{7,1},{8,14},{9,15},{10,... | collective-permute-start | bytes 969416 | tf_op jit(solution)/shard_map/ppermute | solution.py:529
  (195 other events, 1557.6 us)

commit v3 on v2

--- a/solution.py
+++ b/solution.py
@@ -56,6 +56,7 @@
         self.first_heads = [min(first, HEADS - self.window) for first, _ in spans]
         self.wide = self.window * HEAD_DIM
         self.lanes = self.window * LANES
+        self.whole = self.wide == self.chip_cols
         self.by_links = groups == 8
 
     def halves(self, total):
@@ -188,10 +189,12 @@
 def query_chunks(plan):
     both, genes = 2 * plan.gene_rows, 2 * plan.genes
     chunks = []
-    for chip in range(plan.chips):
+    for chip in range(0, plan.chips, 2):
         blocks = [(genes, 2 * plan.prefix, False)]
-        blocks += [(start, both, start == chip * both) for start in range(0, (chip + 1) * both, both)]
-        chunks.append((chip * plan.gene_rows, plan.gene_rows, blocks))
+        blocks += [
+            (start, both, start >= chip * both) for start in range(0, (chip + 2) * both, both)
+        ]
+        chunks.append((chip * plan.gene_rows, both, blocks))
     chunks.append((plan.genes, plan.prefix, [(genes, 2 * plan.prefix, True)]))
     return chunks
 
@@ -207,7 +210,8 @@
     if diagonal:
         block = plan.pre_block if in_prefix else plan.gene_rows
         inner = lax.rem(query_at, block)
-        keep = key_at <= 2 * query_at - inner + core * block
+        before = 0 if in_prefix else start % (4 * block)
+        keep = key_at <= 2 * query_at - inner + core * block - before
     if holes:
         real = lax.rem(key_at, plan.pre_block) < plan.pre_rows
         keep = real if keep is None else keep & real
@@ -225,6 +229,12 @@
 def collect_weight(plan, me, part_refs, weight_ref):
     for at, ref in enumerate(part_refs):
         weight_ref[aligned(me ^ at, plan.part), :] = ref[...]
+
+
+def collect_own(plan, me, part_refs, cut_refs, own_ref, weight_ref):
+    collect_weight(plan, me, part_refs, own_ref if plan.whole else weight_ref)
+    if not plan.whole:
+        own_ref[...] = dot(weight_ref[...], cut_refs[0][...]).astype(BF)
 
 
 def give_blocks(plan, chip, block_refs, rows_ref, weight, weight_dim, pre_ref):
@@ -240,15 +250,18 @@
 def project_kernel(plan, me_ref, *refs):
     chips, groups = plan.chips, plan.groups
     pieces, parts, refs = refs[:chips], refs[chips : chips + groups], refs[chips + groups :]
-    bias_ref, widen_ref, low_ref, query_ref, pair_ref, weight_ref, pre_ref = refs
-    me = me_ref[0]
+    bias_ref, query_ref, pair_ref, pre_ref, low_ref, weight_ref = refs
     collect(plan, me_ref[1], pieces, low_ref, pre_ref)
-    collect_weight(plan, me, parts, weight_ref)
+    collect_weight(plan, me_ref[0], parts, weight_ref)
+    query_ref[...] = jnp.zeros_like(query_ref)
+    pair_ref[...] = jnp.zeros_like(pair_ref)
     for rows in plan.halves(plan.rows):
         narrow = (dot(low_ref[rows, :], weight_ref[...]) + bias_ref[...]).astype(BF)
-        wide = dot(narrow, widen_ref[...]).astype(BF)
-        query_ref[rows, :] = wide[:, : plan.lanes]
-        pair_ref[rows, :] = wide[:, plan.lanes :]
+        for head in range(plan.window):
+            for block, (ref, to) in enumerate(((query_ref, 0), (pair_ref, 0), (pair_ref, HALF))):
+                to += head * LANES
+                begin = block * plan.wide + head * HEAD_DIM
+                ref[rows, to : to + HEAD_DIM] = narrow[:, begin : begin + HEAD_DIM]
 
 
 def order_pairs(plan, core, mine_ref, other_ref, keys_ref, pre_ref):
@@ -264,10 +277,9 @@
 
 
 def attend_kernel(plan, me_ref, *refs):
-    query_ref, mine_ref, other_ref, select_ref, out_weight_ref = refs[:5]
-    keys_ref, mixed_ref, lse_ref = refs[5:8]
-    blocks = refs[8 : 8 + plan.chips]
-    key_pre_ref, out_pre_ref, turned_ref, score_ref, padded_ref = refs[8 + plan.chips :]
+    query_ref, mine_ref, other_ref, out_weight_ref, padded_ref, lse_ref = refs[:6]
+    blocks = refs[6 : 6 + plan.chips]
+    key_pre_ref, out_pre_ref, keys_ref, turned_ref, score_ref = refs[6 + plan.chips :]
     core = me_ref[2]
     order_pairs(plan, core, mine_ref, other_ref, keys_ref, key_pre_ref)
     for head in range(plan.window):
@@ -290,17 +302,17 @@
                 mixed = mixed + dot(turned_ref[:, start : start + size], weights.astype(BF))
             padded_ref[first : first + count, at] = (mixed * (1.0 / total)).T.astype(BF)
             lse_ref[head, :, first : first + count] = top + jnp.log2(total)
-    mixed_ref[...] = dot(padded_ref[...], select_ref[...]).astype(BF)
-    give_blocks(plan, me_ref[1], blocks, mixed_ref, out_weight_ref[...], 0, out_pre_ref)
+    give_blocks(plan, me_ref[1], blocks, padded_ref, out_weight_ref[...], 0, out_pre_ref)
 
 
 def attend_back_kernel(plan, me_ref, *refs):
     pieces, refs = refs[: plan.chips], refs[plan.chips :]
-    out_weight_ref, query_ref, keys_ref, lse_ref = refs[:4]
-    low_ref, query_grad_ref, mine_ref, other_ref, out_bias_ref = refs[4:9]
-    pre_ref, grad_ref, turned_ref, prob_ref, pgrad_ref, pair_ref = refs[9:]
+    out_weight_ref, query_ref, own_pair_ref, other_pair_ref, lse_ref = refs[:5]
+    query_grad_ref, mine_ref, other_ref, out_bias_ref = refs[5:9]
+    pre_ref, key_pre_ref, low_ref, keys_ref, grad_ref, turned_ref, prob_ref, pgrad_ref, pair_ref = refs[9:]
     core = me_ref[2]
     collect(plan, me_ref[1], pieces, low_ref, pre_ref)
+    order_pairs(plan, core, own_pair_ref, other_pair_ref, keys_ref, key_pre_ref)
     out_bias_ref[...] = jnp.sum(low_ref[...].astype(F32), axis=0, keepdims=True)
     for rows in plan.halves(plan.rows):
         grad_ref[rows, :] = dot(low_ref[rows, :], out_weight_ref[...], 1, 1).astype(BF)
@@ -313,6 +325,7 @@
         for first, count, key_parts in query_chunks(plan):
             query = query_ref[first : first + count, at]
             grad = grad_ref[first : first + count, at]
+            both = jnp.concatenate([grad, query], 0)
             lse = lse_ref[head, :, first : first + count]
             delta = 0.0
             for start, size, diagonal in key_parts:
@@ -327,7 +340,9 @@
             for start, size, _ in key_parts:
                 probs = prob_ref[start : start + size, :count]
                 score_grad = (probs * (pgrad_ref[start : start + size, :count] - delta)).astype(BF)
-                pair_ref[start : start + size, :] += dot(probs.astype(BF), grad) + dot(score_grad, query)
+                pair_ref[start : start + size, :] += dot(
+                    jnp.concatenate([probs.astype(BF), score_grad], 1), both
+                )
                 query_grad = query_grad + dot(turned_ref[:, start : start + size], score_grad)
             query_grad_ref[first : first + count, at] = (query_grad.T * SCALE).astype(BF)
         for chip in range(plan.chips):
@@ -344,16 +359,30 @@
 
 
 def project_back_kernel(plan, me_ref, *refs):
-    query_grad_ref, mine_ref, other_ref, select_ref, weight_ref, qkv_grad_ref, bias_ref = refs[:7]
-    blocks, (pre_ref,) = refs[7 : 7 + plan.chips], refs[7 + plan.chips :]
+    groups = plan.groups
+    query_grad_ref, mine_ref, other_ref = refs[:3]
+    parts, refs = refs[3 : 3 + groups], refs[3 + groups :]
+    choices, refs = ([], refs) if plan.whole else (refs[:2], refs[2:])
+    qkv_grad_ref, bias_ref = refs[:2]
+    blocks, (pre_ref, own_ref, weight_ref) = refs[2 : 2 + plan.chips], refs[2 + plan.chips :]
+    collect_own(plan, me_ref[0], parts, choices[1:], own_ref, weight_ref)
     for rows in plan.halves(plan.rows):
         pairs = (mine_ref[rows, :] + other_ref[rows, :].astype(F32)).astype(BF)
-        qkv_grad_ref[rows, :] = (
-            dot(query_grad_ref[rows, :], select_ref[: plan.lanes, :])
-            + dot(pairs, select_ref[plan.lanes :, :])
-        ).astype(BF)
+        if not plan.whole:
+            select_ref = choices[0]
+            qkv_grad_ref[rows, :] = (
+                dot(query_grad_ref[rows, :], select_ref[: plan.lanes, :])
+                + dot(pairs, select_ref[plan.lanes :, :])
+            ).astype(BF)
+            continue
+        queries = query_grad_ref[rows, :]
+        for head in range(plan.window):
+            for block, (value, at) in enumerate(((queries, 0), (pairs, 0), (pairs, HALF))):
+                at += head * LANES
+                to = block * plan.wide + head * HEAD_DIM
+                qkv_grad_ref[rows, to : to + HEAD_DIM] = value[:, at : at + HEAD_DIM]
     bias_ref[...] = jnp.sum(qkv_grad_ref[...].astype(F32), axis=0, keepdims=True)
-    give_blocks(plan, me_ref[1], blocks, qkv_grad_ref, weight_ref[...], 1, pre_ref)
+    give_blocks(plan, me_ref[1], blocks, qkv_grad_ref, own_ref[...], 1, pre_ref)
 
 
 ROOT = math.sqrt(2.0 / math.pi)
@@ -370,51 +399,54 @@
             )
 
 
-def collect_down(plan, level, core, mine_ref, other_ref, down_ref):
+def collect_down(plan, core, mine_ref, other_ref, down_ref):
     if plan.hidden % 16 == 0:
-        down_ref[aligned(core, plan.hidden), :] = mine_ref[level]
-        down_ref[aligned(1 - core, plan.hidden), :] = other_ref[level]
+        down_ref[aligned(core, plan.hidden), :] = mine_ref[...]
+        down_ref[aligned(1 - core, plan.hidden), :] = other_ref[...]
         return
-    mine, other = mine_ref[level].astype(F32), other_ref[level].astype(F32)
+    mine, other = mine_ref[...].astype(F32), other_ref[...].astype(F32)
     halves = [jnp.where(core == 0, mine, other), jnp.where(core == 0, other, mine)]
     down_ref[...] = jnp.concatenate(halves, 0).astype(BF)
 
 
-def lift_kernel(plan, level, me_ref, *refs):
+def lift_kernel(plan, me_ref, *refs):
     chips, groups = plan.chips, plan.groups
     pieces, parts, refs = refs[:chips], refs[chips : chips + groups], refs[chips + groups :]
-    bias_ref, mine_ref, other_ref, low_ref, pre_ref, active_ref, up_ref = refs[:7]
-    blocks, (down_ref,) = refs[7:-1], refs[-1:]
+    bias_ref, mine_ref, other_ref = refs[:3]
+    blocks, (low_ref, up_ref, down_ref) = refs[3 : 3 + chips], refs[3 + chips :]
     collect_weight(plan, me_ref[0], parts, up_ref)
-    collect_down(plan, level, me_ref[2], mine_ref, other_ref, down_ref)
     stack_pieces(plan, pieces, low_ref)
+    collect_down(plan, me_ref[2], mine_ref, other_ref, down_ref)
     size = plan.step_rows
     for first in range(0, plan.all_rows, 2 * size):
         rows = slice(first, first + 2 * size)
         pre = dot(low_ref[rows, :], up_ref[...]) + bias_ref[...]
-        pre_ref[rows, :] = pre
         active = (0.5 * pre * (1.0 + jnp.tanh(ROOT * (pre + CUBE * pre * pre * pre)))).astype(BF)
-        active_ref[rows, :] = active
         lifted = dot(active, down_ref[...])
         for at in range(2):
             blocks[first // size + at][...] = lifted[at * size : at * size + plan.own_rows].astype(BF)
 
 
-def lift_back_kernel(plan, level, me_ref, *refs):
-    pieces, refs = refs[: plan.chips], refs[plan.chips :]
-    up_ref, pre_ref, mine_ref, other_ref, low_ref, pre_grad_ref, down_bias_ref, up_bias_ref = refs[:8]
-    blocks, (down_ref,) = refs[8:-1], refs[-1:]
-    collect_down(plan, level, me_ref[2], mine_ref, other_ref, down_ref)
+def lift_back_kernel(plan, me_ref, *refs):
+    chips, groups = plan.chips, plan.groups
+    pieces, grads, refs = refs[:chips], refs[chips : 2 * chips], refs[2 * chips :]
+    parts, refs = refs[:groups], refs[groups:]
+    bias_ref, mine_ref, other_ref, active_ref, pre_grad_ref, down_bias_ref, up_bias_ref = refs[:7]
+    blocks, (low_ref, grad_ref, up_ref, down_ref) = refs[7 : 7 + chips], refs[7 + chips :]
+    collect_weight(plan, me_ref[0], parts, up_ref)
     stack_pieces(plan, pieces, low_ref)
+    stack_pieces(plan, grads, grad_ref)
+    collect_down(plan, me_ref[2], mine_ref, other_ref, down_ref)
     size = plan.step_rows
-    down_bias_ref[...] = jnp.sum(low_ref[...].astype(F32), axis=0, keepdims=True)
+    down_bias_ref[...] = jnp.sum(grad_ref[...].astype(F32), axis=0, keepdims=True)
     up_bias = 0.0
     for first in range(0, plan.all_rows, 2 * size):
         rows = slice(first, first + 2 * size)
-        act_grad = dot(low_ref[rows, :], down_ref[...], 1, 1)
-        pre = pre_ref[rows, :]
+        pre = dot(low_ref[rows, :], up_ref[...]) + bias_ref[...]
+        act_grad = dot(grad_ref[rows, :], down_ref[...], 1, 1)
         square = pre * pre
         turn = jnp.tanh(ROOT * pre * (1.0 + CUBE * square))
+        active_ref[rows, :] = (0.5 * pre * (1.0 + turn)).astype(BF)
         slope = 0.5 * (1.0 + turn) + (0.5 * ROOT) * pre * (1.0 - turn * turn) * (1.0 + 3.0 * CUBE * square)
         pre_grad = (act_grad * slope).astype(BF)
         pre_grad_ref[rows, :] = pre_grad
@@ -440,8 +472,7 @@
         ref[...] = stack_ref[me_ref[1] ^ at]
 
 
-def weight_grad_kernel(plan, me_ref, left_ref, right_ref, weight_ref, sums_ref, vector_ref, *refs):
-    passengers, (mine_ref, other_ref, whole_ref) = refs[:-3], refs[-3:]
+def norm_weight_grad(plan, left_ref, right_ref, weight_ref, sums_ref, vector_ref, whole_ref):
     width = right_ref.shape[1]
     step = 2 * plan.part
     for first in range(0, plan.features, step):
@@ -454,24 +485,94 @@
         gain_grad = (both - turned[:, 0:1] * shift_grad) / turned[:, 1:2]
         whole_ref[rows, :width] = product
         whole_ref[rows, width : width + 2] = jnp.concatenate([shift_grad, gain_grad], 1)
+
+
+def give_parts(plan, me, whole_ref, mine_ref, other_ref):
+    width = whole_ref.shape[1]
     for at in range(plan.chips):
-        owner = me_ref[0] ^ (2 * at)
-        mine_ref[at, :, : width + 2] = whole_ref[aligned(owner, plan.part), :].astype(BF)
-        other_ref[at, :, : width + 2] = whole_ref[aligned(owner ^ 1, plan.part), :].astype(BF)
-        for ref, rider in zip((mine_ref, other_ref), passengers):
-            rows = rider.shape[0]
-            lanes = slice(at * plan.chip_cols, (at + 1) * plan.chip_cols)
-            filler = jnp.zeros((plan.part - rows, plan.chip_cols), F32)
-            ref[at, :, width + 2 :] = jnp.concatenate([rider[:, lanes], filler], 0).astype(BF)
+        owner = me ^ (2 * at)
+        mine_ref[at, :, :width] = whole_ref[aligned(owner, plan.part), :].astype(BF)
+        other_ref[at, :, :width] = whole_ref[aligned(owner ^ 1, plan.part), :].astype(BF)
+
+
+def lift_grad_kernel(plan, me_ref, *refs):
+    chips, groups = plan.chips, plan.groups
+    pieces, grads, refs = refs[:chips], refs[chips : 2 * chips], refs[2 * chips :]
+    parts, refs = refs[:groups], refs[groups:]
+    active_ref, pre_grad_ref, sums_ref, vector_ref, up_mine, up_other, down_mine, down_other = refs[:8]
+    low_ref, grad_ref, up_ref, whole_ref, down_ref = refs[8:]
+    core = me_ref[2]
+    stack_pieces(plan, pieces, low_ref)
+    collect_weight(plan, me_ref[0], parts, up_ref)
+    norm_weight_grad(plan, low_ref, pre_grad_ref, up_ref, sums_ref, vector_ref, whole_ref)
+    give_parts(plan, me_ref[0], whole_ref, up_mine, up_other)
+    stack_pieces(plan, grads, grad_ref)
+    for rows in plan.halves(plan.chip_hidden):
+        down_ref[rows, :] = dot(active_ref[:, rows], grad_ref[...], 0, 0)
+    size = plan.hidden // 4
+    filler = jnp.zeros((down_mine.shape[1] - size, D), F32)
+    for at in range(4):
+        first = down_ref[at * size : (at + 1) * size, :]
+        second = down_ref[plan.hidden + at * size : plan.hidden + (at + 1) * size, :]
+        for ref, rows in (
+            (down_mine, jnp.where(core == 0, first, second)),
+            (down_other, jnp.where(core == 0, second, first)),
+        ):
+            ref[at] = jnp.concatenate([rows, filler], 0).astype(BF)
+
+
+def attend_grad_kernel(plan, riding, me_ref, *refs):
+    chips, groups = plan.chips, plan.groups
+    pieces, grads, refs = refs[:chips], refs[chips : 2 * chips], refs[2 * chips :]
+    parts, refs = refs[:groups], refs[groups:]
+    choices, refs = ([], refs) if plan.whole else (refs[:2], refs[2:])
+    mixed_ref, qkv_grad_ref, sums_ref, vector_ref, small_ref, mine_ref, other_ref = refs[:7]
+    low_ref, grad_ref, pre_ref, grad_pre_ref, own_ref, weight_ref, whole_ref, out_ref = refs[-8:]
+    core = me_ref[2]
+    collect(plan, me_ref[1], pieces, low_ref, pre_ref)
+    collect_own(plan, me_ref[0], parts, choices[1:], own_ref, weight_ref)
+    norm_weight_grad(plan, low_ref, qkv_grad_ref, own_ref, sums_ref, vector_ref, whole_ref)
+    give_parts(plan, me_ref[0], whole_ref, mine_ref, other_ref)
+    collect(plan, me_ref[1], grads, grad_ref, grad_pre_ref)
+    if plan.whole:
+        for head in range(plan.window):
+            product = dot(mixed_ref[:, head * LANES : (head + 1) * LANES], grad_ref[...], 0, 0)
+            out_ref[head * HEAD_DIM : (head + 1) * HEAD_DIM, :] = product[HALF : HALF + HEAD_DIM]
+    else:
+        own = dot(mixed_ref[...], choices[0][...]).astype(BF)
+        out_ref[...] = dot(own, grad_ref[...], 0, 0)
+    halves = out_ref[: plan.cols, :], out_ref[plan.cols :, :]
+    extra = small_ref.shape[1]
+    filler = jnp.zeros((plan.part - plan.cols - extra, D), F32)
+    first = whole_ref.shape[1]
+    for at, (ref, one, two) in enumerate(((mine_ref, 0, 1), (other_ref, 1, 0))):
+        rows = jnp.where(core == 0, halves[one], halves[two])
+        rows = jnp.concatenate([rows, small_ref[at], filler], 0).astype(BF)
+        if not riding:
+            refs[7 + at][...] = rows
+            continue
+        for chip in range(chips):
+            ref[chip, :, first:] = rows[:, chip * plan.chip_cols : (chip + 1) * plan.chip_cols]
+
+
+def join_down_kernel(plan, *refs):
+    parts, out_ref = refs[:LAYERS], refs[LAYERS]
+    size = plan.hidden // 4
+    for level, ref in enumerate(parts):
+        for at in range(4):
+            out_ref[level, at * size : (at + 1) * size, :] = ref[at, :size, :].astype(F32)
 
 
 def join_kernel(plan, blocks, width, me_ref, *refs):
-    parts, (out_ref, vector_ref) = refs[:LAYERS], refs[LAYERS:]
+    count = LAYERS * plan.chips
+    parts, (out_ref, vector_ref, stack_ref) = refs[:count], refs[count:]
     each = width // blocks
-    for level, ref in enumerate(parts):
+    for level in range(LAYERS):
+        for at in range(plan.chips):
+            stack_ref[at] = parts[level * plan.chips + at][...]
         vectors = 0.0
         for source in range(plan.chips):
-            value = ref[me_ref[1] ^ source].astype(F32)
+            value = stack_ref[me_ref[1] ^ source].astype(F32)
             for block in range(blocks):
                 begin = (block * plan.chips + source) * each
                 out_ref[:, level, begin : begin + each] = value[
@@ -557,22 +658,39 @@
         def __init__(self, mine, other, *steps):
             self.value = (mine.astype(F32) + other.astype(F32)).astype(BF)
             self.steps = list(steps) if cells == 4 else [steps[-1]]
+            self.moves = len(steps)
             waiting.append(self)
+
+        def half(self, bit):
+            halves = self.value.reshape((2, self.value.shape[0] // 2) + self.value.shape[1:])
+            return lax.dynamic_index_in_dim(halves, bit, 0, keepdims=False)
 
         def move(self):
             if cells != 4:
                 return lax.psum(self.value, "cell")
-            inwards, between, outwards = [(0, 1), (3, 2)], [(1, 2), (2, 1)], [(1, 0), (2, 3)]
-            pairs = {3: inwards, 2: between, 1: outwards}[len(self.steps)]
-            return lax.ppermute(self.value, "cell", pairs)
+            left = len(self.steps)
+            if self.moves == 3:
+                inwards, between, outwards = [(0, 1), (3, 2)], [(1, 2), (2, 1)], [(1, 0), (2, 3)]
+                return lax.ppermute(self.value, "cell", {3: inwards, 2: between, 1: outwards}[left])
+            self.away = 1 if left in (1, 4) else 2
+            self.bit = cell // self.away % 2
+            value = self.half(1 - self.bit) if left > 2 else self.value
+            return lax.ppermute(value, "cell", [(at, at ^ self.away) for at in range(4)])
 
         def land(self, got):
+            left = len(self.steps)
             if cells != 4:
                 self.value = got
-            elif len(self.steps) > 1:
-                self.value = (self.value.astype(F32) + got.astype(F32)).astype(BF)
+            elif self.moves == 3 and left == 1:
+                self.value = jnp.where((cell == 1) | (cell == 2), self.value, got)
+            elif left > 2 or self.moves == 3:
+                value = self.value if self.moves == 3 else self.half(self.bit)
+                self.value = (value.astype(F32) + got.astype(F32)).astype(BF)
             else:
-                self.value = jnp.where((cell == 1) | (cell == 2), self.value, got)
+                first, second = (
+                    jnp.where(self.bit == at, self.value, got) for at in range(2)
+                )
+                self.value = jnp.concatenate([first, second], 0)
             self.steps.pop(0)
 
     waiting = []
@@ -608,12 +726,8 @@
         return jnp.where(ok, block * chip_cols + column - offset, -1)
 
     window_at = jnp.arange(3 * wide)
-    block, column = window_at // wide, window_at % wide
-    lane = (column // HEAD_DIM) * LANES + column % HEAD_DIM
-    lane = lane + jnp.where(block == 0, 0, plan.lanes + HALF * (block - 1))
-    widen = chooser(lane, jnp.arange(2 * plan.lanes))
     own_columns = jnp.arange(3 * chip_cols)
-    cut = chooser(own_of(block, column, True), own_columns)
+    cut = chooser(own_of(window_at // wide, window_at % wide, True), own_columns)
     lanes = jnp.arange(2 * plan.lanes)
     inner = lanes % LANES
     is_pair = lanes >= plan.lanes
@@ -627,18 +741,21 @@
     out_ok = (inner >= 0) & (inner < HEAD_DIM)
     out_select = chooser(own_of(0, out_col, out_ok), jnp.arange(chip_cols))
 
-    def by_core(mine, other):
-        first, second = jnp.where(core == 0, mine, other), jnp.where(core == 0, other, mine)
-        return jnp.concatenate([first, second], 1)
-
-    def out_windows(chip_out):
+    def out_windows():
         if plan.by_links:
-            rows, owner = chip_out, chip * chip_cols + jnp.arange(chip_cols)
+            rows = jnp.concatenate([w_out, swap(w_out, 1)], 1)
+            own = jnp.arange(cols)
+            owner = jnp.concatenate([me * cols + own, (me ^ 1) * cols + own])
         else:
             rows = lax.all_gather(w_out, "gene", axis=1, tiled=True)
             owner = jnp.arange(D)
-        pick = chooser(jnp.where(out_ok, first_head * HEAD_DIM + out_col, -1), owner)
-        return [dot(pick, rows[level]).astype(BF) for level in range(LAYERS)]
+        wanted = jnp.where(out_ok, first_head * HEAD_DIM + out_col, -1)
+        is_own = (out_col >= offset) & (out_col < offset + chip_cols)
+        picks = [chooser(wanted, owner)]
+        if not plan.whole:
+            picks.append(chooser(jnp.where(is_own, wanted, -1), owner))
+        got = [[dot(pick, rows[level]).astype(BF) for level in range(LAYERS)] for pick in picks]
+        return got[0], got[-1]
 
     def window_of(vec):
         return lax.dynamic_slice_in_dim(vec, first_head * HEAD_DIM, wide, 1)
@@ -650,9 +767,6 @@
         every = every.transpose(0, 2, 1, 3, 4).reshape(2 * LAYERS, 2, plan.features)
         every = jnp.pad(every, ((0, 0), (0, 6), (0, 0)))
         return [every[at] for at in range(2 * LAYERS)]
-
-    def up_biases_of(token):
-        return lax.dynamic_slice_in_dim(after(bias_up, token), chip * chip_hidden, chip_hidden, 1)
 
     rows_f32 = shape_of(plan.own_rows, D, dtype=F32)
     normed_like = shape_of(plan.own_rows, plan.features)
@@ -681,64 +795,62 @@
     qkv_biases = jnp.concatenate(
         [window_of(bias_q), jnp.zeros((LAYERS, wide), F32), window_of(bias_v)], 1
     )
-    held_out = after(w_out, token)
-    chip_out = by_core(held_out, swap(held_out, 1))
-    out_weights = [chip_out[level] for level in range(LAYERS)]
+    windows, out_weights = out_windows()
     pieces, near, up_sent, _ = together(
-        pieces, near, up_sent, [widen, out_select, qkv_biases] + out_weights
-    )
+        pieces, near, up_sent, [qkv_biases] + windows + out_weights
+    )
+    up_biases = lax.dynamic_slice_in_dim(bias_up, chip * chip_hidden, chip_hidden, 1)
     (qkv_parts[0],) = together(across(near))
 
-    saved = []
+    saved, downs = [], []
     for level in range(LAYERS):
         last = level + 1 == LAYERS
         if level:
             (pieces, far) = together(gather(piece), across(near[chips // 2 :]))
             qkv_parts[level] = qkv_far + far
         up_near = to_chips(after_all(up_sent, *pieces, *qkv_parts[level]))
-        low_one, query, pair, qkv_weight = call(
+        low_one = pieces
+        query, pair = call(
             here(project_kernel, plan),
             "project",
-            [where] + pieces + qkv_parts[level] + [qkv_biases[level : level + 1], widen],
+            [where] + pieces + qkv_parts[level] + [qkv_biases[level : level + 1]],
+            [shape_of(plan.rows, plan.lanes), shape_of(plan.rows, plan.lanes)],
             [
-                shape_of(plan.rows, plan.features),
-                shape_of(plan.rows, plan.lanes),
-                shape_of(plan.rows, plan.lanes),
-                shape_of(plan.features, 3 * wide),
+                pltpu.VMEM((plan.prefix, plan.features), F32),
+                pltpu.VMEM((plan.rows, plan.features), BF),
+                pltpu.VMEM((plan.features, 3 * wide), BF),
             ],
-            [pltpu.VMEM((plan.prefix, plan.features), F32)],
             True,
         )
+        other_pair = swap(pair, 1)
+        own_down = after(w_down, pair)[level]
+        other_down = swap(own_down, 1)
+        if not last:
+            qkv_sent = send(w_qkv, level + 1, qkv_starts, wide, pair)
+            up_sent = send(w_up, level + 1, up_starts, chip_hidden, pair)
+            other_pair = after(other_pair, qkv_sent[-1], up_sent[-1])
         outs = call(
             here(attend_kernel, plan),
             "attend",
-            [where, query, pair, swap(pair, 1), out_select, out_weights[level]],
+            [where, query, pair, other_pair, out_weights[level]],
             [
-                shape_of(2 * plan.rows, plan.lanes),
-                shape_of(plan.rows, chip_cols),
+                shape_of(plan.rows, plan.lanes),
                 shape_of(plan.window, 1, plan.rows, dtype=F32),
             ]
             + row_blocks,
             [
                 pltpu.VMEM((2 * plan.prefix, plan.lanes), F32),
                 pltpu.VMEM((plan.prefix, D), F32),
+                pltpu.VMEM((2 * plan.rows, plan.lanes), BF),
                 pltpu.VMEM((LANES, 2 * plan.rows), BF),
-                pltpu.VMEM((2 * plan.rows, plan.gene_rows), F32),
-                pltpu.VMEM((plan.rows, plan.lanes), BF),
+                pltpu.VMEM((2 * plan.rows, 2 * plan.gene_rows), F32),
             ],
             True,
         )
-        outs, up_near = together(outs, up_near)
-        keys, mixed, lse = outs[:3]
-        spare = []
-        if level == 0:
-            spare = [swap(after(w_down, mixed), 1), up_biases_of(mixed)]
-        if not last:
-            spare = spare + send(w_qkv, level + 1, qkv_starts, wide, mixed)
-        parts, up_far, spare = together(scatter(outs[3:]), across(up_near[: chips // 2]), spare)
-        if level == 0:
-            other_down, up_biases = spare[:2]
-        qkv_sent = spare[-chips:]
+        outs, up_near, (own_down, other_down) = together(outs, up_near, [own_down, other_down])
+        downs.append([own_down, other_down])
+        mixed, lse = outs[:2]
+        parts, up_far = together(scatter(outs[2:]), across(up_near[: chips // 2]))
         middle, piece = call(
             here(middle_kernel, plan, len(parts), level, level),
             "middle",
@@ -754,47 +866,42 @@
             )
             spare = [cot_grad, cot_piece]
         else:
-            spare = send(w_up, level + 1, up_starts, chip_hidden, piece)
+            spare = []
         pieces, far, spare = together(gather(piece), across(up_near[chips // 2 :]), spare)
         up_parts[level] = up_far + far
         if last:
             cot_grad, cot_piece = spare
             near = gather(after(cot_piece, *pieces))
         else:
-            up_sent = spare
             near = to_chips(after_all(qkv_sent, *pieces))
-        outs = call(
-            here(lift_kernel, plan, level),
+        low_two = pieces
+        blocks = call(
+            here(lift_kernel, plan),
             "lift",
             [where]
             + pieces
             + up_parts[level]
-            + [up_biases[level : level + 1], w_down, other_down],
+            + [up_biases[level : level + 1]] + downs[level],
+            row_blocks,
             [
-                shape_of(plan.all_rows, plan.features),
-                shape_of(plan.all_rows, chip_hidden, dtype=F32),
-                shape_of(plan.all_rows, chip_hidden),
-                shape_of(plan.features, chip_hidden),
-            ]
-            + row_blocks,
-            [pltpu.VMEM((chip_hidden, D), BF)],
+                pltpu.VMEM((plan.all_rows, plan.features), BF),
+                pltpu.VMEM((plan.features, chip_hidden), BF),
+                pltpu.VMEM((chip_hidden, D), BF),
+            ],
             True,
         )
-        outs, near = together(outs, near)
-        low_two, pre_act, active, up_weight = outs[:4]
-        saved.append(
-            (rows, low_one, query, keys, mixed, lse, qkv_weight, middle, low_two, pre_act, active, up_weight)
-        )
+        blocks, near = together(blocks, near)
+        saved.append((rows, low_one, query, pair, other_pair, mixed, lse, middle, low_two))
         if last:
             cot_pieces = near
-            last_blocks, last_middle = outs[4:], middle
+            last_blocks, last_middle = blocks, middle
         else:
             spare = []
             if level == 0:
-                spare = out_windows(after(chip_out, low_two)) + [select] + norm_vectors(low_two)
-            parts, qkv_far, spare = together(scatter(outs[4:]), across(near[: chips // 2]), spare)
+                spare = norm_vectors(low_two[0])
+            parts, qkv_far, spare = together(scatter(blocks), across(near[: chips // 2]), spare)
             if level == 0:
-                windows, select, vectors = spare[:LAYERS], spare[LAYERS], spare[LAYERS + 1 :]
+                vectors = spare
             rows, piece = call(
                 here(middle_kernel, plan, len(parts), level, level + 1),
                 "next_rows",
@@ -807,38 +914,66 @@
             lax.dynamic_slice_in_dim(value, at * size, size, dim) for at in (core, 1 - core)
         ]
 
+    def messages_of(item, width):
+        return [item.value[at, :, :width] for at in range(chips)]
+
     grad, pieces = cot_grad, cot_pieces
     down_sums, up_sums, qkv_sums = ([None] * LAYERS for _ in range(3))
     long_rows, short_rows, up_rows = [None] * (2 * LAYERS), [None] * (2 * LAYERS), [None] * LAYERS
+    extra = -(-LAYERS * (4 * cols + hidden) // D)
+    choices = [] if plan.whole else [select, cut]
+    out_choices = [] if plan.whole else [out_select, cut]
+    stacked = pltpu.VMEM((plan.all_rows, plan.features), BF)
+    stacked_grad = pltpu.VMEM((plan.all_rows, D), BF)
+    up_room = pltpu.VMEM((plan.features, chip_hidden), BF)
+    own_room = pltpu.VMEM((plan.features, 3 * chip_cols), BF)
+    window_room = pltpu.VMEM((8, LANES) if plan.whole else (plan.features, 3 * wide), BF)
     for level in reversed(range(LAYERS)):
-        rows, low_one, query, keys, mixed, lse, qkv_weight, middle, low_two, pre_act, active, up_weight = saved[level]
+        rows, low_one, query, pair, other_pair, mixed, lse, middle, low_two = saved[level]
         if level + 1 < LAYERS:
             (pieces,) = beside(f"rows {level}", gather(piece))
+        down_grad = pieces
         outs = call(
-            here(lift_back_kernel, plan, level),
+            here(lift_back_kernel, plan),
             "lift_back",
-            [where] + pieces + [up_weight, pre_act, w_down, other_down],
+            [where]
+            + low_two
+            + pieces
+            + up_parts[level]
+            + [up_biases[level : level + 1]] + downs[level],
             [
-                shape_of(plan.all_rows, D),
+                shape_of(plan.all_rows, chip_hidden),
                 shape_of(plan.all_rows, chip_hidden),
                 vector,
                 shape_of(1, chip_hidden, dtype=F32),
             ]
             + feature_blocks,
-            [pltpu.VMEM((chip_hidden, D), BF)],
+            [stacked, stacked_grad, up_room, pltpu.VMEM((chip_hidden, D), BF)],
             True,
         )
         (outs,) = beside(f"lifted {level}", outs)
-        low_grad, pre_grad, long_rows[level], up_rows[level] = outs[:4]
-        up_mine, up_other = call(
-            here(weight_grad_kernel, plan),
-            "up_grad",
-            [where, low_two, pre_grad, up_weight, up_rows[level], vectors[LAYERS + level]],
-            [shape_of(chips, plan.part, chip_hidden + 2)] * 2,
-            [pltpu.VMEM((plan.features, chip_hidden + 2), F32)],
+        if not level:
+            outs = after_all(outs, up_sums[1].value)
+        active, pre_grad, long_rows[level], up_rows[level] = outs[:4]
+        up_mine, up_other, down_mine, down_other = call(
+            here(lift_grad_kernel, plan),
+            "lift_grad",
+            [where]
+            + low_two
+            + down_grad
+            + up_parts[level]
+            + [active, pre_grad, up_rows[level], vectors[LAYERS + level]],
+            [shape_of(chips, plan.part, chip_hidden + 2)] * 2
+            + [shape_of(4, -(-hidden // 64) * 16, D)] * 2,
+            [
+                stacked,
+                stacked_grad,
+                up_room,
+                pltpu.VMEM((plan.features, chip_hidden + 2), F32),
+                pltpu.VMEM((chip_hidden, D), F32),
+            ],
             True,
         )
-        down_mine, down_other = of_cores(dot(active, low_grad, 0, 0).astype(BF), hidden, 0)
         parts, (up_mine, up_other, down_mine, down_other) = beside(
             f"lift {level}", scatter(outs[4:]), [up_mine, up_other, down_mine, down_other]
         )
@@ -855,15 +990,15 @@
             down_sums[level] = CellSum(down_mine, down_got, "attend 1", "project 1", "lifted 0")
             up_sums[level] = CellSum(up_mine, up_got, "project 1", "lifted 0", "turn 0")
         else:
-            down_sums[level] = CellSum(down_mine, down_got, "attend 0", "qkv 0", "end 1")
-            up_sums[level] = CellSum(up_mine, up_got, "qkv 0", "end 1", "end 2")
+            down_sums[level] = CellSum(down_mine, down_got, "attend 0", "end 1", "end 2")
+            up_sums[level] = CellSum(up_mine, up_got, "end 1", "end 2", "end 3")
         (pieces,) = beside(f"middle {level}", gather(piece))
+        branch_grad = pieces
         outs = call(
             here(attend_back_kernel, plan),
             "attend_back",
-            [where] + pieces + [windows[level], query, keys, lse],
+            [where] + pieces + [windows[level], query, pair, other_pair, lse],
             [
-                shape_of(plan.rows, D),
                 shape_of(plan.rows, plan.lanes),
                 shape_of(plan.rows, plan.lanes, dtype=F32),
                 shape_of(plan.rows, plan.lanes),
@@ -871,32 +1006,37 @@
             ],
             [
                 pltpu.VMEM((plan.prefix, D), F32),
+                pltpu.VMEM((2 * plan.prefix, plan.lanes), F32),
+                pltpu.VMEM((plan.rows, D), BF),
+                pltpu.VMEM((2 * plan.rows, plan.lanes), BF),
                 pltpu.VMEM((plan.rows, plan.lanes), BF),
                 pltpu.VMEM((LANES, 2 * plan.rows), BF),
-                pltpu.VMEM((2 * plan.rows, plan.gene_rows), F32),
-                pltpu.VMEM((2 * plan.rows, plan.gene_rows), F32),
+                pltpu.VMEM((2 * plan.rows, 2 * plan.gene_rows), F32),
+                pltpu.VMEM((2 * plan.rows, 2 * plan.gene_rows), F32),
                 pltpu.VMEM((2 * plan.rows, LANES), F32),
             ],
             True,
         )
-        (outs,) = beside(f"attend {level}", outs)
-        low_grad, query_grad, pair_mine, pair_other, long_rows[LAYERS + level] = outs
-        own_weight = qkv_weight
-        if wide != chip_cols:
-            own_weight = dot(qkv_weight, cut).astype(BF)
+        if level:
+            (outs,) = beside("attend 1", outs)
+        else:
+            up_width, qkv_width = chip_hidden + 2, 3 * chip_cols + 2
+            up_near = to_chips(after_all(messages_of(up_sums[1], up_width), *pieces))
+            outs, up_near = beside("attend 0", outs, up_near)
+        query_grad, pair_mine, pair_other, long_rows[LAYERS + level] = outs
         outs = call(
             here(project_back_kernel, plan),
             "project_back",
-            [where, query_grad, pair_mine, swap(pair_other, 1), select, own_weight],
+            [where, query_grad, pair_mine, swap(pair_other, 1)] + qkv_parts[level] + choices,
             [shape_of(plan.rows, 3 * chip_cols), shape_of(1, 3 * chip_cols, dtype=F32)]
             + feature_blocks,
-            [pltpu.VMEM((plan.prefix, plan.features), F32)],
+            [pltpu.VMEM((plan.prefix, plan.features), F32), own_room, window_room],
             True,
         )
         qkv_grad, qkv_bias = outs[:2]
         short_rows[level] = qkv_bias[:, :chip_cols]
         short_rows[LAYERS + level] = qkv_bias[:, 2 * chip_cols :]
-        riders = of_cores(dot(mixed, low_grad, 0, 0), cols, 0)
+        small = jnp.zeros((2, extra, D), F32)
         if not level:
             long_own = lax.dynamic_slice_in_dim(
                 jnp.concatenate(long_rows, 0), chip * chip_cols, chip_cols, 1
@@ -909,23 +1049,37 @@
                     of_cores(jnp.concatenate(up_rows, 0), hidden, 1),
                 )
             ]
-            extra = -(-small[0].size // D)
-            small = [jnp.pad(vec, (0, extra * D - vec.size)).reshape(extra, D) for vec in small]
-            riders = [jnp.concatenate(pair, 0) for pair in zip(riders, small)]
-        width = 3 * chip_cols + 2 + chip_cols
-        qkv_mine, qkv_other = call(
-            here(weight_grad_kernel, plan),
-            "qkv_grad",
-            [where, low_one, qkv_grad, own_weight, qkv_bias, vectors[level]] + riders,
-            [shape_of(chips, plan.part, width)] * 2,
-            [pltpu.VMEM((plan.features, 3 * chip_cols + 2), F32)],
+            small = jnp.stack(
+                [jnp.pad(vec, (0, extra * D - vec.size)).reshape(extra, D) for vec in small]
+            )
+        width = 3 * chip_cols + 2
+        made = call(
+            here(attend_grad_kernel, plan, bool(level)),
+            "attend_grad",
+            [where]
+            + low_one
+            + branch_grad
+            + qkv_parts[level]
+            + out_choices
+            + [mixed, qkv_grad, qkv_bias, vectors[level], small],
+            [shape_of(chips, plan.part, width + (chip_cols if level else 0))] * 2
+            + [shape_of(plan.part, D)] * (0 if level else 2),
+            [
+                pltpu.VMEM((plan.rows, plan.features), BF),
+                pltpu.VMEM((plan.rows, D), BF),
+                pltpu.VMEM((plan.prefix, plan.features), F32),
+                pltpu.VMEM((plan.prefix, D), F32),
+                own_room,
+                window_room,
+                pltpu.VMEM((plan.features, 3 * chip_cols + 2), F32),
+                pltpu.VMEM((chip_cols, D), F32),
+            ],
             True,
         )
-        parts = scatter(outs[2:])
+        blocks = outs[2:]
         if level:
-            parts, (qkv_mine, qkv_other) = beside(
-                "project 1", parts, [qkv_mine, qkv_other]
-            )
+            parts = scatter(blocks)
+            parts, (qkv_mine, qkv_other) = beside("project 1", parts, made)
             grad, piece = call(
                 here(back_kernel, plan, len(parts), level),
                 "rows_back",
@@ -933,50 +1087,52 @@
                 [rows_f32, grad_like],
             )
             grad, piece, qkv_got = together([grad, piece, swap(qkv_other, 1)])[0]
-            qkv_sums[level] = [CellSum(qkv_mine, qkv_got, "turn 0", "attend 0", "qkv 0")]
-
-    def messages_of(item, width):
-        return [item.value[at, :, :width] for at in range(chips)]
-
-    ((qkv_mine, qkv_other),) = beside("qkv 0", [qkv_mine, qkv_other])
-    (qkv_got,) = together([swap(qkv_other, 1)])[0]
-    qkv_sums[0] = [CellSum(qkv_mine, qkv_got, "end 1", "end 2", "end 3")]
-    (parts,) = beside("end 1", parts)
+            qkv_sums[level] = CellSum(qkv_mine, qkv_got, "lift 0", "attend 0", "end 1")
+
+    (made,) = together(made)
+    qkv_mine, qkv_other, out_mine, out_other = made
+    qkv_got, out_got = together([swap(qkv_other, 1), swap(out_other, 1)])[0]
+    qkv_sums[0] = CellSum(qkv_mine, qkv_got, "end 2", "end 3", "end 4")
+    beside("end 1", [qkv_sums[0].value])
+    parts, _ = beside("end 2", scatter(after_all(blocks, qkv_sums[0].value)), [up_sums[0].value])
     ends = call(
         here(back_end_kernel, plan, len(parts), 0),
         "rows_back_end",
         parts + [rows, norm1_gain, middle_grad],
         ends_like,
     )
-    up_width, qkv_width = chip_hidden + 2, 3 * chip_cols + 2
-    parts, ends = beside(
-        "end 2",
-        scatter(after_all(last_blocks, parts[0])),
-        ends,
-    )
+    out_sum = (after(out_mine, parts[0]).astype(F32) + out_got.astype(F32)).astype(BF)
+    parts, ends = beside("end 3", scatter(after_all(last_blocks, *parts)), ends)
     result = call(
         here(finish_kernel, plan, len(parts), LAYERS - 1),
         "finish",
         parts + [last_middle, bias_down],
         ends_like,
     )
-    near, far, result = beside(
-        "end 3",
-        to_chips(after_all(messages_of(up_sums[1], up_width), result[0])),
-        to_chips(after_all(messages_of(qkv_sums[1][0], qkv_width), result[0])),
-        result,
-    )
-    last_near = to_chips(messages_of(qkv_sums[0][0], qkv_width))
-    last_up = to_chips(messages_of(up_sums[0], up_width))
-    up_parts = [jnp.stack(last_up), jnp.stack(near)]
-    qkv_parts = [jnp.stack(last_near), jnp.stack(far)]
-    out_sums = []
-    for items in qkv_sums:
-        riders = [items[0].value[at, :, qkv_width:] for at in range(chips)]
-        out_sums.append(jnp.concatenate(riders, 1))
-    small = out_sums[0][cols : cols + extra].reshape(-1).astype(F32)
-    out_sums = [value[:cols] for value in out_sums]
-    down_sums = [item.value for item in down_sums]
+    def sum_near(value, away):
+        if cells != 4:
+            return lax.psum(value, "cell") if away == 1 else value
+        got = lax.ppermute(value, "cell", [(at, at ^ away) for at in range(cells)])
+        return (value.astype(F32) + got.astype(F32)).astype(BF)
+
+    near = to_chips(after_all(messages_of(qkv_sums[1], qkv_width), *parts))
+    last_up = to_chips(after_all(messages_of(up_sums[0], up_width), *parts))
+    (out_sum,) = after_all([out_sum], *parts)
+    (g_down,) = call(
+        here(join_down_kernel, plan),
+        "join_down",
+        after_all([item.value for item in down_sums], parts[0]),
+        [shape_of(LAYERS, hidden, D, dtype=F32)],
+    )
+    near, last_up, result, (out_sum, g_down) = beside(
+        "end 4", near, last_up, result, [sum_near(out_sum, 1), g_down]
+    )
+    last_near = to_chips(messages_of(qkv_sums[0], qkv_width))
+    out_sum = sum_near(out_sum, 2)
+    up_parts = [last_up, up_near]
+    riders = [qkv_sums[1].value[at, : plan.cols, qkv_width:] for at in range(chips)]
+    out_sums = [out_sum[:cols], after(jnp.concatenate(riders, 1), last_up[0])]
+    small = out_sum[cols : cols + extra].reshape(-1).astype(F32)
     size = LAYERS * cols
     b_down, b_out, b_q, b_v = (small[at * size : (at + 1) * size].reshape(LAYERS, cols) for at in range(4))
     b_up = small[4 * size : 4 * size + LAYERS * hidden].reshape(LAYERS, hidden)
@@ -985,16 +1141,19 @@
         whole, vectors = call(
             here(join_kernel, plan, blocks, width),
             "join",
-            [where] + parts,
+            [where] + parts[0] + parts[1],
             [
                 shape_of(cols, LAYERS, blocks * D if blocks > 1 else FF, dtype=F32),
                 shape_of(LAYERS, 8, plan.part, dtype=F32),
             ],
+            [pltpu.VMEM((chips, plan.part, width + 2), BF)],
             scalar=True,
         )
         return whole.transpose(1, 0, 2), vectors[:, 0, :cols], vectors[:, 1, :cols]
 
-    g_up, shift_two, gain_two = join(up_parts, 1, chip_hidden)
+    ups = join(up_parts, 1, chip_hidden)
+    last_near, (g_up, shift_two, gain_two) = together(last_near, ups)
+    qkv_parts = [last_near, near]
     g_qkv, shift_one, gain_one = join(qkv_parts, 3, 3 * chip_cols)
     return (
         result[0].T[None],
@@ -1004,7 +1163,7 @@
         g_qkv,
         jnp.stack(out_sums).astype(F32),
         g_up,
-        jnp.stack(down_sums).astype(F32),
+        g_down,
         gain_one,
         shift_one,
         gain_two,

time: 664 us -> 650 us (0.979)
  other arithmetic: 54.1 us -> 43 us
  matrix products: 13.4 us -> 4.34 us
  waiting for transfers between devices: 197 us -> 206 us
  Pallas kernels: 211 us -> 203 us
    dot_general x6 -> x2, matrix products: 13.4 us -> 4.34 us  [dot(): lax.dot_general(left, right, (((left_dim,), (right_dim,)), ((), ())), pre...]
    pallas_call x32 -> x33, Pallas kernels: 211 us -> 203 us  [call(): pl.pallas_call(kernel, in_specs=[SCALAR if scalar and at == 0 else WHOLE...]
    another operation x6 -> x1, other arithmetic: 8.61 us -> 0.62 us  [body(): jnp.stack([jnp.pad(vec, (0, extra * D - vec.size)).reshape(extra, D) for...]
    ppermute x18 -> x20, waiting for transfers between devices: 37.1 us -> 44.8 us  [the longest x18 31.3 us: move(): lax.ppermute(self.value, 'cell', {3: inwards, 2: between, 1: outwards}[le...]
    convert_element_type x17 -> x16, other arithmetic: 29.2 us -> 22.7 us  [the longest x12 20.7 us: land(): self.value = (value.astype(F32) + got.astype(F32)).astype(BF)]
    unnamed x289 -> x268, local copies, waits for them, and re-layouts: 23.1 us -> 28.6 us
    ppermute x18 -> x20, starting transfers between devices: 44 us -> 47.7 us  [the longest x18 43.6 us: move(): lax.ppermute(self.value, 'cell', {3: inwards, 2: between, 1: outwards}[le...]
    ppermute x100 -> x102, waiting for transfers between devices: 160 us -> 161 us  [swap(): lax.ppermute(value, 'gene', [(at, at ^ bits) for at in range(groups)])]
  transfers between devices with their start and end apart: 118 -> 122, of which waited for: 48 -> 44; matrix products, arithmetic and copies ran while one was open for 11% -> 10% of each run, Pallas kernels for 24% -> 26%
where the time goes in v3:
time: 650 us; the launch traced here: 640 us
  waiting for transfers between devices  206 us (32%)
  Pallas kernels  203 us (31%)
  starting transfers between devices  137 us (21%)
  local copies, waits for them, and re-layouts  44.3 us (7%)
  other arithmetic  43 us (7%)
    pallas_call x33, Pallas kernels, call(): pl.pallas_call(kernel, in_specs=[SCALAR if scalar and at == 0 else WHOLE...  203 us
    ppermute x102, waiting for transfers between devices, swap(): lax.ppermute(value, 'gene', [(at, at ^ bits) for at in range(groups)])  161 us
    ppermute x102, starting transfers between devices, swap(): lax.ppermute(value, 'gene', [(at, at ^ bits) for at in range(groups)])  89.1 us
    ppermute x18, starting transfers between devices, move(): lax.ppermute(self.value, 'cell', {3: inwards, 2: between, 1: outwards}[le...  43.6 us
    ppermute x18, waiting for transfers between devices, move(): lax.ppermute(self.value, 'cell', {3: inwards, 2: between, 1: outwards}[le...  31.3 us
    unnamed x268, local copies, waits for them, and re-layouts  28.6 us
    convert_element_type x12, other arithmetic, land(): self.value = (value.astype(F32) + got.astype(F32)).astype(BF)  20.7 us
    ppermute x2, waiting for transfers between devices, sum_near(): got = lax.ppermute(value, 'cell', [(at, at ^ away) for at in range(cells)])  13.5 us
  transfers between devices with their start and end apart: 122, of which 44 were waited for; matrix products, arithmetic and copies ran while one was open for 10% of the time, Pallas kernels for 26%

profile of v3, /device:TPU:0, one launch (start us, length us, event | category | flops | bytes accessed | tf_op | source)
XLA Modules:
  0.0 639.5 jit_solution(15247319655397314704)
XLA Ops:
  4.5 2.9 collective-permute-start
  9.6 3.0 copy.53.weight_ref
  12.6 3.2 send.4
  15.8 2.9 collective-permute-start.5
  22.4 3.2 send.5
  35.4 3.7 collective-permute-done.4.refs_8_.refs_7_.refs_12_
  42.6 5.0 project.2
  52.5 3.2 send.7
  55.7 3.1 send.6
  59.7 9.5 %attend.2 = (bf16[544,640]{1,0:T(8,128)(2,1)}, f32[5,1,544]{2,1,0:T(1,128)}, bf16[136,1120]{1,0:T(8,128)(2,1)}, bf16[136,1120]{1,0:T(8,128)(2,1)}, bf16[136,1120]{1,0:T(8,128)(2,1)}, /*index=5*/bf16[136,1120]{1,0:T(8,128)(2,1)}) custom-call(s32[3]{0:T(128)} %pad_add_fusion.1.me_ref, bf16[544,640]{1,0:T(8,128)(2,1)} %get-tuple-element.440.refs_0_.refs_5_, ...), custom_call_target="tpu_custom_call" | custom-call | flops 1000 | bytes 1000 | tf_op jit(solution)/shard_map/attend/pallas_call | solution.py:72
  73.3 7.0 %collective-permute-done.16.refs_1_ = bf16[136,1120]{1,0:T(8,128)(2,1)S(1)} collective-permute-done((bf16[136,1120]{1,0:T(8,128)(2,1)}, bf16[136,1120]{1,0:T(8,128)(2,1)S(1)}, u32[]{:S(2)}, u32[]{:S(2)}) %collective-permute-start.16) | collective-permute-done | bytes 304672 | tf_op jit(solution)/shard_map/ppermute | solution.py:630
  80.3 7.0 %collective-permute-done.17.refs_2_ = bf16[136,1120]{1,0:T(8,128)(2,1)S(1)} collective-permute-done((bf16[136,1120]{1,0:T(8,128)(2,1)}, bf16[136,1120]{1,0:T(8,128)(2,1)S(1)}, u32[]{:S(2)}, u32[]{:S(2)}) %collective-permute-start.17) | collective-permute-done | bytes 304672 | tf_op jit(solution)/shard_map/ppermute | solution.py:630
  94.5 6.9 %collective-permute-done.21.refs_1_ = bf16[136,1152]{1,0:T(8,128)(2,1)S(1)} collective-permute-done((bf16[136,1152]{1,0:T(8,128)(2,1)}, bf16[136,1152]{1,0:T(8,128)(2,1)S(1)}, u32[]{:S(2)}, u32[]{:S(2)}) %collective-permute-start.21) | collective-permute-done | bytes 313376 | tf_op jit(solution)/shard_map/ppermute | solution.py:630
  101.4 6.6 %collective-permute-done.22.refs_2_ = bf16[136,1152]{1,0:T(8,128)(2,1)} collective-permute-done((bf16[136,1152]{1,0:T(8,128)(2,1)}, bf16[136,1152]{1,0:T(8,128)(2,1)}, u32[]{:S(2)}, u32[]{:S(2)}) %collective-permute-start.22) | collective-permute-done | bytes 313376 | tf_op jit(solution)/shard_map/ppermute | solution.py:630
  113.1 8.0 %lift.2 = (bf16[136,1120]{1,0:T(8,128)(2,1)}, bf16[136,1120]{1,0:T(8,128)(2,1)}, bf16[136,1120]{1,0:T(8,128)(2,1)}, bf16[136,1120]{1,0:T(8,128)(2,1)}) custom-call(s32[3]{0:T(128)} %pad_add_fusion.1.me_ref, bf16[136,1152]{1,0:T(8,128)(2,1)} %get-tuple-element.475.refs_0_, bf16[136,1152]{1,0:T(8,128)(2,1)} %copy-done.24, ...), custom_call_target="tpu_custom_call" | custom-call | flops 1000 | bytes 1000 | tf_op jit(solution)/shard_map/lift/pallas_call | solution.py:72
  128.1 4.9 collective-permute-done.29.refs_1_
  133.1 4.3 collective-permute-done.30.refs_2_
  146.6 4.1 collective-permute-done.34.refs_1_
  150.6 5.3 collective-permute-done.35.refs_2_
  156.8 4.9 project.3
  167.4 9.2 %attend.3 = (bf16[544,640]{1,0:T(8,128)(2,1)}, f32[5,1,544]{2,1,0:T(1,128)}, bf16[136,1120]{1,0:T(8,128)(2,1)}, bf16[136,1120]{1,0:T(8,128)(2,1)}, bf16[136,1120]{1,0:T(8,128)(2,1)}, /*index=5*/bf16[136,1120]{1,0:T(8,128)(2,1)}) custom-call(s32[3]{0:T(128)} %pad_add_fusion.1.me_ref, bf16[544,640]{1,0:T(8,128)(2,1)} %get-tuple-element.527.refs_0_.refs_5_, ...), custom_call_target="tpu_custom_call" | custom-call | flops 1000 | bytes 1000 | tf_op jit(solution)/shard_map/attend/pallas_call | solution.py:72
  176.6 4.0 collective-permute-done.41.refs_8_.refs_12_
  184.7 7.0 %collective-permute-done.44.refs_1_ = bf16[136,1120]{1,0:T(8,128)(2,1)S(1)} collective-permute-done((bf16[136,1120]{1,0:T(8,128)(2,1)}, bf16[136,1120]{1,0:T(8,128)(2,1)S(1)}, u32[]{:S(2)}, u32[]{:S(2)}) %collective-permute-start.44) | collective-permute-done | bytes 304672 | tf_op jit(solution)/shard_map/ppermute | solution.py:630
  191.7 7.3 %collective-permute-done.45.refs_2_ = bf16[136,1120]{1,0:T(8,128)(2,1)S(1)} collective-permute-done((bf16[136,1120]{1,0:T(8,128)(2,1)}, bf16[136,1120]{1,0:T(8,128)(2,1)S(1)}, u32[]{:S(2)}, u32[]{:S(2)}) %collective-permute-start.45) | collective-permute-done | bytes 304672 | tf_op jit(solution)/shard_map/ppermute | solution.py:630
  208.3 4.7 collective-permute-done.49.refs_1_
  213.0 6.2 collective-permute-done.50.refs_2_
  222.9 8.0 %lift.3 = (bf16[136,1120]{1,0:T(8,128)(2,1)}, bf16[136,1120]{1,0:T(8,128)(2,1)}, bf16[136,1120]{1,0:T(8,128)(2,1)}, bf16[136,1120]{1,0:T(8,128)(2,1)}) custom-call(s32[3]{0:T(128)} %pad_add_fusion.1.me_ref, bf16[136,1152]{1,0:T(8,128)(2,1)} %get-tuple-element.560.refs_0_, bf16[136,1152]{1,0:T(8,128)(2,1)} %copy-done.25, bf16[136,1152]{1,0:T(8,128)(2,1)} %copy-done.26, ...), custom_call_target="tpu_custom_call" | custom-call | flops 1000 | bytes 1000 | tf_op jit(solution)/shard_map/lift/pallas_call | solution.py:72
  230.9 5.3 collective-permute-done.55.refs_6_
  237.1 10.5 %lift_back.2 = (bf16[576,1120]{1,0:T(8,128)(2,1)}, bf16[576,1120]{1,0:T(8,128)(2,1)}, f32[1,1120]{1,0:T(1,128)}, f32[1,1120]{1,0:T(1,128)}, bf16[136,1152]{1,0:T...) custom-call(s32[3]{0:T(128)} %pad_add_fusion.1.me_ref, ...), custom_call_target="tpu_custom_call" | custom-call | flops 1000 | bytes 1000 | tf_op jit(solution)/shard_map/lift_back/pallas_call | solution.py:72
  251.2 10.1 %lift_grad.2 = (bf16[4,144,1122]{2,1,0:T(8,128)(2,1)}, bf16[4,144,1122]{2,1,0:T(8,128)(2,1)}, bf16[4,144,1120]{2,1,0:T(8,128)(2,1)}, bf16[4,144,1120]{2,1,0:T(8,128)(2,1)}) custom-call(s32[3]{0:T(128)} %pad_add_fusion.1.me_ref, bf16[136,1152]{1,0:T(8,128)(2,1)} %get-tuple-element.560.refs_0_, bf16[136,1152]{1,0:T(8,128)(2,1)} %copy-done.25, ...), custom_call_target="tpu_custom_call" | custom-call | flops 1000 | bytes 1000 | tf_op jit(solution)/shard_map/lift_grad/pallas_call | solution.py:72
  263.1 3.7 middle_back.2
  270.3 4.7 collective-permute-start.65
  280.2 5.1 collective-permute-done.62.refs_1_.refs_5_
  285.3 7.0 %collective-permute-done.63.refs_2_.refs_6_ = bf16[136,1120]{1,0:T(8,128)(2,1)S(1)} collective-permute-done((bf16[136,1120]{1,0:T(8,128)(2,1)S(1)}, bf16[136,1120]{1,0:T(8,128)(2,1)S(1)}, u32[]{:S(2)}, u32[]{:S(2)}) %collective-permute-start.63) | collective-permute-done | bytes 304672 | tf_op jit(solution)/shard_map/ppermute | solution.py:630
  293.0 13.4 %attend_back.2 = (bf16[544,640]{1,0:T(8,128)(2,1)}, f32[544,640]{1,0:T(8,128)}, bf16[544,640]{1,0:T(8,128)(2,1)}, f32[1,1120]{1,0:T(1,128)}) custom-call(s32[3]{0:T(128)} %pad_add_fusion.1.me_ref, bf16[136,1120]{1,0:T(8,128)(2,1)} %get-tuple-element.607.refs_0_.refs_4_, bf16[136,1120]{1,0:T(8,128)(2,1)} %copy-done.70, bf16[136,1120]{1,0:T(8,128)(2,1)} %copy-done.71, ...), custom_call_target="tpu_custom_call" | custom-call | flops 1000 | bytes 1000 | tf_op jit(solution)/shard_map/attend_back/pallas_call | solution.py:72
  312.2 6.9 %project_back.2 = (bf16[544,840]{1,0:T(8,128)(2,1)}, f32[1,840]{1,0:T(1,128)}, bf16[136,1152]{1,0:T(8,128)(2,1)}, bf16[136,1152]{1,0:T(8,128)(2,1)}, bf16[136,11...) custom-call(s32[3]{0:T(128)} %pad_add_fusion.1.me_ref, bf16[544,640]{1,0:T(8,128)(2,1)} %get-tuple-element.618.refs_0_, ...), custom_call_target="tpu_custom_call" | custom-call | flops 1000 | bytes 1000 | tf_op jit(solution)/shard_map/project_back/pallas_call | solution.py:72
  323.2 8.4 %attend_grad.2 = (bf16[4,144,1122]{2,1,0:T(8,128)(2,1)}, bf16[4,144,1122]{2,1,0:T(8,128)(2,1)}) custom-call(s32[3]{0:T(128)} %pad_add_fusion.1.me_ref, bf16[136,1152]{1,0:T(8,128)(2,1)} %get-tuple-element.515.refs_0_, bf16[136,1152]{1,0:T(8,128)(2,1)} %copy-done.63, bf16[136,1152]{1,0:T(8,128)(2,1)} %copy-done.64, bf16[136,1152]{1,0:T(8,128)(2,1)} %copy-done.65, ...), custom_call_target="tpu_custom_call" | custom-call | flops 1000 | bytes 1000 | tf_op jit(solution)/shard_map/attend_grad/pallas_call | solution.py:72
  331.6 3.9 collective-permute-done.68.refs_2_
  342.7 3.3 rows_back.1
  349.4 9.7 %collective-permute-start.81 = (bf16[4,144,1122]{2,1,0:T(8,128)(2,1)S(1)}, bf16[4,144,1122]{2,1,0:T(8,128)(2,1)}, u32[]{:S(2)}, u32[]{:S(2)}) collective-permute-start(bf16[4,144,1122]{2,1,0:T(8,128)(2,1)S(1)} %add_convert_fusion.11), channel_id=1, source_target_pairs={{0,8},{24,16},{1,9},{25,17},{2,10},{26,18},{3,11},{27,19},{4,12},{... | collective-permute-start | bytes 3877640 | tf_op jit(solution)/shard_map/ppermute | solution.py:674
  361.0 13.4 %collective-permute-done.74.refs_6_ = bf16[136,1120]{1,0:T(8,128)(2,1)S(1)} collective-permute-done((bf16[136,1120]{1,0:T(8,128)(2,1)S(1)}, bf16[136,1120]{1,0:T(8,128)(2,1)S(1)}, u32[]{:S(2)}, u32[]{:S(2)}) %collective-permute-start.74) | collective-permute-done | bytes 304672 | tf_op jit(solution)/shard_map/ppermute | solution.py:630
  375.1 10.5 %lift_back.3 = (bf16[576,1120]{1,0:T(8,128)(2,1)}, bf16[576,1120]{1,0:T(8,128)(2,1)}, f32[1,1120]{1,0:T(1,128)}, f32[1,1120]{1,0:T(1,128)}, bf16[136,1152]{1,0:T...) custom-call(s32[3]{0:T(128)} %pad_add_fusion.1.me_ref, ...), custom_call_target="tpu_custom_call" | custom-call | flops 1000 | bytes 1000 | tf_op jit(solution)/shard_map/lift_back/pallas_call | solution.py:72
  392.4 10.1 %lift_grad.3 = (bf16[4,144,1122]{2,1,0:T(8,128)(2,1)}, bf16[4,144,1122]{2,1,0:T(8,128)(2,1)}, bf16[4,144,1120]{2,1,0:T(8,128)(2,1)}, bf16[4,144,1120]{2,1,0:T(8,128)(2,1)}) custom-call(s32[3]{0:T(128)} %pad_add_fusion.1.me_ref, bf16[136,1152]{1,0:T(8,128)(2,1)} %get-tuple-element.475.refs_0_, bf16[136,1152]{1,0:T(8,128)(2,1)} %copy-done.24, ...), custom_call_target="tpu_custom_call" | custom-call | flops 1000 | bytes 1000 | tf_op jit(solution)/shard_map/lift_grad/pallas_call | solution.py:72
  408.2 3.4 middle_back.3
  411.6 10.5 %collective-permute-done.84 = bf16[4,144,1122]{2,1,0:T(8,128)(2,1)} collective-permute-done((bf16[4,144,1122]{2,1,0:T(8,128)(2,1)S(1)}, bf16[4,144,1122]{2,1,0:T(8,128)(2,1)}, u32[]{:S(2)}, u32[]{:S(2)}) %collective-permute-start.84) | collective-permute-done | bytes 1292576 | tf_op jit(solution)/shard_map/ppermute | solution.py:674
  427.6 2.9 collective-permute-start.92
  441.6 13.4 %attend_back.3 = (bf16[544,640]{1,0:T(8,128)(2,1)}, f32[544,640]{1,0:T(8,128)}, bf16[544,640]{1,0:T(8,128)(2,1)}, f32[1,1120]{1,0:T(1,128)}) custom-call(s32[3]{0:T(128)} %pad_add_fusion.1.me_ref, bf16[136,1120]{1,0:T(8,128)(2,1)} %get-tuple-element.691.refs_0_.refs_4_, bf16[136,1120]{1,0:T(8,128)(2,1)} %copy-done.66, bf16[136,1120]{1,0:T(8,128)(2,1)} %copy-done.67, ...), custom_call_target="tpu_custom_call" | custom-call | flops 1000 | bytes 1000 | tf_op jit(solution)/shard_map/attend_back/pallas_call | solution.py:72
  462.3 3.1 add_convert_fusion.5
  467.8 7.0 %project_back.3 = (bf16[544,840]{1,0:T(8,128)(2,1)}, f32[1,840]{1,0:T(1,128)}, bf16[136,1152]{1,0:T(8,128)(2,1)}, bf16[136,1152]{1,0:T(8,128)(2,1)}, bf16[136,11...) custom-call(s32[3]{0:T(128)} %pad_add_fusion.1.me_ref, bf16[544,640]{1,0:T(8,128)(2,1)} %get-tuple-element.709.refs_0_, ...), custom_call_target="tpu_custom_call" | custom-call | flops 1000 | bytes 1000 | tf_op jit(solution)/shard_map/project_back/pallas_call | solution.py:72
  476.7 8.1 %attend_grad.3 = (bf16[4,144,842]{2,1,0:T(8,128)(2,1)}, bf16[4,144,842]{2,1,0:T(8,128)(2,1)}, bf16[144,1120]{1,0:T(8,128)(2,1)}, bf16[144,1120]{1,0:T(8,128)(2,1)}) custom-call(s32[3]{0:T(128)} %pad_add_fusion.1.me_ref, bf16[136,1152]{1,0:T(8,128)(2,1)} %get-tuple-element.424.refs_0_, bf16[136,1152]{1,0:T(8,128)(2,1)} %copy-done.61, ...), custom_call_target="tpu_custom_call" | custom-call | flops 1000 | bytes 1000 | tf_op jit(solution)/shard_map/attend_grad/pallas_call | solution.py:72
  490.5 6.2 collective-permute-start.104
  496.7 3.3 collective-permute-done.96
  511.2 10.7 %collective-permute-done.100.refs_2_ = bf16[136,1152]{1,0:T(8,128)(2,1)S(1)} collective-permute-done((bf16[136,1152]{1,0:T(8,128)(2,1)S(1)}, bf16[136,1152]{1,0:T(8,128)(2,1)S(1)}, u32[]{:S(2)}, u32[]{:S(2)}) %collective-permute-start.100) | collective-permute-done | bytes 313376 | tf_op jit(solution)/shard_map/ppermute | solution.py:630
  525.4 4.8 collective-permute-done.99.refs_1_
  530.2 4.8 collective-permute-done.102
  538.3 3.3 rows_back_end.1
  548.5 3.6 collective-permute-done.105.refs_1_
  552.2 5.2 collective-permute-done.106.refs_2_
  557.4 12.7 %collective-permute-done.108 = bf16[4,144,1122]{2,1,0:T(8,128)(2,1)} collective-permute-done((bf16[4,144,1122]{2,1,0:T(8,128)(2,1)S(1)}, bf16[4,144,1122]{2,1,0:T(8,128)(2,1)}, u32[]{:S(2)}, u32[]{:S(2)}) %collective-permute-start.108) | collective-permute-done | bytes 1292576 | tf_op jit(solution)/shard_map/ppermute | solution.py:674
  583.9 4.4 join_down.1
  590.0 13.5 %collective-permute-done.116 = bf16[144,1120]{1,0:T(8,128)(2,1)} collective-permute-done((bf16[144,1120]{1,0:T(8,128)(2,1)}, bf16[144,1120]{1,0:T(8,128)(2,1)}, u32[]{:S(2)}, u32[]{:S(2)}) %collective-permute-start.116) | collective-permute-done | bytes 322592 | tf_op jit(solution)/shard_map/ppermute | solution.py:1115
  604.8 5.9 collective-permute-done.112.refs_7_
  617.7 6.4 join.2
  627.0 7.0 %join.3 = (f32[140,2,3360]{2,1,0:T(2,128)}, f32[2,8,144]{2,1,0:T(8,128)}) custom-call(s32[3]{0:T(128)} %pad_add_fusion.1.me_ref, bf16[144,842]{1,0:T(8,128)(2,1)} %get-tuple-element.793.refs_0_, bf16[144,842]{1,0:T(8,128)(2,1)} %copy-done.108, bf16[144,842]{1,0:T(8,128)(2,1)} %copy-done.109, bf16[144,842]{1,0:T(8,128)(2,1)} %copy-done.110, ...), custom_call_target="tpu_custom_call" | custom-call | flops 1000 | bytes 1000 | tf_op jit(solution)/shard_map/join/pallas_call | solution.py:72
  (563 shorter events, 225.6 us)
Async XLA Ops:
  4.5 34.6 %collective-permute-start = (bf16[136,1152]{1,0:T(8,128)(2,1)}, bf16[136,1152]{1,0:T(8,128)(2,1)S(1)}, u32[]{:S(2)}, u32[]{:S(2)}) collective-permute-start(bf16[136,1152]{1,0:T(8,128)(2,1)} %get-tuple-element.424.refs_0_), channel_id=1, source_target_pairs={{0,2},{1,3},{2,0},{3,1},{4,6},{5,7},{6,4},{7,5},{8,10},{9,11},{10,... | collective-permute-start | bytes 940040 | tf_op jit(solution)/shard_map/ppermute | solution.py:630
  7.5 31.7 %collective-permute-start.1 = (bf16[136,1152]{1,0:T(8,128)(2,1)}, bf16[136,1152]{1,0:T(8,128)(2,1)S(1)}, u32[]{:S(2)}, u32[]{:S(2)}) collective-permute-start(bf16[136,1152]{1,0:T(8,128)(2,1)} %get-tuple-element.424.refs_0_), channel_id=1, source_target_pairs={{0,4},{1,5},{2,6},{3,7},{4,0},{5,1},{6,2},{7,3},{8,12},{9,13},{10,... | collective-permute-start | bytes 940040 | tf_op jit(solution)/shard_map/ppermute | solution.py:630
  9.0 30.2 %collective-permute-start.2 = (bf16[136,1152]{1,0:T(8,128)(2,1)}, bf16[136,1152]{1,0:T(8,128)(2,1)}, u32[]{:S(2)}, u32[]{:S(2)}) collective-permute-start(bf16[136,1152]{1,0:T(8,128)(2,1)} %get-tuple-element.424.refs_0_), channel_id=1, source_target_pairs={{0,6},{1,7},{2,4},{3,5},{4,2},{5,3},{6,0},{7,1},{8,14},{9,15},{10,... | collective-permute-start | bytes 940040 | tf_op jit(solution)/shard_map/ppermute | solution.py:630
  15.8 14.9 %collective-permute-start.5 = (bf16[144,840]{1,0:T(8,128)(2,1)}, bf16[144,840]{1,0:T(8,128)(2,1)S(1)}, u32[]{:S(2)}, u32[]{:S(2)}) collective-permute-start(bf16[144,840]{1,0:T(8,128)(2,1)} %get-tuple-element.418), channel_id=1, source_target_pairs={{0,6},{1,7},{2,4},{3,5},{4,2},{5,3},{6,0},{7,1},{8,14},{9,15},{10,... | collective-permute-start | bytes 725768 | tf_op jit(solution)/shard_map/ppermute | solution.py:630
  47.7 21.6 %collective-permute-start.15 = (bf16[560,1120]{1,0:T(8,128)(2,1)S(1)}, bf16[560,1120]{1,0:T(8,128)(2,1)S(1)}, u32[]{:S(2)}, u32[]{:S(2)}) collective-permute-start(bf16[560,1120]{1,0:T(8,128)(2,1)S(1)} %slice_bitcast_fusion.1.refs_13_.refs_17_), channel_id=1, source_target_pairs={{0,1},{1,0},{2,3},{3,2},{4,5},{5,4},{6,7},{7,6},{8,9},{9,8},{10,11... | collective-permute-start | bytes 3763208 | tf_op jit(solution)/shard_map/ppermute | solution.py:630
  49.0 20.2 %collective-permute-start.12 = (bf16[144,1120]{1,0:T(8,128)(2,1)}, bf16[144,1120]{1,0:T(8,128)(2,1)S(1)}, u32[]{:S(2)}, u32[]{:S(2)}) collective-permute-start(bf16[144,1120]{1,0:T(8,128)(2,1)} %get-tuple-element.457), channel_id=1, source_target_pairs={{0,2},{1,3},{2,0},{3,1},{4,6},{5,7},{6,4},{7,5},{8,10},{9,11},{10,... | collective-permute-start | bytes 967688 | tf_op jit(solution)/shard_map/ppermute | solution.py:630
  50.5 18.7 %collective-permute-start.13 = (bf16[144,1120]{1,0:T(8,128)(2,1)}, bf16[144,1120]{1,0:T(8,128)(2,1)S(1)}, u32[]{:S(2)}, u32[]{:S(2)}) collective-permute-start(bf16[144,1120]{1,0:T(8,128)(2,1)} %get-tuple-element.458), channel_id=1, source_target_pairs={{0,4},{1,5},{2,6},{3,7},{4,0},{5,1},{6,2},{7,3},{8,12},{9,13},{10,... | collective-permute-start | bytes 967688 | tf_op jit(solution)/shard_map/ppermute | solution.py:630
  51.0 18.2 %collective-permute-start.14 = (bf16[144,1120]{1,0:T(8,128)(2,1)}, bf16[144,1120]{1,0:T(8,128)(2,1)S(1)}, u32[]{:S(2)}, u32[]{:S(2)}) collective-permute-start(bf16[144,1120]{1,0:T(8,128)(2,1)} %get-tuple-element.459), channel_id=1, source_target_pairs={{0,6},{1,7},{2,4},{3,5},{4,2},{5,3},{6,0},{7,1},{8,14},{9,15},{10,... | collective-permute-start | bytes 967688 | tf_op jit(solution)/shard_map/ppermute | solution.py:630
  69.3 18.1 %collective-permute-start.19 = (bf16[144,1120]{1,0:T(8,128)(2,1)S(1)}, bf16[144,1120]{1,0:T(8,128)(2,1)S(1)}, u32[]{:S(2)}, u32[]{:S(2)}) collective-permute-start(bf16[144,1120]{1,0:T(8,128)(2,1)S(1)} %copy-done.10), channel_id=1, source_target_pairs={{0,1},{1,0},{2,3},{3,2},{4,5},{5,4},{6,7},{7,6},{8,9},{9,8},{10,11... | collective-permute-start | bytes 967688 | tf_op jit(solution)/shard_map/ppermute | solution.py:630
  69.3 18.1 %collective-permute-start.20 = (bf16[144,1120]{1,0:T(8,128)(2,1)S(1)}, bf16[144,1120]{1,0:T(8,128)(2,1)S(1)}, u32[]{:S(2)}, u32[]{:S(2)}) collective-permute-start(bf16[144,1120]{1,0:T(8,128)(2,1)S(1)} %collective-permute-done.12.refs_6_.refs_10_), channel_id=1, source_target_pairs={{0,1},{1,0},{2,3},{3,2},{4,5},{5,4},{6,7},{7,6},{8,9},{9,8},{10,11... | collective-permute-start | bytes 967688 | tf_op jit(solution)/shard_map/ppermute | solution.py:630
  71.3 16.0 %collective-permute-start.17 = (bf16[136,1120]{1,0:T(8,128)(2,1)}, bf16[136,1120]{1,0:T(8,128)(2,1)S(1)}, u32[]{:S(2)}, u32[]{:S(2)}) collective-permute-start(bf16[136,1120]{1,0:T(8,128)(2,1)} %get-tuple-element.463), channel_id=1, source_target_pairs={{0,4},{1,5},{2,6},{3,7},{4,0},{5,1},{6,2},{7,3},{8,12},{9,13},{10,... | collective-permute-start | bytes 913928 | tf_op jit(solution)/shard_map/ppermute | solution.py:630
  71.8 15.5 %collective-permute-start.18 = (bf16[136,1120]{1,0:T(8,128)(2,1)}, bf16[136,1120]{1,0:T(8,128)(2,1)S(1)}, u32[]{:S(2)}, u32[]{:S(2)}) collective-permute-start(bf16[136,1120]{1,0:T(8,128)(2,1)} %get-tuple-element.464), channel_id=1, source_target_pairs={{0,6},{1,7},{2,4},{3,5},{4,2},{5,3},{6,0},{7,1},{8,14},{9,15},{10,... | collective-permute-start | bytes 913928 | tf_op jit(solution)/shard_map/ppermute | solution.py:630
  91.5 16.5 %collective-permute-start.22 = (bf16[136,1152]{1,0:T(8,128)(2,1)}, bf16[136,1152]{1,0:T(8,128)(2,1)}, u32[]{:S(2)}, u32[]{:S(2)}) collective-permute-start(bf16[136,1152]{1,0:T(8,128)(2,1)} %get-tuple-element.475.refs_0_), channel_id=1, source_target_pairs={{0,4},{1,5},{2,6},{3,7},{4,0},{5,1},{6,2},{7,3},{8,12},{9,13},{10,... | collective-permute-start | bytes 940040 | tf_op jit(solution)/shard_map/ppermute | solution.py:630
  92.6 15.4 %collective-permute-start.23 = (bf16[136,1152]{1,0:T(8,128)(2,1)}, bf16[136,1152]{1,0:T(8,128)(2,1)}, u32[]{:S(2)}, u32[]{:S(2)}) collective-permute-start(bf16[136,1152]{1,0:T(8,128)(2,1)} %get-tuple-element.475.refs_0_), channel_id=1, source_target_pairs={{0,6},{1,7},{2,4},{3,5},{4,2},{5,3},{6,0},{7,1},{8,14},{9,15},{10,... | collective-permute-start | bytes 940040 | tf_op jit(solution)/shard_map/ppermute | solution.py:630
  161.9 18.7 %collective-permute-start.43 = (bf16[560,1120]{1,0:T(8,128)(2,1)S(1)}, bf16[560,1120]{1,0:T(8,128)(2,1)S(1)}, u32[]{:S(2)}, u32[]{:S(2)}) collective-permute-start(bf16[560,1120]{1,0:T(8,128)(2,1)S(1)} %slice_bitcast_fusion.refs_13_.refs_17_), channel_id=1, source_target_pairs={{0,1},{1,0},{2,3},{3,2},{4,5},{5,4},{6,7},{7,6},{8,9},{9,8},{10,11... | collective-permute-start | bytes 3763208 | tf_op jit(solution)/shard_map/ppermute | solution.py:630
  163.2 17.4 %collective-permute-start.41 = (bf16[144,1120]{1,0:T(8,128)(2,1)}, bf16[144,1120]{1,0:T(8,128)(2,1)S(1)}, u32[]{:S(2)}, u32[]{:S(2)}) collective-permute-start(bf16[144,1120]{1,0:T(8,128)(2,1)} %get-tuple-element.540), channel_id=1, source_target_pairs={{0,4},{1,5},{2,6},{3,7},{4,0},{5,1},{6,2},{7,3},{8,12},{9,13},{10,... | collective-permute-start | bytes 967688 | tf_op jit(solution)/shard_map/ppermute | solution.py:630
  164.9 15.7 %collective-permute-start.42 = (bf16[144,1120]{1,0:T(8,128)(2,1)S(1)}, bf16[144,1120]{1,0:T(8,128)(2,1)S(1)}, u32[]{:S(2)}, u32[]{:S(2)}) collective-permute-start(bf16[144,1120]{1,0:T(8,128)(2,1)S(1)} %copy-done.124), channel_id=1, source_target_pairs={{0,6},{1,7},{2,4},{3,5},{4,2},{5,3},{6,0},{7,1},{8,14},{9,15},{10,... | collective-permute-start | bytes 967688 | tf_op jit(solution)/shard_map/ppermute | solution.py:630
  180.6 18.4 %collective-permute-start.47 = (bf16[144,1120]{1,0:T(8,128)(2,1)S(1)}, bf16[144,1120]{1,0:T(8,128)(2,1)S(1)}, u32[]{:S(2)}, u32[]{:S(2)}) collective-permute-start(bf16[144,1120]{1,0:T(8,128)(2,1)S(1)} %copy-done.16), channel_id=1, source_target_pairs={{0,1},{1,0},{2,3},{3,2},{4,5},{5,4},{6,7},{7,6},{8,9},{9,8},{10,11... | collective-permute-start | bytes 967688 | tf_op jit(solution)/shard_map/ppermute | solution.py:630
  180.7 18.3 %collective-permute-start.48 = (bf16[144,1120]{1,0:T(8,128)(2,1)S(1)}, bf16[144,1120]{1,0:T(8,128)(2,1)S(1)}, u32[]{:S(2)}, u32[]{:S(2)}) collective-permute-start(bf16[144,1120]{1,0:T(8,128)(2,1)S(1)} %collective-permute-done.40.refs_6_.refs_10_), channel_id=1, source_target_pairs={{0,1},{1,0},{2,3},{3,2},{4,5},{5,4},{6,7},{7,6},{8,9},{9,8},{10,11... | collective-permute-start | bytes 967688 | tf_op jit(solution)/shard_map/ppermute | solution.py:630
  182.9 16.0 %collective-permute-start.45 = (bf16[136,1120]{1,0:T(8,128)(2,1)}, bf16[136,1120]{1,0:T(8,128)(2,1)S(1)}, u32[]{:S(2)}, u32[]{:S(2)}) collective-permute-start(bf16[136,1120]{1,0:T(8,128)(2,1)} %get-tuple-element.545), channel_id=1, source_target_pairs={{0,4},{1,5},{2,6},{3,7},{4,0},{5,1},{6,2},{7,3},{8,12},{9,13},{10,... | collective-permute-start | bytes 913928 | tf_op jit(solution)/shard_map/ppermute | solution.py:630
  183.2 15.8 %collective-permute-start.46 = (bf16[136,1120]{1,0:T(8,128)(2,1)}, bf16[136,1120]{1,0:T(8,128)(2,1)S(1)}, u32[]{:S(2)}, u32[]{:S(2)}) collective-permute-start(bf16[136,1120]{1,0:T(8,128)(2,1)} %get-tuple-element.546), channel_id=1, source_target_pairs={{0,6},{1,7},{2,4},{3,5},{4,2},{5,3},{6,0},{7,1},{8,14},{9,15},{10,... | collective-permute-start | bytes 913928 | tf_op jit(solution)/shard_map/ppermute | solution.py:630
  191.7 16.6 %collective-permute-start.52 = (bf16[144,1120]{1,0:T(8,128)(2,1)S(1)}, bf16[144,1120]{1,0:T(8,128)(2,1)S(1)}, u32[]{:S(2)}, u32[]{:S(2)}) collective-permute-start(bf16[144,1120]{1,0:T(8,128)(2,1)S(1)} %collective-permute-done.41.refs_8_.refs_12_), channel_id=1, source_target_pairs={{0,1},{1,0},{2,3},{3,2},{4,5},{5,4},{6,7},{7,6},{8,9},{9,8},{10,11... | collective-permute-start | bytes 967688 | tf_op jit(solution)/shard_map/ppermute | solution.py:630
  202.9 16.4 %collective-permute-start.50 = (bf16[136,1152]{1,0:T(8,128)(2,1)}, bf16[136,1152]{1,0:T(8,128)(2,1)S(1)}, u32[]{:S(2)}, u32[]{:S(2)}) collective-permute-start(bf16[136,1152]{1,0:T(8,128)(2,1)} %get-tuple-element.560.refs_0_), channel_id=1, source_target_pairs={{0,4},{1,5},{2,6},{3,7},{4,0},{5,1},{6,2},{7,3},{8,12},{9,13},{10,... | collective-permute-start | bytes 940040 | tf_op jit(solution)/shard_map/ppermute | solution.py:630
  204.4 14.8 %collective-permute-start.51 = (bf16[136,1152]{1,0:T(8,128)(2,1)}, bf16[136,1152]{1,0:T(8,128)(2,1)S(1)}, u32[]{:S(2)}, u32[]{:S(2)}) collective-permute-start(bf16[136,1152]{1,0:T(8,128)(2,1)} %get-tuple-element.560.refs_0_), channel_id=1, source_target_pairs={{0,6},{1,7},{2,4},{3,5},{4,2},{5,3},{6,0},{7,1},{8,14},{9,15},{10,... | collective-permute-start | bytes 940040 | tf_op jit(solution)/shard_map/ppermute | solution.py:630
  221.1 15.1 %collective-permute-start.55 = (bf16[136,1120]{1,0:T(8,128)(2,1)}, bf16[136,1120]{1,0:T(8,128)(2,1)S(1)}, u32[]{:S(2)}, u32[]{:S(2)}) collective-permute-start(bf16[136,1120]{1,0:T(8,128)(2,1)} %get-tuple-element.580.refs_4_), channel_id=1, source_target_pairs={{0,4},{1,5},{2,6},{3,7},{4,0},{5,1},{6,2},{7,3},{8,12},{9,13},{10,... | collective-permute-start | bytes 913928 | tf_op jit(solution)/shard_map/ppermute | solution.py:630
  221.4 14.8 %collective-permute-start.56 = (bf16[136,1120]{1,0:T(8,128)(2,1)}, bf16[136,1120]{1,0:T(8,128)(2,1)S(1)}, u32[]{:S(2)}, u32[]{:S(2)}) collective-permute-start(bf16[136,1120]{1,0:T(8,128)(2,1)} %get-tuple-element.580.refs_4_), channel_id=1, source_target_pairs={{0,6},{1,7},{2,4},{3,5},{4,2},{5,3},{6,0},{7,1},{8,14},{9,15},{10,... | collective-permute-start | bytes 913928 | tf_op jit(solution)/shard_map/ppermute | solution.py:630
  270.3 36.1 %collective-permute-start.65 = (bf16[4,144,1120]{2,1,0:T(8,128)(2,1)S(1)}, bf16[4,144,1120]{2,1,0:T(8,128)(2,1)}, u32[]{:S(2)}, u32[]{:S(2)}) collective-permute-start(bf16[4,144,1120]{2,1,0:T(8,128)(2,1)S(1)} %add_convert_fusion.14), channel_id=1, source_target_pairs={{0,8},{24,16},{1,9},{25,17},{2,10},{26,18},{3,11},{27,19},{4,12},{... | collective-permute-start | bytes 3870728 | tf_op jit(solution)/shard_map/ppermute | solution.py:674
  276.6 15.6 %collective-permute-start.63 = (bf16[136,1120]{1,0:T(8,128)(2,1)S(1)}, bf16[136,1120]{1,0:T(8,128)(2,1)S(1)}, u32[]{:S(2)}, u32[]{:S(2)}) collective-permute-start(bf16[136,1120]{1,0:T(8,128)(2,1)S(1)} %copy-done.69), channel_id=1, source_target_pairs={{0,4},{1,5},{2,6},{3,7},{4,0},{5,1},{6,2},{7,3},{8,12},{9,13},{10,... | collective-permute-start | bytes 913928 | tf_op jit(solution)/shard_map/ppermute | solution.py:630
  276.9 16.1 %collective-permute-start.64 = (bf16[136,1120]{1,0:T(8,128)(2,1)S(1)}, bf16[136,1120]{1,0:T(8,128)(2,1)}, u32[]{:S(2)}, u32[]{:S(2)}) collective-permute-start(bf16[136,1120]{1,0:T(8,128)(2,1)S(1)} %copy-done.69), channel_id=1, source_target_pairs={{0,6},{1,7},{2,4},{3,5},{4,2},{5,3},{6,0},{7,1},{8,14},{9,15},{10,... | collective-permute-start | bytes 913928 | tf_op jit(solution)/shard_map/ppermute | solution.py:630
  278.8 52.8 %collective-permute-start.71 = (bf16[4,144,1122]{2,1,0:T(8,128)(2,1)S(1)}, bf16[4,144,1122]{2,1,0:T(8,128)(2,1)S(1)}, u32[]{:S(2)}, u32[]{:S(2)}) collective-permute-start(bf16[4,144,1122]{2,1,0:T(8,128)(2,1)S(1)} %add_convert_fusion.12), channel_id=1, source_target_pairs={{0,8},{24,16},{1,9},{25,17},{2,10},{26,18},{3,11},{27,19},{4,12},{... | collective-permute-start | bytes 3877640 | tf_op jit(solution)/shard_map/ppermute | solution.py:674
  308.2 27.4 %collective-permute-start.70 = (bf16[4,144,1120]{2,1,0:T(8,128)(2,1)S(1)}, bf16[4,144,1120]{2,1,0:T(8,128)(2,1)S(1)}, u32[]{:S(2)}, u32[]{:S(2)}) collective-permute-start(bf16[4,144,1120]{2,1,0:T(8,128)(2,1)S(1)} %add_convert_fusion.13), channel_id=1, source_target_pairs={{8,16},{16,8},{9,17},{17,9},{10,18},{18,10},{11,19},{19,11},{12,20... | collective-permute-start | bytes 3870728 | tf_op jit(solution)/shard_map/ppermute | solution.py:674
  319.5 16.1 %collective-permute-start.68 = (bf16[136,1152]{1,0:T(8,128)(2,1)}, bf16[136,1152]{1,0:T(8,128)(2,1)S(1)}, u32[]{:S(2)}, u32[]{:S(2)}) collective-permute-start(bf16[136,1152]{1,0:T(8,128)(2,1)} %get-tuple-element.623), channel_id=1, source_target_pairs={{0,4},{1,5},{2,6},{3,7},{4,0},{5,1},{6,2},{7,3},{8,12},{9,13},{10,... | collective-permute-start | bytes 940040 | tf_op jit(solution)/shard_map/ppermute | solution.py:630
  320.2 15.3 %collective-permute-start.69 = (bf16[136,1152]{1,0:T(8,128)(2,1)}, bf16[136,1152]{1,0:T(8,128)(2,1)}, u32[]{:S(2)}, u32[]{:S(2)}) collective-permute-start(bf16[136,1152]{1,0:T(8,128)(2,1)} %get-tuple-element.624), channel_id=1, source_target_pairs={{0,6},{1,7},{2,4},{3,5},{4,2},{5,3},{6,0},{7,1},{8,14},{9,15},{10,... | collective-permute-start | bytes 940040 | tf_op jit(solution)/shard_map/ppermute | solution.py:630
  337.9 47.8 %collective-permute-start.77 = (bf16[4,144,1122]{2,1,0:T(8,128)(2,1)S(1)}, bf16[4,144,1122]{2,1,0:T(8,128)(2,1)}, u32[]{:S(2)}, u32[]{:S(2)}) collective-permute-start(bf16[4,144,1122]{2,1,0:T(8,128)(2,1)S(1)} %add_convert_fusion.9), channel_id=1, source_target_pairs={{8,16},{16,8},{9,17},{17,9},{10,18},{18,10},{11,19},{19,11},{12,20... | collective-permute-start | bytes 3877640 | tf_op jit(solution)/shard_map/ppermute | solution.py:674
  341.3 44.3 %collective-permute-start.76 = (bf16[4,144,1120]{2,1,0:T(8,128)(2,1)S(1)}, bf16[4,144,1120]{2,1,0:T(8,128)(2,1)}, u32[]{:S(2)}, u32[]{:S(2)}) collective-permute-start(bf16[4,144,1120]{2,1,0:T(8,128)(2,1)S(1)} %add_convert_fusion.10), channel_id=1, source_target_pairs={{8,0},{16,24},{9,1},{17,25},{10,2},{18,26},{11,3},{19,27},{12,4},{... | collective-permute-start | bytes 3870728 | tf_op jit(solution)/shard_map/ppermute | solution.py:674
  349.4 53.3 %collective-permute-start.81 = (bf16[4,144,1122]{2,1,0:T(8,128)(2,1)S(1)}, bf16[4,144,1122]{2,1,0:T(8,128)(2,1)}, u32[]{:S(2)}, u32[]{:S(2)}) collective-permute-start(bf16[4,144,1122]{2,1,0:T(8,128)(2,1)S(1)} %add_convert_fusion.11), channel_id=1, source_target_pairs={{0,8},{24,16},{1,9},{25,17},{2,10},{26,18},{3,11},{27,19},{4,12},{... | collective-permute-start | bytes 3877640 | tf_op jit(solution)/shard_map/ppermute | solution.py:674
  359.1 15.3 %collective-permute-start.74 = (bf16[136,1120]{1,0:T(8,128)(2,1)S(1)}, bf16[136,1120]{1,0:T(8,128)(2,1)S(1)}, u32[]{:S(2)}, u32[]{:S(2)}) collective-permute-start(bf16[136,1120]{1,0:T(8,128)(2,1)S(1)} %copy-done.55), channel_id=1, source_target_pairs={{0,4},{1,5},{2,6},{3,7},{4,0},{5,1},{6,2},{7,3},{8,12},{9,13},{10,... | collective-permute-start | bytes 913928 | tf_op jit(solution)/shard_map/ppermute | solution.py:630
  359.5 15.6 %collective-permute-start.75 = (bf16[136,1120]{1,0:T(8,128)(2,1)S(1)}, bf16[136,1120]{1,0:T(8,128)(2,1)}, u32[]{:S(2)}, u32[]{:S(2)}) collective-permute-start(bf16[136,1120]{1,0:T(8,128)(2,1)S(1)} %copy-done.55), channel_id=1, source_target_pairs={{0,6},{1,7},{2,4},{3,5},{4,2},{5,3},{6,0},{7,1},{8,14},{9,15},{10,... | collective-permute-start | bytes 913928 | tf_op jit(solution)/shard_map/ppermute | solution.py:630
  387.3 15.2 %collective-permute-start.78 = (bf16[136,1152]{1,0:T(8,128)(2,1)}, bf16[136,1152]{1,0:T(8,128)(2,1)S(1)}, u32[]{:S(2)}, u32[]{:S(2)}) collective-permute-start(bf16[136,1152]{1,0:T(8,128)(2,1)} %get-tuple-element.669), channel_id=1, source_target_pairs={{0,2},{1,3},{2,0},{3,1},{4,6},{5,7},{6,4},{7,5},{8,10},{9,11},{10,... | collective-permute-start | bytes 940040 | tf_op jit(solution)/shard_map/ppermute | solution.py:630
  387.7 15.0 %collective-permute-start.79 = (bf16[136,1152]{1,0:T(8,128)(2,1)}, bf16[136,1152]{1,0:T(8,128)(2,1)S(1)}, u32[]{:S(2)}, u32[]{:S(2)}) collective-permute-start(bf16[136,1152]{1,0:T(8,128)(2,1)} %get-tuple-element.670), channel_id=1, source_target_pairs={{0,4},{1,5},{2,6},{3,7},{4,0},{5,1},{6,2},{7,3},{8,12},{9,13},{10,... | collective-permute-start | bytes 940040 | tf_op jit(solution)/shard_map/ppermute | solution.py:630
  390.9 31.2 %collective-permute-start.84 = (bf16[4,144,1122]{2,1,0:T(8,128)(2,1)S(1)}, bf16[4,144,1122]{2,1,0:T(8,128)(2,1)}, u32[]{:S(2)}, u32[]{:S(2)}) collective-permute-start(bf16[4,144,1122]{2,1,0:T(8,128)(2,1)S(1)} %add_convert_fusion.8), channel_id=1, source_target_pairs={{8,0},{16,24},{9,1},{17,25},{10,2},{18,26},{11,3},{19,27},{12,4},{... | collective-permute-start | bytes 3877640 | tf_op jit(solution)/shard_map/ppermute | solution.py:674
  403.5 18.6 %collective-permute-start.82 = (bf16[4,144,1122]{2,1,0:T(8,128)(2,1)}, bf16[4,144,1122]{2,1,0:T(8,128)(2,1)}, u32[]{:S(2)}, u32[]{:S(2)}) collective-permute-start(bf16[4,144,1122]{2,1,0:T(8,128)(2,1)} %get-tuple-element.688), channel_id=1, source_target_pairs={{0,1},{1,0},{2,3},{3,2},{4,5},{5,4},{6,7},{7,6},{8,9},{9,8},{10,11... | collective-permute-start | bytes 3877640 | tf_op jit(solution)/shard_map/ppermute | solution.py:630
  403.5 18.6 %collective-permute-start.83 = (bf16[4,144,1120]{2,1,0:T(8,128)(2,1)}, bf16[4,144,1120]{2,1,0:T(8,128)(2,1)}, u32[]{:S(2)}, u32[]{:S(2)}) collective-permute-start(bf16[4,144,1120]{2,1,0:T(8,128)(2,1)} %get-tuple-element.689), channel_id=1, source_target_pairs={{0,1},{1,0},{2,3},{3,2},{4,5},{5,4},{6,7},{7,6},{8,9},{9,8},{10,11... | collective-permute-start | bytes 3870728 | tf_op jit(solution)/shard_map/ppermute | solution.py:630
  406.4 48.6 %collective-permute-start.91 = (bf16[4,144,1122]{2,1,0:T(8,128)(2,1)S(1)}, bf16[4,144,1122]{2,1,0:T(8,128)(2,1)}, u32[]{:S(2)}, u32[]{:S(2)}) collective-permute-start(bf16[4,144,1122]{2,1,0:T(8,128)(2,1)S(1)} %add_convert_fusion.7), channel_id=1, source_target_pairs={{8,16},{16,8},{9,17},{17,9},{10,18},{18,10},{11,19},{19,11},{12,20... | collective-permute-start | bytes 3877640 | tf_op jit(solution)/shard_map/ppermute | solution.py:674
  427.6 29.9 %collective-permute-start.92 = (bf16[4,144,1120]{2,1,0:T(8,128)(2,1)S(1)}, bf16[4,144,1120]{2,1,0:T(8,128)(2,1)}, u32[]{:S(2)}, u32[]{:S(2)}) collective-permute-start(bf16[4,144,1120]{2,1,0:T(8,128)(2,1)S(1)} %add_convert_fusion.6), channel_id=1, source_target_pairs={{0,8},{24,16},{1,9},{25,17},{2,10},{26,18},{3,11},{27,19},{4,12},{... | collective-permute-start | bytes 3870728 | tf_op jit(solution)/shard_map/ppermute | solution.py:674
  436.0 21.6 %collective-permute-start.88 = (bf16[144,1122]{1,0:T(8,128)(2,1)}, bf16[144,1122]{1,0:T(8,128)(2,1)}, u32[]{:S(2)}, u32[]{:S(2)}) collective-permute-start(bf16[144,1122]{1,0:T(8,128)(2,1)} %get-tuple-element.702), channel_id=1, source_target_pairs={{0,2},{1,3},{2,0},{3,1},{4,6},{5,7},{6,4},{7,5},{8,10},{9,11},{10,... | collective-permute-start | bytes 969416 | tf_op jit(solution)/shard_map/ppermute | solution.py:630
  438.3 19.2 %collective-permute-start.89 = (bf16[144,1122]{1,0:T(8,128)(2,1)}, bf16[144,1122]{1,0:T(8,128)(2,1)}, u32[]{:S(2)}, u32[]{:S(2)}) collective-permute-start(bf16[144,1122]{1,0:T(8,128)(2,1)} %get-tuple-element.703), channel_id=1, source_target_pairs={{0,4},{1,5},{2,6},{3,7},{4,0},{5,1},{6,2},{7,3},{8,12},{9,13},{10,... | collective-permute-start | bytes 969416 | tf_op jit(solution)/shard_map/ppermute | solution.py:630
  438.4 19.1 %collective-permute-start.90 = (bf16[144,1122]{1,0:T(8,128)(2,1)}, bf16[144,1122]{1,0:T(8,128)(2,1)}, u32[]{:S(2)}, u32[]{:S(2)}) collective-permute-start(bf16[144,1122]{1,0:T(8,128)(2,1)} %get-tuple-element.704), channel_id=1, source_target_pairs={{0,6},{1,7},{2,4},{3,5},{4,2},{5,3},{6,0},{7,1},{8,14},{9,15},{10,... | collective-permute-start | bytes 969416 | tf_op jit(solution)/shard_map/ppermute | solution.py:630
  455.0 41.7 %collective-permute-start.98 = (bf16[4,144,1122]{2,1,0:T(8,128)(2,1)S(1)}, bf16[4,144,1122]{2,1,0:T(8,128)(2,1)}, u32[]{:S(2)}, u32[]{:S(2)}) collective-permute-start(bf16[4,144,1122]{2,1,0:T(8,128)(2,1)S(1)} %add_convert_fusion.3), channel_id=1, source_target_pairs={{0,8},{24,16},{1,9},{25,17},{2,10},{26,18},{3,11},{27,19},{4,12},{... | collective-permute-start | bytes 3877640 | tf_op jit(solution)/shard_map/ppermute | solution.py:674
  460.3 36.4 %collective-permute-start.97 = (bf16[4,144,1120]{2,1,0:T(8,128)(2,1)}, bf16[4,144,1120]{2,1,0:T(8,128)(2,1)}, u32[]{:S(2)}, u32[]{:S(2)}) collective-permute-start(bf16[4,144,1120]{2,1,0:T(8,128)(2,1)} %add_convert_fusion.4), channel_id=1, source_target_pairs={{8,16},{16,8},{9,17},{17,9},{10,18},{18,10},{11,19},{19,11},{12,20... | collective-permute-start | bytes 3870728 | tf_op jit(solution)/shard_map/ppermute | solution.py:674
  465.4 34.5 %collective-permute-start.96 = (bf16[4,144,1122]{2,1,0:T(8,128)(2,1)}, bf16[4,144,1122]{2,1,0:T(8,128)(2,1)}, u32[]{:S(2)}, u32[]{:S(2)}) collective-permute-start(bf16[4,144,1122]{2,1,0:T(8,128)(2,1)} %add_convert_fusion.5), channel_id=1, source_target_pairs={{8,0},{16,24},{9,1},{17,25},{10,2},{18,26},{11,3},{19,27},{12,4},{... | collective-permute-start | bytes 3877640 | tf_op jit(solution)/shard_map/ppermute | solution.py:674
  490.5 39.7 %collective-permute-start.104 = (bf16[4,144,842]{2,1,0:T(8,128)(2,1)S(1)}, bf16[4,144,842]{2,1,0:T(8,128)(2,1)S(1)}, u32[]{:S(2)}, u32[]{:S(2)}) collective-permute-start(bf16[4,144,842]{2,1,0:T(8,128)(2,1)S(1)} %add_convert_fusion.17), channel_id=1, source_target_pairs={{0,8},{24,16},{1,9},{25,17},{2,10},{26,18},{3,11},{27,19},{4,12},{... | collective-permute-start | bytes 2909960 | tf_op jit(solution)/shard_map/ppermute | solution.py:674
  502.0 32.9 %collective-permute-start.102 = (bf16[4,144,1120]{2,1,0:T(8,128)(2,1)S(1)}, bf16[4,144,1120]{2,1,0:T(8,128)(2,1)S(1)}, u32[]{:S(2)}, u32[]{:S(2)}) collective-permute-start(bf16[4,144,1120]{2,1,0:T(8,128)(2,1)S(1)} %add_convert_fusion.1), channel_id=1, source_target_pairs={{8,0},{16,24},{9,1},{17,25},{10,2},{18,26},{11,3},{19,27},{12,4},{... | collective-permute-start | bytes 3870728 | tf_op jit(solution)/shard_map/ppermute | solution.py:674
  505.1 29.9 %collective-permute-start.103 = (bf16[4,144,1122]{2,1,0:T(8,128)(2,1)S(1)}, bf16[4,144,1122]{2,1,0:T(8,128)(2,1)S(1)}, u32[]{:S(2)}, u32[]{:S(2)}) collective-permute-start(bf16[4,144,1122]{2,1,0:T(8,128)(2,1)S(1)} %add_convert_fusion.2), channel_id=1, source_target_pairs={{8,16},{16,8},{9,17},{17,9},{10,18},{18,10},{11,19},{19,11},{12,20... | collective-permute-start | bytes 3877640 | tf_op jit(solution)/shard_map/ppermute | solution.py:674
  505.9 16.0 %collective-permute-start.100 = (bf16[136,1152]{1,0:T(8,128)(2,1)S(1)}, bf16[136,1152]{1,0:T(8,128)(2,1)S(1)}, u32[]{:S(2)}, u32[]{:S(2)}) collective-permute-start(bf16[136,1152]{1,0:T(8,128)(2,1)S(1)} %copy-done.127), channel_id=1, source_target_pairs={{0,4},{1,5},{2,6},{3,7},{4,0},{5,1},{6,2},{7,3},{8,12},{9,13},{10,... | collective-permute-start | bytes 940040 | tf_op jit(solution)/shard_map/ppermute | solution.py:630
  509.8 15.5 %collective-permute-start.101 = (bf16[136,1152]{1,0:T(8,128)(2,1)S(1)}, bf16[136,1152]{1,0:T(8,128)(2,1)S(1)}, u32[]{:S(2)}, u32[]{:S(2)}) collective-permute-start(bf16[136,1152]{1,0:T(8,128)(2,1)S(1)} %copy-done.126), channel_id=1, source_target_pairs={{0,6},{1,7},{2,4},{3,5},{4,2},{5,3},{6,0},{7,1},{8,14},{9,15},{10,... | collective-permute-start | bytes 940040 | tf_op jit(solution)/shard_map/ppermute | solution.py:630
  536.0 34.1 %collective-permute-start.108 = (bf16[4,144,1122]{2,1,0:T(8,128)(2,1)S(1)}, bf16[4,144,1122]{2,1,0:T(8,128)(2,1)}, u32[]{:S(2)}, u32[]{:S(2)}) collective-permute-start(bf16[4,144,1122]{2,1,0:T(8,128)(2,1)S(1)} %add_convert_fusion), channel_id=1, source_target_pairs={{8,0},{16,24},{9,1},{17,25},{10,2},{18,26},{11,3},{19,27},{12,4},{... | collective-permute-start | bytes 3877640 | tf_op jit(solution)/shard_map/ppermute | solution.py:674
  537.6 19.8 %collective-permute-start.109 = (bf16[4,144,842]{2,1,0:T(8,128)(2,1)S(1)}, bf16[4,144,842]{2,1,0:T(8,128)(2,1)S(1)}, u32[]{:S(2)}, u32[]{:S(2)}) collective-permute-start(bf16[4,144,842]{2,1,0:T(8,128)(2,1)S(1)} %add_convert_fusion.16), channel_id=1, source_target_pairs={{8,16},{16,8},{9,17},{17,9},{10,18},{18,10},{11,19},{19,11},{12,20... | collective-permute-start | bytes 2909960 | tf_op jit(solution)/shard_map/ppermute | solution.py:674
  571.6 39.2 %collective-permute-start.117 = (bf16[4,144,842]{2,1,0:T(8,128)(2,1)S(1)}, bf16[4,144,842]{2,1,0:T(8,128)(2,1)S(1)}, u32[]{:S(2)}, u32[]{:S(2)}) collective-permute-start(bf16[4,144,842]{2,1,0:T(8,128)(2,1)S(1)} %add_convert_fusion.15), channel_id=1, source_target_pairs={{8,0},{16,24},{9,1},{17,25},{10,2},{18,26},{11,3},{19,27},{12,4},{... | collective-permute-start | bytes 2909960 | tf_op jit(solution)/shard_map/ppermute | solution.py:674
  573.1 30.4 %collective-permute-start.116 = (bf16[144,1120]{1,0:T(8,128)(2,1)}, bf16[144,1120]{1,0:T(8,128)(2,1)}, u32[]{:S(2)}, u32[]{:S(2)}) collective-permute-start(bf16[144,1120]{1,0:T(8,128)(2,1)} %add_convert_fusion.20), channel_id=1, source_target_pairs={{0,8},{8,0},{16,24},{24,16},{1,9},{9,1},{17,25},{25,17},{2,10},{10... | collective-permute-start | bytes 967688 | tf_op jit(solution)/shard_map/ppermute | solution.py:1115
  582.0 28.7 %collective-permute-start.113 = (bf16[144,1122]{1,0:T(8,128)(2,1)}, bf16[144,1122]{1,0:T(8,128)(2,1)S(1)}, u32[]{:S(2)}, u32[]{:S(2)}) collective-permute-start(bf16[144,1122]{1,0:T(8,128)(2,1)} %get-tuple-element.764), channel_id=1, source_target_pairs={{0,2},{1,3},{2,0},{3,1},{4,6},{5,7},{6,4},{7,5},{8,10},{9,11},{10,... | collective-permute-start | bytes 969416 | tf_op jit(solution)/shard_map/ppermute | solution.py:630
  588.4 22.3 %collective-permute-start.114 = (bf16[144,1122]{1,0:T(8,128)(2,1)}, bf16[144,1122]{1,0:T(8,128)(2,1)S(1)}, u32[]{:S(2)}, u32[]{:S(2)}) collective-permute-start(bf16[144,1122]{1,0:T(8,128)(2,1)} %get-tuple-element.765), channel_id=1, source_target_pairs={{0,4},{1,5},{2,6},{3,7},{4,0},{5,1},{6,2},{7,3},{8,12},{9,13},{10,... | collective-permute-start | bytes 969416 | tf_op jit(solution)/shard_map/ppermute | solution.py:630
  589.5 21.2 %collective-permute-start.115 = (bf16[144,1122]{1,0:T(8,128)(2,1)}, bf16[144,1122]{1,0:T(8,128)(2,1)S(1)}, u32[]{:S(2)}, u32[]{:S(2)}) collective-permute-start(bf16[144,1122]{1,0:T(8,128)(2,1)} %get-tuple-element.766), channel_id=1, source_target_pairs={{0,6},{1,7},{2,4},{3,5},{4,2},{5,3},{6,0},{7,1},{8,14},{9,15},{10,... | collective-permute-start | bytes 969416 | tf_op jit(solution)/shard_map/ppermute | solution.py:630
  616.5 19.5 %collective-permute-start.121 = (bf16[144,1120]{1,0:T(8,128)(2,1)S(1)}, bf16[144,1120]{1,0:T(8,128)(2,1)S(1)}, u32[]{:S(2)}, u32[]{:S(2)}) collective-permute-start(bf16[144,1120]{1,0:T(8,128)(2,1)S(1)} %add_convert_fusion.19), channel_id=1, source_target_pairs={{0,16},{8,24},{16,0},{24,8},{1,17},{9,25},{17,1},{25,9},{2,18},{10... | collective-permute-start | bytes 967688 | tf_op jit(solution)/shard_map/ppermute | solution.py:1115
  (188 other events, 1937.2 us)

commit v4 on v3

--- a/solution.py
+++ b/solution.py
@@ -1021,8 +1021,7 @@
             (outs,) = beside("attend 1", outs)
         else:
             up_width, qkv_width = chip_hidden + 2, 3 * chip_cols + 2
-            up_near = to_chips(after_all(messages_of(up_sums[1], up_width), *pieces))
-            outs, up_near = beside("attend 0", outs, up_near)
+            (outs,) = beside("attend 0", outs)
         query_grad, pair_mine, pair_other, long_rows[LAYERS + level] = outs
         outs = call(
             here(project_back_kernel, plan),
@@ -1102,41 +1101,36 @@
         ends_like,
     )
     out_sum = (after(out_mine, parts[0]).astype(F32) + out_got.astype(F32)).astype(BF)
-    parts, ends = beside("end 3", scatter(after_all(last_blocks, *parts)), ends)
+    up_near = to_chips(after_all(messages_of(up_sums[1], up_width), *parts))
+    parts, ends, up_near = beside(
+        "end 3", scatter(after_all(last_blocks, *parts)), ends, up_near
+    )
     result = call(
         here(finish_kernel, plan, len(parts), LAYERS - 1),
         "finish",
         parts + [last_middle, bias_down],
         ends_like,
     )
+    near = to_chips(after_all(messages_of(qkv_sums[1], qkv_width), *parts))
+    last_up = to_chips(after_all(messages_of(up_sums[0], up_width), *parts))
     def sum_near(value, away):
         if cells != 4:
             return lax.psum(value, "cell") if away == 1 else value
         got = lax.ppermute(value, "cell", [(at, at ^ away) for at in range(cells)])
         return (value.astype(F32) + got.astype(F32)).astype(BF)
 
-    near = to_chips(after_all(messages_of(qkv_sums[1], qkv_width), *parts))
-    last_up = to_chips(after_all(messages_of(up_sums[0], up_width), *parts))
-    (out_sum,) = after_all([out_sum], *parts)
     (g_down,) = call(
         here(join_down_kernel, plan),
         "join_down",
         after_all([item.value for item in down_sums], parts[0]),
         [shape_of(LAYERS, hidden, D, dtype=F32)],
     )
-    near, last_up, result, (out_sum, g_down) = beside(
-        "end 4", near, last_up, result, [sum_near(out_sum, 1), g_down]
-    )
-    last_near = to_chips(messages_of(qkv_sums[0], qkv_width))
-    out_sum = sum_near(out_sum, 2)
+    near, last_up, result, (g_down,) = beside("end 4", near, last_up, result, [g_down])
+    messages = after_all(messages_of(qkv_sums[0], qkv_width))
+    last_near = to_chips(messages)
+    (out_sum,) = after_all([out_sum], *messages)
+    last_up, up_near = (after_all(values, *messages) for values in (last_up, up_near))
     up_parts = [last_up, up_near]
-    riders = [qkv_sums[1].value[at, : plan.cols, qkv_width:] for at in range(chips)]
-    out_sums = [out_sum[:cols], after(jnp.concatenate(riders, 1), last_up[0])]
-    small = out_sum[cols : cols + extra].reshape(-1).astype(F32)
-    size = LAYERS * cols
-    b_down, b_out, b_q, b_v = (small[at * size : (at + 1) * size].reshape(LAYERS, cols) for at in range(4))
-    b_up = small[4 * size : 4 * size + LAYERS * hidden].reshape(LAYERS, hidden)
-
     def join(parts, blocks, width):
         whole, vectors = call(
             here(join_kernel, plan, blocks, width),
@@ -1152,9 +1146,19 @@
         return whole.transpose(1, 0, 2), vectors[:, 0, :cols], vectors[:, 1, :cols]
 
     ups = join(up_parts, 1, chip_hidden)
-    last_near, (g_up, shift_two, gain_two) = together(last_near, ups)
+    last_near, (g_up, shift_two, gain_two), (out_sum,) = together(
+        last_near, ups, [sum_near(out_sum, 1)]
+    )
+    out_sum = sum_near(out_sum, 2)
     qkv_parts = [last_near, near]
     g_qkv, shift_one, gain_one = join(qkv_parts, 3, 3 * chip_cols)
+    riders = [qkv_sums[1].value[at, : plan.cols, qkv_width:] for at in range(chips)]
+    out_sums = [out_sum[:cols], after(jnp.concatenate(riders, 1), last_up[0])]
+    small = out_sum[cols : cols + extra].reshape(-1).astype(F32)
+    size = LAYERS * cols
+    b_down, b_out, b_q, b_v = (small[at * size : (at + 1) * size].reshape(LAYERS, cols) for at in range(4))
+    b_up = small[4 * size : 4 * size + LAYERS * hidden].reshape(LAYERS, hidden)
+
     return (
         result[0].T[None],
         result[1][: plan.pre_rows][None],

time: 650 us -> 643 us (0.989)
    ppermute x2, waiting for transfers between devices: 13.5 us -> 2.89 us  [sum_near(): got = lax.ppermute(value, 'cell', [(at, at ^ away) for at in range(cells)])]
    unnamed x268 -> x270, local copies, waits for them, and re-layouts: 28.6 us -> 27.9 us
  transfers between devices with their start and end apart: 122 -> 122, of which waited for: 44 -> 54; matrix products, arithmetic and copies ran while one was open for 10% -> 10% of each run, Pallas kernels for 26% -> 26%
where the time goes in v4:
time: 643 us; the launch traced here: 632 us
  Pallas kernels  202 us (31%)
  waiting for transfers between devices  202 us (31%)
  starting transfers between devices  136 us (21%)
  local copies, waits for them, and re-layouts  44.7 us (7%)
  other arithmetic  39.8 us (6%)
    pallas_call x33, Pallas kernels, call(): pl.pallas_call(kernel, in_specs=[SCALAR if scalar and at == 0 else WHOLE...  202 us
    ppermute x102, waiting for transfers between devices, swap(): lax.ppermute(value, 'gene', [(at, at ^ bits) for at in range(groups)])  167 us
    ppermute x102, starting transfers between devices, swap(): lax.ppermute(value, 'gene', [(at, at ^ bits) for at in range(groups)])  88.4 us
    ppermute x18, starting transfers between devices, move(): lax.ppermute(self.value, 'cell', {3: inwards, 2: between, 1: outwards}[le...  44.7 us
    ppermute x18, waiting for transfers between devices, move(): lax.ppermute(self.value, 'cell', {3: inwards, 2: between, 1: outwards}[le...  32.5 us
    unnamed x270, local copies, waits for them, and re-layouts  27.9 us
    convert_element_type x12, other arithmetic, land(): self.value = (value.astype(F32) + got.astype(F32)).astype(BF)  19.1 us
  transfers between devices with their start and end apart: 122, of which 54 were waited for; matrix products, arithmetic and copies ran while one was open for 10% of the time, Pallas kernels for 26%

profile of v4, /device:TPU:0, one launch (start us, length us, event | category | flops | bytes accessed | tf_op | source)
XLA Modules:
  0.0 632.1 jit_solution(5868639872194593476)
XLA Ops:
  12.5 3.2 send.4
  22.4 3.2 send.5
  35.5 3.5 collective-permute-done.4.refs_8_.refs_7_.refs_12_
  42.4 5.0 project.2
  52.4 3.3 send.7
  55.7 3.1 send.6
  59.6 9.5 %attend.2 = (bf16[544,640]{1,0:T(8,128)(2,1)}, f32[5,1,544]{2,1,0:T(1,128)}, bf16[136,1120]{1,0:T(8,128)(2,1)}, bf16[136,1120]{1,0:T(8,128)(2,1)}, bf16[136,1120]{1,0:T(8,128)(2,1)}, /*index=5*/bf16[136,1120]{1,0:T(8,128)(2,1)}) custom-call(s32[3]{0:T(128)} %pad_add_fusion.1.me_ref, bf16[544,640]{1,0:T(8,128)(2,1)} %get-tuple-element.452.refs_0_.refs_5_, ...), custom_call_target="tpu_custom_call" | custom-call | flops 1000 | bytes 1000 | tf_op jit(solution)/shard_map/attend/pallas_call | solution.py:72
  73.3 7.0 %collective-permute-done.16.refs_1_ = bf16[136,1120]{1,0:T(8,128)(2,1)S(1)} collective-permute-done((bf16[136,1120]{1,0:T(8,128)(2,1)}, bf16[136,1120]{1,0:T(8,128)(2,1)S(1)}, u32[]{:S(2)}, u32[]{:S(2)}) %collective-permute-start.16) | collective-permute-done | bytes 304672 | tf_op jit(solution)/shard_map/ppermute | solution.py:630
  80.3 7.1 %collective-permute-done.17.refs_2_ = bf16[136,1120]{1,0:T(8,128)(2,1)S(1)} collective-permute-done((bf16[136,1120]{1,0:T(8,128)(2,1)}, bf16[136,1120]{1,0:T(8,128)(2,1)S(1)}, u32[]{:S(2)}, u32[]{:S(2)}) %collective-permute-start.17) | collective-permute-done | bytes 304672 | tf_op jit(solution)/shard_map/ppermute | solution.py:630
  94.4 6.9 %collective-permute-done.21.refs_1_ = bf16[136,1152]{1,0:T(8,128)(2,1)S(1)} collective-permute-done((bf16[136,1152]{1,0:T(8,128)(2,1)}, bf16[136,1152]{1,0:T(8,128)(2,1)S(1)}, u32[]{:S(2)}, u32[]{:S(2)}) %collective-permute-start.21) | collective-permute-done | bytes 313376 | tf_op jit(solution)/shard_map/ppermute | solution.py:630
  101.3 6.6 %collective-permute-done.22.refs_2_ = bf16[136,1152]{1,0:T(8,128)(2,1)} collective-permute-done((bf16[136,1152]{1,0:T(8,128)(2,1)}, bf16[136,1152]{1,0:T(8,128)(2,1)}, u32[]{:S(2)}, u32[]{:S(2)}) %collective-permute-start.22) | collective-permute-done | bytes 313376 | tf_op jit(solution)/shard_map/ppermute | solution.py:630
  113.0 8.0 %lift.2 = (bf16[136,1120]{1,0:T(8,128)(2,1)}, bf16[136,1120]{1,0:T(8,128)(2,1)}, bf16[136,1120]{1,0:T(8,128)(2,1)}, bf16[136,1120]{1,0:T(8,128)(2,1)}) custom-call(s32[3]{0:T(128)} %pad_add_fusion.1.me_ref, bf16[136,1152]{1,0:T(8,128)(2,1)} %get-tuple-element.487.refs_0_, bf16[136,1152]{1,0:T(8,128)(2,1)} %copy-done.21, ...), custom_call_target="tpu_custom_call" | custom-call | flops 1000 | bytes 1000 | tf_op jit(solution)/shard_map/lift/pallas_call | solution.py:72
  128.1 4.9 collective-permute-done.29.refs_1_
  133.0 4.3 collective-permute-done.30.refs_2_
  146.5 4.1 collective-permute-done.34.refs_1_
  150.6 5.3 collective-permute-done.35.refs_2_
  156.7 4.8 project.3
  168.2 9.2 %attend.3 = (bf16[544,640]{1,0:T(8,128)(2,1)}, f32[5,1,544]{2,1,0:T(1,128)}, bf16[136,1120]{1,0:T(8,128)(2,1)}, bf16[136,1120]{1,0:T(8,128)(2,1)}, bf16[136,1120]{1,0:T(8,128)(2,1)}, /*index=5*/bf16[136,1120]{1,0:T(8,128)(2,1)}) custom-call(s32[3]{0:T(128)} %pad_add_fusion.1.me_ref, bf16[544,640]{1,0:T(8,128)(2,1)} %get-tuple-element.539.refs_0_.refs_5_, ...), custom_call_target="tpu_custom_call" | custom-call | flops 1000 | bytes 1000 | tf_op jit(solution)/shard_map/attend/pallas_call | solution.py:72
  177.4 3.4 collective-permute-done.41.refs_8_.refs_12_
  184.9 7.0 %collective-permute-done.44.refs_1_ = bf16[136,1120]{1,0:T(8,128)(2,1)S(1)} collective-permute-done((bf16[136,1120]{1,0:T(8,128)(2,1)}, bf16[136,1120]{1,0:T(8,128)(2,1)S(1)}, u32[]{:S(2)}, u32[]{:S(2)}) %collective-permute-start.44) | collective-permute-done | bytes 304672 | tf_op jit(solution)/shard_map/ppermute | solution.py:630
  191.9 7.2 %collective-permute-done.45.refs_2_ = bf16[136,1120]{1,0:T(8,128)(2,1)S(1)} collective-permute-done((bf16[136,1120]{1,0:T(8,128)(2,1)}, bf16[136,1120]{1,0:T(8,128)(2,1)S(1)}, u32[]{:S(2)}, u32[]{:S(2)}) %collective-permute-start.45) | collective-permute-done | bytes 304672 | tf_op jit(solution)/shard_map/ppermute | solution.py:630
  208.5 4.6 collective-permute-done.49.refs_1_
  213.2 6.3 collective-permute-done.50.refs_2_
  223.1 8.0 %lift.3 = (bf16[136,1120]{1,0:T(8,128)(2,1)}, bf16[136,1120]{1,0:T(8,128)(2,1)}, bf16[136,1120]{1,0:T(8,128)(2,1)}, bf16[136,1120]{1,0:T(8,128)(2,1)}) custom-call(s32[3]{0:T(128)} %pad_add_fusion.1.me_ref, bf16[136,1152]{1,0:T(8,128)(2,1)} %get-tuple-element.572.refs_0_, bf16[136,1152]{1,0:T(8,128)(2,1)} %copy-done.22, bf16[136,1152]{1,0:T(8,128)(2,1)} %copy-done.23, ...), custom_call_target="tpu_custom_call" | custom-call | flops 1000 | bytes 1000 | tf_op jit(solution)/shard_map/lift/pallas_call | solution.py:72
  231.2 5.2 collective-permute-done.55.refs_6_
  237.3 10.5 %lift_back.2 = (bf16[576,1120]{1,0:T(8,128)(2,1)}, bf16[576,1120]{1,0:T(8,128)(2,1)}, f32[1,1120]{1,0:T(1,128)}, f32[1,1120]{1,0:T(1,128)}, bf16[136,1152]{1,0:T...) custom-call(s32[3]{0:T(128)} %pad_add_fusion.1.me_ref, ...), custom_call_target="tpu_custom_call" | custom-call | flops 1000 | bytes 1000 | tf_op jit(solution)/shard_map/lift_back/pallas_call | solution.py:72
  251.3 10.1 %lift_grad.2 = (bf16[4,144,1122]{2,1,0:T(8,128)(2,1)}, bf16[4,144,1122]{2,1,0:T(8,128)(2,1)}, bf16[4,144,1120]{2,1,0:T(8,128)(2,1)}, bf16[4,144,1120]{2,1,0:T(8,128)(2,1)}) custom-call(s32[3]{0:T(128)} %pad_add_fusion.1.me_ref, bf16[136,1152]{1,0:T(8,128)(2,1)} %get-tuple-element.572.refs_0_, bf16[136,1152]{1,0:T(8,128)(2,1)} %copy-done.22, ...), custom_call_target="tpu_custom_call" | custom-call | flops 1000 | bytes 1000 | tf_op jit(solution)/shard_map/lift_grad/pallas_call | solution.py:72
  263.3 3.7 middle_back.2
  269.1 3.7 collective-permute-start.65
  279.1 4.1 collective-permute-done.62.refs_1_.refs_5_
  283.2 7.0 %collective-permute-done.63.refs_2_.refs_6_ = bf16[136,1120]{1,0:T(8,128)(2,1)S(1)} collective-permute-done((bf16[136,1120]{1,0:T(8,128)(2,1)S(1)}, bf16[136,1120]{1,0:T(8,128)(2,1)S(1)}, u32[]{:S(2)}, u32[]{:S(2)}) %collective-permute-start.63) | collective-permute-done | bytes 304672 | tf_op jit(solution)/shard_map/ppermute | solution.py:630
  290.9 13.4 %attend_back.2 = (bf16[544,640]{1,0:T(8,128)(2,1)}, f32[544,640]{1,0:T(8,128)}, bf16[544,640]{1,0:T(8,128)(2,1)}, f32[1,1120]{1,0:T(1,128)}) custom-call(s32[3]{0:T(128)} %pad_add_fusion.1.me_ref, bf16[136,1120]{1,0:T(8,128)(2,1)} %get-tuple-element.619.refs_0_.refs_4_, bf16[136,1120]{1,0:T(8,128)(2,1)} %copy-done.68, bf16[136,1120]{1,0:T(8,128)(2,1)} %copy-done.69, ...), custom_call_target="tpu_custom_call" | custom-call | flops 1000 | bytes 1000 | tf_op jit(solution)/shard_map/attend_back/pallas_call | solution.py:72
  308.7 6.9 %project_back.2 = (bf16[544,840]{1,0:T(8,128)(2,1)}, f32[1,840]{1,0:T(1,128)}, bf16[136,1152]{1,0:T(8,128)(2,1)}, bf16[136,1152]{1,0:T(8,128)(2,1)}, bf16[136,11...) custom-call(s32[3]{0:T(128)} %pad_add_fusion.1.me_ref, bf16[544,640]{1,0:T(8,128)(2,1)} %get-tuple-element.630.refs_0_, ...), custom_call_target="tpu_custom_call" | custom-call | flops 1000 | bytes 1000 | tf_op jit(solution)/shard_map/project_back/pallas_call | solution.py:72
  319.7 8.4 %attend_grad.2 = (bf16[4,144,1122]{2,1,0:T(8,128)(2,1)}, bf16[4,144,1122]{2,1,0:T(8,128)(2,1)}) custom-call(s32[3]{0:T(128)} %pad_add_fusion.1.me_ref, bf16[136,1152]{1,0:T(8,128)(2,1)} %get-tuple-element.527.refs_0_, bf16[136,1152]{1,0:T(8,128)(2,1)} %copy-done.60, bf16[136,1152]{1,0:T(8,128)(2,1)} %copy-done.61, bf16[136,1152]{1,0:T(8,128)(2,1)} %copy-done.62, ...), custom_call_target="tpu_custom_call" | custom-call | flops 1000 | bytes 1000 | tf_op jit(solution)/shard_map/attend_grad/pallas_call | solution.py:72
  339.4 3.4 rows_back.1
  346.2 10.2 %collective-permute-start.81 = (bf16[4,144,1122]{2,1,0:T(8,128)(2,1)S(1)}, bf16[4,144,1122]{2,1,0:T(8,128)(2,1)}, u32[]{:S(2)}, u32[]{:S(2)}) collective-permute-start(bf16[4,144,1122]{2,1,0:T(8,128)(2,1)S(1)} %add_convert_fusion.11), channel_id=1, source_target_pairs={{0,8},{24,16},{1,9},{25,17},{2,10},{26,18},{3,11},{27,19},{4,12},{... | collective-permute-start | bytes 3877640 | tf_op jit(solution)/shard_map/ppermute | solution.py:674
  358.2 13.4 %collective-permute-done.74.refs_6_ = bf16[136,1120]{1,0:T(8,128)(2,1)S(1)} collective-permute-done((bf16[136,1120]{1,0:T(8,128)(2,1)S(1)}, bf16[136,1120]{1,0:T(8,128)(2,1)S(1)}, u32[]{:S(2)}, u32[]{:S(2)}) %collective-permute-start.74) | collective-permute-done | bytes 304672 | tf_op jit(solution)/shard_map/ppermute | solution.py:630
  372.3 10.5 %lift_back.3 = (bf16[576,1120]{1,0:T(8,128)(2,1)}, bf16[576,1120]{1,0:T(8,128)(2,1)}, f32[1,1120]{1,0:T(1,128)}, f32[1,1120]{1,0:T(1,128)}, bf16[136,1152]{1,0:T...) custom-call(s32[3]{0:T(128)} %pad_add_fusion.1.me_ref, ...), custom_call_target="tpu_custom_call" | custom-call | flops 1000 | bytes 1000 | tf_op jit(solution)/shard_map/lift_back/pallas_call | solution.py:72
  389.6 10.0 %lift_grad.3 = (bf16[4,144,1122]{2,1,0:T(8,128)(2,1)}, bf16[4,144,1122]{2,1,0:T(8,128)(2,1)}, bf16[4,144,1120]{2,1,0:T(8,128)(2,1)}, bf16[4,144,1120]{2,1,0:T(8,128)(2,1)}) custom-call(s32[3]{0:T(128)} %pad_add_fusion.1.me_ref, bf16[136,1152]{1,0:T(8,128)(2,1)} %get-tuple-element.487.refs_0_, bf16[136,1152]{1,0:T(8,128)(2,1)} %copy-done.21, ...), custom_call_target="tpu_custom_call" | custom-call | flops 1000 | bytes 1000 | tf_op jit(solution)/shard_map/lift_grad/pallas_call | solution.py:72
  405.1 3.4 middle_back.3
  408.5 10.7 %collective-permute-done.84 = bf16[4,144,1122]{2,1,0:T(8,128)(2,1)S(1)} collective-permute-done((bf16[4,144,1122]{2,1,0:T(8,128)(2,1)S(1)}, bf16[4,144,1122]{2,1,0:T(8,128)(2,1)S(1)}, u32[]{:S(2)}, u32[]{:S(2)}) %collective-permute-start.84) | collective-permute-done | bytes 1292576 | tf_op jit(solution)/shard_map/ppermute | solution.py:674
  419.2 3.2 add_convert_fusion.6
  428.8 3.1 add_convert_fusion.3
  432.0 3.2 collective-permute-done.85.refs_1_.refs_5_
  440.0 13.4 %attend_back.3 = (bf16[544,640]{1,0:T(8,128)(2,1)}, f32[544,640]{1,0:T(8,128)}, bf16[544,640]{1,0:T(8,128)(2,1)}, f32[1,1120]{1,0:T(1,128)}) custom-call(s32[3]{0:T(128)} %pad_add_fusion.1.me_ref, bf16[136,1120]{1,0:T(8,128)(2,1)} %get-tuple-element.703.refs_0_.refs_4_, bf16[136,1120]{1,0:T(8,128)(2,1)} %copy-done.64, bf16[136,1120]{1,0:T(8,128)(2,1)} %copy-done.65, ...), custom_call_target="tpu_custom_call" | custom-call | flops 1000 | bytes 1000 | tf_op jit(solution)/shard_map/attend_back/pallas_call | solution.py:72
  453.8 3.1 add_convert_fusion.4
  459.0 3.1 add_convert_fusion.5
  464.4 6.9 %project_back.3 = (bf16[544,840]{1,0:T(8,128)(2,1)}, f32[1,840]{1,0:T(1,128)}, bf16[136,1152]{1,0:T(8,128)(2,1)}, bf16[136,1152]{1,0:T(8,128)(2,1)}, bf16[136,11...) custom-call(s32[3]{0:T(128)} %pad_add_fusion.1.me_ref, bf16[544,640]{1,0:T(8,128)(2,1)} %get-tuple-element.716.refs_0_, ...), custom_call_target="tpu_custom_call" | custom-call | flops 1000 | bytes 1000 | tf_op jit(solution)/shard_map/project_back/pallas_call | solution.py:72
  473.3 8.0 %attend_grad.3 = (bf16[4,144,842]{2,1,0:T(8,128)(2,1)}, bf16[4,144,842]{2,1,0:T(8,128)(2,1)}, bf16[144,1120]{1,0:T(8,128)(2,1)}, bf16[144,1120]{1,0:T(8,128)(2,1)}) custom-call(s32[3]{0:T(128)} %pad_add_fusion.1.me_ref, bf16[136,1152]{1,0:T(8,128)(2,1)} %get-tuple-element.436.refs_0_, bf16[136,1152]{1,0:T(8,128)(2,1)} %collective-permute-done.refs_1_, ...), custom_call_target="tpu_custom_call" | custom-call | flops 1000 | bytes 1000 | tf_op jit(solution)/shard_map/attend_grad/pallas_call | solution.py:72
  486.8 9.4 %collective-permute-done.93 = bf16[4,144,1122]{2,1,0:T(8,128)(2,1)} collective-permute-done((bf16[4,144,1122]{2,1,0:T(8,128)(2,1)}, bf16[4,144,1122]{2,1,0:T(8,128)(2,1)}, u32[]{:S(2)}, u32[]{:S(2)}) %collective-permute-start.93) | collective-permute-done | bytes 1292576 | tf_op jit(solution)/shard_map/ppermute | solution.py:674
  505.0 6.5 %collective-permute-start.101 = (bf16[4,144,842]{2,1,0:T(8,128)(2,1)S(1)}, bf16[4,144,842]{2,1,0:T(8,128)(2,1)S(1)}, u32[]{:S(2)}, u32[]{:S(2)}) collective-permute-start(bf16[4,144,842]{2,1,0:T(8,128)(2,1)S(1)} %add_convert_fusion.17), channel_id=1, source_target_pairs={{0,8},{24,16},{1,9},{25,17},{2,10},{26,18},{3,11},{27,19},{4,12},{... | collective-permute-start | bytes 2909960 | tf_op jit(solution)/shard_map/ppermute | solution.py:674
  513.3 6.7 %collective-permute-done.96.refs_1_ = bf16[136,1152]{1,0:T(8,128)(2,1)S(1)} collective-permute-done((bf16[136,1152]{1,0:T(8,128)(2,1)S(1)}, bf16[136,1152]{1,0:T(8,128)(2,1)S(1)}, u32[]{:S(2)}, u32[]{:S(2)}) %collective-permute-start.96) | collective-permute-done | bytes 313376 | tf_op jit(solution)/shard_map/ppermute | solution.py:630
  522.0 6.4 %collective-permute-done.98.refs_3_ = bf16[136,1152]{1,0:T(8,128)(2,1)S(1)} collective-permute-done((bf16[136,1152]{1,0:T(8,128)(2,1)S(1)}, bf16[136,1152]{1,0:T(8,128)(2,1)S(1)}, u32[]{:S(2)}, u32[]{:S(2)}) %collective-permute-start.98) | collective-permute-done | bytes 313376 | tf_op jit(solution)/shard_map/ppermute | solution.py:630
  528.4 4.7 collective-permute-done.101
  541.9 3.3 rows_back_end.1
  549.6 3.5 collective-permute-done.104.refs_3_
  557.2 3.2 collective-permute-done.105.refs_5_
  560.4 4.5 collective-permute-done.106.refs_6_
  564.9 5.6 collective-permute-done.108
  578.9 4.1 collective-permute-done.110.refs_5_
  589.3 4.4 join_down.1
  593.8 5.7 collective-permute-done.112.refs_7_
  607.3 6.4 %join.2 = (f32[140,2,4480]{2,1,0:T(2,128)}, f32[2,8,144]{2,1,0:T(8,128)}) custom-call(s32[3]{0:T(128)} %pad_add_fusion.1.me_ref, bf16[144,1122]{1,0:T(8,128)(2,1)} %get-tuple-element.799.refs_0_, bf16[144,1122]{1,0:T(8,128)(2,1)} %copy-done.79, bf16[144,1122]{1,0:T(8,128)(2,1)} %copy-done.80, bf16[144,1122]{1,0:T(8,128)(2,1)} %copy-done.81, ...), custom_call_target="tpu_custom_call" | custom-call | flops 1000 | bytes 1000 | tf_op jit(solution)/shard_map/join/pallas_call | solution.py:72
  616.6 7.0 %join.3 = (f32[140,2,3360]{2,1,0:T(2,128)}, f32[2,8,144]{2,1,0:T(8,128)}) custom-call(s32[3]{0:T(128)} %pad_add_fusion.1.me_ref, bf16[144,842]{1,0:T(8,128)(2,1)} %get-tuple-element.817.refs_0_, bf16[144,842]{1,0:T(8,128)(2,1)} %copy-done.104, bf16[144,842]{1,0:T(8,128)(2,1)} %copy-done.105, bf16[144,842]{1,0:T(8,128)(2,1)} %copy-done.106, ...), custom_call_target="tpu_custom_call" | custom-call | flops 1000 | bytes 1000 | tf_op jit(solution)/shard_map/join/pallas_call | solution.py:72
  (565 shorter events, 234.2 us)
Async XLA Ops:
  4.5 34.5 %collective-permute-start = (bf16[136,1152]{1,0:T(8,128)(2,1)}, bf16[136,1152]{1,0:T(8,128)(2,1)}, u32[]{:S(2)}, u32[]{:S(2)}) collective-permute-start(bf16[136,1152]{1,0:T(8,128)(2,1)} %get-tuple-element.436.refs_0_), channel_id=1, source_target_pairs={{0,2},{1,3},{2,0},{3,1},{4,6},{5,7},{6,4},{7,5},{8,10},{9,11},{10,... | collective-permute-start | bytes 940040 | tf_op jit(solution)/shard_map/ppermute | solution.py:630
  7.4 31.5 %collective-permute-start.1 = (bf16[136,1152]{1,0:T(8,128)(2,1)}, bf16[136,1152]{1,0:T(8,128)(2,1)}, u32[]{:S(2)}, u32[]{:S(2)}) collective-permute-start(bf16[136,1152]{1,0:T(8,128)(2,1)} %get-tuple-element.436.refs_0_), channel_id=1, source_target_pairs={{0,4},{1,5},{2,6},{3,7},{4,0},{5,1},{6,2},{7,3},{8,12},{9,13},{10,... | collective-permute-start | bytes 940040 | tf_op jit(solution)/shard_map/ppermute | solution.py:630
  8.9 30.0 %collective-permute-start.2 = (bf16[136,1152]{1,0:T(8,128)(2,1)}, bf16[136,1152]{1,0:T(8,128)(2,1)}, u32[]{:S(2)}, u32[]{:S(2)}) collective-permute-start(bf16[136,1152]{1,0:T(8,128)(2,1)} %get-tuple-element.436.refs_0_), channel_id=1, source_target_pairs={{0,6},{1,7},{2,4},{3,5},{4,2},{5,3},{6,0},{7,1},{8,14},{9,15},{10,... | collective-permute-start | bytes 940040 | tf_op jit(solution)/shard_map/ppermute | solution.py:630
  15.7 14.8 %collective-permute-start.5 = (bf16[144,840]{1,0:T(8,128)(2,1)}, bf16[144,840]{1,0:T(8,128)(2,1)S(1)}, u32[]{:S(2)}, u32[]{:S(2)}) collective-permute-start(bf16[144,840]{1,0:T(8,128)(2,1)} %get-tuple-element.430), channel_id=1, source_target_pairs={{0,6},{1,7},{2,4},{3,5},{4,2},{5,3},{6,0},{7,1},{8,14},{9,15},{10,... | collective-permute-start | bytes 725768 | tf_op jit(solution)/shard_map/ppermute | solution.py:630
  47.5 21.7 %collective-permute-start.15 = (bf16[560,1120]{1,0:T(8,128)(2,1)S(1)}, bf16[560,1120]{1,0:T(8,128)(2,1)S(1)}, u32[]{:S(2)}, u32[]{:S(2)}) collective-permute-start(bf16[560,1120]{1,0:T(8,128)(2,1)S(1)} %slice_bitcast_fusion.1.refs_13_.refs_17_), channel_id=1, source_target_pairs={{0,1},{1,0},{2,3},{3,2},{4,5},{5,4},{6,7},{7,6},{8,9},{9,8},{10,11... | collective-permute-start | bytes 3763208 | tf_op jit(solution)/shard_map/ppermute | solution.py:630
  48.9 20.2 %collective-permute-start.12 = (bf16[144,1120]{1,0:T(8,128)(2,1)S(1)}, bf16[144,1120]{1,0:T(8,128)(2,1)S(1)}, u32[]{:S(2)}, u32[]{:S(2)}) collective-permute-start(bf16[144,1120]{1,0:T(8,128)(2,1)S(1)} %copy-done.126), channel_id=1, source_target_pairs={{0,2},{1,3},{2,0},{3,1},{4,6},{5,7},{6,4},{7,5},{8,10},{9,11},{10,... | collective-permute-start | bytes 967688 | tf_op jit(solution)/shard_map/ppermute | solution.py:630
  50.4 18.8 %collective-permute-start.13 = (bf16[144,1120]{1,0:T(8,128)(2,1)S(1)}, bf16[144,1120]{1,0:T(8,128)(2,1)}, u32[]{:S(2)}, u32[]{:S(2)}) collective-permute-start(bf16[144,1120]{1,0:T(8,128)(2,1)S(1)} %copy-done.125), channel_id=1, source_target_pairs={{0,4},{1,5},{2,6},{3,7},{4,0},{5,1},{6,2},{7,3},{8,12},{9,13},{10,... | collective-permute-start | bytes 967688 | tf_op jit(solution)/shard_map/ppermute | solution.py:630
  50.9 18.3 %collective-permute-start.14 = (bf16[144,1120]{1,0:T(8,128)(2,1)S(1)}, bf16[144,1120]{1,0:T(8,128)(2,1)}, u32[]{:S(2)}, u32[]{:S(2)}) collective-permute-start(bf16[144,1120]{1,0:T(8,128)(2,1)S(1)} %copy-done.124), channel_id=1, source_target_pairs={{0,6},{1,7},{2,4},{3,5},{4,2},{5,3},{6,0},{7,1},{8,14},{9,15},{10,... | collective-permute-start | bytes 967688 | tf_op jit(solution)/shard_map/ppermute | solution.py:630
  69.2 18.1 %collective-permute-start.19 = (bf16[144,1120]{1,0:T(8,128)(2,1)S(1)}, bf16[144,1120]{1,0:T(8,128)(2,1)S(1)}, u32[]{:S(2)}, u32[]{:S(2)}) collective-permute-start(bf16[144,1120]{1,0:T(8,128)(2,1)S(1)} %copy-done.8), channel_id=1, source_target_pairs={{0,1},{1,0},{2,3},{3,2},{4,5},{5,4},{6,7},{7,6},{8,9},{9,8},{10,11... | collective-permute-start | bytes 967688 | tf_op jit(solution)/shard_map/ppermute | solution.py:630
  69.3 18.1 %collective-permute-start.20 = (bf16[144,1120]{1,0:T(8,128)(2,1)S(1)}, bf16[144,1120]{1,0:T(8,128)(2,1)S(1)}, u32[]{:S(2)}, u32[]{:S(2)}) collective-permute-start(bf16[144,1120]{1,0:T(8,128)(2,1)S(1)} %collective-permute-done.12.refs_6_.refs_10_), channel_id=1, source_target_pairs={{0,1},{1,0},{2,3},{3,2},{4,5},{5,4},{6,7},{7,6},{8,9},{9,8},{10,11... | collective-permute-start | bytes 967688 | tf_op jit(solution)/shard_map/ppermute | solution.py:630
  71.3 16.0 %collective-permute-start.17 = (bf16[136,1120]{1,0:T(8,128)(2,1)}, bf16[136,1120]{1,0:T(8,128)(2,1)S(1)}, u32[]{:S(2)}, u32[]{:S(2)}) collective-permute-start(bf16[136,1120]{1,0:T(8,128)(2,1)} %get-tuple-element.475), channel_id=1, source_target_pairs={{0,4},{1,5},{2,6},{3,7},{4,0},{5,1},{6,2},{7,3},{8,12},{9,13},{10,... | collective-permute-start | bytes 913928 | tf_op jit(solution)/shard_map/ppermute | solution.py:630
  71.8 15.5 %collective-permute-start.18 = (bf16[136,1120]{1,0:T(8,128)(2,1)}, bf16[136,1120]{1,0:T(8,128)(2,1)S(1)}, u32[]{:S(2)}, u32[]{:S(2)}) collective-permute-start(bf16[136,1120]{1,0:T(8,128)(2,1)} %get-tuple-element.476), channel_id=1, source_target_pairs={{0,6},{1,7},{2,4},{3,5},{4,2},{5,3},{6,0},{7,1},{8,14},{9,15},{10,... | collective-permute-start | bytes 913928 | tf_op jit(solution)/shard_map/ppermute | solution.py:630
  80.3 14.2 %collective-permute-start.24 = (bf16[144,1120]{1,0:T(8,128)(2,1)}, bf16[144,1120]{1,0:T(8,128)(2,1)S(1)}, u32[]{:S(2)}, u32[]{:S(2)}) collective-permute-start(bf16[144,1120]{1,0:T(8,128)(2,1)} %collective-permute-done.13.refs_8_.refs_12_), channel_id=1, source_target_pairs={{0,1},{1,0},{2,3},{3,2},{4,5},{5,4},{6,7},{7,6},{8,9},{9,8},{10,11... | collective-permute-start | bytes 967688 | tf_op jit(solution)/shard_map/ppermute | solution.py:630
  91.5 16.5 %collective-permute-start.22 = (bf16[136,1152]{1,0:T(8,128)(2,1)}, bf16[136,1152]{1,0:T(8,128)(2,1)}, u32[]{:S(2)}, u32[]{:S(2)}) collective-permute-start(bf16[136,1152]{1,0:T(8,128)(2,1)} %get-tuple-element.487.refs_0_), channel_id=1, source_target_pairs={{0,4},{1,5},{2,6},{3,7},{4,0},{5,1},{6,2},{7,3},{8,12},{9,13},{10,... | collective-permute-start | bytes 940040 | tf_op jit(solution)/shard_map/ppermute | solution.py:630
  92.6 15.4 %collective-permute-start.23 = (bf16[136,1152]{1,0:T(8,128)(2,1)}, bf16[136,1152]{1,0:T(8,128)(2,1)}, u32[]{:S(2)}, u32[]{:S(2)}) collective-permute-start(bf16[136,1152]{1,0:T(8,128)(2,1)} %get-tuple-element.487.refs_0_), channel_id=1, source_target_pairs={{0,6},{1,7},{2,4},{3,5},{4,2},{5,3},{6,0},{7,1},{8,14},{9,15},{10,... | collective-permute-start | bytes 940040 | tf_op jit(solution)/shard_map/ppermute | solution.py:630
  123.0 14.2 %collective-permute-start.30 = (bf16[136,1120]{1,0:T(8,128)(2,1)}, bf16[136,1120]{1,0:T(8,128)(2,1)S(1)}, u32[]{:S(2)}, u32[]{:S(2)}) collective-permute-start(bf16[136,1120]{1,0:T(8,128)(2,1)} %get-tuple-element.514), channel_id=1, source_target_pairs={{0,4},{1,5},{2,6},{3,7},{4,0},{5,1},{6,2},{7,3},{8,12},{9,13},{10,... | collective-permute-start | bytes 913928 | tf_op jit(solution)/shard_map/ppermute | solution.py:630
  163.1 17.7 %collective-permute-start.43 = (bf16[560,1120]{1,0:T(8,128)(2,1)S(1)}, bf16[560,1120]{1,0:T(8,128)(2,1)S(1)}, u32[]{:S(2)}, u32[]{:S(2)}) collective-permute-start(bf16[560,1120]{1,0:T(8,128)(2,1)S(1)} %slice_bitcast_fusion.refs_13_.refs_17_), channel_id=1, source_target_pairs={{0,1},{1,0},{2,3},{3,2},{4,5},{5,4},{6,7},{7,6},{8,9},{9,8},{10,11... | collective-permute-start | bytes 3763208 | tf_op jit(solution)/shard_map/ppermute | solution.py:630
  164.0 16.8 %collective-permute-start.41 = (bf16[144,1120]{1,0:T(8,128)(2,1)S(1)}, bf16[144,1120]{1,0:T(8,128)(2,1)S(1)}, u32[]{:S(2)}, u32[]{:S(2)}) collective-permute-start(bf16[144,1120]{1,0:T(8,128)(2,1)S(1)} %copy-done.122), channel_id=1, source_target_pairs={{0,4},{1,5},{2,6},{3,7},{4,0},{5,1},{6,2},{7,3},{8,12},{9,13},{10,... | collective-permute-start | bytes 967688 | tf_op jit(solution)/shard_map/ppermute | solution.py:630
  165.7 15.1 %collective-permute-start.42 = (bf16[144,1120]{1,0:T(8,128)(2,1)S(1)}, bf16[144,1120]{1,0:T(8,128)(2,1)S(1)}, u32[]{:S(2)}, u32[]{:S(2)}) collective-permute-start(bf16[144,1120]{1,0:T(8,128)(2,1)S(1)} %copy-done.121), channel_id=1, source_target_pairs={{0,6},{1,7},{2,4},{3,5},{4,2},{5,3},{6,0},{7,1},{8,14},{9,15},{10,... | collective-permute-start | bytes 967688 | tf_op jit(solution)/shard_map/ppermute | solution.py:630
  180.9 18.3 %collective-permute-start.47 = (bf16[144,1120]{1,0:T(8,128)(2,1)S(1)}, bf16[144,1120]{1,0:T(8,128)(2,1)S(1)}, u32[]{:S(2)}, u32[]{:S(2)}) collective-permute-start(bf16[144,1120]{1,0:T(8,128)(2,1)S(1)} %copy-done.13), channel_id=1, source_target_pairs={{0,1},{1,0},{2,3},{3,2},{4,5},{5,4},{6,7},{7,6},{8,9},{9,8},{10,11... | collective-permute-start | bytes 967688 | tf_op jit(solution)/shard_map/ppermute | solution.py:630
  180.9 18.2 %collective-permute-start.48 = (bf16[144,1120]{1,0:T(8,128)(2,1)S(1)}, bf16[144,1120]{1,0:T(8,128)(2,1)S(1)}, u32[]{:S(2)}, u32[]{:S(2)}) collective-permute-start(bf16[144,1120]{1,0:T(8,128)(2,1)S(1)} %collective-permute-done.40.refs_6_.refs_10_), channel_id=1, source_target_pairs={{0,1},{1,0},{2,3},{3,2},{4,5},{5,4},{6,7},{7,6},{8,9},{9,8},{10,11... | collective-permute-start | bytes 967688 | tf_op jit(solution)/shard_map/ppermute | solution.py:630
  183.1 16.0 %collective-permute-start.45 = (bf16[136,1120]{1,0:T(8,128)(2,1)}, bf16[136,1120]{1,0:T(8,128)(2,1)S(1)}, u32[]{:S(2)}, u32[]{:S(2)}) collective-permute-start(bf16[136,1120]{1,0:T(8,128)(2,1)} %get-tuple-element.557), channel_id=1, source_target_pairs={{0,4},{1,5},{2,6},{3,7},{4,0},{5,1},{6,2},{7,3},{8,12},{9,13},{10,... | collective-permute-start | bytes 913928 | tf_op jit(solution)/shard_map/ppermute | solution.py:630
  183.4 15.8 %collective-permute-start.46 = (bf16[136,1120]{1,0:T(8,128)(2,1)}, bf16[136,1120]{1,0:T(8,128)(2,1)S(1)}, u32[]{:S(2)}, u32[]{:S(2)}) collective-permute-start(bf16[136,1120]{1,0:T(8,128)(2,1)} %get-tuple-element.558), channel_id=1, source_target_pairs={{0,6},{1,7},{2,4},{3,5},{4,2},{5,3},{6,0},{7,1},{8,14},{9,15},{10,... | collective-permute-start | bytes 913928 | tf_op jit(solution)/shard_map/ppermute | solution.py:630
  191.9 16.6 %collective-permute-start.52 = (bf16[144,1120]{1,0:T(8,128)(2,1)S(1)}, bf16[144,1120]{1,0:T(8,128)(2,1)S(1)}, u32[]{:S(2)}, u32[]{:S(2)}) collective-permute-start(bf16[144,1120]{1,0:T(8,128)(2,1)S(1)} %collective-permute-done.41.refs_8_.refs_12_), channel_id=1, source_target_pairs={{0,1},{1,0},{2,3},{3,2},{4,5},{5,4},{6,7},{7,6},{8,9},{9,8},{10,11... | collective-permute-start | bytes 967688 | tf_op jit(solution)/shard_map/ppermute | solution.py:630
  203.1 16.4 %collective-permute-start.50 = (bf16[136,1152]{1,0:T(8,128)(2,1)}, bf16[136,1152]{1,0:T(8,128)(2,1)S(1)}, u32[]{:S(2)}, u32[]{:S(2)}) collective-permute-start(bf16[136,1152]{1,0:T(8,128)(2,1)} %get-tuple-element.572.refs_0_), channel_id=1, source_target_pairs={{0,4},{1,5},{2,6},{3,7},{4,0},{5,1},{6,2},{7,3},{8,12},{9,13},{10,... | collective-permute-start | bytes 940040 | tf_op jit(solution)/shard_map/ppermute | solution.py:630
  204.6 14.9 %collective-permute-start.51 = (bf16[136,1152]{1,0:T(8,128)(2,1)}, bf16[136,1152]{1,0:T(8,128)(2,1)S(1)}, u32[]{:S(2)}, u32[]{:S(2)}) collective-permute-start(bf16[136,1152]{1,0:T(8,128)(2,1)} %get-tuple-element.572.refs_0_), channel_id=1, source_target_pairs={{0,6},{1,7},{2,4},{3,5},{4,2},{5,3},{6,0},{7,1},{8,14},{9,15},{10,... | collective-permute-start | bytes 940040 | tf_op jit(solution)/shard_map/ppermute | solution.py:630
  221.2 15.1 %collective-permute-start.55 = (bf16[136,1120]{1,0:T(8,128)(2,1)}, bf16[136,1120]{1,0:T(8,128)(2,1)S(1)}, u32[]{:S(2)}, u32[]{:S(2)}) collective-permute-start(bf16[136,1120]{1,0:T(8,128)(2,1)} %get-tuple-element.592.refs_4_), channel_id=1, source_target_pairs={{0,4},{1,5},{2,6},{3,7},{4,0},{5,1},{6,2},{7,3},{8,12},{9,13},{10,... | collective-permute-start | bytes 913928 | tf_op jit(solution)/shard_map/ppermute | solution.py:630
  221.6 15.0 %collective-permute-start.56 = (bf16[136,1120]{1,0:T(8,128)(2,1)}, bf16[136,1120]{1,0:T(8,128)(2,1)S(1)}, u32[]{:S(2)}, u32[]{:S(2)}) collective-permute-start(bf16[136,1120]{1,0:T(8,128)(2,1)} %get-tuple-element.592.refs_4_), channel_id=1, source_target_pairs={{0,6},{1,7},{2,4},{3,5},{4,2},{5,3},{6,0},{7,1},{8,14},{9,15},{10,... | collective-permute-start | bytes 913928 | tf_op jit(solution)/shard_map/ppermute | solution.py:630
  269.1 35.2 %collective-permute-start.65 = (bf16[4,144,1120]{2,1,0:T(8,128)(2,1)S(1)}, bf16[4,144,1120]{2,1,0:T(8,128)(2,1)S(1)}, u32[]{:S(2)}, u32[]{:S(2)}) collective-permute-start(bf16[4,144,1120]{2,1,0:T(8,128)(2,1)S(1)} %add_convert_fusion.14), channel_id=1, source_target_pairs={{0,8},{24,16},{1,9},{25,17},{2,10},{26,18},{3,11},{27,19},{4,12},{... | collective-permute-start | bytes 3870728 | tf_op jit(solution)/shard_map/ppermute | solution.py:674
  274.5 15.6 %collective-permute-start.63 = (bf16[136,1120]{1,0:T(8,128)(2,1)S(1)}, bf16[136,1120]{1,0:T(8,128)(2,1)S(1)}, u32[]{:S(2)}, u32[]{:S(2)}) collective-permute-start(bf16[136,1120]{1,0:T(8,128)(2,1)S(1)} %copy-done.67), channel_id=1, source_target_pairs={{0,4},{1,5},{2,6},{3,7},{4,0},{5,1},{6,2},{7,3},{8,12},{9,13},{10,... | collective-permute-start | bytes 913928 | tf_op jit(solution)/shard_map/ppermute | solution.py:630
  274.8 16.0 %collective-permute-start.64 = (bf16[136,1120]{1,0:T(8,128)(2,1)S(1)}, bf16[136,1120]{1,0:T(8,128)(2,1)}, u32[]{:S(2)}, u32[]{:S(2)}) collective-permute-start(bf16[136,1120]{1,0:T(8,128)(2,1)S(1)} %copy-done.67), channel_id=1, source_target_pairs={{0,6},{1,7},{2,4},{3,5},{4,2},{5,3},{6,0},{7,1},{8,14},{9,15},{10,... | collective-permute-start | bytes 913928 | tf_op jit(solution)/shard_map/ppermute | solution.py:630
  276.7 53.1 %collective-permute-start.71 = (bf16[4,144,1122]{2,1,0:T(8,128)(2,1)S(1)}, bf16[4,144,1122]{2,1,0:T(8,128)(2,1)}, u32[]{:S(2)}, u32[]{:S(2)}) collective-permute-start(bf16[4,144,1122]{2,1,0:T(8,128)(2,1)S(1)} %add_convert_fusion.12), channel_id=1, source_target_pairs={{0,8},{24,16},{1,9},{25,17},{2,10},{26,18},{3,11},{27,19},{4,12},{... | collective-permute-start | bytes 3877640 | tf_op jit(solution)/shard_map/ppermute | solution.py:674
  304.6 27.4 %collective-permute-start.70 = (bf16[4,144,1120]{2,1,0:T(8,128)(2,1)S(1)}, bf16[4,144,1120]{2,1,0:T(8,128)(2,1)S(1)}, u32[]{:S(2)}, u32[]{:S(2)}) collective-permute-start(bf16[4,144,1120]{2,1,0:T(8,128)(2,1)S(1)} %add_convert_fusion.13), channel_id=1, source_target_pairs={{8,16},{16,8},{9,17},{17,9},{10,18},{18,10},{11,19},{19,11},{12,20... | collective-permute-start | bytes 3870728 | tf_op jit(solution)/shard_map/ppermute | solution.py:674
  315.6 14.2 %collective-permute-start.67 = (bf16[136,1152]{1,0:T(8,128)(2,1)}, bf16[136,1152]{1,0:T(8,128)(2,1)S(1)}, u32[]{:S(2)}, u32[]{:S(2)}) collective-permute-start(bf16[136,1152]{1,0:T(8,128)(2,1)} %get-tuple-element.634), channel_id=1, source_target_pairs={{0,2},{1,3},{2,0},{3,1},{4,6},{5,7},{6,4},{7,5},{8,10},{9,11},{10,... | collective-permute-start | bytes 940040 | tf_op jit(solution)/shard_map/ppermute | solution.py:630
  316.0 16.1 %collective-permute-start.68 = (bf16[136,1152]{1,0:T(8,128)(2,1)}, bf16[136,1152]{1,0:T(8,128)(2,1)S(1)}, u32[]{:S(2)}, u32[]{:S(2)}) collective-permute-start(bf16[136,1152]{1,0:T(8,128)(2,1)} %get-tuple-element.635), channel_id=1, source_target_pairs={{0,4},{1,5},{2,6},{3,7},{4,0},{5,1},{6,2},{7,3},{8,12},{9,13},{10,... | collective-permute-start | bytes 940040 | tf_op jit(solution)/shard_map/ppermute | solution.py:630
  316.7 15.3 %collective-permute-start.69 = (bf16[136,1152]{1,0:T(8,128)(2,1)}, bf16[136,1152]{1,0:T(8,128)(2,1)S(1)}, u32[]{:S(2)}, u32[]{:S(2)}) collective-permute-start(bf16[136,1152]{1,0:T(8,128)(2,1)} %get-tuple-element.636), channel_id=1, source_target_pairs={{0,6},{1,7},{2,4},{3,5},{4,2},{5,3},{6,0},{7,1},{8,14},{9,15},{10,... | collective-permute-start | bytes 940040 | tf_op jit(solution)/shard_map/ppermute | solution.py:630
  334.5 48.3 %collective-permute-start.77 = (bf16[4,144,1122]{2,1,0:T(8,128)(2,1)S(1)}, bf16[4,144,1122]{2,1,0:T(8,128)(2,1)}, u32[]{:S(2)}, u32[]{:S(2)}) collective-permute-start(bf16[4,144,1122]{2,1,0:T(8,128)(2,1)S(1)} %add_convert_fusion.9), channel_id=1, source_target_pairs={{8,16},{16,8},{9,17},{17,9},{10,18},{18,10},{11,19},{19,11},{12,20... | collective-permute-start | bytes 3877640 | tf_op jit(solution)/shard_map/ppermute | solution.py:674
  338.0 44.8 %collective-permute-start.76 = (bf16[4,144,1120]{2,1,0:T(8,128)(2,1)S(1)}, bf16[4,144,1120]{2,1,0:T(8,128)(2,1)}, u32[]{:S(2)}, u32[]{:S(2)}) collective-permute-start(bf16[4,144,1120]{2,1,0:T(8,128)(2,1)S(1)} %add_convert_fusion.10), channel_id=1, source_target_pairs={{8,0},{16,24},{9,1},{17,25},{10,2},{18,26},{11,3},{19,27},{12,4},{... | collective-permute-start | bytes 3870728 | tf_op jit(solution)/shard_map/ppermute | solution.py:674
  346.2 53.8 %collective-permute-start.81 = (bf16[4,144,1122]{2,1,0:T(8,128)(2,1)S(1)}, bf16[4,144,1122]{2,1,0:T(8,128)(2,1)}, u32[]{:S(2)}, u32[]{:S(2)}) collective-permute-start(bf16[4,144,1122]{2,1,0:T(8,128)(2,1)S(1)} %add_convert_fusion.11), channel_id=1, source_target_pairs={{0,8},{24,16},{1,9},{25,17},{2,10},{26,18},{3,11},{27,19},{4,12},{... | collective-permute-start | bytes 3877640 | tf_op jit(solution)/shard_map/ppermute | solution.py:674
  356.3 15.3 %collective-permute-start.74 = (bf16[136,1120]{1,0:T(8,128)(2,1)S(1)}, bf16[136,1120]{1,0:T(8,128)(2,1)S(1)}, u32[]{:S(2)}, u32[]{:S(2)}) collective-permute-start(bf16[136,1120]{1,0:T(8,128)(2,1)S(1)} %copy-done.54), channel_id=1, source_target_pairs={{0,4},{1,5},{2,6},{3,7},{4,0},{5,1},{6,2},{7,3},{8,12},{9,13},{10,... | collective-permute-start | bytes 913928 | tf_op jit(solution)/shard_map/ppermute | solution.py:630
  356.7 15.6 %collective-permute-start.75 = (bf16[136,1120]{1,0:T(8,128)(2,1)S(1)}, bf16[136,1120]{1,0:T(8,128)(2,1)}, u32[]{:S(2)}, u32[]{:S(2)}) collective-permute-start(bf16[136,1120]{1,0:T(8,128)(2,1)S(1)} %copy-done.54), channel_id=1, source_target_pairs={{0,6},{1,7},{2,4},{3,5},{4,2},{5,3},{6,0},{7,1},{8,14},{9,15},{10,... | collective-permute-start | bytes 913928 | tf_op jit(solution)/shard_map/ppermute | solution.py:630
  384.5 15.1 %collective-permute-start.78 = (bf16[136,1152]{1,0:T(8,128)(2,1)}, bf16[136,1152]{1,0:T(8,128)(2,1)S(1)}, u32[]{:S(2)}, u32[]{:S(2)}) collective-permute-start(bf16[136,1152]{1,0:T(8,128)(2,1)} %get-tuple-element.681), channel_id=1, source_target_pairs={{0,2},{1,3},{2,0},{3,1},{4,6},{5,7},{6,4},{7,5},{8,10},{9,11},{10,... | collective-permute-start | bytes 940040 | tf_op jit(solution)/shard_map/ppermute | solution.py:630
  384.9 15.0 %collective-permute-start.79 = (bf16[136,1152]{1,0:T(8,128)(2,1)}, bf16[136,1152]{1,0:T(8,128)(2,1)S(1)}, u32[]{:S(2)}, u32[]{:S(2)}) collective-permute-start(bf16[136,1152]{1,0:T(8,128)(2,1)} %get-tuple-element.682), channel_id=1, source_target_pairs={{0,4},{1,5},{2,6},{3,7},{4,0},{5,1},{6,2},{7,3},{8,12},{9,13},{10,... | collective-permute-start | bytes 940040 | tf_op jit(solution)/shard_map/ppermute | solution.py:630
  388.0 31.1 %collective-permute-start.84 = (bf16[4,144,1122]{2,1,0:T(8,128)(2,1)S(1)}, bf16[4,144,1122]{2,1,0:T(8,128)(2,1)S(1)}, u32[]{:S(2)}, u32[]{:S(2)}) collective-permute-start(bf16[4,144,1122]{2,1,0:T(8,128)(2,1)S(1)} %add_convert_fusion.8), channel_id=1, source_target_pairs={{8,0},{16,24},{9,1},{17,25},{10,2},{18,26},{11,3},{19,27},{12,4},{... | collective-permute-start | bytes 3877640 | tf_op jit(solution)/shard_map/ppermute | solution.py:674
  399.9 19.2 %collective-permute-start.82 = (bf16[4,144,1122]{2,1,0:T(8,128)(2,1)}, bf16[4,144,1122]{2,1,0:T(8,128)(2,1)}, u32[]{:S(2)}, u32[]{:S(2)}) collective-permute-start(bf16[4,144,1122]{2,1,0:T(8,128)(2,1)} %get-tuple-element.700), channel_id=1, source_target_pairs={{0,1},{1,0},{2,3},{3,2},{4,5},{5,4},{6,7},{7,6},{8,9},{9,8},{10,11... | collective-permute-start | bytes 3877640 | tf_op jit(solution)/shard_map/ppermute | solution.py:630
  400.0 19.2 %collective-permute-start.83 = (bf16[4,144,1120]{2,1,0:T(8,128)(2,1)}, bf16[4,144,1120]{2,1,0:T(8,128)(2,1)}, u32[]{:S(2)}, u32[]{:S(2)}) collective-permute-start(bf16[4,144,1120]{2,1,0:T(8,128)(2,1)} %get-tuple-element.701), channel_id=1, source_target_pairs={{0,1},{1,0},{2,3},{3,2},{4,5},{5,4},{6,7},{7,6},{8,9},{9,8},{10,11... | collective-permute-start | bytes 3870728 | tf_op jit(solution)/shard_map/ppermute | solution.py:630
  403.2 50.2 %collective-permute-start.88 = (bf16[4,144,1122]{2,1,0:T(8,128)(2,1)}, bf16[4,144,1122]{2,1,0:T(8,128)(2,1)}, u32[]{:S(2)}, u32[]{:S(2)}) collective-permute-start(bf16[4,144,1122]{2,1,0:T(8,128)(2,1)} %add_convert_fusion.7), channel_id=1, source_target_pairs={{8,16},{16,8},{9,17},{17,9},{10,18},{18,10},{11,19},{19,11},{12,20... | collective-permute-start | bytes 3877640 | tf_op jit(solution)/shard_map/ppermute | solution.py:674
  422.4 31.3 %collective-permute-start.89 = (bf16[4,144,1120]{2,1,0:T(8,128)(2,1)}, bf16[4,144,1120]{2,1,0:T(8,128)(2,1)}, u32[]{:S(2)}, u32[]{:S(2)}) collective-permute-start(bf16[4,144,1120]{2,1,0:T(8,128)(2,1)} %add_convert_fusion.6), channel_id=1, source_target_pairs={{0,8},{24,16},{1,9},{25,17},{2,10},{26,18},{3,11},{27,19},{4,12},{... | collective-permute-start | bytes 3870728 | tf_op jit(solution)/shard_map/ppermute | solution.py:674
  435.1 51.6 %collective-permute-start.95 = (bf16[4,144,1122]{2,1,0:T(8,128)(2,1)}, bf16[4,144,1122]{2,1,0:T(8,128)(2,1)}, u32[]{:S(2)}, u32[]{:S(2)}) collective-permute-start(bf16[4,144,1122]{2,1,0:T(8,128)(2,1)} %add_convert_fusion.3), channel_id=1, source_target_pairs={{0,8},{24,16},{1,9},{25,17},{2,10},{26,18},{3,11},{27,19},{4,12},{... | collective-permute-start | bytes 3877640 | tf_op jit(solution)/shard_map/ppermute | solution.py:674
  456.9 29.8 %collective-permute-start.94 = (bf16[4,144,1120]{2,1,0:T(8,128)(2,1)}, bf16[4,144,1120]{2,1,0:T(8,128)(2,1)}, u32[]{:S(2)}, u32[]{:S(2)}) collective-permute-start(bf16[4,144,1120]{2,1,0:T(8,128)(2,1)} %add_convert_fusion.4), channel_id=1, source_target_pairs={{8,16},{16,8},{9,17},{17,9},{10,18},{18,10},{11,19},{19,11},{12,20... | collective-permute-start | bytes 3870728 | tf_op jit(solution)/shard_map/ppermute | solution.py:674
  462.1 34.1 %collective-permute-start.93 = (bf16[4,144,1122]{2,1,0:T(8,128)(2,1)}, bf16[4,144,1122]{2,1,0:T(8,128)(2,1)}, u32[]{:S(2)}, u32[]{:S(2)}) collective-permute-start(bf16[4,144,1122]{2,1,0:T(8,128)(2,1)} %add_convert_fusion.5), channel_id=1, source_target_pairs={{8,0},{16,24},{9,1},{17,25},{10,2},{18,26},{11,3},{19,27},{12,4},{... | collective-permute-start | bytes 3877640 | tf_op jit(solution)/shard_map/ppermute | solution.py:674
  498.2 34.9 %collective-permute-start.99 = (bf16[4,144,1120]{2,1,0:T(8,128)(2,1)S(1)}, bf16[4,144,1120]{2,1,0:T(8,128)(2,1)S(1)}, u32[]{:S(2)}, u32[]{:S(2)}) collective-permute-start(bf16[4,144,1120]{2,1,0:T(8,128)(2,1)S(1)} %add_convert_fusion.1), channel_id=1, source_target_pairs={{8,0},{16,24},{9,1},{17,25},{10,2},{18,26},{11,3},{19,27},{12,4},{... | collective-permute-start | bytes 3870728 | tf_op jit(solution)/shard_map/ppermute | solution.py:674
  501.6 31.5 %collective-permute-start.100 = (bf16[4,144,1122]{2,1,0:T(8,128)(2,1)S(1)}, bf16[4,144,1122]{2,1,0:T(8,128)(2,1)S(1)}, u32[]{:S(2)}, u32[]{:S(2)}) collective-permute-start(bf16[4,144,1122]{2,1,0:T(8,128)(2,1)S(1)} %add_convert_fusion.2), channel_id=1, source_target_pairs={{8,16},{16,8},{9,17},{17,9},{10,18},{18,10},{11,19},{19,11},{12,20... | collective-permute-start | bytes 3877640 | tf_op jit(solution)/shard_map/ppermute | solution.py:674
  505.0 28.0 %collective-permute-start.101 = (bf16[4,144,842]{2,1,0:T(8,128)(2,1)S(1)}, bf16[4,144,842]{2,1,0:T(8,128)(2,1)S(1)}, u32[]{:S(2)}, u32[]{:S(2)}) collective-permute-start(bf16[4,144,842]{2,1,0:T(8,128)(2,1)S(1)} %add_convert_fusion.17), channel_id=1, source_target_pairs={{0,8},{24,16},{1,9},{25,17},{2,10},{26,18},{3,11},{27,19},{4,12},{... | collective-permute-start | bytes 2909960 | tf_op jit(solution)/shard_map/ppermute | solution.py:674
  533.3 31.6 %collective-permute-start.109 = (bf16[4,144,842]{2,1,0:T(8,128)(2,1)S(1)}, bf16[4,144,842]{2,1,0:T(8,128)(2,1)S(1)}, u32[]{:S(2)}, u32[]{:S(2)}) collective-permute-start(bf16[4,144,842]{2,1,0:T(8,128)(2,1)S(1)} %add_convert_fusion.16), channel_id=1, source_target_pairs={{8,16},{16,8},{9,17},{17,9},{10,18},{18,10},{11,19},{19,11},{12,20... | collective-permute-start | bytes 2909960 | tf_op jit(solution)/shard_map/ppermute | solution.py:674
  534.4 36.2 %collective-permute-start.108 = (bf16[4,144,1122]{2,1,0:T(8,128)(2,1)S(1)}, bf16[4,144,1122]{2,1,0:T(8,128)(2,1)}, u32[]{:S(2)}, u32[]{:S(2)}) collective-permute-start(bf16[4,144,1122]{2,1,0:T(8,128)(2,1)S(1)} %add_convert_fusion), channel_id=1, source_target_pairs={{8,0},{16,24},{9,1},{17,25},{10,2},{18,26},{11,3},{19,27},{12,4},{... | collective-permute-start | bytes 3877640 | tf_op jit(solution)/shard_map/ppermute | solution.py:674
  537.4 15.7 %collective-permute-start.104 = (bf16[136,1120]{1,0:T(8,128)(2,1)}, bf16[136,1120]{1,0:T(8,128)(2,1)}, u32[]{:S(2)}, u32[]{:S(2)}) collective-permute-start(bf16[136,1120]{1,0:T(8,128)(2,1)} %get-tuple-element.755), channel_id=1, source_target_pairs={{0,6},{1,7},{2,4},{3,5},{4,2},{5,3},{6,0},{7,1},{8,14},{9,15},{10,... | collective-permute-start | bytes 913928 | tf_op jit(solution)/shard_map/ppermute | solution.py:630
  549.6 15.3 %collective-permute-start.106 = (bf16[144,1122]{1,0:T(8,128)(2,1)}, bf16[144,1122]{1,0:T(8,128)(2,1)S(1)}, u32[]{:S(2)}, u32[]{:S(2)}) collective-permute-start(bf16[144,1122]{1,0:T(8,128)(2,1)} %get-tuple-element.762), channel_id=1, source_target_pairs={{0,4},{1,5},{2,6},{3,7},{4,0},{5,1},{6,2},{7,3},{8,12},{9,13},{10,... | collective-permute-start | bytes 969416 | tf_op jit(solution)/shard_map/ppermute | solution.py:630
  570.9 28.8 %collective-permute-start.116 = (bf16[4,144,842]{2,1,0:T(8,128)(2,1)S(1)}, bf16[4,144,842]{2,1,0:T(8,128)(2,1)S(1)}, u32[]{:S(2)}, u32[]{:S(2)}) collective-permute-start(bf16[4,144,842]{2,1,0:T(8,128)(2,1)S(1)} %add_convert_fusion.15), channel_id=1, source_target_pairs={{8,0},{16,24},{9,1},{17,25},{10,2},{18,26},{11,3},{19,27},{12,4},{... | collective-permute-start | bytes 2909960 | tf_op jit(solution)/shard_map/ppermute | solution.py:674
  576.3 23.2 %collective-permute-start.113 = (bf16[144,1122]{1,0:T(8,128)(2,1)}, bf16[144,1122]{1,0:T(8,128)(2,1)S(1)}, u32[]{:S(2)}, u32[]{:S(2)}) collective-permute-start(bf16[144,1122]{1,0:T(8,128)(2,1)} %get-tuple-element.776), channel_id=1, source_target_pairs={{0,2},{1,3},{2,0},{3,1},{4,6},{5,7},{6,4},{7,5},{8,10},{9,11},{10,... | collective-permute-start | bytes 969416 | tf_op jit(solution)/shard_map/ppermute | solution.py:630
  577.2 22.5 %collective-permute-start.114 = (bf16[144,1122]{1,0:T(8,128)(2,1)}, bf16[144,1122]{1,0:T(8,128)(2,1)S(1)}, u32[]{:S(2)}, u32[]{:S(2)}) collective-permute-start(bf16[144,1122]{1,0:T(8,128)(2,1)} %get-tuple-element.777), channel_id=1, source_target_pairs={{0,4},{1,5},{2,6},{3,7},{4,0},{5,1},{6,2},{7,3},{8,12},{9,13},{10,... | collective-permute-start | bytes 969416 | tf_op jit(solution)/shard_map/ppermute | solution.py:630
  583.1 16.6 %collective-permute-start.115 = (bf16[144,1122]{1,0:T(8,128)(2,1)S(1)}, bf16[144,1122]{1,0:T(8,128)(2,1)S(1)}, u32[]{:S(2)}, u32[]{:S(2)}) collective-permute-start(bf16[144,1122]{1,0:T(8,128)(2,1)S(1)} %get-tuple-element.778), channel_id=1, source_target_pairs={{0,6},{1,7},{2,4},{3,5},{4,2},{5,3},{6,0},{7,1},{8,14},{9,15},{10,... | collective-permute-start | bytes 969416 | tf_op jit(solution)/shard_map/ppermute | solution.py:630
  584.5 15.0 %collective-permute-start.112 = (bf16[144,842]{1,0:T(8,128)(2,1)}, bf16[144,842]{1,0:T(8,128)(2,1)}, u32[]{:S(2)}, u32[]{:S(2)}) collective-permute-start(bf16[144,842]{1,0:T(8,128)(2,1)} %get-tuple-element.773), channel_id=1, source_target_pairs={{0,6},{1,7},{2,4},{3,5},{4,2},{5,3},{6,0},{7,1},{8,14},{9,15},{10,... | collective-permute-start | bytes 727496 | tf_op jit(solution)/shard_map/ppermute | solution.py:630
  601.3 14.3 %collective-permute-start.120 = (bf16[144,1120]{1,0:T(8,128)(2,1)S(1)}, bf16[144,1120]{1,0:T(8,128)(2,1)S(1)}, u32[]{:S(2)}, u32[]{:S(2)}) collective-permute-start(bf16[144,1120]{1,0:T(8,128)(2,1)S(1)} %add_convert_fusion.20), channel_id=1, source_target_pairs={{0,8},{8,0},{16,24},{24,16},{1,9},{9,1},{17,25},{25,17},{2,10},{10... | collective-permute-start | bytes 967688 | tf_op jit(solution)/shard_map/ppermute | solution.py:1119
  (189 other events, 1707.9 us)

commit v5 on v4

--- a/solution.py
+++ b/solution.py
@@ -121,7 +121,7 @@
 def normed_piece(plan, rows, gain_ref, shift_ref, level):
     unit, _ = normed_of(rows)
     normed = unit * gain_ref[level : level + 1, :] + shift_ref[level : level + 1, :]
-    return spread(plan, real_rows(plan, normed)).astype(BF)
+    return spread(plan, real_rows(plan, normed).astype(BF))
 
 
 def begin_kernel(plan, gene_ref, pre_ref, gain_ref, shift_ref, rows_ref, piece_ref):
@@ -367,7 +367,7 @@
     blocks, (pre_ref, own_ref, weight_ref) = refs[2 : 2 + plan.chips], refs[2 + plan.chips :]
     collect_own(plan, me_ref[0], parts, choices[1:], own_ref, weight_ref)
     for rows in plan.halves(plan.rows):
-        pairs = (mine_ref[rows, :] + other_ref[rows, :].astype(F32)).astype(BF)
+        pairs = (mine_ref[rows, :].astype(F32) + other_ref[rows, :].astype(F32)).astype(BF)
         if not plan.whole:
             select_ref = choices[0]
             qkv_grad_ref[rows, :] = (
@@ -1000,7 +1000,7 @@
             [where] + pieces + [windows[level], query, pair, other_pair, lse],
             [
                 shape_of(plan.rows, plan.lanes),
-                shape_of(plan.rows, plan.lanes, dtype=F32),
+                shape_of(plan.rows, plan.lanes),
                 shape_of(plan.rows, plan.lanes),
                 vector,
             ],

time: 643 us -> 643 us (level)
  transfers between devices with their start and end apart: 122 -> 122, of which waited for: 54 -> 53; matrix products, arithmetic and copies ran while one was open for 10% -> 10% of each run, Pallas kernels for 26% -> 26%
where the time goes in v5:
time: 643 us; the launch traced here: 632 us
  waiting for transfers between devices  203 us (32%)
  Pallas kernels  202 us (31%)
  starting transfers between devices  136 us (21%)
  local copies, waits for them, and re-layouts  45.1 us (7%)
  other arithmetic  39.7 us (6%)
    pallas_call x33, Pallas kernels, call(): pl.pallas_call(kernel, in_specs=[SCALAR if scalar and at == 0 else WHOLE...  202 us
    ppermute x102, waiting for transfers between devices, swap(): lax.ppermute(value, 'gene', [(at, at ^ bits) for at in range(groups)])  167 us
    ppermute x102, starting transfers between devices, swap(): lax.ppermute(value, 'gene', [(at, at ^ bits) for at in range(groups)])  88.3 us
    ppermute x18, starting transfers between devices, move(): lax.ppermute(self.value, 'cell', {3: inwards, 2: between, 1: outwards}[le...  44.9 us
    ppermute x18, waiting for transfers between devices, move(): lax.ppermute(self.value, 'cell', {3: inwards, 2: between, 1: outwards}[le...  33.4 us
    unnamed x270, local copies, waits for them, and re-layouts  28.3 us
    convert_element_type x12, other arithmetic, land(): self.value = (value.astype(F32) + got.astype(F32)).astype(BF)  19.1 us
  transfers between devices with their start and end apart: 122, of which 53 were waited for; matrix products, arithmetic and copies ran while one was open for 10% of the time, Pallas kernels for 26%

profile of v5, /device:TPU:0, one launch (start us, length us, event | category | flops | bytes accessed | tf_op | source)
XLA Modules:
  0.0 632.1 jit_solution(14699002990873701674)
XLA Ops:
  12.5 3.2 send.4
  22.4 3.2 send.5
  35.5 3.5 collective-permute-done.4.refs_8_.refs_7_.refs_12_
  42.4 5.0 project.2
  52.4 3.3 send.7
  55.6 3.1 send.6
  59.6 9.5 %attend.2 = (bf16[544,640]{1,0:T(8,128)(2,1)}, f32[5,1,544]{2,1,0:T(1,128)}, bf16[136,1120]{1,0:T(8,128)(2,1)}, bf16[136,1120]{1,0:T(8,128)(2,1)}, bf16[136,1120]{1,0:T(8,128)(2,1)}, /*index=5*/bf16[136,1120]{1,0:T(8,128)(2,1)}) custom-call(s32[3]{0:T(128)} %pad_add_fusion.1.me_ref, bf16[544,640]{1,0:T(8,128)(2,1)} %get-tuple-element.452.refs_0_.refs_5_, ...), custom_call_target="tpu_custom_call" | custom-call | flops 1000 | bytes 1000 | tf_op jit(solution)/shard_map/attend/pallas_call | solution.py:72
  73.2 7.0 %collective-permute-done.16.refs_1_ = bf16[136,1120]{1,0:T(8,128)(2,1)S(1)} collective-permute-done((bf16[136,1120]{1,0:T(8,128)(2,1)}, bf16[136,1120]{1,0:T(8,128)(2,1)S(1)}, u32[]{:S(2)}, u32[]{:S(2)}) %collective-permute-start.16) | collective-permute-done | bytes 304672 | tf_op jit(solution)/shard_map/ppermute | solution.py:630
  80.2 7.1 %collective-permute-done.17.refs_2_ = bf16[136,1120]{1,0:T(8,128)(2,1)S(1)} collective-permute-done((bf16[136,1120]{1,0:T(8,128)(2,1)}, bf16[136,1120]{1,0:T(8,128)(2,1)S(1)}, u32[]{:S(2)}, u32[]{:S(2)}) %collective-permute-start.17) | collective-permute-done | bytes 304672 | tf_op jit(solution)/shard_map/ppermute | solution.py:630
  94.4 6.9 %collective-permute-done.21.refs_1_ = bf16[136,1152]{1,0:T(8,128)(2,1)S(1)} collective-permute-done((bf16[136,1152]{1,0:T(8,128)(2,1)}, bf16[136,1152]{1,0:T(8,128)(2,1)S(1)}, u32[]{:S(2)}, u32[]{:S(2)}) %collective-permute-start.21) | collective-permute-done | bytes 313376 | tf_op jit(solution)/shard_map/ppermute | solution.py:630
  101.3 6.6 %collective-permute-done.22.refs_2_ = bf16[136,1152]{1,0:T(8,128)(2,1)} collective-permute-done((bf16[136,1152]{1,0:T(8,128)(2,1)}, bf16[136,1152]{1,0:T(8,128)(2,1)}, u32[]{:S(2)}, u32[]{:S(2)}) %collective-permute-start.22) | collective-permute-done | bytes 313376 | tf_op jit(solution)/shard_map/ppermute | solution.py:630
  113.0 8.0 %lift.2 = (bf16[136,1120]{1,0:T(8,128)(2,1)}, bf16[136,1120]{1,0:T(8,128)(2,1)}, bf16[136,1120]{1,0:T(8,128)(2,1)}, bf16[136,1120]{1,0:T(8,128)(2,1)}) custom-call(s32[3]{0:T(128)} %pad_add_fusion.1.me_ref, bf16[136,1152]{1,0:T(8,128)(2,1)} %get-tuple-element.487.refs_0_, bf16[136,1152]{1,0:T(8,128)(2,1)} %copy-done.21, ...), custom_call_target="tpu_custom_call" | custom-call | flops 1000 | bytes 1000 | tf_op jit(solution)/shard_map/lift/pallas_call | solution.py:72
  128.0 4.9 collective-permute-done.29.refs_1_
  133.0 4.3 collective-permute-done.30.refs_2_
  146.5 4.2 collective-permute-done.34.refs_1_
  150.6 5.2 collective-permute-done.35.refs_2_
  156.7 4.8 project.3
  168.2 9.2 %attend.3 = (bf16[544,640]{1,0:T(8,128)(2,1)}, f32[5,1,544]{2,1,0:T(1,128)}, bf16[136,1120]{1,0:T(8,128)(2,1)}, bf16[136,1120]{1,0:T(8,128)(2,1)}, bf16[136,1120]{1,0:T(8,128)(2,1)}, /*index=5*/bf16[136,1120]{1,0:T(8,128)(2,1)}) custom-call(s32[3]{0:T(128)} %pad_add_fusion.1.me_ref, bf16[544,640]{1,0:T(8,128)(2,1)} %get-tuple-element.539.refs_0_.refs_5_, ...), custom_call_target="tpu_custom_call" | custom-call | flops 1000 | bytes 1000 | tf_op jit(solution)/shard_map/attend/pallas_call | solution.py:72
  177.4 3.4 collective-permute-done.41.refs_8_.refs_12_
  184.9 7.0 %collective-permute-done.44.refs_1_ = bf16[136,1120]{1,0:T(8,128)(2,1)S(1)} collective-permute-done((bf16[136,1120]{1,0:T(8,128)(2,1)}, bf16[136,1120]{1,0:T(8,128)(2,1)S(1)}, u32[]{:S(2)}, u32[]{:S(2)}) %collective-permute-start.44) | collective-permute-done | bytes 304672 | tf_op jit(solution)/shard_map/ppermute | solution.py:630
  191.9 7.2 %collective-permute-done.45.refs_2_ = bf16[136,1120]{1,0:T(8,128)(2,1)S(1)} collective-permute-done((bf16[136,1120]{1,0:T(8,128)(2,1)}, bf16[136,1120]{1,0:T(8,128)(2,1)S(1)}, u32[]{:S(2)}, u32[]{:S(2)}) %collective-permute-start.45) | collective-permute-done | bytes 304672 | tf_op jit(solution)/shard_map/ppermute | solution.py:630
  208.5 4.6 collective-permute-done.49.refs_1_
  213.2 6.3 %collective-permute-done.50.refs_2_ = bf16[136,1152]{1,0:T(8,128)(2,1)S(1)} collective-permute-done((bf16[136,1152]{1,0:T(8,128)(2,1)}, bf16[136,1152]{1,0:T(8,128)(2,1)S(1)}, u32[]{:S(2)}, u32[]{:S(2)}) %collective-permute-start.50) | collective-permute-done | bytes 313376 | tf_op jit(solution)/shard_map/ppermute | solution.py:630
  223.1 8.0 %lift.3 = (bf16[136,1120]{1,0:T(8,128)(2,1)}, bf16[136,1120]{1,0:T(8,128)(2,1)}, bf16[136,1120]{1,0:T(8,128)(2,1)}, bf16[136,1120]{1,0:T(8,128)(2,1)}) custom-call(s32[3]{0:T(128)} %pad_add_fusion.1.me_ref, bf16[136,1152]{1,0:T(8,128)(2,1)} %get-tuple-element.572.refs_0_, bf16[136,1152]{1,0:T(8,128)(2,1)} %copy-done.22, bf16[136,1152]{1,0:T(8,128)(2,1)} %copy-done.23, ...), custom_call_target="tpu_custom_call" | custom-call | flops 1000 | bytes 1000 | tf_op jit(solution)/shard_map/lift/pallas_call | solution.py:72
  231.2 5.2 collective-permute-done.55.refs_6_
  237.2 10.5 %lift_back.2 = (bf16[576,1120]{1,0:T(8,128)(2,1)}, bf16[576,1120]{1,0:T(8,128)(2,1)}, f32[1,1120]{1,0:T(1,128)}, f32[1,1120]{1,0:T(1,128)}, bf16[136,1152]{1,0:T...) custom-call(s32[3]{0:T(128)} %pad_add_fusion.1.me_ref, ...), custom_call_target="tpu_custom_call" | custom-call | flops 1000 | bytes 1000 | tf_op jit(solution)/shard_map/lift_back/pallas_call | solution.py:72
  251.2 10.1 %lift_grad.2 = (bf16[4,144,1122]{2,1,0:T(8,128)(2,1)}, bf16[4,144,1122]{2,1,0:T(8,128)(2,1)}, bf16[4,144,1120]{2,1,0:T(8,128)(2,1)}, bf16[4,144,1120]{2,1,0:T(8,128)(2,1)}) custom-call(s32[3]{0:T(128)} %pad_add_fusion.1.me_ref, bf16[136,1152]{1,0:T(8,128)(2,1)} %get-tuple-element.572.refs_0_, bf16[136,1152]{1,0:T(8,128)(2,1)} %copy-done.22, ...), custom_call_target="tpu_custom_call" | custom-call | flops 1000 | bytes 1000 | tf_op jit(solution)/shard_map/lift_grad/pallas_call | solution.py:72
  263.3 3.7 middle_back.2
  269.1 3.7 collective-permute-start.65
  279.1 4.1 collective-permute-done.62.refs_1_.refs_5_
  283.1 7.0 %collective-permute-done.63.refs_2_.refs_6_ = bf16[136,1120]{1,0:T(8,128)(2,1)S(1)} collective-permute-done((bf16[136,1120]{1,0:T(8,128)(2,1)S(1)}, bf16[136,1120]{1,0:T(8,128)(2,1)S(1)}, u32[]{:S(2)}, u32[]{:S(2)}) %collective-permute-start.63) | collective-permute-done | bytes 304672 | tf_op jit(solution)/shard_map/ppermute | solution.py:630
  290.9 13.2 %attend_back.2 = (bf16[544,640]{1,0:T(8,128)(2,1)}, bf16[544,640]{1,0:T(8,128)(2,1)}, bf16[544,640]{1,0:T(8,128)(2,1)}, f32[1,1120]{1,0:T(1,128)}) custom-call(s32[3]{0:T(128)} %pad_add_fusion.1.me_ref, bf16[136,1120]{1,0:T(8,128)(2,1)} %get-tuple-element.619.refs_0_.refs_4_, bf16[136,1120]{1,0:T(8,128)(2,1)} %copy-done.68, bf16[136,1120]{1,0:T(8,128)(2,1)} %copy-done.69, ...), custom_call_target="tpu_custom_call" | custom-call | flops 1000 | bytes 1000 | tf_op jit(solution)/shard_map/attend_back/pallas_call | solution.py:72
  308.5 6.7 %project_back.2 = (bf16[544,840]{1,0:T(8,128)(2,1)}, f32[1,840]{1,0:T(1,128)}, bf16[136,1152]{1,0:T(8,128)(2,1)}, bf16[136,1152]{1,0:T(8,128)(2,1)}, bf16[136,11...) custom-call(s32[3]{0:T(128)} %pad_add_fusion.1.me_ref, bf16[544,640]{1,0:T(8,128)(2,1)} %get-tuple-element.630.refs_0_, ...), custom_call_target="tpu_custom_call" | custom-call | flops 1000 | bytes 1000 | tf_op jit(solution)/shard_map/project_back/pallas_call | solution.py:72
  319.3 8.4 %attend_grad.2 = (bf16[4,144,1122]{2,1,0:T(8,128)(2,1)}, bf16[4,144,1122]{2,1,0:T(8,128)(2,1)}) custom-call(s32[3]{0:T(128)} %pad_add_fusion.1.me_ref, bf16[136,1152]{1,0:T(8,128)(2,1)} %get-tuple-element.527.refs_0_, bf16[136,1152]{1,0:T(8,128)(2,1)} %copy-done.60, bf16[136,1152]{1,0:T(8,128)(2,1)} %copy-done.61, bf16[136,1152]{1,0:T(8,128)(2,1)} %copy-done.62, ...), custom_call_target="tpu_custom_call" | custom-call | flops 1000 | bytes 1000 | tf_op jit(solution)/shard_map/attend_grad/pallas_call | solution.py:72
  339.1 3.4 rows_back.1
  345.8 10.5 %collective-permute-start.81 = (bf16[4,144,1122]{2,1,0:T(8,128)(2,1)S(1)}, bf16[4,144,1122]{2,1,0:T(8,128)(2,1)}, u32[]{:S(2)}, u32[]{:S(2)}) collective-permute-start(bf16[4,144,1122]{2,1,0:T(8,128)(2,1)S(1)} %add_convert_fusion.11), channel_id=1, source_target_pairs={{0,8},{24,16},{1,9},{25,17},{2,10},{26,18},{3,11},{27,19},{4,12},{... | collective-permute-start | bytes 3877640 | tf_op jit(solution)/shard_map/ppermute | solution.py:674
  358.2 13.4 %collective-permute-done.74.refs_6_ = bf16[136,1120]{1,0:T(8,128)(2,1)S(1)} collective-permute-done((bf16[136,1120]{1,0:T(8,128)(2,1)S(1)}, bf16[136,1120]{1,0:T(8,128)(2,1)S(1)}, u32[]{:S(2)}, u32[]{:S(2)}) %collective-permute-start.74) | collective-permute-done | bytes 304672 | tf_op jit(solution)/shard_map/ppermute | solution.py:630
  372.3 10.5 %lift_back.3 = (bf16[576,1120]{1,0:T(8,128)(2,1)}, bf16[576,1120]{1,0:T(8,128)(2,1)}, f32[1,1120]{1,0:T(1,128)}, f32[1,1120]{1,0:T(1,128)}, bf16[136,1152]{1,0:T...) custom-call(s32[3]{0:T(128)} %pad_add_fusion.1.me_ref, ...), custom_call_target="tpu_custom_call" | custom-call | flops 1000 | bytes 1000 | tf_op jit(solution)/shard_map/lift_back/pallas_call | solution.py:72
  389.6 10.0 %lift_grad.3 = (bf16[4,144,1122]{2,1,0:T(8,128)(2,1)}, bf16[4,144,1122]{2,1,0:T(8,128)(2,1)}, bf16[4,144,1120]{2,1,0:T(8,128)(2,1)}, bf16[4,144,1120]{2,1,0:T(8,128)(2,1)}) custom-call(s32[3]{0:T(128)} %pad_add_fusion.1.me_ref, bf16[136,1152]{1,0:T(8,128)(2,1)} %get-tuple-element.487.refs_0_, bf16[136,1152]{1,0:T(8,128)(2,1)} %copy-done.21, ...), custom_call_target="tpu_custom_call" | custom-call | flops 1000 | bytes 1000 | tf_op jit(solution)/shard_map/lift_grad/pallas_call | solution.py:72
  405.1 3.4 middle_back.3
  408.5 10.7 %collective-permute-done.84 = bf16[4,144,1122]{2,1,0:T(8,128)(2,1)S(1)} collective-permute-done((bf16[4,144,1122]{2,1,0:T(8,128)(2,1)S(1)}, bf16[4,144,1122]{2,1,0:T(8,128)(2,1)S(1)}, u32[]{:S(2)}, u32[]{:S(2)}) %collective-permute-start.84) | collective-permute-done | bytes 1292576 | tf_op jit(solution)/shard_map/ppermute | solution.py:674
  419.2 3.2 add_convert_fusion.6
  428.8 3.1 add_convert_fusion.3
  431.9 3.2 collective-permute-done.85.refs_1_.refs_5_
  440.0 13.2 %attend_back.3 = (bf16[544,640]{1,0:T(8,128)(2,1)}, bf16[544,640]{1,0:T(8,128)(2,1)}, bf16[544,640]{1,0:T(8,128)(2,1)}, f32[1,1120]{1,0:T(1,128)}) custom-call(s32[3]{0:T(128)} %pad_add_fusion.1.me_ref, bf16[136,1120]{1,0:T(8,128)(2,1)} %get-tuple-element.703.refs_0_.refs_4_, bf16[136,1120]{1,0:T(8,128)(2,1)} %copy-done.64, bf16[136,1120]{1,0:T(8,128)(2,1)} %copy-done.65, ...), custom_call_target="tpu_custom_call" | custom-call | flops 1000 | bytes 1000 | tf_op jit(solution)/shard_map/attend_back/pallas_call | solution.py:72
  453.7 3.1 add_convert_fusion.4
  458.9 3.1 add_convert_fusion.5
  464.3 6.8 %project_back.3 = (bf16[544,840]{1,0:T(8,128)(2,1)}, f32[1,840]{1,0:T(1,128)}, bf16[136,1152]{1,0:T(8,128)(2,1)}, bf16[136,1152]{1,0:T(8,128)(2,1)}, bf16[136,11...) custom-call(s32[3]{0:T(128)} %pad_add_fusion.1.me_ref, bf16[544,640]{1,0:T(8,128)(2,1)} %get-tuple-element.716.refs_0_, ...), custom_call_target="tpu_custom_call" | custom-call | flops 1000 | bytes 1000 | tf_op jit(solution)/shard_map/project_back/pallas_call | solution.py:72
  473.1 8.1 %attend_grad.3 = (bf16[4,144,842]{2,1,0:T(8,128)(2,1)}, bf16[4,144,842]{2,1,0:T(8,128)(2,1)}, bf16[144,1120]{1,0:T(8,128)(2,1)}, bf16[144,1120]{1,0:T(8,128)(2,1)}) custom-call(s32[3]{0:T(128)} %pad_add_fusion.1.me_ref, bf16[136,1152]{1,0:T(8,128)(2,1)} %get-tuple-element.436.refs_0_, bf16[136,1152]{1,0:T(8,128)(2,1)} %collective-permute-done.refs_1_, ...), custom_call_target="tpu_custom_call" | custom-call | flops 1000 | bytes 1000 | tf_op jit(solution)/shard_map/attend_grad/pallas_call | solution.py:72
  486.6 9.8 %collective-permute-done.93 = bf16[4,144,1122]{2,1,0:T(8,128)(2,1)} collective-permute-done((bf16[4,144,1122]{2,1,0:T(8,128)(2,1)}, bf16[4,144,1122]{2,1,0:T(8,128)(2,1)}, u32[]{:S(2)}, u32[]{:S(2)}) %collective-permute-start.93) | collective-permute-done | bytes 1292576 | tf_op jit(solution)/shard_map/ppermute | solution.py:674
  505.2 6.3 %collective-permute-start.101 = (bf16[4,144,842]{2,1,0:T(8,128)(2,1)S(1)}, bf16[4,144,842]{2,1,0:T(8,128)(2,1)S(1)}, u32[]{:S(2)}, u32[]{:S(2)}) collective-permute-start(bf16[4,144,842]{2,1,0:T(8,128)(2,1)S(1)} %add_convert_fusion.17), channel_id=1, source_target_pairs={{0,8},{24,16},{1,9},{25,17},{2,10},{26,18},{3,11},{27,19},{4,12},{... | collective-permute-start | bytes 2909960 | tf_op jit(solution)/shard_map/ppermute | solution.py:674
  513.2 6.8 %collective-permute-done.96.refs_1_ = bf16[136,1152]{1,0:T(8,128)(2,1)S(1)} collective-permute-done((bf16[136,1152]{1,0:T(8,128)(2,1)S(1)}, bf16[136,1152]{1,0:T(8,128)(2,1)S(1)}, u32[]{:S(2)}, u32[]{:S(2)}) %collective-permute-start.96) | collective-permute-done | bytes 313376 | tf_op jit(solution)/shard_map/ppermute | solution.py:630
  521.9 6.5 %collective-permute-done.98.refs_3_ = bf16[136,1152]{1,0:T(8,128)(2,1)S(1)} collective-permute-done((bf16[136,1152]{1,0:T(8,128)(2,1)S(1)}, bf16[136,1152]{1,0:T(8,128)(2,1)S(1)}, u32[]{:S(2)}, u32[]{:S(2)}) %collective-permute-start.98) | collective-permute-done | bytes 313376 | tf_op jit(solution)/shard_map/ppermute | solution.py:630
  528.3 4.7 collective-permute-done.101
  541.9 3.3 rows_back_end.1
  549.6 3.5 collective-permute-done.104.refs_3_
  557.2 3.2 collective-permute-done.105.refs_5_
  560.4 4.5 collective-permute-done.106.refs_6_
  564.9 5.6 collective-permute-done.108
  578.9 4.1 collective-permute-done.110.refs_5_
  589.3 4.4 join_down.1
  593.8 5.7 collective-permute-done.112.refs_7_
  607.2 6.4 %join.2 = (f32[140,2,4480]{2,1,0:T(2,128)}, f32[2,8,144]{2,1,0:T(8,128)}) custom-call(s32[3]{0:T(128)} %pad_add_fusion.1.me_ref, bf16[144,1122]{1,0:T(8,128)(2,1)} %get-tuple-element.799.refs_0_, bf16[144,1122]{1,0:T(8,128)(2,1)} %copy-done.79, bf16[144,1122]{1,0:T(8,128)(2,1)} %copy-done.80, bf16[144,1122]{1,0:T(8,128)(2,1)} %copy-done.81, ...), custom_call_target="tpu_custom_call" | custom-call | flops 1000 | bytes 1000 | tf_op jit(solution)/shard_map/join/pallas_call | solution.py:72
  616.5 7.0 %join.3 = (f32[140,2,3360]{2,1,0:T(2,128)}, f32[2,8,144]{2,1,0:T(8,128)}) custom-call(s32[3]{0:T(128)} %pad_add_fusion.1.me_ref, bf16[144,842]{1,0:T(8,128)(2,1)} %get-tuple-element.817.refs_0_, bf16[144,842]{1,0:T(8,128)(2,1)} %copy-done.104, bf16[144,842]{1,0:T(8,128)(2,1)} %copy-done.105, bf16[144,842]{1,0:T(8,128)(2,1)} %copy-done.106, ...), custom_call_target="tpu_custom_call" | custom-call | flops 1000 | bytes 1000 | tf_op jit(solution)/shard_map/join/pallas_call | solution.py:72
  (565 shorter events, 234.2 us)
Async XLA Ops:
  4.5 34.5 %collective-permute-start = (bf16[136,1152]{1,0:T(8,128)(2,1)}, bf16[136,1152]{1,0:T(8,128)(2,1)}, u32[]{:S(2)}, u32[]{:S(2)}) collective-permute-start(bf16[136,1152]{1,0:T(8,128)(2,1)} %get-tuple-element.436.refs_0_), channel_id=1, source_target_pairs={{0,2},{1,3},{2,0},{3,1},{4,6},{5,7},{6,4},{7,5},{8,10},{9,11},{10,... | collective-permute-start | bytes 940040 | tf_op jit(solution)/shard_map/ppermute | solution.py:630
  7.4 31.5 %collective-permute-start.1 = (bf16[136,1152]{1,0:T(8,128)(2,1)}, bf16[136,1152]{1,0:T(8,128)(2,1)}, u32[]{:S(2)}, u32[]{:S(2)}) collective-permute-start(bf16[136,1152]{1,0:T(8,128)(2,1)} %get-tuple-element.436.refs_0_), channel_id=1, source_target_pairs={{0,4},{1,5},{2,6},{3,7},{4,0},{5,1},{6,2},{7,3},{8,12},{9,13},{10,... | collective-permute-start | bytes 940040 | tf_op jit(solution)/shard_map/ppermute | solution.py:630
  8.9 30.0 %collective-permute-start.2 = (bf16[136,1152]{1,0:T(8,128)(2,1)}, bf16[136,1152]{1,0:T(8,128)(2,1)}, u32[]{:S(2)}, u32[]{:S(2)}) collective-permute-start(bf16[136,1152]{1,0:T(8,128)(2,1)} %get-tuple-element.436.refs_0_), channel_id=1, source_target_pairs={{0,6},{1,7},{2,4},{3,5},{4,2},{5,3},{6,0},{7,1},{8,14},{9,15},{10,... | collective-permute-start | bytes 940040 | tf_op jit(solution)/shard_map/ppermute | solution.py:630
  15.7 14.8 %collective-permute-start.5 = (bf16[144,840]{1,0:T(8,128)(2,1)}, bf16[144,840]{1,0:T(8,128)(2,1)S(1)}, u32[]{:S(2)}, u32[]{:S(2)}) collective-permute-start(bf16[144,840]{1,0:T(8,128)(2,1)} %get-tuple-element.430), channel_id=1, source_target_pairs={{0,6},{1,7},{2,4},{3,5},{4,2},{5,3},{6,0},{7,1},{8,14},{9,15},{10,... | collective-permute-start | bytes 725768 | tf_op jit(solution)/shard_map/ppermute | solution.py:630
  47.5 21.7 %collective-permute-start.15 = (bf16[560,1120]{1,0:T(8,128)(2,1)S(1)}, bf16[560,1120]{1,0:T(8,128)(2,1)S(1)}, u32[]{:S(2)}, u32[]{:S(2)}) collective-permute-start(bf16[560,1120]{1,0:T(8,128)(2,1)S(1)} %slice_bitcast_fusion.1.refs_13_.refs_17_), channel_id=1, source_target_pairs={{0,1},{1,0},{2,3},{3,2},{4,5},{5,4},{6,7},{7,6},{8,9},{9,8},{10,11... | collective-permute-start | bytes 3763208 | tf_op jit(solution)/shard_map/ppermute | solution.py:630
  48.9 20.2 %collective-permute-start.12 = (bf16[144,1120]{1,0:T(8,128)(2,1)S(1)}, bf16[144,1120]{1,0:T(8,128)(2,1)S(1)}, u32[]{:S(2)}, u32[]{:S(2)}) collective-permute-start(bf16[144,1120]{1,0:T(8,128)(2,1)S(1)} %copy-done.126), channel_id=1, source_target_pairs={{0,2},{1,3},{2,0},{3,1},{4,6},{5,7},{6,4},{7,5},{8,10},{9,11},{10,... | collective-permute-start | bytes 967688 | tf_op jit(solution)/shard_map/ppermute | solution.py:630
  50.4 18.8 %collective-permute-start.13 = (bf16[144,1120]{1,0:T(8,128)(2,1)S(1)}, bf16[144,1120]{1,0:T(8,128)(2,1)}, u32[]{:S(2)}, u32[]{:S(2)}) collective-permute-start(bf16[144,1120]{1,0:T(8,128)(2,1)S(1)} %copy-done.125), channel_id=1, source_target_pairs={{0,4},{1,5},{2,6},{3,7},{4,0},{5,1},{6,2},{7,3},{8,12},{9,13},{10,... | collective-permute-start | bytes 967688 | tf_op jit(solution)/shard_map/ppermute | solution.py:630
  50.9 18.3 %collective-permute-start.14 = (bf16[144,1120]{1,0:T(8,128)(2,1)S(1)}, bf16[144,1120]{1,0:T(8,128)(2,1)}, u32[]{:S(2)}, u32[]{:S(2)}) collective-permute-start(bf16[144,1120]{1,0:T(8,128)(2,1)S(1)} %copy-done.124), channel_id=1, source_target_pairs={{0,6},{1,7},{2,4},{3,5},{4,2},{5,3},{6,0},{7,1},{8,14},{9,15},{10,... | collective-permute-start | bytes 967688 | tf_op jit(solution)/shard_map/ppermute | solution.py:630
  69.2 18.1 %collective-permute-start.19 = (bf16[144,1120]{1,0:T(8,128)(2,1)S(1)}, bf16[144,1120]{1,0:T(8,128)(2,1)S(1)}, u32[]{:S(2)}, u32[]{:S(2)}) collective-permute-start(bf16[144,1120]{1,0:T(8,128)(2,1)S(1)} %copy-done.8), channel_id=1, source_target_pairs={{0,1},{1,0},{2,3},{3,2},{4,5},{5,4},{6,7},{7,6},{8,9},{9,8},{10,11... | collective-permute-start | bytes 967688 | tf_op jit(solution)/shard_map/ppermute | solution.py:630
  69.3 18.1 %collective-permute-start.20 = (bf16[144,1120]{1,0:T(8,128)(2,1)S(1)}, bf16[144,1120]{1,0:T(8,128)(2,1)S(1)}, u32[]{:S(2)}, u32[]{:S(2)}) collective-permute-start(bf16[144,1120]{1,0:T(8,128)(2,1)S(1)} %collective-permute-done.12.refs_6_.refs_10_), channel_id=1, source_target_pairs={{0,1},{1,0},{2,3},{3,2},{4,5},{5,4},{6,7},{7,6},{8,9},{9,8},{10,11... | collective-permute-start | bytes 967688 | tf_op jit(solution)/shard_map/ppermute | solution.py:630
  71.3 16.0 %collective-permute-start.17 = (bf16[136,1120]{1,0:T(8,128)(2,1)}, bf16[136,1120]{1,0:T(8,128)(2,1)S(1)}, u32[]{:S(2)}, u32[]{:S(2)}) collective-permute-start(bf16[136,1120]{1,0:T(8,128)(2,1)} %get-tuple-element.475), channel_id=1, source_target_pairs={{0,4},{1,5},{2,6},{3,7},{4,0},{5,1},{6,2},{7,3},{8,12},{9,13},{10,... | collective-permute-start | bytes 913928 | tf_op jit(solution)/shard_map/ppermute | solution.py:630
  71.8 15.5 %collective-permute-start.18 = (bf16[136,1120]{1,0:T(8,128)(2,1)}, bf16[136,1120]{1,0:T(8,128)(2,1)S(1)}, u32[]{:S(2)}, u32[]{:S(2)}) collective-permute-start(bf16[136,1120]{1,0:T(8,128)(2,1)} %get-tuple-element.476), channel_id=1, source_target_pairs={{0,6},{1,7},{2,4},{3,5},{4,2},{5,3},{6,0},{7,1},{8,14},{9,15},{10,... | collective-permute-start | bytes 913928 | tf_op jit(solution)/shard_map/ppermute | solution.py:630
  91.4 16.5 %collective-permute-start.22 = (bf16[136,1152]{1,0:T(8,128)(2,1)}, bf16[136,1152]{1,0:T(8,128)(2,1)}, u32[]{:S(2)}, u32[]{:S(2)}) collective-permute-start(bf16[136,1152]{1,0:T(8,128)(2,1)} %get-tuple-element.487.refs_0_), channel_id=1, source_target_pairs={{0,4},{1,5},{2,6},{3,7},{4,0},{5,1},{6,2},{7,3},{8,12},{9,13},{10,... | collective-permute-start | bytes 940040 | tf_op jit(solution)/shard_map/ppermute | solution.py:630
  92.5 15.4 %collective-permute-start.23 = (bf16[136,1152]{1,0:T(8,128)(2,1)}, bf16[136,1152]{1,0:T(8,128)(2,1)}, u32[]{:S(2)}, u32[]{:S(2)}) collective-permute-start(bf16[136,1152]{1,0:T(8,128)(2,1)} %get-tuple-element.487.refs_0_), channel_id=1, source_target_pairs={{0,6},{1,7},{2,4},{3,5},{4,2},{5,3},{6,0},{7,1},{8,14},{9,15},{10,... | collective-permute-start | bytes 940040 | tf_op jit(solution)/shard_map/ppermute | solution.py:630
  163.1 17.8 %collective-permute-start.43 = (bf16[560,1120]{1,0:T(8,128)(2,1)S(1)}, bf16[560,1120]{1,0:T(8,128)(2,1)S(1)}, u32[]{:S(2)}, u32[]{:S(2)}) collective-permute-start(bf16[560,1120]{1,0:T(8,128)(2,1)S(1)} %slice_bitcast_fusion.refs_13_.refs_17_), channel_id=1, source_target_pairs={{0,1},{1,0},{2,3},{3,2},{4,5},{5,4},{6,7},{7,6},{8,9},{9,8},{10,11... | collective-permute-start | bytes 3763208 | tf_op jit(solution)/shard_map/ppermute | solution.py:630
  164.0 16.8 %collective-permute-start.41 = (bf16[144,1120]{1,0:T(8,128)(2,1)S(1)}, bf16[144,1120]{1,0:T(8,128)(2,1)S(1)}, u32[]{:S(2)}, u32[]{:S(2)}) collective-permute-start(bf16[144,1120]{1,0:T(8,128)(2,1)S(1)} %copy-done.122), channel_id=1, source_target_pairs={{0,4},{1,5},{2,6},{3,7},{4,0},{5,1},{6,2},{7,3},{8,12},{9,13},{10,... | collective-permute-start | bytes 967688 | tf_op jit(solution)/shard_map/ppermute | solution.py:630
  165.7 15.1 %collective-permute-start.42 = (bf16[144,1120]{1,0:T(8,128)(2,1)S(1)}, bf16[144,1120]{1,0:T(8,128)(2,1)S(1)}, u32[]{:S(2)}, u32[]{:S(2)}) collective-permute-start(bf16[144,1120]{1,0:T(8,128)(2,1)S(1)} %copy-done.121), channel_id=1, source_target_pairs={{0,6},{1,7},{2,4},{3,5},{4,2},{5,3},{6,0},{7,1},{8,14},{9,15},{10,... | collective-permute-start | bytes 967688 | tf_op jit(solution)/shard_map/ppermute | solution.py:630
  180.9 18.3 %collective-permute-start.47 = (bf16[144,1120]{1,0:T(8,128)(2,1)S(1)}, bf16[144,1120]{1,0:T(8,128)(2,1)S(1)}, u32[]{:S(2)}, u32[]{:S(2)}) collective-permute-start(bf16[144,1120]{1,0:T(8,128)(2,1)S(1)} %copy-done.13), channel_id=1, source_target_pairs={{0,1},{1,0},{2,3},{3,2},{4,5},{5,4},{6,7},{7,6},{8,9},{9,8},{10,11... | collective-permute-start | bytes 967688 | tf_op jit(solution)/shard_map/ppermute | solution.py:630
  180.9 18.2 %collective-permute-start.48 = (bf16[144,1120]{1,0:T(8,128)(2,1)S(1)}, bf16[144,1120]{1,0:T(8,128)(2,1)S(1)}, u32[]{:S(2)}, u32[]{:S(2)}) collective-permute-start(bf16[144,1120]{1,0:T(8,128)(2,1)S(1)} %collective-permute-done.40.refs_6_.refs_10_), channel_id=1, source_target_pairs={{0,1},{1,0},{2,3},{3,2},{4,5},{5,4},{6,7},{7,6},{8,9},{9,8},{10,11... | collective-permute-start | bytes 967688 | tf_op jit(solution)/shard_map/ppermute | solution.py:630
  183.1 16.0 %collective-permute-start.45 = (bf16[136,1120]{1,0:T(8,128)(2,1)}, bf16[136,1120]{1,0:T(8,128)(2,1)S(1)}, u32[]{:S(2)}, u32[]{:S(2)}) collective-permute-start(bf16[136,1120]{1,0:T(8,128)(2,1)} %get-tuple-element.557), channel_id=1, source_target_pairs={{0,4},{1,5},{2,6},{3,7},{4,0},{5,1},{6,2},{7,3},{8,12},{9,13},{10,... | collective-permute-start | bytes 913928 | tf_op jit(solution)/shard_map/ppermute | solution.py:630
  183.4 15.8 %collective-permute-start.46 = (bf16[136,1120]{1,0:T(8,128)(2,1)}, bf16[136,1120]{1,0:T(8,128)(2,1)S(1)}, u32[]{:S(2)}, u32[]{:S(2)}) collective-permute-start(bf16[136,1120]{1,0:T(8,128)(2,1)} %get-tuple-element.558), channel_id=1, source_target_pairs={{0,6},{1,7},{2,4},{3,5},{4,2},{5,3},{6,0},{7,1},{8,14},{9,15},{10,... | collective-permute-start | bytes 913928 | tf_op jit(solution)/shard_map/ppermute | solution.py:630
  191.9 16.6 %collective-permute-start.52 = (bf16[144,1120]{1,0:T(8,128)(2,1)S(1)}, bf16[144,1120]{1,0:T(8,128)(2,1)S(1)}, u32[]{:S(2)}, u32[]{:S(2)}) collective-permute-start(bf16[144,1120]{1,0:T(8,128)(2,1)S(1)} %collective-permute-done.41.refs_8_.refs_12_), channel_id=1, source_target_pairs={{0,1},{1,0},{2,3},{3,2},{4,5},{5,4},{6,7},{7,6},{8,9},{9,8},{10,11... | collective-permute-start | bytes 967688 | tf_op jit(solution)/shard_map/ppermute | solution.py:630
  203.1 16.4 %collective-permute-start.50 = (bf16[136,1152]{1,0:T(8,128)(2,1)}, bf16[136,1152]{1,0:T(8,128)(2,1)S(1)}, u32[]{:S(2)}, u32[]{:S(2)}) collective-permute-start(bf16[136,1152]{1,0:T(8,128)(2,1)} %get-tuple-element.572.refs_0_), channel_id=1, source_target_pairs={{0,4},{1,5},{2,6},{3,7},{4,0},{5,1},{6,2},{7,3},{8,12},{9,13},{10,... | collective-permute-start | bytes 940040 | tf_op jit(solution)/shard_map/ppermute | solution.py:630
  204.6 14.9 %collective-permute-start.51 = (bf16[136,1152]{1,0:T(8,128)(2,1)}, bf16[136,1152]{1,0:T(8,128)(2,1)S(1)}, u32[]{:S(2)}, u32[]{:S(2)}) collective-permute-start(bf16[136,1152]{1,0:T(8,128)(2,1)} %get-tuple-element.572.refs_0_), channel_id=1, source_target_pairs={{0,6},{1,7},{2,4},{3,5},{4,2},{5,3},{6,0},{7,1},{8,14},{9,15},{10,... | collective-permute-start | bytes 940040 | tf_op jit(solution)/shard_map/ppermute | solution.py:630
  221.2 15.1 %collective-permute-start.55 = (bf16[136,1120]{1,0:T(8,128)(2,1)}, bf16[136,1120]{1,0:T(8,128)(2,1)S(1)}, u32[]{:S(2)}, u32[]{:S(2)}) collective-permute-start(bf16[136,1120]{1,0:T(8,128)(2,1)} %get-tuple-element.592.refs_4_), channel_id=1, source_target_pairs={{0,4},{1,5},{2,6},{3,7},{4,0},{5,1},{6,2},{7,3},{8,12},{9,13},{10,... | collective-permute-start | bytes 913928 | tf_op jit(solution)/shard_map/ppermute | solution.py:630
  221.5 14.8 %collective-permute-start.56 = (bf16[136,1120]{1,0:T(8,128)(2,1)}, bf16[136,1120]{1,0:T(8,128)(2,1)S(1)}, u32[]{:S(2)}, u32[]{:S(2)}) collective-permute-start(bf16[136,1120]{1,0:T(8,128)(2,1)} %get-tuple-element.592.refs_4_), channel_id=1, source_target_pairs={{0,6},{1,7},{2,4},{3,5},{4,2},{5,3},{6,0},{7,1},{8,14},{9,15},{10,... | collective-permute-start | bytes 913928 | tf_op jit(solution)/shard_map/ppermute | solution.py:630
  248.2 14.2 %collective-permute-start.58 = (bf16[136,1152]{1,0:T(8,128)(2,1)}, bf16[136,1152]{1,0:T(8,128)(2,1)S(1)}, u32[]{:S(2)}, u32[]{:S(2)}) collective-permute-start(bf16[136,1152]{1,0:T(8,128)(2,1)} %get-tuple-element.598), channel_id=1, source_target_pairs={{0,4},{1,5},{2,6},{3,7},{4,0},{5,1},{6,2},{7,3},{8,12},{9,13},{10,... | collective-permute-start | bytes 940040 | tf_op jit(solution)/shard_map/ppermute | solution.py:630
  269.1 35.0 %collective-permute-start.65 = (bf16[4,144,1120]{2,1,0:T(8,128)(2,1)S(1)}, bf16[4,144,1120]{2,1,0:T(8,128)(2,1)S(1)}, u32[]{:S(2)}, u32[]{:S(2)}) collective-permute-start(bf16[4,144,1120]{2,1,0:T(8,128)(2,1)S(1)} %add_convert_fusion.14), channel_id=1, source_target_pairs={{0,8},{24,16},{1,9},{25,17},{2,10},{26,18},{3,11},{27,19},{4,12},{... | collective-permute-start | bytes 3870728 | tf_op jit(solution)/shard_map/ppermute | solution.py:674
  274.5 15.6 %collective-permute-start.63 = (bf16[136,1120]{1,0:T(8,128)(2,1)S(1)}, bf16[136,1120]{1,0:T(8,128)(2,1)S(1)}, u32[]{:S(2)}, u32[]{:S(2)}) collective-permute-start(bf16[136,1120]{1,0:T(8,128)(2,1)S(1)} %copy-done.67), channel_id=1, source_target_pairs={{0,4},{1,5},{2,6},{3,7},{4,0},{5,1},{6,2},{7,3},{8,12},{9,13},{10,... | collective-permute-start | bytes 913928 | tf_op jit(solution)/shard_map/ppermute | solution.py:630
  274.8 16.0 %collective-permute-start.64 = (bf16[136,1120]{1,0:T(8,128)(2,1)S(1)}, bf16[136,1120]{1,0:T(8,128)(2,1)}, u32[]{:S(2)}, u32[]{:S(2)}) collective-permute-start(bf16[136,1120]{1,0:T(8,128)(2,1)S(1)} %copy-done.67), channel_id=1, source_target_pairs={{0,6},{1,7},{2,4},{3,5},{4,2},{5,3},{6,0},{7,1},{8,14},{9,15},{10,... | collective-permute-start | bytes 913928 | tf_op jit(solution)/shard_map/ppermute | solution.py:630
  276.7 53.1 %collective-permute-start.71 = (bf16[4,144,1122]{2,1,0:T(8,128)(2,1)S(1)}, bf16[4,144,1122]{2,1,0:T(8,128)(2,1)}, u32[]{:S(2)}, u32[]{:S(2)}) collective-permute-start(bf16[4,144,1122]{2,1,0:T(8,128)(2,1)S(1)} %add_convert_fusion.12), channel_id=1, source_target_pairs={{0,8},{24,16},{1,9},{25,17},{2,10},{26,18},{3,11},{27,19},{4,12},{... | collective-permute-start | bytes 3877640 | tf_op jit(solution)/shard_map/ppermute | solution.py:674
  304.4 27.2 %collective-permute-start.70 = (bf16[4,144,1120]{2,1,0:T(8,128)(2,1)S(1)}, bf16[4,144,1120]{2,1,0:T(8,128)(2,1)S(1)}, u32[]{:S(2)}, u32[]{:S(2)}) collective-permute-start(bf16[4,144,1120]{2,1,0:T(8,128)(2,1)S(1)} %add_convert_fusion.13), channel_id=1, source_target_pairs={{8,16},{16,8},{9,17},{17,9},{10,18},{18,10},{11,19},{19,11},{12,20... | collective-permute-start | bytes 3870728 | tf_op jit(solution)/shard_map/ppermute | solution.py:674
  315.2 14.6 %collective-permute-start.67 = (bf16[136,1152]{1,0:T(8,128)(2,1)}, bf16[136,1152]{1,0:T(8,128)(2,1)S(1)}, u32[]{:S(2)}, u32[]{:S(2)}) collective-permute-start(bf16[136,1152]{1,0:T(8,128)(2,1)} %get-tuple-element.634), channel_id=1, source_target_pairs={{0,2},{1,3},{2,0},{3,1},{4,6},{5,7},{6,4},{7,5},{8,10},{9,11},{10,... | collective-permute-start | bytes 940040 | tf_op jit(solution)/shard_map/ppermute | solution.py:630
  315.6 16.1 %collective-permute-start.68 = (bf16[136,1152]{1,0:T(8,128)(2,1)}, bf16[136,1152]{1,0:T(8,128)(2,1)S(1)}, u32[]{:S(2)}, u32[]{:S(2)}) collective-permute-start(bf16[136,1152]{1,0:T(8,128)(2,1)} %get-tuple-element.635), channel_id=1, source_target_pairs={{0,4},{1,5},{2,6},{3,7},{4,0},{5,1},{6,2},{7,3},{8,12},{9,13},{10,... | collective-permute-start | bytes 940040 | tf_op jit(solution)/shard_map/ppermute | solution.py:630
  316.3 15.3 %collective-permute-start.69 = (bf16[136,1152]{1,0:T(8,128)(2,1)}, bf16[136,1152]{1,0:T(8,128)(2,1)S(1)}, u32[]{:S(2)}, u32[]{:S(2)}) collective-permute-start(bf16[136,1152]{1,0:T(8,128)(2,1)} %get-tuple-element.636), channel_id=1, source_target_pairs={{0,6},{1,7},{2,4},{3,5},{4,2},{5,3},{6,0},{7,1},{8,14},{9,15},{10,... | collective-permute-start | bytes 940040 | tf_op jit(solution)/shard_map/ppermute | solution.py:630
  334.1 48.7 %collective-permute-start.77 = (bf16[4,144,1122]{2,1,0:T(8,128)(2,1)S(1)}, bf16[4,144,1122]{2,1,0:T(8,128)(2,1)}, u32[]{:S(2)}, u32[]{:S(2)}) collective-permute-start(bf16[4,144,1122]{2,1,0:T(8,128)(2,1)S(1)} %add_convert_fusion.9), channel_id=1, source_target_pairs={{8,16},{16,8},{9,17},{17,9},{10,18},{18,10},{11,19},{19,11},{12,20... | collective-permute-start | bytes 3877640 | tf_op jit(solution)/shard_map/ppermute | solution.py:674
  337.6 45.2 %collective-permute-start.76 = (bf16[4,144,1120]{2,1,0:T(8,128)(2,1)S(1)}, bf16[4,144,1120]{2,1,0:T(8,128)(2,1)}, u32[]{:S(2)}, u32[]{:S(2)}) collective-permute-start(bf16[4,144,1120]{2,1,0:T(8,128)(2,1)S(1)} %add_convert_fusion.10), channel_id=1, source_target_pairs={{8,0},{16,24},{9,1},{17,25},{10,2},{18,26},{11,3},{19,27},{12,4},{... | collective-permute-start | bytes 3870728 | tf_op jit(solution)/shard_map/ppermute | solution.py:674
  342.4 14.3 %collective-permute-start.73 = (bf16[136,1120]{1,0:T(8,128)(2,1)}, bf16[136,1120]{1,0:T(8,128)(2,1)S(1)}, u32[]{:S(2)}, u32[]{:S(2)}) collective-permute-start(bf16[136,1120]{1,0:T(8,128)(2,1)} %get-tuple-element.657.refs_4_), channel_id=1, source_target_pairs={{0,2},{1,3},{2,0},{3,1},{4,6},{5,7},{6,4},{7,5},{8,10},{9,11},{10,... | collective-permute-start | bytes 913928 | tf_op jit(solution)/shard_map/ppermute | solution.py:630
  345.8 54.1 %collective-permute-start.81 = (bf16[4,144,1122]{2,1,0:T(8,128)(2,1)S(1)}, bf16[4,144,1122]{2,1,0:T(8,128)(2,1)}, u32[]{:S(2)}, u32[]{:S(2)}) collective-permute-start(bf16[4,144,1122]{2,1,0:T(8,128)(2,1)S(1)} %add_convert_fusion.11), channel_id=1, source_target_pairs={{0,8},{24,16},{1,9},{25,17},{2,10},{26,18},{3,11},{27,19},{4,12},{... | collective-permute-start | bytes 3877640 | tf_op jit(solution)/shard_map/ppermute | solution.py:674
  356.3 15.3 %collective-permute-start.74 = (bf16[136,1120]{1,0:T(8,128)(2,1)S(1)}, bf16[136,1120]{1,0:T(8,128)(2,1)S(1)}, u32[]{:S(2)}, u32[]{:S(2)}) collective-permute-start(bf16[136,1120]{1,0:T(8,128)(2,1)S(1)} %copy-done.54), channel_id=1, source_target_pairs={{0,4},{1,5},{2,6},{3,7},{4,0},{5,1},{6,2},{7,3},{8,12},{9,13},{10,... | collective-permute-start | bytes 913928 | tf_op jit(solution)/shard_map/ppermute | solution.py:630
  356.7 15.6 %collective-permute-start.75 = (bf16[136,1120]{1,0:T(8,128)(2,1)S(1)}, bf16[136,1120]{1,0:T(8,128)(2,1)}, u32[]{:S(2)}, u32[]{:S(2)}) collective-permute-start(bf16[136,1120]{1,0:T(8,128)(2,1)S(1)} %copy-done.54), channel_id=1, source_target_pairs={{0,6},{1,7},{2,4},{3,5},{4,2},{5,3},{6,0},{7,1},{8,14},{9,15},{10,... | collective-permute-start | bytes 913928 | tf_op jit(solution)/shard_map/ppermute | solution.py:630
  384.5 15.1 %collective-permute-start.78 = (bf16[136,1152]{1,0:T(8,128)(2,1)}, bf16[136,1152]{1,0:T(8,128)(2,1)S(1)}, u32[]{:S(2)}, u32[]{:S(2)}) collective-permute-start(bf16[136,1152]{1,0:T(8,128)(2,1)} %get-tuple-element.681), channel_id=1, source_target_pairs={{0,2},{1,3},{2,0},{3,1},{4,6},{5,7},{6,4},{7,5},{8,10},{9,11},{10,... | collective-permute-start | bytes 940040 | tf_op jit(solution)/shard_map/ppermute | solution.py:630
  384.9 15.0 %collective-permute-start.79 = (bf16[136,1152]{1,0:T(8,128)(2,1)}, bf16[136,1152]{1,0:T(8,128)(2,1)S(1)}, u32[]{:S(2)}, u32[]{:S(2)}) collective-permute-start(bf16[136,1152]{1,0:T(8,128)(2,1)} %get-tuple-element.682), channel_id=1, source_target_pairs={{0,4},{1,5},{2,6},{3,7},{4,0},{5,1},{6,2},{7,3},{8,12},{9,13},{10,... | collective-permute-start | bytes 940040 | tf_op jit(solution)/shard_map/ppermute | solution.py:630
  388.0 31.1 %collective-permute-start.84 = (bf16[4,144,1122]{2,1,0:T(8,128)(2,1)S(1)}, bf16[4,144,1122]{2,1,0:T(8,128)(2,1)S(1)}, u32[]{:S(2)}, u32[]{:S(2)}) collective-permute-start(bf16[4,144,1122]{2,1,0:T(8,128)(2,1)S(1)} %add_convert_fusion.8), channel_id=1, source_target_pairs={{8,0},{16,24},{9,1},{17,25},{10,2},{18,26},{11,3},{19,27},{12,4},{... | collective-permute-start | bytes 3877640 | tf_op jit(solution)/shard_map/ppermute | solution.py:674
  399.9 19.2 %collective-permute-start.82 = (bf16[4,144,1122]{2,1,0:T(8,128)(2,1)}, bf16[4,144,1122]{2,1,0:T(8,128)(2,1)}, u32[]{:S(2)}, u32[]{:S(2)}) collective-permute-start(bf16[4,144,1122]{2,1,0:T(8,128)(2,1)} %get-tuple-element.700), channel_id=1, source_target_pairs={{0,1},{1,0},{2,3},{3,2},{4,5},{5,4},{6,7},{7,6},{8,9},{9,8},{10,11... | collective-permute-start | bytes 3877640 | tf_op jit(solution)/shard_map/ppermute | solution.py:630
  400.0 19.2 %collective-permute-start.83 = (bf16[4,144,1120]{2,1,0:T(8,128)(2,1)}, bf16[4,144,1120]{2,1,0:T(8,128)(2,1)}, u32[]{:S(2)}, u32[]{:S(2)}) collective-permute-start(bf16[4,144,1120]{2,1,0:T(8,128)(2,1)} %get-tuple-element.701), channel_id=1, source_target_pairs={{0,1},{1,0},{2,3},{3,2},{4,5},{5,4},{6,7},{7,6},{8,9},{9,8},{10,11... | collective-permute-start | bytes 3870728 | tf_op jit(solution)/shard_map/ppermute | solution.py:630
  403.2 50.0 %collective-permute-start.88 = (bf16[4,144,1122]{2,1,0:T(8,128)(2,1)}, bf16[4,144,1122]{2,1,0:T(8,128)(2,1)}, u32[]{:S(2)}, u32[]{:S(2)}) collective-permute-start(bf16[4,144,1122]{2,1,0:T(8,128)(2,1)} %add_convert_fusion.7), channel_id=1, source_target_pairs={{8,16},{16,8},{9,17},{17,9},{10,18},{18,10},{11,19},{19,11},{12,20... | collective-permute-start | bytes 3877640 | tf_op jit(solution)/shard_map/ppermute | solution.py:674
  422.4 31.3 %collective-permute-start.89 = (bf16[4,144,1120]{2,1,0:T(8,128)(2,1)}, bf16[4,144,1120]{2,1,0:T(8,128)(2,1)}, u32[]{:S(2)}, u32[]{:S(2)}) collective-permute-start(bf16[4,144,1120]{2,1,0:T(8,128)(2,1)} %add_convert_fusion.6), channel_id=1, source_target_pairs={{0,8},{24,16},{1,9},{25,17},{2,10},{26,18},{3,11},{27,19},{4,12},{... | collective-permute-start | bytes 3870728 | tf_op jit(solution)/shard_map/ppermute | solution.py:674
  435.1 51.4 %collective-permute-start.95 = (bf16[4,144,1122]{2,1,0:T(8,128)(2,1)}, bf16[4,144,1122]{2,1,0:T(8,128)(2,1)}, u32[]{:S(2)}, u32[]{:S(2)}) collective-permute-start(bf16[4,144,1122]{2,1,0:T(8,128)(2,1)} %add_convert_fusion.3), channel_id=1, source_target_pairs={{0,8},{24,16},{1,9},{25,17},{2,10},{26,18},{3,11},{27,19},{4,12},{... | collective-permute-start | bytes 3877640 | tf_op jit(solution)/shard_map/ppermute | solution.py:674
  456.9 29.7 %collective-permute-start.94 = (bf16[4,144,1120]{2,1,0:T(8,128)(2,1)}, bf16[4,144,1120]{2,1,0:T(8,128)(2,1)}, u32[]{:S(2)}, u32[]{:S(2)}) collective-permute-start(bf16[4,144,1120]{2,1,0:T(8,128)(2,1)} %add_convert_fusion.4), channel_id=1, source_target_pairs={{8,16},{16,8},{9,17},{17,9},{10,18},{18,10},{11,19},{19,11},{12,20... | collective-permute-start | bytes 3870728 | tf_op jit(solution)/shard_map/ppermute | solution.py:674
  462.0 34.3 %collective-permute-start.93 = (bf16[4,144,1122]{2,1,0:T(8,128)(2,1)}, bf16[4,144,1122]{2,1,0:T(8,128)(2,1)}, u32[]{:S(2)}, u32[]{:S(2)}) collective-permute-start(bf16[4,144,1122]{2,1,0:T(8,128)(2,1)} %add_convert_fusion.5), channel_id=1, source_target_pairs={{8,0},{16,24},{9,1},{17,25},{10,2},{18,26},{11,3},{19,27},{12,4},{... | collective-permute-start | bytes 3877640 | tf_op jit(solution)/shard_map/ppermute | solution.py:674
  498.4 34.6 %collective-permute-start.99 = (bf16[4,144,1120]{2,1,0:T(8,128)(2,1)S(1)}, bf16[4,144,1120]{2,1,0:T(8,128)(2,1)S(1)}, u32[]{:S(2)}, u32[]{:S(2)}) collective-permute-start(bf16[4,144,1120]{2,1,0:T(8,128)(2,1)S(1)} %add_convert_fusion.1), channel_id=1, source_target_pairs={{8,0},{16,24},{9,1},{17,25},{10,2},{18,26},{11,3},{19,27},{12,4},{... | collective-permute-start | bytes 3870728 | tf_op jit(solution)/shard_map/ppermute | solution.py:674
  501.7 31.3 %collective-permute-start.100 = (bf16[4,144,1122]{2,1,0:T(8,128)(2,1)S(1)}, bf16[4,144,1122]{2,1,0:T(8,128)(2,1)S(1)}, u32[]{:S(2)}, u32[]{:S(2)}) collective-permute-start(bf16[4,144,1122]{2,1,0:T(8,128)(2,1)S(1)} %add_convert_fusion.2), channel_id=1, source_target_pairs={{8,16},{16,8},{9,17},{17,9},{10,18},{18,10},{11,19},{19,11},{12,20... | collective-permute-start | bytes 3877640 | tf_op jit(solution)/shard_map/ppermute | solution.py:674
  505.2 27.8 %collective-permute-start.101 = (bf16[4,144,842]{2,1,0:T(8,128)(2,1)S(1)}, bf16[4,144,842]{2,1,0:T(8,128)(2,1)S(1)}, u32[]{:S(2)}, u32[]{:S(2)}) collective-permute-start(bf16[4,144,842]{2,1,0:T(8,128)(2,1)S(1)} %add_convert_fusion.17), channel_id=1, source_target_pairs={{0,8},{24,16},{1,9},{25,17},{2,10},{26,18},{3,11},{27,19},{4,12},{... | collective-permute-start | bytes 2909960 | tf_op jit(solution)/shard_map/ppermute | solution.py:674
  533.3 31.6 %collective-permute-start.109 = (bf16[4,144,842]{2,1,0:T(8,128)(2,1)S(1)}, bf16[4,144,842]{2,1,0:T(8,128)(2,1)S(1)}, u32[]{:S(2)}, u32[]{:S(2)}) collective-permute-start(bf16[4,144,842]{2,1,0:T(8,128)(2,1)S(1)} %add_convert_fusion.16), channel_id=1, source_target_pairs={{8,16},{16,8},{9,17},{17,9},{10,18},{18,10},{11,19},{19,11},{12,20... | collective-permute-start | bytes 2909960 | tf_op jit(solution)/shard_map/ppermute | solution.py:674
  534.4 36.2 %collective-permute-start.108 = (bf16[4,144,1122]{2,1,0:T(8,128)(2,1)S(1)}, bf16[4,144,1122]{2,1,0:T(8,128)(2,1)}, u32[]{:S(2)}, u32[]{:S(2)}) collective-permute-start(bf16[4,144,1122]{2,1,0:T(8,128)(2,1)S(1)} %add_convert_fusion), channel_id=1, source_target_pairs={{8,0},{16,24},{9,1},{17,25},{10,2},{18,26},{11,3},{19,27},{12,4},{... | collective-permute-start | bytes 3877640 | tf_op jit(solution)/shard_map/ppermute | solution.py:674
  537.3 15.8 %collective-permute-start.104 = (bf16[136,1120]{1,0:T(8,128)(2,1)}, bf16[136,1120]{1,0:T(8,128)(2,1)}, u32[]{:S(2)}, u32[]{:S(2)}) collective-permute-start(bf16[136,1120]{1,0:T(8,128)(2,1)} %get-tuple-element.755), channel_id=1, source_target_pairs={{0,6},{1,7},{2,4},{3,5},{4,2},{5,3},{6,0},{7,1},{8,14},{9,15},{10,... | collective-permute-start | bytes 913928 | tf_op jit(solution)/shard_map/ppermute | solution.py:630
  549.6 15.3 %collective-permute-start.106 = (bf16[144,1122]{1,0:T(8,128)(2,1)}, bf16[144,1122]{1,0:T(8,128)(2,1)S(1)}, u32[]{:S(2)}, u32[]{:S(2)}) collective-permute-start(bf16[144,1122]{1,0:T(8,128)(2,1)} %get-tuple-element.762), channel_id=1, source_target_pairs={{0,4},{1,5},{2,6},{3,7},{4,0},{5,1},{6,2},{7,3},{8,12},{9,13},{10,... | collective-permute-start | bytes 969416 | tf_op jit(solution)/shard_map/ppermute | solution.py:630
  570.9 28.8 %collective-permute-start.116 = (bf16[4,144,842]{2,1,0:T(8,128)(2,1)S(1)}, bf16[4,144,842]{2,1,0:T(8,128)(2,1)S(1)}, u32[]{:S(2)}, u32[]{:S(2)}) collective-permute-start(bf16[4,144,842]{2,1,0:T(8,128)(2,1)S(1)} %add_convert_fusion.15), channel_id=1, source_target_pairs={{8,0},{16,24},{9,1},{17,25},{10,2},{18,26},{11,3},{19,27},{12,4},{... | collective-permute-start | bytes 2909960 | tf_op jit(solution)/shard_map/ppermute | solution.py:674
  576.2 23.3 %collective-permute-start.113 = (bf16[144,1122]{1,0:T(8,128)(2,1)}, bf16[144,1122]{1,0:T(8,128)(2,1)S(1)}, u32[]{:S(2)}, u32[]{:S(2)}) collective-permute-start(bf16[144,1122]{1,0:T(8,128)(2,1)} %get-tuple-element.776), channel_id=1, source_target_pairs={{0,2},{1,3},{2,0},{3,1},{4,6},{5,7},{6,4},{7,5},{8,10},{9,11},{10,... | collective-permute-start | bytes 969416 | tf_op jit(solution)/shard_map/ppermute | solution.py:630
  577.1 22.5 %collective-permute-start.114 = (bf16[144,1122]{1,0:T(8,128)(2,1)}, bf16[144,1122]{1,0:T(8,128)(2,1)S(1)}, u32[]{:S(2)}, u32[]{:S(2)}) collective-permute-start(bf16[144,1122]{1,0:T(8,128)(2,1)} %get-tuple-element.777), channel_id=1, source_target_pairs={{0,4},{1,5},{2,6},{3,7},{4,0},{5,1},{6,2},{7,3},{8,12},{9,13},{10,... | collective-permute-start | bytes 969416 | tf_op jit(solution)/shard_map/ppermute | solution.py:630
  583.0 16.6 %collective-permute-start.115 = (bf16[144,1122]{1,0:T(8,128)(2,1)S(1)}, bf16[144,1122]{1,0:T(8,128)(2,1)S(1)}, u32[]{:S(2)}, u32[]{:S(2)}) collective-permute-start(bf16[144,1122]{1,0:T(8,128)(2,1)S(1)} %get-tuple-element.778), channel_id=1, source_target_pairs={{0,6},{1,7},{2,4},{3,5},{4,2},{5,3},{6,0},{7,1},{8,14},{9,15},{10,... | collective-permute-start | bytes 969416 | tf_op jit(solution)/shard_map/ppermute | solution.py:630
  584.3 15.1 %collective-permute-start.112 = (bf16[144,842]{1,0:T(8,128)(2,1)}, bf16[144,842]{1,0:T(8,128)(2,1)}, u32[]{:S(2)}, u32[]{:S(2)}) collective-permute-start(bf16[144,842]{1,0:T(8,128)(2,1)} %get-tuple-element.773), channel_id=1, source_target_pairs={{0,6},{1,7},{2,4},{3,5},{4,2},{5,3},{6,0},{7,1},{8,14},{9,15},{10,... | collective-permute-start | bytes 727496 | tf_op jit(solution)/shard_map/ppermute | solution.py:630
  601.3 14.3 %collective-permute-start.120 = (bf16[144,1120]{1,0:T(8,128)(2,1)S(1)}, bf16[144,1120]{1,0:T(8,128)(2,1)S(1)}, u32[]{:S(2)}, u32[]{:S(2)}) collective-permute-start(bf16[144,1120]{1,0:T(8,128)(2,1)S(1)} %add_convert_fusion.20), channel_id=1, source_target_pairs={{0,8},{8,0},{16,24},{24,16},{1,9},{9,1},{17,25},{25,17},{2,10},{10... | collective-permute-start | bytes 967688 | tf_op jit(solution)/shard_map/ppermute | solution.py:1119
  (189 other events, 1707.9 us)
